TPU v7x, 128 devices: a whole 4x4x4 slice. The times are simulated.
128 devices in a mesh: gx: 8 (over y, core), gy: 16 (over x, z).
Axes of the slice: x: 4, y: 4, z: 4, core: 2. Of those that a mesh axis runs over, the one named last changes fastest.
Arguments:
- velocity: float32 [3, 6, 2048, 4096], P(None, None, 'gx', 'gy'), may hold values from -6 to 6
- threshold: float32 [2048, 4096], P('gx', 'gy'), may hold values from 0.1 to 2
- dust_mass: float32 [7168, 16, 2, 1024], P(('gx', 'gy')), may hold values from 0 to 2
- settle_speed: float32 [16], replicated, may hold values from 0.02 to 1
- bin_share: float32 [16], replicated, may hold values from 0.02 to 0.3
- active_tiles: int32 [7168], replicated, may hold values from 0 to 8191, as said below
- tile_owner: int32 [7168], replicated, may hold values from 0 to 7167, as said below
Outputs:
- new_velocity: float32 [3, 6, 2048, 4096], P(None, None, 'gx', 'gy')
- dust_out: float32 [7168, 16, 2, 1024], P(('gx', 'gy'))
Inputs may be any that keep to these rules, and one draw needn't show every extreme that they name: `active_tiles`: distinct tiles; the grid part of device (gx, gy) holds the tiles with tx // 8 == gx and ty // 8 == gy. `tile_owner`: One-to-one onto all 7168 slots, devices counted with gx slowest; one device holds at most 1 tile of any one device's grid part, and in every draw some device holds exactly 1 tile from some grid part.
All inputs are finite; a program needn't handle non-finite values.
Results may differ from a plain program's by a relative error of at most 0.0003.
Values sent between devices are 32-bit elements; how exact they have to be, the bound alone decides.
No kernel may reach another device: no remote copies, remote signals or barrier semaphores. Data moves between devices by JAX's collectives and lax.ppermute only.
A program may use at most 192 MiB of HBM per device.

v0:
```python
import jax
import jax.numpy as jnp
from jax import lax
from jax.sharding import PartitionSpec as P

TZ = 2
TILE = 32


time_step = 0.1
viscosity = 0.2
dust_step = 0.1
diffusion = 0.1
roughness = 0.5
emit_rate = 0.5


def shifted(value, axis, steps):
    count = lax.axis_size(axis)
    pairs = [(source, (source + steps) % count) for source in range(count)]
    return lax.ppermute(value, axis, pairs)


def with_halo(x, sides, width):
    for axis, dim in sides:
        peers, length = (lax.axis_size(axis), x.shape[dim])
        up = [(i, (i + 1) % peers) for i in range(peers)]
        down = [(j, i) for i, j in up]
        last = lax.slice_in_dim(x, length - width, length, axis=dim)
        first = lax.slice_in_dim(x, 0, width, axis=dim)
        before = lax.ppermute(last, axis, up)
        after = lax.ppermute(first, axis, down)
        x = jnp.concatenate([before, x, after], axis=dim)
    return x


def advance(padded):
    centre = padded[:, :, 1:-1, 1:-1]
    east_cell = padded[:, :, 2:, 1:-1]
    west_cell = padded[:, :, :-2, 1:-1]
    north_cell = padded[:, :, 1:-1, 2:]
    south_cell = padded[:, :, 1:-1, :-2]
    lower_cell = jnp.concatenate([-centre[:, :1], centre[:, :-1]], axis=1)
    upper_cell = jnp.concatenate([centre[:, 1:], centre[:, -1:]], axis=1)
    carried = 0.5 * (
        centre[0] * (east_cell - west_cell)
        + centre[1] * (north_cell - south_cell)
        + centre[2] * (upper_cell - lower_cell)
    )
    spread = (
        east_cell + west_cell + north_cell + south_cell + upper_cell + lower_cell - 6.0 * centre
    )
    return centre + time_step * (viscosity * spread - carried)


def emission(new_velocity, threshold):
    stress = roughness * (
        new_velocity[0, 0] * new_velocity[0, 0] + new_velocity[1, 0] * new_velocity[1, 0]
    )
    return emit_rate * stress * jnp.maximum(stress - threshold, 0.0)


def edge_strips(dust):
    tile_count, bin_count, layer_count, cell_count = dust.shape
    block_cube = dust.reshape(tile_count, bin_count, layer_count, TILE, TILE)
    return jnp.stack(
        [
            block_cube[:, :, :, 0, :],
            block_cube[:, :, :, -1, :],
            block_cube[:, :, :, :, 0],
            block_cube[:, :, :, :, -1],
        ],
        axis=1,
    )


def upwind(speed, minus, centre, plus):
    return jnp.where(speed > 0, speed * (centre - minus), speed * (plus - centre))


def dust_update(
    dust, low_x, high_x, low_y, high_y, wind_tiles, uplift_tiles, settle_speed, bin_share
):
    tile_count, bin_count, layer_count, cell_count = dust.shape
    block_cube = dust.reshape(tile_count, bin_count, layer_count, TILE, TILE)
    along_x = jnp.concatenate(
        [low_x[:, :, :, None, :], block_cube, high_x[:, :, :, None, :]], axis=3
    )
    along_y = jnp.concatenate(
        [low_y[:, :, :, :, None], block_cube, high_y[:, :, :, :, None]], axis=4
    )
    ground_zero = jnp.zeros_like(block_cube[:, :, :1])
    lower_cell = jnp.concatenate([ground_zero, block_cube[:, :, :-1]], axis=2)
    upper_cell = jnp.concatenate([block_cube[:, :, 1:], ground_zero], axis=2)
    west_cell = along_x[:, :, :, :-2]
    east_cell = along_x[:, :, :, 2:]
    south_cell = along_y[:, :, :, :, :-2]
    north_cell = along_y[:, :, :, :, 2:]
    shaped = wind_tiles.reshape(tile_count, 3, 1, layer_count, TILE, TILE)
    speed_east = shaped[:, 0]
    speed_north = shaped[:, 1]
    speed_up = shaped[:, 2] - settle_speed[None, :, None, None, None]
    carried = (
        upwind(speed_east, west_cell, block_cube, east_cell)
        + upwind(speed_north, south_cell, block_cube, north_cell)
        + upwind(speed_up, lower_cell, block_cube, upper_cell)
    )
    spread = (
        west_cell + east_cell + south_cell + north_cell + lower_cell + upper_cell - 6.0 * block_cube
    )
    source = uplift_tiles.reshape(tile_count, 1, TILE, TILE) * bin_share[None, :, None, None]
    lifted = jnp.concatenate([source[:, :, None], jnp.zeros_like(block_cube[:, :, 1:])], axis=2)
    return (block_cube + dust_step * (diffusion * spread - carried + lifted)).reshape(dust.shape)


def take_rows(table, index, valid):
    taken = jnp.take(table, jnp.maximum(index, 0), axis=0)
    return jnp.where(valid.reshape((-1,) + (1,) * (table.ndim - 1)), taken, 0.0)


def relay_rows(rows):
    return lax.all_to_all(rows, ("gx", "gy"), split_axis=0, concat_axis=0, tiled=True)


def border_ghosts(edge_grid):
    from_west = shifted(edge_grid[-1, :, 1], "gx", 1)
    from_east = shifted(edge_grid[0, :, 0], "gx", -1)
    from_south = shifted(edge_grid[:, -1, 3], "gy", 1)
    from_north = shifted(edge_grid[:, 0, 2], "gy", -1)
    low_x = jnp.concatenate([from_west[None], edge_grid[:-1, :, 1]], axis=0)
    high_x = jnp.concatenate([edge_grid[1:, :, 0], from_east[None]], axis=0)
    low_y = jnp.concatenate([from_south[:, None], edge_grid[:, :-1, 3]], axis=1)
    high_y = jnp.concatenate([edge_grid[:, 1:, 2], from_north[:, None]], axis=1)
    return jnp.stack([low_x, high_x, low_y, high_y], axis=2)


def per_device(velocity, threshold, dust_mass, settle_speed, bin_share, active_tiles, tile_owner):
    padded = with_halo(velocity, (("gx", 2), ("gy", 3)), 1)
    new_velocity = advance(padded)
    uplift = emission(new_velocity, threshold)
    owners = lax.axis_size(("gx", "gy"))
    grid_cols = lax.axis_size("gy")
    self_index = lax.axis_index(("gx", "gy"))
    slot_count = dust_mass.shape[0]
    bin_count = dust_mass.shape[1]
    tiles_x = velocity.shape[2] // TILE
    tiles_y = velocity.shape[3] // TILE
    per_home = tiles_x * tiles_y
    per_pair = (per_home + owners - 1) // owners
    rows_total = owners * per_pair
    tiles_across = tiles_y * grid_cols
    tile_x = active_tiles // tiles_across
    tile_y = active_tiles % tiles_across
    home_dev = tile_x // tiles_x * grid_cols + tile_y // tiles_y
    local_tile = tile_x % tiles_x * tiles_y + tile_y % tiles_y
    marked = jnp.where(home_dev == self_index, local_tile + 1, 0)
    inverse = jnp.argsort(tile_owner)
    slot_grid = jnp.take(marked, inverse).reshape(owners, slot_count)
    present = slot_grid > 0
    running = jnp.cumsum(present.astype(jnp.int32), axis=1)
    rank_ids = jnp.arange(per_pair, dtype=jnp.int32)
    matched = present[:, :, None] & (running[:, :, None] == rank_ids[None, None, :] + 1)
    pick_rows = (jnp.sum(jnp.where(matched, slot_grid[:, :, None], 0), axis=1) - 1).reshape(
        rows_total
    )
    pick_valid = pick_rows >= 0
    home_full = jnp.take(home_dev, inverse)
    my_homes = lax.dynamic_slice_in_dim(home_full, self_index * slot_count, slot_count)
    slot_ids = jnp.arange(slot_count, dtype=jnp.int32)
    earlier = (my_homes[None, :] == my_homes[:, None]) & (slot_ids[None, :] < slot_ids[:, None])
    recv_row = my_homes * per_pair + jnp.sum(earlier.astype(jnp.int32), axis=1)
    row_ids = jnp.arange(rows_total, dtype=jnp.int32)
    to_home = recv_row[None, :] == row_ids[:, None]
    back_valid = jnp.any(to_home, axis=1)
    back_slot = jnp.sum(jnp.where(to_home, slot_ids[None, :], 0), axis=1)
    home_tiles = jnp.arange(per_home, dtype=jnp.int32)
    from_row = pick_rows[None, :] == home_tiles[:, None]
    local_valid = jnp.any(from_row, axis=1)
    local_row = jnp.sum(jnp.where(from_row, row_ids[None, :], 0), axis=1)
    wind_home = (
        new_velocity[:, :TZ]
        .reshape(3, TZ, tiles_x, TILE, tiles_y, TILE)
        .transpose(2, 4, 0, 1, 3, 5)
        .reshape(per_home, 3, TZ, TILE * TILE)
    )
    uplift_home = (
        uplift.reshape(tiles_x, TILE, tiles_y, TILE)
        .transpose(0, 2, 1, 3)
        .reshape(per_home, TILE * TILE)
    )
    wind_recv, uplift_recv = (
        lax.all_to_all(
            take_rows(wind_home, pick_rows, pick_valid),
            ("gx", "gy"),
            split_axis=0,
            concat_axis=0,
            tiled=True,
        ),
        lax.all_to_all(
            take_rows(uplift_home, pick_rows, pick_valid),
            ("gx", "gy"),
            split_axis=0,
            concat_axis=0,
            tiled=True,
        ),
    )
    wind_tiles = jnp.take(wind_recv, recv_row, axis=0)
    uplift_tiles = jnp.take(uplift_recv, recv_row, axis=0)
    dust = dust_mass
    for substep in range(2):
        edge_rows = edge_strips(dust).reshape(slot_count, -1)
        at_home = relay_rows(take_rows(edge_rows, back_slot, back_valid))
        edge_grid = take_rows(at_home, local_row, local_valid).reshape(tiles_x, tiles_y, 4, -1)
        ghosts = border_ghosts(edge_grid).reshape(per_home, -1)
        returned = relay_rows(take_rows(ghosts, pick_rows, pick_valid))
        my_rims = jnp.take(returned, recv_row, axis=0).reshape(slot_count, 4, bin_count, TZ, TILE)
        dust = dust_update(
            dust,
            my_rims[:, 0],
            my_rims[:, 1],
            my_rims[:, 2],
            my_rims[:, 3],
            wind_tiles,
            uplift_tiles,
            settle_speed,
            bin_share,
        )
    return (new_velocity, dust)


def solution(mesh):
    in_specs = (
        P(None, None, "gx", "gy"),
        P("gx", "gy"),
        P(("gx", "gy"), None, None, None),
        P(),
        P(),
        P(),
        P(),
    )
    out_specs = (P(None, None, "gx", "gy"), P(("gx", "gy"), None, None, None))
    return jax.shard_map(
        per_device, mesh=mesh, in_specs=in_specs, out_specs=out_specs, check_vma=False
    )
```

profile of v0, /device:TPU:1, one launch (start us, length us, event | category | flops | bytes accessed | tf_op | source)
XLA Modules:
  0.0 575.6 jit_solution(7370933437251639910)
XLA Ops:
  5.0 7.4 %sort.17 = (s32[7168]{0:T(1024)}, s32[7168]{0:T(1024)S(1)}) sort(s32[7168]{0:T(1024)} %param.23, s32[7168]{0:T(1024)S(1)} %iota.23), dimensions={0}, to_apply=%region_0.1 | sort | flops 93184 | bytes 114688 | tf_op jit(solution)/shard_map/jit(argsort)/sort | solution.py:157
  13.2 39.9 %gather_fusion.4 = s32[7168]{0:T(1024)S(1)} fusion(s32[7168]{0:T(1024)S(1)} %get-tuple-element.23, s32[7168]{0:T(1024)S(1)} %get-tuple-element.78), kind=kCustom, calls=%fused_computation.clone | custom fusion | bytes 86016 | tf_op jit(solution)/shard_map/jit(_take)/gather | solution.py:158
  53.1 39.9 %gather_fusion.5 = s32[7168]{0:T(1024)S(1)} fusion(s32[7168]{0:T(1024)S(1)} %get-tuple-element.24, s32[7168]{0:T(1024)S(1)} %get-tuple-element.78), kind=kCustom, calls=%fused_computation.5.clone | custom fusion | bytes 86016 | tf_op jit(solution)/shard_map/jit(_take)/gather | solution.py:167
  106.5 15.4 %copy.205 = f32[56,16,2,1024]{0,3,2,1:T(8,128)} copy(f32[56,16,2,1024]{3,2,1,0:T(2,128)} %param.19) | data formatting | bytes 14680064 | tf_op args[2]
  158.4 19.1 %multiply_add_fusion.1 = f32[3,6,256,256]{3,2,1,0:T(8,128)S(1)} fusion(f32[3,6,256,256]{3,2,1,0:T(8,128)} %param.17, f32[3,5,256,256]{3,2,1,0:T(8,128)} %get-tuple-element.45, f32[3,1,256,256]{3,2,1,0:T(8,128)} %get-tuple-element.47, f32[3,1,256,256]{3,2,1,0:T(8,128)S(1)} %copy-done.5, f32[3,5,256,256]{3,2,1,0:T(8,128)} %get-tuple-element.44, ...), kind=kLoop, calls=%fused_computation.89 | loop fusion | flops 35389440 | bytes 23666976 | tf_op jit(solution)/shard_map/add | solution.py:53
  183.0 6.5 %all-to-all-start.3 = ((f32[128,1,1024]{2,1,0:T(1,128)}), f32[128,1,1024]{2,1,0:T(1,128)S(1)}, u32[]{:S(2)}, u32[]{:S(2)}) async-start(f32[128,1,1024]{2,1,0:T(1,128)} %copy.226), calls=%async_computation.3 | async-start | bytes 1048576 | tf_op jit(solution)/shard_map/all_to_all | solution.py:199
  189.7 13.3 %all-to-all-done.3 = f32[128,1,1024]{2,1,0:T(1,128)S(1)} async-done(((f32[128,1,1024]{2,1,0:T(1,128)}), f32[128,1,1024]{2,1,0:T(1,128)S(1)}, u32[]{:S(2)}, u32[]{:S(2)}) %all-to-all-start.3) | async-done | bytes 524320 | tf_op jit(solution)/shard_map/all_to_all | solution.py:199
  202.9 6.1 %all-to-all-start = ((f32[128,1,4096]{2,1,0:T(1,128)}), f32[128,1,4096]{2,1,0:T(1,128)}, u32[]{:S(2)}, u32[]{:S(2)}) async-start(f32[128,1,4096]{2,1,0:T(1,128)} %copy.212), calls=%async_computation | async-start | bytes 4194304 | tf_op jit(solution)/shard_map/all_to_all | solution.py:122
  209.2 10.7 %fusion.69 = (f32[56,16,1,32,32]{0,4,3,2,1:T(8,128)}, f32[56,16,1,32,32]{0,4,3,2,1:T(8,128)}) fusion(f32[56,16,2,32,32]{0,4,3,2,1:T(8,128)} %bitcast.181), kind=kLoop, calls=%fused_computation.229 | loop fusion | bytes 14680064 | tf_op jit(solution)/shard_map/slice | solution.py:93
  223.5 6.5 %copy.240 = f32[8,8,3,2,32,32]{5,4,3,2,1,0:T(8,128)} copy(f32[8,8,3,2,32,32]{5,1,4,0,3,2:T(8,128)} %bitcast.192) | data formatting | bytes 3145728 | tf_op jit(solution)/shard_map/reshape | solution.py:184
  230.1 5.4 reshape.436
  235.4 5.4 gather_fusion
  240.8 6.0 %select_select_fusion = f32[128,3,2,1024]{3,2,1,0:T(2,128)} fusion(f32[128,3,2,1024]{3,2,1,0:T(2,128)} %gather_fusion, pred[128]{0:T(512)(128)(4,1)S(1)} %get-tuple-element.77, pred[128]{0:T(512)(128)(4,1)S(1)} %get-tuple-element.76), kind=kLoop, calls=%fused_computation.91 | loop fusion | flops 1572864 | bytes 6291712 | tf_op jit(solution)/shard_map/jit(_where)/select_n | solution.py:118
  248.6 10.7 %all-to-all-start.2 = ((f32[128,3,2,1024]{3,2,1,0:T(2,128)}), f32[128,3,2,1024]{3,2,1,0:T(2,128)}, u32[]{:S(2)}, u32[]{:S(2)}) async-start(f32[128,3,2,1024]{3,2,1,0:T(2,128)} %select_select_fusion), calls=%async_computation.2 | async-start | bytes 6291456 | tf_op jit(solution)/shard_map/all_to_all | solution.py:192
  271.2 27.8 %collective-permute-done.6 = f32[8,1024]{1,0:T(8,128)S(1)} collective-permute-done((f32[8,1024]{1,0:T(8,128)S(1)}, f32[8,1024]{1,0:T(8,128)S(1)}, u32[]{:S(2)}, u32[]{:S(2)}) %collective-permute-start.6) | collective-permute-done | bytes 32800 | tf_op jit(solution)/shard_map/ppermute | solution.py:21
  304.6 6.9 %all-to-all-start.1 = ((f32[128,1,4096]{2,1,0:T(1,128)}), f32[128,1,4096]{2,1,0:T(1,128)}, u32[]{:S(2)}, u32[]{:S(2)}) async-start(f32[128,1,4096]{2,1,0:T(1,128)} %copy.219), calls=%async_computation.1 | async-start | bytes 4194304 | tf_op jit(solution)/shard_map/all_to_all | solution.py:122
  327.0 13.6 %all-to-all-done.1 = f32[128,1,4096]{2,1,0:T(1,128)} async-done(((f32[128,1,4096]{2,1,0:T(1,128)}), f32[128,1,4096]{2,1,0:T(1,128)}, u32[]{:S(2)}, u32[]{:S(2)}) %all-to-all-start.1) | async-done | bytes 2097184 | tf_op jit(solution)/shard_map/all_to_all | solution.py:122
  352.9 43.0 %multiply_add_fusion = f32[56,16,2,32,32]{0,4,3,2,1:T(8,128)} fusion(f32[56,16,2,32,32]{0,4,3,2,1:T(8,128)} %bitcast.182, f32[56,16,1,32,32]{0,4,3,2,1:T(8,128)} %broadcast_multiply_fusion, f32[56,16,1,32,32]{0,4,3,2,1:T(8,128)} %get-tuple-element.36, f32[56,16,1,32,32]{0,4,3,2,1:T(8,128)} %get-tuple-element.35, f32[56,16,2,32,1]{0,4,3,2,1:T(1,128)S(1)} %bitcast.209, ...), kind=kLoop, calls=%fused_computation.77 | loop fusion | flops 64225280 | bytes 28213312 | tf_op jit(solution)/shard_map/add | solution.py:113
  412.0 34.1 %all_to_all.62 = f32[128,1,4096]{2,1,0:T(1,128)S(1)} all-to-all(f32[128,1,4096]{2,1,0:T(1,128)S(1)} %copy.230), channel_id=1, replica_groups=mesh['gx'=8,'gy'=16] {'gx','gy'}, dimensions={0} | all-to-all | bytes 4194304 | tf_op jit(solution)/shard_map/all_to_all | solution.py:122
  470.0 5.5 all-to-all-start.5
  475.6 10.6 %fusion.67 = (f32[56,16,1,32,32]{0,4,3,2,1:T(8,128)}, f32[56,16,1,32,32]{0,4,3,2,1:T(8,128)}) fusion(f32[56,16,2,32,32]{0,4,3,2,1:T(8,128)} %multiply_add_fusion), kind=kLoop, calls=%fused_computation.227 | loop fusion | bytes 14680064 | tf_op jit(solution)/shard_map/slice | solution.py:94
  486.2 18.7 %all-to-all-done.5 = f32[128,1,4096]{2,1,0:T(1,128)} async-done(((f32[128,1,4096]{2,1,0:T(1,128)}), f32[128,1,4096]{2,1,0:T(1,128)}, u32[]{:S(2)}, u32[]{:S(2)}) %all-to-all-start.5) | async-done | bytes 2097184 | tf_op jit(solution)/shard_map/all_to_all | solution.py:122
  517.2 42.5 %fusion.9 = f32[56,16,2,32,32]{0,4,3,2,1:T(8,128)} fusion(f32[56,16,2,32,32]{0,4,3,2,1:T(8,128)} %multiply_add_fusion, f32[56,16,1,32,32]{0,4,3,2,1:T(8,128)} %broadcast_multiply_fusion, f32[56,16,1,32,32]{0,4,3,2,1:T(8,128)} %get-tuple-element.30, f32[56,16,1,32,32]{0,4,3,2,1:T(8,128)} %get-tuple-element.29, f32[56,16,2,32,1]{0,4,3,2,1:T(1,128)S(1)} %bitcast.207, ...), kind=kLoop, calls=%fused_computation.38 | loop fusion | flops 64225280 | bytes 28213312 | tf_op jit(solution)/shard_map/add | solution.py:113
  559.7 15.7 %copy.239 = f32[56,16,2,1024]{3,2,1,0:T(2,128)} copy(f32[56,16,2,1024]{0,3,2,1:T(8,128)} %bitcast.185) | data formatting | bytes 14680064
  (185 shorter events, 163.3 us)
Async XLA Ops:
  2.3 131.9 %collective-permute-start.1 = (f32[3,6,1,256]{3,2,1,0:T(1,128)}, f32[3,6,1,256]{3,2,1,0:T(1,128)}, u32[]{:S(2)}, u32[]{:S(2)}) collective-permute-start(f32[3,6,1,256]{3,2,1,0:T(1,128)} %get-tuple-element.42), channel_id=1, source_target_pairs={{0,16},{16,32},{32,48},{48,64},{64,80},{80,96},{96,112},{112,0},{1... | collective-permute-start | bytes 55304 | tf_op jit(solution)/shard_map/ppermute | solution.py:31
  4.9 129.2 %collective-permute-start = (f32[3,6,1,256]{3,2,1,0:T(1,128)}, f32[3,6,1,256]{3,2,1,0:T(1,128)}, u32[]{:S(2)}, u32[]{:S(2)}) collective-permute-start(f32[3,6,1,256]{3,2,1,0:T(1,128)} %get-tuple-element.43), channel_id=1, source_target_pairs={{16,0},{32,16},{48,32},{64,48},{80,64},{96,80},{112,96},{0,112},{1... | collective-permute-start | bytes 55304 | tf_op jit(solution)/shard_map/ppermute | solution.py:32
  93.3 9.0 %copy-start.14 = (s32[56]{0:T(128)}, s32[56]{0:T(128)S(1)}, u32[]{:S(2)}) copy-start(s32[56]{0:T(128)S(1)} %get-tuple-element.20) | copy-start | bytes 676
  143.6 14.8 %copy-start.5 = (f32[3,1,256,256]{3,2,1,0:T(8,128)S(1)}, f32[3,1,256,256]{3,2,1,0:T(8,128)}, u32[]{:S(2)}) copy-start(f32[3,1,256,256]{3,2,1,0:T(8,128)} %get-tuple-element.46) | copy-start | bytes 2359300
  143.6 12.5 %collective-permute-start.3 = (f32[3,6,258,1]{2,1,3,0:T(8,128)S(1)}, f32[3,6,258,1]{2,1,3,0:T(8,128)S(1)}, u32[]{:S(2)}, u32[]{:S(2)}) collective-permute-start(f32[3,6,258,1]{2,1,3,0:T(8,128)S(1)} %copy.203), channel_id=1, source_target_pairs={{0,1},{1,2},{2,3},{3,4},{4,5},{5,6},{6,7},{7,8},{8,9},{9,10},{10,1... | collective-permute-start | bytes 55736 | tf_op jit(solution)/shard_map/ppermute | solution.py:31
  145.3 10.0 %collective-permute-start.2 = (f32[3,6,258,1]{2,1,3,0:T(8,128)S(1)}, f32[3,6,258,1]{2,1,3,0:T(8,128)S(1)}, u32[]{:S(2)}, u32[]{:S(2)}) collective-permute-start(f32[3,6,258,1]{2,1,3,0:T(8,128)S(1)} %copy.201), channel_id=1, source_target_pairs={{1,0},{2,1},{3,2},{4,3},{5,4},{6,5},{7,6},{8,7},{9,8},{10,9},{11,1... | collective-permute-start | bytes 55736 | tf_op jit(solution)/shard_map/ppermute | solution.py:32
  158.4 21.3 %copy-start.7 = (f32[256,256]{1,0:T(8,128)S(1)}, f32[256,256]{1,0:T(8,128)}, u32[]{:S(2)}) copy-start(f32[256,256]{1,0:T(8,128)} %param.18) | copy-start | bytes 786436
  180.2 9.4 %copy-start.15 = (s32[56]{0:T(128)S(1)}, s32[56]{0:T(128)}, u32[]{:S(2)}) copy-start(s32[56]{0:T(128)} %copy-done.14) | copy-start | bytes 676
  183.0 19.9 %all-to-all-start.3 = ((f32[128,1,1024]{2,1,0:T(1,128)}), f32[128,1,1024]{2,1,0:T(1,128)S(1)}, u32[]{:S(2)}, u32[]{:S(2)}) async-start(f32[128,1,1024]{2,1,0:T(1,128)} %copy.226), calls=%async_computation.3 | async-start | bytes 1048576 | tf_op jit(solution)/shard_map/all_to_all | solution.py:199
  202.9 45.7 %all-to-all-start = ((f32[128,1,4096]{2,1,0:T(1,128)}), f32[128,1,4096]{2,1,0:T(1,128)}, u32[]{:S(2)}, u32[]{:S(2)}) async-start(f32[128,1,4096]{2,1,0:T(1,128)} %copy.212), calls=%async_computation | async-start | bytes 4194304 | tf_op jit(solution)/shard_map/all_to_all | solution.py:122
  209.2 10.7 %slice-start.2 = ((f32[3,6,256,256]{3,2,1,0:T(8,128)}), f32[3,2,256,256]{3,2,1,0:T(8,128)S(1)}, s32[]{:S(2)}) async-start(f32[3,6,256,256]{3,2,1,0:T(8,128)} %copy-done), calls=%async_computation.8 | async-start | bytes 3145728 | tf_op jit(solution)/shard_map/slice | solution.py:181
  248.6 56.0 %all-to-all-start.2 = ((f32[128,3,2,1024]{3,2,1,0:T(2,128)}), f32[128,3,2,1024]{3,2,1,0:T(2,128)}, u32[]{:S(2)}, u32[]{:S(2)}) async-start(f32[128,3,2,1024]{3,2,1,0:T(2,128)} %select_select_fusion), calls=%async_computation.2 | async-start | bytes 6291456 | tf_op jit(solution)/shard_map/all_to_all | solution.py:192
  263.7 35.2 %collective-permute-start.6 = (f32[8,1024]{1,0:T(8,128)S(1)}, f32[8,1024]{1,0:T(8,128)S(1)}, u32[]{:S(2)}, u32[]{:S(2)}) collective-permute-start(f32[8,1024]{1,0:T(8,128)S(1)} %bitcast.220), channel_id=1, source_target_pairs={{0,1},{1,2},{2,3},{3,4},{4,5},{5,6},{6,7},{7,8},{8,9},{9,10},{10,1... | collective-permute-start | bytes 98312 | tf_op jit(solution)/shard_map/ppermute | solution.py:21
  265.4 33.7 %collective-permute-start.7 = (f32[8,1024]{1,0:T(8,128)S(1)}, f32[8,1024]{1,0:T(8,128)S(1)}, u32[]{:S(2)}, u32[]{:S(2)}) collective-permute-start(f32[8,1024]{1,0:T(8,128)S(1)} %bitcast.221), channel_id=1, source_target_pairs={{0,15},{1,0},{2,1},{3,2},{4,3},{5,4},{6,5},{7,6},{8,7},{9,8},{10,9... | collective-permute-start | bytes 98312 | tf_op jit(solution)/shard_map/ppermute | solution.py:21
  269.4 29.6 %collective-permute-start.4 = (f32[8,1024]{1,0:T(8,128)S(1)}, f32[8,1024]{1,0:T(8,128)S(1)}, u32[]{:S(2)}, u32[]{:S(2)}) collective-permute-start(f32[8,1024]{1,0:T(8,128)S(1)} %get-tuple-element.66), channel_id=1, source_target_pairs={{0,16},{16,32},{32,48},{48,64},{64,80},{80,96},{96,112},{112,0},{1... | collective-permute-start | bytes 98312 | tf_op jit(solution)/shard_map/ppermute | solution.py:21
  271.2 28.0 %collective-permute-start.5 = (f32[8,1024]{1,0:T(8,128)S(1)}, f32[8,1024]{1,0:T(8,128)S(1)}, u32[]{:S(2)}, u32[]{:S(2)}) collective-permute-start(f32[8,1024]{1,0:T(8,128)S(1)} %get-tuple-element.67), channel_id=1, source_target_pairs={{0,112},{16,0},{32,16},{48,32},{64,48},{80,64},{96,80},{112,96},{1... | collective-permute-start | bytes 98312 | tf_op jit(solution)/shard_map/ppermute | solution.py:21
  301.1 10.4 %copy-start.6 = (f32[56,32,32]{0,2,1:T(8,128)S(1)}, f32[56,32,32]{0,2,1:T(8,128)}, u32[]{:S(2)}) copy-start(f32[56,32,32]{0,2,1:T(8,128)} %broadcast_select_fusion.3) | copy-start | bytes 688132
  301.1 10.4 %copy-start.11 = (f32[16]{0:T(128)S(1)}, f32[16]{0:T(128)}, u32[]{:S(2)}) copy-start(f32[16]{0:T(128)} %param.21) | copy-start | bytes 196
  304.6 36.0 %all-to-all-start.1 = ((f32[128,1,4096]{2,1,0:T(1,128)}), f32[128,1,4096]{2,1,0:T(1,128)}, u32[]{:S(2)}, u32[]{:S(2)}) async-start(f32[128,1,4096]{2,1,0:T(1,128)} %copy.219), calls=%async_computation.1 | async-start | bytes 4194304 | tf_op jit(solution)/shard_map/all_to_all | solution.py:122
  451.1 7.1 %collective-permute-start.10 = (f32[8,1024]{1,0:T(8,128)S(1)}, f32[8,1024]{1,0:T(8,128)S(1)}, u32[]{:S(2)}, u32[]{:S(2)}) collective-permute-start(f32[8,1024]{1,0:T(8,128)S(1)} %bitcast.225), channel_id=1, source_target_pairs={{0,1},{1,2},{2,3},{3,4},{4,5},{5,6},{6,7},{7,8},{8,9},{9,10},{10,1... | collective-permute-start | bytes 98312 | tf_op jit(solution)/shard_map/ppermute | solution.py:21
  451.7 7.5 %collective-permute-start.11 = (f32[8,1024]{1,0:T(8,128)S(1)}, f32[8,1024]{1,0:T(8,128)S(1)}, u32[]{:S(2)}, u32[]{:S(2)}) collective-permute-start(f32[8,1024]{1,0:T(8,128)S(1)} %bitcast.223), channel_id=1, source_target_pairs={{0,15},{1,0},{2,1},{3,2},{4,3},{5,4},{6,5},{7,6},{8,7},{9,8},{10,9... | collective-permute-start | bytes 98312 | tf_op jit(solution)/shard_map/ppermute | solution.py:21
  456.3 3.0 collective-permute-start.8
  458.2 3.6 collective-permute-start.9
  470.0 34.8 %all-to-all-start.5 = ((f32[128,1,4096]{2,1,0:T(1,128)}), f32[128,1,4096]{2,1,0:T(1,128)}, u32[]{:S(2)}, u32[]{:S(2)}) async-start(f32[128,1,4096]{2,1,0:T(1,128)} %copy.237), calls=%async_computation.5 | async-start | bytes 4194304 | tf_op jit(solution)/shard_map/all_to_all | solution.py:122
  (12 other events, 58.5 us)
where the time goes:
time: 586 us; the launch traced here: 576 us
  local copies, waits for them, and re-layouts  254 us (43%)
  other arithmetic  150 us (26%)
  waiting for transfers between devices  76.8 us (13%)
  starting transfers between devices  59.4 us (10%)
  blocking collectives  34.1 us (6%)
    add x2, other arithmetic, dust_update(): block_cube + dust_step * (diffusion * spread - carried + lifted)  85.5 us
    unnamed x47, local copies, waits for them, and re-layouts  44.8 us
    gather x1, local copies, waits for them, and re-layouts, per_device(): slot_grid = jnp.take(marked, inverse).reshape(owners, slot_count)  39.9 us
    gather x1, local copies, waits for them, and re-layouts, per_device(): home_full = jnp.take(home_dev, inverse)  39.9 us
    all_to_all x1, blocking collectives, relay_rows(): lax.all_to_all(rows, ('gx', 'gy'), split_axis=0, concat_axis=0, tiled=True)  34.1 us
    all_to_all x3, waiting for transfers between devices, relay_rows(): lax.all_to_all(rows, ('gx', 'gy'), split_axis=0, concat_axis=0, tiled=True)  32.3 us
    ppermute x8, waiting for transfers between devices, shifted(): return lax.ppermute(value, axis, pairs)  31.2 us
    add x1, other arithmetic, advance(): return centre + time_step * (viscosity * spread - carried)  19.1 us
  transfers between devices with their start and end apart: 17, of which 6 were waited for; matrix products, arithmetic and copies ran while one was open for 37% of the time, Pallas kernels for 0%

commit v1 on v0

v1 whole, which is shorter than its diff:
```python
import functools

import jax
import jax.numpy as jnp
from jax import lax
from jax.experimental import pallas as pl
from jax.experimental.pallas import tpu as pltpu
from jax.sharding import PartitionSpec as P

TZ = 2
TILE = 32
LANES = 128
ROWS = TILE * TILE // LANES
PLANES = 7
AXES = ("gx", "gy")

time_step = 0.1
viscosity = 0.2
dust_step = 0.1
diffusion = 0.1
roughness = 0.5
emit_rate = 0.5

WEST, SOUTH, NORTH, EAST = range(4)


def iotas(shape=(ROWS, LANES)):
    return lax.broadcasted_iota(jnp.int32, shape, 0), lax.broadcasted_iota(jnp.int32, shape, 1)


def lane_gather(x, index):
    return jnp.take_along_axis(x, index, axis=1)


def ring_pattern(depth):
    row, lane = iotas()
    group, within = lane // TILE, lane % TILE
    side = jnp.where(group == SOUTH, depth, TILE - 1 - depth)
    index = (within % 4) * TILE + side
    index = jnp.where(group == WEST, depth * TILE + within, index)
    index = jnp.where(group == EAST, (3 - depth) * TILE + within, index)
    source = jnp.where(group == WEST, 0, jnp.where(group == EAST, ROWS - 1, within // 4))
    return index, row == source


def ring_of(x, pattern):
    index, taken = pattern
    return jnp.sum(jnp.where(taken, lane_gather(x, index), 0.0), axis=0, keepdims=True)


def spread_rows(row):
    return jnp.broadcast_to(row, (ROWS, LANES))


def strips_kernel(home_ref, dust_ref, send_ref, rings, sems, *, block, bins):
    step = pl.program_id(0)
    slots = rings.shape[0]
    patterns = [ring_pattern(0), ring_pattern(1)]

    def one(j, carry):
        s = step * block + j
        for b in range(bins):
            for level in range(TZ):
                x = dust_ref[j, b, pl.ds(level, ROWS, stride=TZ), :]
                for depth in range(2):
                    at = depth * bins * TZ + b * TZ + level
                    rings[s, at : at + 1, :] = ring_of(x, patterns[depth])
        pltpu.make_async_copy(rings.at[s], send_ref.at[home_ref[s]], sems.at[s]).start()
        return carry

    lax.fori_loop(0, block, one, 0)

    @pl.when(step == pl.num_programs(0) - 1)
    def _():
        def wait(s, carry):
            pltpu.make_async_copy(rings.at[s], send_ref.at[home_ref[s]], sems.at[s]).wait()
            return carry

        lax.fori_loop(0, slots, wait, 0)


def dust_strips(home_of_slot, dust, owners):
    slots, bins = dust.shape[:2]
    block = 8 if slots % 8 == 0 else 4
    rows = 2 * bins * TZ
    return pl.pallas_call(
        functools.partial(strips_kernel, block=block, bins=bins),
        grid=(slots // block,),
        in_specs=[
            pl.BlockSpec(memory_space=pltpu.SMEM),
            pl.BlockSpec((block,) + dust.shape[1:], lambda i: (i, 0, 0, 0)),
        ],
        out_specs=pl.BlockSpec(memory_space=pl.ANY),
        out_shape=jax.ShapeDtypeStruct((owners, rows, LANES), jnp.float32),
        scratch_shapes=[
            pltpu.VMEM((slots, rows, LANES), jnp.float32),
            pltpu.SemaphoreType.DMA((slots,)),
        ],
        compiler_params=pltpu.CompilerParams(vmem_limit_bytes=32 << 20),
        cost_estimate=pl.CostEstimate(
            flops=20 * dust.size, bytes_accessed=dust.size * 4 + slots * rows * LANES * 4, transcendentals=0
        ),
        name="dust_strips",
    )(home_of_slot, dust)


def wind_kernel(
    owner_ref, vel_ref, xlo_ref, xhi_ref, ylo_ref, yhi_ref, thr_ref,
    new_ref, send_ref, ring_ref, padded, strip, tiles, load_sem, sems, *, levels
):
    fields, nx, ny = new_ref.shape
    load = pltpu.make_async_copy(vel_ref, padded.at[:, pl.ds(8, nx), :], load_sem)
    load.start()
    load.wait()
    padded[:, 7:8, :] = xlo_ref[...]
    padded[:, 8 + nx : 9 + nx, :] = xhi_ref[...]
    half = 16
    halves = ny // LANES
    tiles_y = ny // TILE
    pattern = ring_pattern(0)
    _, lane8 = iotas()
    group = lane8 // TILE

    def one_strip(ix, carry):
        for sub in range(TILE // half):
            base = pl.multiple_of(ix * TILE + sub * half, 8)
            lane = lax.broadcasted_iota(jnp.int32, (half, ny), 1)
            low = {}
            for z in range(levels):
                u, v, w = (padded[c * levels + z, pl.ds(base + 8, half), :] for c in range(3))
                for c in range(3):
                    f = c * levels + z
                    block = padded[f, pl.ds(base, half + 16), :]
                    centre = (u, v, w)[c]
                    west = pltpu.roll(block, 1, 0)[8 : 8 + half]
                    east = pltpu.roll(block, half + 15, 0)[8 : 8 + half]
                    south = jnp.where(lane == 0, ylo_ref[f, pl.ds(base, half), :], pltpu.roll(centre, 1, 1))
                    north = jnp.where(
                        lane == ny - 1, yhi_ref[f, pl.ds(base, half), :], pltpu.roll(centre, ny - 1, 1)
                    )
                    lower = -centre if z == 0 else padded[f - 1, pl.ds(base + 8, half), :]
                    upper = centre if z == levels - 1 else padded[f + 1, pl.ds(base + 8, half), :]
                    carried = 0.5 * (u * (east - west) + v * (north - south) + w * (upper - lower))
                    spread = east + west + north + south + upper + lower - 6.0 * centre
                    new = centre + time_step * (viscosity * spread - carried)
                    new_ref[f, pl.ds(base, half), :] = new
                    if z < TZ:
                        low[c * TZ + z] = new
            stress = roughness * (low[0] * low[0] + low[TZ] * low[TZ])
            low[PLANES - 1] = emit_rate * stress * jnp.maximum(
                stress - thr_ref[pl.ds(base, half), :], 0.0
            )
            for p in range(PLANES):
                for h in range(halves):
                    strip[p * halves + h, sub * half : (sub + 1) * half, :] = low[p][
                        :, h * LANES : (h + 1) * LANES
                    ]
        for p in range(PLANES):
            for h in range(halves):
                parts = [strip[p * halves + h, pl.ds(k, ROWS, stride=4), :] for k in range(4)]
                for t in range(4):
                    tile = ix * tiles_y + h * 4 + t
                    cells = pltpu.roll(parts[0], (-t * TILE) % LANES, 1) if t else parts[0]
                    for k in range(1, 4):
                        moved = pltpu.roll(parts[k], ((k - t) * TILE) % LANES, 1) if k != t else parts[k]
                        cells = jnp.where(group == k, moved, cells)
                    tiles[tile, p * ROWS : (p + 1) * ROWS, :] = cells
                    ring_ref[tile, p : p + 1, :] = ring_of(cells, pattern)

        def send(t, inner):
            tile = ix * tiles_y + t
            owner = owner_ref[tile]

            @pl.when(owner >= 0)
            def _():
                pltpu.make_async_copy(tiles.at[tile], send_ref.at[owner], sems.at[tile]).start()

            return inner

        lax.fori_loop(0, tiles_y, send, 0)
        return carry

    lax.fori_loop(0, nx // TILE, one_strip, 0)

    def wait(tile, carry):
        owner = owner_ref[tile]

        @pl.when(owner >= 0)
        def _():
            pltpu.make_async_copy(tiles.at[tile], send_ref.at[owner], sems.at[tile]).wait()

        return carry

    lax.fori_loop(0, tiles.shape[0], wait, 0)


def wind_step(owner_of_tile, velocity, xlo, xhi, ylo, yhi, threshold, owners):
    comps, levels, nx, ny = velocity.shape
    fields = comps * levels
    per_home = (nx // TILE) * (ny // TILE)
    smem = pl.BlockSpec(memory_space=pltpu.SMEM)
    hbm = pl.BlockSpec(memory_space=pl.ANY)
    vmem = pl.BlockSpec(memory_space=pltpu.VMEM)
    new, send, ring = pl.pallas_call(
        functools.partial(wind_kernel, levels=levels),
        in_specs=[smem, hbm, vmem, vmem, vmem, vmem, vmem],
        out_specs=[vmem, hbm, vmem],
        out_shape=[
            jax.ShapeDtypeStruct((fields, nx, ny), jnp.float32),
            jax.ShapeDtypeStruct((owners, PLANES * ROWS, LANES), jnp.float32),
            jax.ShapeDtypeStruct((per_home, 8, LANES), jnp.float32),
        ],
        scratch_shapes=[
            pltpu.VMEM((fields, nx + 16, ny), jnp.float32),
            pltpu.VMEM((PLANES * (ny // LANES), TILE, LANES), jnp.float32),
            pltpu.VMEM((per_home, PLANES * ROWS, LANES), jnp.float32),
            pltpu.SemaphoreType.DMA,
            pltpu.SemaphoreType.DMA((per_home,)),
        ],
        compiler_params=pltpu.CompilerParams(vmem_limit_bytes=40 << 20),
        cost_estimate=pl.CostEstimate(
            flops=40 * velocity.size, bytes_accessed=velocity.size * 10, transcendentals=0
        ),
        name="wind_step",
    )(
        owner_of_tile,
        velocity.reshape(fields, nx, ny),
        xlo.reshape(fields, 1, ny),
        xhi.reshape(fields, 1, ny),
        ylo.reshape(fields, nx, 1),
        yhi.reshape(fields, nx, 1),
        threshold,
    )
    return new.reshape(velocity.shape), send, ring


def pack_borders(outs, ring_at, tiles_x, tiles_y):
    rows = outs[0].shape[1]
    lane = lax.broadcasted_iota(jnp.int32, (rows, LANES), 1)
    borders = (
        (EAST, [((tiles_x - 1) * tiles_y + n) for n in range(tiles_y)]),
        (WEST, [n for n in range(tiles_y)]),
        (NORTH, [n * tiles_y + tiles_y - 1 for n in range(tiles_x)]),
        (SOUTH, [n * tiles_y for n in range(tiles_x)]),
    )
    for out, (side, tiles) in zip(outs, borders):
        for g in range(len(tiles) // 4):
            packed = None
            for q in range(4):
                strip = ring_at(tiles[4 * g + q])
                if q != side:
                    strip = pltpu.roll(strip, ((q - side) * TILE) % LANES, 1)
                packed = strip if packed is None else jnp.where(lane // TILE == q, strip, packed)
            out[g] = packed


def fill_halo(ext, borders, tiles_x, tiles_y):
    from_west, from_east, from_south, from_north = borders
    wide = tiles_y + 2
    for ref, side, places in (
        (from_west, EAST, [n + 1 for n in range(tiles_y)]),
        (from_east, WEST, [(tiles_x + 1) * wide + n + 1 for n in range(tiles_y)]),
        (from_south, NORTH, [(n + 1) * wide for n in range(tiles_x)]),
        (from_north, SOUTH, [(n + 1) * wide + tiles_y + 1 for n in range(tiles_x)]),
    ):
        for n, place in enumerate(places):
            strip = ref[n // 4]
            if n % 4 != side:
                strip = pltpu.roll(strip, ((side - n % 4) * TILE) % LANES, 1)
            ext[place] = strip


def seen_by(ext, place, wide):
    west, east = ext[place - wide], ext[place + wide]
    south, north = ext[place - 1], ext[place + 1]
    lane = lax.broadcasted_iota(jnp.int32, west.shape, 1)
    up = pltpu.roll(jnp.where(lane < 2 * TILE, north, west), TILE, 1)
    down = pltpu.roll(jnp.where(lane < 2 * TILE, east, south), LANES - TILE, 1)
    return jnp.where((lane // TILE) % 2 == 0, up, down)


def gather_rings_kernel(owner_ref, recv_ref, rings_ref, e_ref, w_ref, n_ref, s_ref, sems, *, tiles_x, tiles_y):
    per_home = tiles_x * tiles_y
    rows = e_ref.shape[1]

    def start(t, carry):
        owner = owner_ref[t]

        @pl.when(owner >= 0)
        def _():
            pltpu.make_async_copy(recv_ref.at[owner], rings_ref.at[t], sems.at[t]).start()

        @pl.when(owner < 0)
        def _():
            rings_ref[t] = jnp.zeros(rings_ref.shape[1:], jnp.float32)

        return carry

    lax.fori_loop(0, per_home, start, 0)

    def wait(t, carry):
        owner = owner_ref[t]

        @pl.when(owner >= 0)
        def _():
            pltpu.make_async_copy(recv_ref.at[owner], rings_ref.at[t], sems.at[t]).wait()

        return carry

    lax.fori_loop(0, per_home, wait, 0)
    pack_borders((e_ref, w_ref, n_ref, s_ref), lambda t: rings_ref[t, :rows, :], tiles_x, tiles_y)


def advance_rings_kernel(
    owner_ref, rings_ref, fw_ref, fe_ref, fs_ref, fn_ref, wind_ref, settle_ref, share_ref,
    seen_ref, later_ref, e_ref, w_ref, n_ref, s_ref, ext, *, tiles_x, tiles_y
):
    per_home = tiles_x * tiles_y
    rows = e_ref.shape[1]
    wide = tiles_y + 2
    fill_halo(ext, (fw_ref, fe_ref, fs_ref, fn_ref), tiles_x, tiles_y)

    def place_of(t):
        return (t // tiles_y + 1) * wide + t % tiles_y + 1

    def inner(t, carry):
        ext[place_of(t)] = rings_ref[t, :rows, :]
        return carry

    lax.fori_loop(0, per_home, inner, 0)

    row, lane = iotas()
    group, within = lane // TILE, lane % TILE
    even = row % 2 == 0
    on_x = (group == WEST) | (group == EAST)
    first, last = within == 0, within == TILE - 1
    high = jnp.where((group == EAST) | (group == NORTH), TILE - 1, 0)
    corner = jnp.where(
        on_x,
        jnp.where(first, SOUTH, NORTH) * TILE + high,
        jnp.where(first, WEST, EAST) * TILE + high,
    )

    def one(t, carry):
        place = place_of(t)
        seen = seen_by(ext, place, wide)
        seen_ref[t] = seen

        def level_rows(p):
            return jnp.where(even, spread_rows(wind_ref[t, p : p + 1, :]), spread_rows(wind_ref[t, p + 1 : p + 2, :]))

        u, v, w = (dust_step * level_rows(c * TZ) for c in range(3))
        uplift = dust_step * spread_rows(wind_ref[t, PLANES - 1 : PLANES, :])
        mix = dust_step * diffusion
        from_west = mix + jnp.maximum(u, 0.0)
        from_east = mix + jnp.maximum(-u, 0.0)
        from_south = mix + jnp.maximum(v, 0.0)
        from_north = mix + jnp.maximum(-v, 0.0)
        keep = 1.0 - 6.0 * mix - jnp.abs(u) - jnp.abs(v)
        active = owner_ref[t] >= 0
        for chunk in range(rows // ROWS):
            at = chunk * ROWS
            q = rings_ref[t, at : at + ROWS, :]
            deep = rings_ref[t, rows + at : rows + at + ROWS, :]
            out = seen[at : at + ROWS, :]
            beyond = lane_gather(out, corner)
            before = jnp.where(first, beyond, pltpu.roll(q, 1, 1))
            after = jnp.where(last, beyond, pltpu.roll(q, LANES - 1, 1))
            west = jnp.where(group == WEST, out, jnp.where(group == EAST, deep, before))
            east = jnp.where(group == WEST, deep, jnp.where(group == EAST, out, after))
            south = jnp.where(on_x, before, jnp.where(group == SOUTH, out, deep))
            north = jnp.where(on_x, after, jnp.where(group == SOUTH, deep, out))
            other = jnp.where(even, pltpu.roll(q, ROWS - 1, 0), pltpu.roll(q, 1, 0))
            rise = w - dust_step * settle_ref[at : at + ROWS, :]
            up = jnp.maximum(rise, 0.0)
            down = up - rise
            new = (
                (keep - up - down) * q
                + from_west * west
                + from_east * east
                + from_south * south
                + from_north * north
                + (mix + jnp.where(even, down, up)) * other
                + uplift * share_ref[at : at + ROWS, :]
            )
            later_ref[t, at : at + ROWS, :] = jnp.where(active, new, 0.0)
        return carry

    lax.fori_loop(0, per_home, one, 0)
    pack_borders((e_ref, w_ref, n_ref, s_ref), lambda t: later_ref[t], tiles_x, tiles_y)


def send_seen_kernel(
    owner_ref, later_ref, fw_ref, fe_ref, fs_ref, fn_ref, seen_ref, send_ref, ext, both, sems, *, tiles_x, tiles_y
):
    per_home = tiles_x * tiles_y
    rows = later_ref.shape[1]
    wide = tiles_y + 2
    fill_halo(ext, (fw_ref, fe_ref, fs_ref, fn_ref), tiles_x, tiles_y)

    def place_of(t):
        return (t // tiles_y + 1) * wide + t % tiles_y + 1

    def inner(t, carry):
        ext[place_of(t)] = later_ref[t]
        return carry

    lax.fori_loop(0, per_home, inner, 0)

    def one(t, carry):
        both[t, :rows, :] = seen_ref[t]
        both[t, rows:, :] = seen_by(ext, place_of(t), wide)
        owner = owner_ref[t]

        @pl.when(owner >= 0)
        def _():
            pltpu.make_async_copy(both.at[t], send_ref.at[owner], sems.at[t]).start()

        return carry

    lax.fori_loop(0, per_home, one, 0)

    def wait(t, carry):
        owner = owner_ref[t]

        @pl.when(owner >= 0)
        def _():
            pltpu.make_async_copy(both.at[t], send_ref.at[owner], sems.at[t]).wait()

        return carry

    lax.fori_loop(0, per_home, wait, 0)


def shifted(value, axis, steps):
    count = lax.axis_size(axis)
    return lax.ppermute(value, axis, [(source, (source + steps) % count) for source in range(count)])


def exchange_borders(borders):
    east, west, north, south = borders
    return shifted(east, "gx", 1), shifted(west, "gx", -1), shifted(north, "gy", 1), shifted(south, "gy", -1)


def relay_strips(owner_of_tile, received, wind_ring, settle_speed, bin_share, tiles_x, tiles_y):
    owners, both_rows, _ = received.shape
    rows = both_rows // 2
    per_home = tiles_x * tiles_y
    smem = pl.BlockSpec(memory_space=pltpu.SMEM)
    hbm = pl.BlockSpec(memory_space=pl.ANY)
    vmem = pl.BlockSpec(memory_space=pltpu.VMEM)
    f32 = lambda *shape: jax.ShapeDtypeStruct(shape, jnp.float32)
    packs = [f32(tiles_y // 4, rows, LANES)] * 2 + [f32(tiles_x // 4, rows, LANES)] * 2
    sizes = dict(tiles_x=tiles_x, tiles_y=tiles_y)
    params = pltpu.CompilerParams(vmem_limit_bytes=32 << 20)
    ext = pltpu.VMEM(((tiles_x + 2) * (tiles_y + 2), rows, LANES), jnp.float32)
    sems = pltpu.SemaphoreType.DMA((per_home,))
    cost = pl.CostEstimate(flops=1 << 22, bytes_accessed=per_home * both_rows * LANES * 12, transcendentals=0)
    rings, *borders = pl.pallas_call(
        functools.partial(gather_rings_kernel, **sizes),
        in_specs=[smem, hbm],
        out_specs=[vmem] * 5,
        out_shape=[f32(per_home, both_rows, LANES)] + packs,
        scratch_shapes=[sems],
        compiler_params=params,
        cost_estimate=cost,
        name="gather_rings",
    )(owner_of_tile, received)
    settle_rows = jnp.broadcast_to(jnp.repeat(settle_speed, TZ)[:, None], (rows, LANES))
    share_rows = jnp.broadcast_to(
        jnp.stack([bin_share, jnp.zeros_like(bin_share)], axis=1).reshape(-1, 1), (rows, LANES)
    )
    seen, later, *borders = pl.pallas_call(
        functools.partial(advance_rings_kernel, **sizes),
        in_specs=[smem] + [vmem] * 8,
        out_specs=[vmem] * 6,
        out_shape=[f32(per_home, rows, LANES)] * 2 + packs,
        scratch_shapes=[ext],
        compiler_params=params,
        cost_estimate=cost,
        name="advance_rings",
    )(owner_of_tile, rings, *exchange_borders(borders), wind_ring, settle_rows, share_rows)
    return pl.pallas_call(
        functools.partial(send_seen_kernel, **sizes),
        in_specs=[smem] + [vmem] * 6,
        out_specs=hbm,
        out_shape=f32(owners, both_rows, LANES),
        scratch_shapes=[ext, pltpu.VMEM((per_home, both_rows, LANES), jnp.float32), sems],
        compiler_params=params,
        cost_estimate=cost,
        name="send_seen",
    )(owner_of_tile, later, *exchange_borders(borders), seen)


def dust_kernel(
    home_ref, settle_ref, share_ref, dust_ref, wind_hbm, seen_hbm, out_ref, wind, seen, wind_sems, seen_sems,
    *, block, bins
):
    step = pl.program_id(0)
    slots = wind.shape[0]

    def wind_copy(s):
        return pltpu.make_async_copy(wind_hbm.at[home_ref[s]], wind.at[s], wind_sems.at[s])

    def seen_copy(s):
        return pltpu.make_async_copy(seen_hbm.at[home_ref[s]], seen.at[s], seen_sems.at[s])

    @pl.when(step == 0)
    def _():
        def start(s, carry):
            wind_copy(s).start()
            seen_copy(s).start()
            return carry

        lax.fori_loop(0, slots, start, 0)

    row, lane = iotas()
    within = lane % TILE
    first_y, last_y = within == 0, within == TILE - 1
    first_x = (row == 0) & (lane < TILE)
    last_x = (row == ROWS - 1) & (lane >= LANES - TILE)
    low_lanes, high_lanes = lane < TILE, lane >= LANES - TILE
    along = 4 * row + lane // TILE
    from_sides = jnp.where(first_y, SOUTH * TILE, NORTH * TILE) + along
    mix = dust_step * diffusion
    rows = bins * TZ

    def one(j, carry):
        s = step * block + j
        wind_copy(s).wait()
        seen_copy(s).wait()
        plane = [wind[s, p * ROWS : (p + 1) * ROWS, :] * dust_step for p in range(PLANES)]
        west_by, east_by, south_by, north_by, keep = [], [], [], [], []
        for level in range(TZ):
            u, v = plane[level], plane[TZ + level]
            west_by.append(mix + jnp.maximum(u, 0.0))
            east_by.append(mix + jnp.maximum(-u, 0.0))
            south_by.append(mix + jnp.maximum(v, 0.0))
            north_by.append(mix + jnp.maximum(-v, 0.0))
            keep.append(1.0 - 6.0 * mix - jnp.abs(u) - jnp.abs(v))
        for b in range(bins):
            q = [dust_ref[j, b, pl.ds(level, ROWS, stride=TZ), :] for level in range(TZ)]
            settle = settle_ref[b] * dust_step
            stay, mixed = [], []
            for level in range(TZ):
                rise = plane[2 * TZ + level] - settle
                up = jnp.maximum(rise, 0.0)
                down = up - rise
                stay.append(keep[level] - up - down)
                mixed.append(mix + (down if level == 0 else up))
            source = plane[PLANES - 1] * share_ref[b]
            for substep in range(2):
                new = []
                for level in range(TZ):
                    c = q[level]
                    at = substep * rows + b * TZ + level
                    edge = spread_rows(seen[s, at : at + 1, :])
                    side = lane_gather(edge, from_sides)
                    right = pltpu.roll(c, TILE, 1)
                    left = pltpu.roll(c, LANES - TILE, 1)
                    west = jnp.where(low_lanes, pltpu.roll(right, 1, 0), right)
                    west = jnp.where(first_x, edge, west)
                    east = jnp.where(high_lanes, pltpu.roll(left, ROWS - 1, 0), left)
                    east = jnp.where(last_x, edge, east)
                    south = jnp.where(first_y, side, pltpu.roll(c, 1, 1))
                    north = jnp.where(last_y, side, pltpu.roll(c, LANES - 1, 1))
                    value = (
                        stay[level] * c
                        + west_by[level] * west
                        + east_by[level] * east
                        + south_by[level] * south
                        + north_by[level] * north
                        + mixed[level] * q[1 - level]
                    )
                    if level == 0:
                        value = value + source
                    new.append(value)
                q = new
            for level in range(TZ):
                out_ref[j, b, pl.ds(level, ROWS, stride=TZ), :] = q[level]
        return carry

    lax.fori_loop(0, block, one, 0)


def dust_steps(home_of_slot, dust, wind_recv, seen_recv, settle_speed, bin_share):
    slots, bins = dust.shape[:2]
    block = 8 if slots % 8 == 0 else 4
    smem = pl.BlockSpec(memory_space=pltpu.SMEM)
    hbm = pl.BlockSpec(memory_space=pl.ANY)
    tile = pl.BlockSpec((block,) + dust.shape[1:], lambda i: (i, 0, 0, 0))
    return pl.pallas_call(
        functools.partial(dust_kernel, block=block, bins=bins),
        grid=(slots // block,),
        in_specs=[smem, smem, smem, tile, hbm, hbm],
        out_specs=tile,
        out_shape=jax.ShapeDtypeStruct(dust.shape, jnp.float32),
        scratch_shapes=[
            pltpu.VMEM((slots,) + wind_recv.shape[1:], jnp.float32),
            pltpu.VMEM((slots,) + seen_recv.shape[1:], jnp.float32),
            pltpu.SemaphoreType.DMA((slots,)),
            pltpu.SemaphoreType.DMA((slots,)),
        ],
        compiler_params=pltpu.CompilerParams(vmem_limit_bytes=32 << 20),
        cost_estimate=pl.CostEstimate(flops=60 * dust.size, bytes_accessed=dust.size * 12, transcendentals=0),
        name="dust_steps",
    )(home_of_slot, settle_speed, bin_share, dust, wind_recv, seen_recv)


def relay_rows(rows):
    return lax.all_to_all(rows, AXES, split_axis=0, concat_axis=0, tiled=True)


def per_device(velocity, threshold, dust_mass, settle_speed, bin_share, active_tiles, tile_owner):
    owners = lax.axis_size(AXES)
    grid_cols = lax.axis_size("gy")
    self_index = lax.axis_index(AXES)
    slots, bins = dust_mass.shape[:2]
    tiles_x = velocity.shape[2] // TILE
    tiles_y = velocity.shape[3] // TILE
    per_home = tiles_x * tiles_y
    tiles_across = tiles_y * grid_cols

    tile_x = active_tiles // tiles_across
    tile_y = active_tiles % tiles_across
    home_dev = tile_x // tiles_x * grid_cols + tile_y // tiles_y
    local_tile = tile_x % tiles_x * tiles_y + tile_y % tiles_y
    own_slot = tile_owner - self_index * slots
    mine = jnp.where(home_dev == self_index, local_tile, -1)
    slot_ids = jnp.arange(slots, dtype=jnp.int32)
    home_of_slot = jnp.sum(jnp.where(own_slot[None, :] == slot_ids[:, None], home_dev[None, :], 0), axis=1)
    tile_ids = jnp.arange(per_home, dtype=jnp.int32)
    owner_of_tile = jnp.max(
        jnp.where(mine[None, :] == tile_ids[:, None], (tile_owner // slots)[None, :], -1), axis=1
    )

    dust = dust_mass.reshape(slots, bins, TZ, ROWS, LANES).transpose(0, 1, 3, 2, 4)
    dust = dust.reshape(slots, bins, ROWS * TZ, LANES)

    xlo = shifted(velocity[:, :, -1, :], "gx", 1)
    xhi = shifted(velocity[:, :, 0, :], "gx", -1)
    ylo = shifted(velocity[:, :, :, -1], "gy", 1)
    yhi = shifted(velocity[:, :, :, 0], "gy", -1)

    strips = relay_rows(dust_strips(home_of_slot, dust, owners))
    new_velocity, wind_send, wind_ring = wind_step(
        owner_of_tile, velocity, xlo, xhi, ylo, yhi, threshold, owners
    )
    wind_recv = relay_rows(wind_send)
    seen_send = relay_strips(owner_of_tile, strips, wind_ring, settle_speed, bin_share, tiles_x, tiles_y)
    seen_recv = relay_rows(seen_send)
    out = dust_steps(home_of_slot, dust, wind_recv, seen_recv, settle_speed, bin_share)
    out = out.reshape(slots, bins, ROWS, TZ, LANES).transpose(0, 1, 3, 2, 4).reshape(dust_mass.shape)
    return new_velocity, out


def solution(mesh):
    in_specs = (
        P(None, None, "gx", "gy"),
        P("gx", "gy"),
        P(AXES, None, None, None),
        P(),
        P(),
        P(),
        P(),
    )
    out_specs = (P(None, None, "gx", "gy"), P(AXES, None, None, None))
    return jax.shard_map(
        per_device, mesh=mesh, in_specs=in_specs, out_specs=out_specs, check_vma=False
    )
```

time: 586 us -> 345 us (0.59); the launches traced: 576 us -> 345 us
  local copies, waits for them, and re-layouts: 254 us -> 31.5 us
  other arithmetic: 150 us -> 1.47 us
  Pallas kernels: 0 us -> 138 us
  blocking collectives: 34.1 us -> 62.4 us
  starting transfers between devices: 59.4 us -> 41.4 us
  waiting for transfers between devices: 76.8 us -> 68.7 us
    pallas_call x0 -> x6, Pallas kernels: none -> 138 us  [the longest x1 65 us: dust_steps(): pl.pallas_call(functools.partial(dust_kernel, block=block, bins=bins), gr...]
    gather x16 -> x0, local copies, waits for them, and re-layouts: 109 us -> none  [the longest x1 39.9 us: per_device(): slot_grid = jnp.take(marked, inverse).reshape(owners, slot_count)]
    add x3 -> x0, other arithmetic: 105 us -> none  [the longest x2 85.5 us: dust_update(): block_cube + dust_step * (diffusion * spread - carried + lifted)]
    all_to_all x5 -> x2, waiting for transfers between devices: 45.6 us -> 0.01 us  [relay_rows(): return lax.all_to_all(rows, AXES, split_axis=0, concat_axis=0, tiled=True)]
    ppermute x12, waiting for transfers between devices: 31.2 us -> 68.7 us  [shifted(): lax.ppermute(value, axis, [(source, (source + steps) % count) for source...]
    slice x13 -> x2, local copies, waits for them, and re-layouts: 42.6 us -> 5.55 us  [the longest x1 4.54 us: per_device(): yhi = shifted(velocity[:, :, :, 0], 'gy', -1)]
    all_to_all x1, blocking collectives: 34.1 us -> 62.4 us  [relay_rows(): return lax.all_to_all(rows, AXES, split_axis=0, concat_axis=0, tiled=True)]
    unnamed x47 -> x25, local copies, waits for them, and re-layouts: 44.8 us -> 19.6 us
  transfers between devices with their start and end apart: 17 -> 14, of which waited for: 6 -> 7; matrix products, arithmetic and copies ran while one was open for 37% -> 5% of each run, Pallas kernels for 0% -> 18%
where the time goes in v1:
time: 345 us
  Pallas kernels  138 us (40%)
  waiting for transfers between devices  68.7 us (20%)
  blocking collectives  62.4 us (18%)
  starting transfers between devices  41.4 us (12%)
  local copies, waits for them, and re-layouts  31.5 us (9%)
    ppermute x12, waiting for transfers between devices, shifted(): lax.ppermute(value, axis, [(source, (source + steps) % count) for source...  68.7 us
    pallas_call x1, Pallas kernels, dust_steps(): pl.pallas_call(functools.partial(dust_kernel, block=block, bins=bins), gr...  65 us
    all_to_all x1, blocking collectives, relay_rows(): return lax.all_to_all(rows, AXES, split_axis=0, concat_axis=0, tiled=True)  62.4 us
    pallas_call x1, Pallas kernels, wind_step(): pl.pallas_call(functools.partial(wind_kernel, levels=levels), in_specs=[s...  36.7 us
    all_to_all x2, starting transfers between devices, relay_rows(): return lax.all_to_all(rows, AXES, split_axis=0, concat_axis=0, tiled=True)  20.8 us
    ppermute x12, starting transfers between devices, shifted(): lax.ppermute(value, axis, [(source, (source + steps) % count) for source...  20.6 us
    unnamed x25, local copies, waits for them, and re-layouts  19.6 us
    pallas_call x1, Pallas kernels, dust_strips(): pl.pallas_call(functools.partial(strips_kernel, block=block, bins=bins),...  12.3 us
  transfers between devices with their start and end apart: 14, of which 7 were waited for; matrix products, arithmetic and copies ran while one was open for 5% of the time, Pallas kernels for 18%

profile of v1, /device:TPU:1, one launch (start us, length us, event | category | flops | bytes accessed | tf_op | source)
XLA Modules:
  0.0 344.6 jit_solution(13848388386906470609)
XLA Ops:
  1.8 3.1 copy-done
  4.9 12.3 %dust_strips.1 = f32[128,64,128]{2,1,0:T(8,128)S(1)} custom-call(s32[56]{0:T(128)S(1)} %select_reduce_fusion.1.home_ref, f32[56,16,16,128]{3,2,1,0:T(8,128)S(1)} %bitcast.21), custom_call_target="tpu_custom_call" | custom-call | flops 36700160 | bytes 9175040 | tf_op jit(solution)/shard_map/dust_strips/pallas_call | solution.py:86
  19.1 12.0 %all-to-all-start.1 = ((f32[128,64,128]{2,1,0:T(8,128)}), f32[128,64,128]{2,1,0:T(8,128)}, u32[]{:S(2)}, u32[]{:S(2)}) async-start(f32[128,64,128]{2,1,0:T(8,128)} %copy-done.3), calls=%async_computation.1 | async-start | bytes 8388608 | tf_op jit(solution)/shard_map/all_to_all | solution.py:611
  33.8 4.5 %fusion.13 = (f32[3,6,256,1]{3,2,1,0:T(8,128)S(1)}, f32[3,6,256,1]{3,2,1,0:T(8,128)}) fusion(f32[3,6,256,256]{3,2,1,0:T(8,128)} %param.7), kind=kLoop, calls=%fused_computation.40 | loop fusion | bytes 73728 | tf_op jit(solution)/shard_map/slice | solution.py:643
  38.3 2.6 copy.32
  43.2 4.0 %collective-permute-start.3 = (f32[3,6,256]{2,1,0:T(8,128)S(1)}, f32[3,6,256]{2,1,0:T(8,128)S(1)}, u32[]{:S(2)}, u32[]{:S(2)}) collective-permute-start(f32[3,6,256]{2,1,0:T(8,128)S(1)} %bitcast.27), channel_id=1, source_target_pairs={{0,15},{1,0},{2,1},{3,2},{4,3},{5,4},{6,5},{7,6},{8,7},{9,8},{10,9... | collective-permute-start | bytes 55304 | tf_op jit(solution)/shard_map/ppermute | solution.py:437
  47.5 18.1 %collective-permute-done = f32[3,6,256]{2,1,0:T(8,128)S(1)} collective-permute-done((f32[3,6,256]{2,1,0:T(8,128)S(1)}, f32[3,6,256]{2,1,0:T(8,128)S(1)}, u32[]{:S(2)}, u32[]{:S(2)}) %collective-permute-start) | collective-permute-done | bytes 18464 | tf_op jit(solution)/shard_map/ppermute | solution.py:437
  65.6 8.8 %collective-permute-done.1 = f32[3,6,256]{2,1,0:T(8,128)S(1)} collective-permute-done((f32[3,6,256]{2,1,0:T(8,128)S(1)}, f32[3,6,256]{2,1,0:T(8,128)S(1)}, u32[]{:S(2)}, u32[]{:S(2)}) %collective-permute-start.1) | collective-permute-done | bytes 18464 | tf_op jit(solution)/shard_map/ppermute | solution.py:437
  76.7 5.2 %collective-permute-done.2 = f32[3,6,256]{2,1,0:T(8,128)S(1)} collective-permute-done((f32[3,6,256]{2,1,0:T(8,128)S(1)}, f32[3,6,256]{2,1,0:T(8,128)S(1)}, u32[]{:S(2)}, u32[]{:S(2)}) %collective-permute-start.2) | collective-permute-done | bytes 18464 | tf_op jit(solution)/shard_map/ppermute | solution.py:437
  81.9 3.6 %reshape.51.ylo_ref = f32[18,256,1]{2,1,0:T(8,128)} reshape(f32[3,6,256]{2,1,0:T(8,128)S(1)} %collective-permute-done.2) | data formatting | bytes 36864 | tf_op jit(solution)/shard_map/reshape | solution.py:230
  85.5 2.3 copy-done.2
  89.5 36.7 %wind_step.1 = (f32[18,256,256]{2,1,0:T(8,128)}, f32[128,56,128]{2,1,0:T(8,128)S(1)}, f32[64,8,128]{2,1,0:T(8,128)S(1)}) custom-call(s32[64]{0:T(128)S(1)} %select_reduce_fusion.owner_ref, f32[18,256,256]{2,1,0:T(8,128)S(1)} %bitcast.23, f32[18,1,256]{2,1,0:T(1,128)S(1)} %reshape.42.xlo_ref, f32[18,1,256]{2,1,0:T(1,128)S(1)} %reshape.43.xhi_ref, ...), custom_call_target="tpu_custom_call" | custom-call | flops 47185920 | bytes 11796480 | tf_op jit(solution)/shard_map/wind_step/pallas_call | solution.py:204
  128.1 8.9 %all-to-all-start = ((f32[128,56,128]{2,1,0:T(8,128)}), f32[128,56,128]{2,1,0:T(8,128)}, u32[]{:S(2)}, u32[]{:S(2)}) async-start(f32[128,56,128]{2,1,0:T(8,128)} %copy-done.6), calls=%async_computation | async-start | bytes 7340032 | tf_op jit(solution)/shard_map/all_to_all | solution.py:611
  137.0 3.1 gather_rings.1
  142.9 3.8 %collective-permute-start.7 = (f32[2,32,128]{2,1,0:T(8,128)S(1)}, f32[2,32,128]{2,1,0:T(8,128)S(1)}, u32[]{:S(2)}, u32[]{:S(2)}) collective-permute-start(f32[2,32,128]{2,1,0:T(8,128)S(1)} %get-tuple-element.22), channel_id=1, source_target_pairs={{0,15},{1,0},{2,1},{3,2},{4,3},{5,4},{6,5},{7,6},{8,7},{9,8},{10,9... | collective-permute-start | bytes 98312 | tf_op jit(solution)/shard_map/ppermute | solution.py:437
  147.0 19.7 %collective-permute-done.4.fw_ref = f32[2,32,128]{2,1,0:T(8,128)S(1)} collective-permute-done((f32[2,32,128]{2,1,0:T(8,128)S(1)}, f32[2,32,128]{2,1,0:T(8,128)S(1)}, u32[]{:S(2)}, u32[]{:S(2)}) %collective-permute-start.4) | collective-permute-done | bytes 32800 | tf_op jit(solution)/shard_map/ppermute | solution.py:437
  166.8 7.9 %collective-permute-done.5.fe_ref = f32[2,32,128]{2,1,0:T(8,128)S(1)} collective-permute-done((f32[2,32,128]{2,1,0:T(8,128)S(1)}, f32[2,32,128]{2,1,0:T(8,128)S(1)}, u32[]{:S(2)}, u32[]{:S(2)}) %collective-permute-start.5) | collective-permute-done | bytes 32800 | tf_op jit(solution)/shard_map/ppermute | solution.py:437
  174.6 7.8 %collective-permute-done.6.fs_ref = f32[2,32,128]{2,1,0:T(8,128)S(1)} collective-permute-done((f32[2,32,128]{2,1,0:T(8,128)S(1)}, f32[2,32,128]{2,1,0:T(8,128)S(1)}, u32[]{:S(2)}, u32[]{:S(2)}) %collective-permute-start.6) | collective-permute-done | bytes 32800 | tf_op jit(solution)/shard_map/ppermute | solution.py:437
  182.5 11.9 %advance_rings.1 = (f32[64,32,128]{2,1,0:T(8,128)S(1)}, f32[64,32,128]{2,1,0:T(8,128)S(1)}, f32[2,32,128]{2,1,0:T(8,128)S(1)}, f32[2,32,128]{2,1,0:T(8,128)S(1)}...) custom-call(s32[64]{0:T(128)S(1)} %select_reduce_fusion.owner_ref, ...), custom_call_target="tpu_custom_call" | custom-call | flops 4194304 | bytes 6291456 | tf_op jit(solution)/shard_map/advance_rings/pallas_call | solution.py:473
  196.7 4.8 %collective-permute-start.11 = (f32[2,32,128]{2,1,0:T(8,128)S(1)}, f32[2,32,128]{2,1,0:T(8,128)S(1)}, u32[]{:S(2)}, u32[]{:S(2)}) collective-permute-start(f32[2,32,128]{2,1,0:T(8,128)S(1)} %get-tuple-element.28), channel_id=1, source_target_pairs={{0,15},{1,0},{2,1},{3,2},{4,3},{5,4},{6,5},{7,6},{8,7},{9,8},{10,9... | collective-permute-start | bytes 98312 | tf_op jit(solution)/shard_map/ppermute | solution.py:437
  202.8 9.2 %send_seen.1 = f32[128,64,128]{2,1,0:T(8,128)S(1)} custom-call(s32[64]{0:T(128)S(1)} %select_reduce_fusion.owner_ref, f32[64,32,128]{2,1,0:T(8,128)S(1)} %get-tuple-element.24.later_ref, f32[2,32,128]{2,1,0:T(8,128)S(1)} %collective-permute-done.8.fw_ref, f32[2,32,128]{2,1,0:T(8,128)S(1)} %collective-permute-done.9.fe_ref, ...), custom_call_target="tpu_custom_call" | custom-call | flops 4194304 | bytes 6291456 | tf_op jit(solution)/shard_map/send_seen/pallas_call | solution.py:483
  214.1 62.4 %all_to_all.15.seen_hbm = f32[128,64,128]{2,1,0:T(8,128)S(1)} all-to-all(f32[128,64,128]{2,1,0:T(8,128)} %copy-done.4), channel_id=1, replica_groups=mesh['gx'=8,'gy'=16] {'gx','gy'}, dimensions={0} | all-to-all | bytes 8388608 | tf_op jit(solution)/shard_map/all_to_all | solution.py:611
  276.5 3.1 copy-done.1
  279.6 65.0 %dust_steps.1 = f32[56,16,16,128]{3,2,1,0:T(8,128)} custom-call(s32[56]{0:T(128)S(1)} %select_reduce_fusion.1.home_ref, f32[16]{0:T(128)S(1)} %copy-done.8, f32[16]{0:T(128)S(1)} %copy-done.9, f32[56,16,16,128]{3,2,1,0:T(8,128)S(1)} %bitcast.22, f32[128,56,128]{2,1,0:T(8,128)} %all-to-all-done.wind_hbm, f32[128,64,128]{2,1,0:T(8,128)S(1)} %all_to_all.15.seen_hbm), custom_call_target="tpu_custom_call" | custom-call | flops 110100480 | bytes 22020096 | tf_op jit(solution)/shard_map/dust_steps/pallas_call | solution.py:592
  (51 shorter events, 23.1 us)
Async XLA Ops:
  1.8 3.1 copy-start
  17.1 2.0 copy-start.3
  19.1 108.9 %all-to-all-start.1 = ((f32[128,64,128]{2,1,0:T(8,128)}), f32[128,64,128]{2,1,0:T(8,128)}, u32[]{:S(2)}, u32[]{:S(2)}) async-start(f32[128,64,128]{2,1,0:T(8,128)} %copy-done.3), calls=%async_computation.1 | async-start | bytes 8388608 | tf_op jit(solution)/shard_map/all_to_all | solution.py:611
  32.1 33.5 %collective-permute-start = (f32[3,6,256]{2,1,0:T(8,128)S(1)}, f32[3,6,256]{2,1,0:T(8,128)S(1)}, u32[]{:S(2)}, u32[]{:S(2)}) collective-permute-start(f32[3,6,256]{2,1,0:T(8,128)S(1)} %bitcast.28), channel_id=1, source_target_pairs={{0,16},{16,32},{32,48},{48,64},{64,80},{80,96},{96,112},{112,0},{1... | collective-permute-start | bytes 55304 | tf_op jit(solution)/shard_map/ppermute | solution.py:437
  33.8 40.7 %collective-permute-start.1 = (f32[3,6,256]{2,1,0:T(8,128)S(1)}, f32[3,6,256]{2,1,0:T(8,128)S(1)}, u32[]{:S(2)}, u32[]{:S(2)}) collective-permute-start(f32[3,6,256]{2,1,0:T(8,128)S(1)} %bitcast.29), channel_id=1, source_target_pairs={{0,112},{16,0},{32,16},{48,32},{64,48},{80,64},{96,80},{112,96},{1... | collective-permute-start | bytes 55304 | tf_op jit(solution)/shard_map/ppermute | solution.py:437
  40.9 41.0 %collective-permute-start.2 = (f32[3,6,256]{2,1,0:T(8,128)S(1)}, f32[3,6,256]{2,1,0:T(8,128)S(1)}, u32[]{:S(2)}, u32[]{:S(2)}) collective-permute-start(f32[3,6,256]{2,1,0:T(8,128)S(1)} %bitcast.26), channel_id=1, source_target_pairs={{0,1},{1,2},{2,3},{3,4},{4,5},{5,6},{6,7},{7,8},{8,9},{9,10},{10,1... | collective-permute-start | bytes 55304 | tf_op jit(solution)/shard_map/ppermute | solution.py:437
  43.2 31.3 %collective-permute-start.3 = (f32[3,6,256]{2,1,0:T(8,128)S(1)}, f32[3,6,256]{2,1,0:T(8,128)S(1)}, u32[]{:S(2)}, u32[]{:S(2)}) collective-permute-start(f32[3,6,256]{2,1,0:T(8,128)S(1)} %bitcast.27), channel_id=1, source_target_pairs={{0,15},{1,0},{2,1},{3,2},{4,3},{5,4},{6,5},{7,6},{8,7},{9,8},{10,9... | collective-permute-start | bytes 55304 | tf_op jit(solution)/shard_map/ppermute | solution.py:437
  74.5 11.0 %copy-start.7 = (f32[256,256]{1,0:T(8,128)S(1)}, f32[256,256]{1,0:T(8,128)}, u32[]{:S(2)}) copy-start(f32[256,256]{1,0:T(8,128)} %thr_ref.1) | copy-start | bytes 786436
  85.5 2.3 copy-start.2
  87.9 1.7 copy-start.5
  126.2 1.9 copy-start.6
  128.1 86.0 %all-to-all-start = ((f32[128,56,128]{2,1,0:T(8,128)}), f32[128,56,128]{2,1,0:T(8,128)}, u32[]{:S(2)}, u32[]{:S(2)}) async-start(f32[128,56,128]{2,1,0:T(8,128)} %copy-done.6), calls=%async_computation | async-start | bytes 7340032 | tf_op jit(solution)/shard_map/all_to_all | solution.py:611
  137.0 9.7 %copy-start.9 = (f32[16]{0:T(128)S(1)}, f32[16]{0:T(128)}, u32[]{:S(2)}) copy-start(f32[16]{0:T(128)} %share_ref.1) | copy-start | bytes 196
  137.0 9.9 %copy-start.8 = (f32[16]{0:T(128)S(1)}, f32[16]{0:T(128)}, u32[]{:S(2)}) copy-start(f32[16]{0:T(128)} %settle_ref.1) | copy-start | bytes 196
  140.1 26.6 %collective-permute-start.4 = (f32[2,32,128]{2,1,0:T(8,128)S(1)}, f32[2,32,128]{2,1,0:T(8,128)S(1)}, u32[]{:S(2)}, u32[]{:S(2)}) collective-permute-start(f32[2,32,128]{2,1,0:T(8,128)S(1)} %get-tuple-element.19), channel_id=1, source_target_pairs={{0,16},{16,32},{32,48},{48,64},{64,80},{80,96},{96,112},{112,0},{1... | collective-permute-start | bytes 98312 | tf_op jit(solution)/shard_map/ppermute | solution.py:437
  141.4 33.2 %collective-permute-start.5 = (f32[2,32,128]{2,1,0:T(8,128)S(1)}, f32[2,32,128]{2,1,0:T(8,128)S(1)}, u32[]{:S(2)}, u32[]{:S(2)}) collective-permute-start(f32[2,32,128]{2,1,0:T(8,128)S(1)} %get-tuple-element.20), channel_id=1, source_target_pairs={{0,112},{16,0},{32,16},{48,32},{64,48},{80,64},{96,80},{112,96},{1... | collective-permute-start | bytes 98312 | tf_op jit(solution)/shard_map/ppermute | solution.py:437
  141.4 41.0 %collective-permute-start.6 = (f32[2,32,128]{2,1,0:T(8,128)S(1)}, f32[2,32,128]{2,1,0:T(8,128)S(1)}, u32[]{:S(2)}, u32[]{:S(2)}) collective-permute-start(f32[2,32,128]{2,1,0:T(8,128)S(1)} %get-tuple-element.21), channel_id=1, source_target_pairs={{0,1},{1,2},{2,3},{3,4},{4,5},{5,6},{6,7},{7,8},{8,9},{9,10},{10,1... | collective-permute-start | bytes 98312 | tf_op jit(solution)/shard_map/ppermute | solution.py:437
  142.9 39.5 %collective-permute-start.7 = (f32[2,32,128]{2,1,0:T(8,128)S(1)}, f32[2,32,128]{2,1,0:T(8,128)S(1)}, u32[]{:S(2)}, u32[]{:S(2)}) collective-permute-start(f32[2,32,128]{2,1,0:T(8,128)S(1)} %get-tuple-element.22), channel_id=1, source_target_pairs={{0,15},{1,0},{2,1},{3,2},{4,3},{5,4},{6,5},{7,6},{8,7},{9,8},{10,9... | collective-permute-start | bytes 98312 | tf_op jit(solution)/shard_map/ppermute | solution.py:437
  194.5 7.1 %collective-permute-start.8 = (f32[2,32,128]{2,1,0:T(8,128)S(1)}, f32[2,32,128]{2,1,0:T(8,128)S(1)}, u32[]{:S(2)}, u32[]{:S(2)}) collective-permute-start(f32[2,32,128]{2,1,0:T(8,128)S(1)} %get-tuple-element.25), channel_id=1, source_target_pairs={{0,16},{16,32},{32,48},{48,64},{64,80},{80,96},{96,112},{112,0},{1... | collective-permute-start | bytes 98312 | tf_op jit(solution)/shard_map/ppermute | solution.py:437
  196.7 4.8 %collective-permute-start.9 = (f32[2,32,128]{2,1,0:T(8,128)S(1)}, f32[2,32,128]{2,1,0:T(8,128)S(1)}, u32[]{:S(2)}, u32[]{:S(2)}) collective-permute-start(f32[2,32,128]{2,1,0:T(8,128)S(1)} %get-tuple-element.26), channel_id=1, source_target_pairs={{0,112},{16,0},{32,16},{48,32},{64,48},{80,64},{96,80},{112,96},{1... | collective-permute-start | bytes 98312 | tf_op jit(solution)/shard_map/ppermute | solution.py:437
  196.7 6.1 %collective-permute-start.10 = (f32[2,32,128]{2,1,0:T(8,128)S(1)}, f32[2,32,128]{2,1,0:T(8,128)S(1)}, u32[]{:S(2)}, u32[]{:S(2)}) collective-permute-start(f32[2,32,128]{2,1,0:T(8,128)S(1)} %get-tuple-element.27), channel_id=1, source_target_pairs={{0,1},{1,2},{2,3},{3,4},{4,5},{5,6},{6,7},{7,8},{8,9},{9,10},{10,1... | collective-permute-start | bytes 98312 | tf_op jit(solution)/shard_map/ppermute | solution.py:437
  196.7 6.1 %collective-permute-start.11 = (f32[2,32,128]{2,1,0:T(8,128)S(1)}, f32[2,32,128]{2,1,0:T(8,128)S(1)}, u32[]{:S(2)}, u32[]{:S(2)}) collective-permute-start(f32[2,32,128]{2,1,0:T(8,128)S(1)} %get-tuple-element.28), channel_id=1, source_target_pairs={{0,15},{1,0},{2,1},{3,2},{4,3},{5,4},{6,5},{7,6},{8,7},{9,8},{10,9... | collective-permute-start | bytes 98312 | tf_op jit(solution)/shard_map/ppermute | solution.py:437
  212.1 2.0 copy-start.4
  276.5 3.1 copy-start.1

commit v2 on v1

--- a/solution.py
+++ b/solution.py
@@ -2,6 +2,8 @@
 
 import jax
 import jax.numpy as jnp
+import ml_dtypes
+import numpy as np
 from jax import lax
 from jax.experimental import pallas as pl
 from jax.experimental.pallas import tpu as pltpu
@@ -52,23 +54,79 @@
     return jnp.broadcast_to(row, (ROWS, LANES))
 
 
-def strips_kernel(home_ref, dust_ref, send_ref, rings, sems, *, block, bins):
+def halves_of(x):
+    high = x.astype(jnp.bfloat16)
+    return high, (x - high.astype(jnp.float32)).astype(jnp.bfloat16)
+
+
+def moves(sources):
+    lanes = np.arange(LANES)[:, None]
+    once = (lanes == np.asarray(sources)[None, :]).astype(ml_dtypes.bfloat16)
+    return np.concatenate([once, once], axis=0)
+
+
+def ring_matrix():
+    lane = np.arange(LANES)
+    group, within = lane // TILE, lane % TILE
+    blocks = []
+    for r in range(ROWS):
+        columns = []
+        for depth in range(2):
+            side = np.where(group == SOUTH, depth, TILE - 1 - depth)
+            source = np.where(within // 4 == r, (within % 4) * TILE + side, -1)
+            source = np.where(group == WEST, depth * TILE + within if r == 0 else -1, source)
+            source = np.where(group == EAST, (3 - depth) * TILE + within if r == ROWS - 1 else -1, source)
+            columns.append(source)
+        blocks.append(moves(np.concatenate(columns)))
+    return np.concatenate(blocks, axis=0)
+
+
+def shift_matrix():
+    lane = np.arange(LANES)
+    return moves(np.concatenate([(lane + d) % LANES for d in (-1, 1, -TILE, TILE)]))
+
+
+def side_matrix():
+    lane = np.arange(LANES)
+    columns = []
+    for r in range(ROWS):
+        along = 4 * r + lane // TILE
+        source = np.where(lane % TILE == 0, SOUTH * TILE + along, -1)
+        columns.append(np.where(lane % TILE == TILE - 1, NORTH * TILE + along, source))
+    return moves(np.concatenate(columns))
+
+
+def strips_kernel(home_ref, dust_ref, matrix_ref, send_ref, rings, sems, *, block, bins):
     step = pl.program_id(0)
     slots = rings.shape[0]
-    patterns = [ring_pattern(0), ring_pattern(1)]
-
-    def one(j, carry):
+    each = TZ * bins
+
+    parts = []
+    for r in range(ROWS):
+        x = jnp.concatenate(
+            [
+                dust_ref[j, pl.ds(r * TZ + level, bins, stride=ROWS * TZ), :]
+                for j in range(block)
+                for level in range(TZ)
+            ],
+            axis=0,
+        )
+        parts += halves_of(x)
+    found = jnp.dot(
+        jnp.concatenate(parts, axis=1), matrix_ref[...], preferred_element_type=jnp.float32
+    )
+    for j in range(block):
+        for depth in range(2):
+            rings[step * block + j, depth * each : (depth + 1) * each, :] = found[
+                j * each : (j + 1) * each, depth * LANES : (depth + 1) * LANES
+            ]
+
+    def send(j, carry):
         s = step * block + j
-        for b in range(bins):
-            for level in range(TZ):
-                x = dust_ref[j, b, pl.ds(level, ROWS, stride=TZ), :]
-                for depth in range(2):
-                    at = depth * bins * TZ + b * TZ + level
-                    rings[s, at : at + 1, :] = ring_of(x, patterns[depth])
         pltpu.make_async_copy(rings.at[s], send_ref.at[home_ref[s]], sems.at[s]).start()
         return carry
 
-    lax.fori_loop(0, block, one, 0)
+    lax.fori_loop(0, block, send, 0)
 
     @pl.when(step == pl.num_programs(0) - 1)
     def _():
@@ -79,16 +137,18 @@
         lax.fori_loop(0, slots, wait, 0)
 
 
-def dust_strips(home_of_slot, dust, owners):
-    slots, bins = dust.shape[:2]
+def dust_strips(home_of_slot, dust, bins, owners):
+    slots, cells = dust.shape[:2]
     block = 8 if slots % 8 == 0 else 4
     rows = 2 * bins * TZ
+    matrix = jnp.asarray(ring_matrix())
     return pl.pallas_call(
         functools.partial(strips_kernel, block=block, bins=bins),
         grid=(slots // block,),
         in_specs=[
             pl.BlockSpec(memory_space=pltpu.SMEM),
-            pl.BlockSpec((block,) + dust.shape[1:], lambda i: (i, 0, 0, 0)),
+            pl.BlockSpec((block, cells, LANES), lambda i: (i, 0, 0)),
+            pl.BlockSpec(matrix.shape, lambda i: (0, 0)),
         ],
         out_specs=pl.BlockSpec(memory_space=pl.ANY),
         out_shape=jax.ShapeDtypeStruct((owners, rows, LANES), jnp.float32),
@@ -101,7 +161,7 @@
             flops=20 * dust.size, bytes_accessed=dust.size * 4 + slots * rows * LANES * 4, transcendentals=0
         ),
         name="dust_strips",
-    )(home_of_slot, dust)
+    )(home_of_slot, dust, matrix)
 
 
 def wind_kernel(
@@ -279,35 +339,16 @@
     return jnp.where((lane // TILE) % 2 == 0, up, down)
 
 
-def gather_rings_kernel(owner_ref, recv_ref, rings_ref, e_ref, w_ref, n_ref, s_ref, sems, *, tiles_x, tiles_y):
-    per_home = tiles_x * tiles_y
+def gather_rings_kernel(owner_ref, recv_ref, rings_ref, e_ref, w_ref, n_ref, s_ref, *, tiles_x, tiles_y):
     rows = e_ref.shape[1]
 
-    def start(t, carry):
+    def one(t, carry):
         owner = owner_ref[t]
-
-        @pl.when(owner >= 0)
-        def _():
-            pltpu.make_async_copy(recv_ref.at[owner], rings_ref.at[t], sems.at[t]).start()
-
-        @pl.when(owner < 0)
-        def _():
-            rings_ref[t] = jnp.zeros(rings_ref.shape[1:], jnp.float32)
-
-        return carry
-
-    lax.fori_loop(0, per_home, start, 0)
-
-    def wait(t, carry):
-        owner = owner_ref[t]
-
-        @pl.when(owner >= 0)
-        def _():
-            pltpu.make_async_copy(recv_ref.at[owner], rings_ref.at[t], sems.at[t]).wait()
-
-        return carry
-
-    lax.fori_loop(0, per_home, wait, 0)
+        rings = recv_ref[jnp.maximum(owner, 0)]
+        rings_ref[t] = jnp.where(owner >= 0, rings, 0.0)
+        return carry
+
+    lax.fori_loop(0, tiles_x * tiles_y, one, 0)
     pack_borders((e_ref, w_ref, n_ref, s_ref), lambda t: rings_ref[t, :rows, :], tiles_x, tiles_y)
 
 
@@ -329,9 +370,8 @@
 
     lax.fori_loop(0, per_home, inner, 0)
 
-    row, lane = iotas()
+    _, lane = iotas()
     group, within = lane // TILE, lane % TILE
-    even = row % 2 == 0
     on_x = (group == WEST) | (group == EAST)
     first, last = within == 0, within == TILE - 1
     high = jnp.where((group == EAST) | (group == NORTH), TILE - 1, 0)
@@ -346,20 +386,22 @@
         seen = seen_by(ext, place, wide)
         seen_ref[t] = seen
 
-        def level_rows(p):
-            return jnp.where(even, spread_rows(wind_ref[t, p : p + 1, :]), spread_rows(wind_ref[t, p + 1 : p + 2, :]))
-
-        u, v, w = (dust_step * level_rows(c * TZ) for c in range(3))
         uplift = dust_step * spread_rows(wind_ref[t, PLANES - 1 : PLANES, :])
         mix = dust_step * diffusion
-        from_west = mix + jnp.maximum(u, 0.0)
-        from_east = mix + jnp.maximum(-u, 0.0)
-        from_south = mix + jnp.maximum(v, 0.0)
-        from_north = mix + jnp.maximum(-v, 0.0)
-        keep = 1.0 - 6.0 * mix - jnp.abs(u) - jnp.abs(v)
         active = owner_ref[t] >= 0
+        bins = rows // TZ
         for chunk in range(rows // ROWS):
             at = chunk * ROWS
+            level, bin_at = at // bins, at % bins
+            if bin_at == 0:
+                u, v, w = (
+                    dust_step * spread_rows(wind_ref[t, c * TZ + level : c * TZ + level + 1, :]) for c in range(3)
+                )
+                from_west = mix + jnp.maximum(u, 0.0)
+                from_east = mix + jnp.maximum(-u, 0.0)
+                from_south = mix + jnp.maximum(v, 0.0)
+                from_north = mix + jnp.maximum(-v, 0.0)
+                keep = 1.0 - 6.0 * mix - jnp.abs(u) - jnp.abs(v)
             q = rings_ref[t, at : at + ROWS, :]
             deep = rings_ref[t, rows + at : rows + at + ROWS, :]
             out = seen[at : at + ROWS, :]
@@ -370,8 +412,9 @@
             east = jnp.where(group == WEST, deep, jnp.where(group == EAST, out, after))
             south = jnp.where(on_x, before, jnp.where(group == SOUTH, out, deep))
             north = jnp.where(on_x, after, jnp.where(group == SOUTH, deep, out))
-            other = jnp.where(even, pltpu.roll(q, ROWS - 1, 0), pltpu.roll(q, 1, 0))
-            rise = w - dust_step * settle_ref[at : at + ROWS, :]
+            other_at = (1 - level) * bins + bin_at
+            other = rings_ref[t, other_at : other_at + ROWS, :]
+            rise = w - dust_step * settle_ref[bin_at : bin_at + ROWS, :]
             up = jnp.maximum(rise, 0.0)
             down = up - rise
             new = (
@@ -380,9 +423,10 @@
                 + from_east * east
                 + from_south * south
                 + from_north * north
-                + (mix + jnp.where(even, down, up)) * other
-                + uplift * share_ref[at : at + ROWS, :]
+                + (mix + (down if level == 0 else up)) * other
             )
+            if level == 0:
+                new = new + uplift * share_ref[bin_at : bin_at + ROWS, :]
             later_ref[t, at : at + ROWS, :] = jnp.where(active, new, 0.0)
         return carry
 
@@ -442,169 +486,214 @@
     return shifted(east, "gx", 1), shifted(west, "gx", -1), shifted(north, "gy", 1), shifted(south, "gy", -1)
 
 
-def relay_strips(owner_of_tile, received, wind_ring, settle_speed, bin_share, tiles_x, tiles_y):
-    owners, both_rows, _ = received.shape
+def f32(*shape):
+    return jax.ShapeDtypeStruct(shape, jnp.float32)
+
+
+def ring_call(kernel, tiles_x, tiles_y, rows, outs, scratch, name, hbm_out=False):
+    smem = pl.BlockSpec(memory_space=pltpu.SMEM)
+    vmem = pl.BlockSpec(memory_space=pltpu.VMEM)
+    size = tiles_x * tiles_y * rows * LANES
+
+    def call(owner_of_tile, *inputs):
+        return pl.pallas_call(
+            functools.partial(kernel, tiles_x=tiles_x, tiles_y=tiles_y),
+            in_specs=[smem] + [vmem] * len(inputs),
+            out_specs=pl.BlockSpec(memory_space=pl.ANY) if hbm_out else [vmem] * len(outs),
+            out_shape=outs[0] if hbm_out else outs,
+            scratch_shapes=scratch,
+            compiler_params=pltpu.CompilerParams(vmem_limit_bytes=32 << 20),
+            cost_estimate=pl.CostEstimate(flops=16 * size, bytes_accessed=16 * size, transcendentals=0),
+            name=name,
+        )(owner_of_tile, *inputs)
+
+    return call
+
+
+def border_shapes(tiles_x, tiles_y, rows):
+    return [f32(tiles_y // 4, rows, LANES)] * 2 + [f32(tiles_x // 4, rows, LANES)] * 2
+
+
+def gather_rings(owner_of_tile, received, tiles_x, tiles_y):
+    both_rows = received.shape[1]
     rows = both_rows // 2
-    per_home = tiles_x * tiles_y
-    smem = pl.BlockSpec(memory_space=pltpu.SMEM)
-    hbm = pl.BlockSpec(memory_space=pl.ANY)
-    vmem = pl.BlockSpec(memory_space=pltpu.VMEM)
-    f32 = lambda *shape: jax.ShapeDtypeStruct(shape, jnp.float32)
-    packs = [f32(tiles_y // 4, rows, LANES)] * 2 + [f32(tiles_x // 4, rows, LANES)] * 2
-    sizes = dict(tiles_x=tiles_x, tiles_y=tiles_y)
-    params = pltpu.CompilerParams(vmem_limit_bytes=32 << 20)
+    outs = [f32(tiles_x * tiles_y, both_rows, LANES)] + border_shapes(tiles_x, tiles_y, rows)
+    return ring_call(gather_rings_kernel, tiles_x, tiles_y, rows, outs, [], "gather_rings")(owner_of_tile, received)
+
+
+def relay_rings(owner_of_tile, rings, borders, wind_ring, settle_speed, bin_share, tiles_x, tiles_y, owners):
+    per_home, both_rows, _ = rings.shape
+    rows = both_rows // 2
     ext = pltpu.VMEM(((tiles_x + 2) * (tiles_y + 2), rows, LANES), jnp.float32)
-    sems = pltpu.SemaphoreType.DMA((per_home,))
-    cost = pl.CostEstimate(flops=1 << 22, bytes_accessed=per_home * both_rows * LANES * 12, transcendentals=0)
-    rings, *borders = pl.pallas_call(
-        functools.partial(gather_rings_kernel, **sizes),
-        in_specs=[smem, hbm],
-        out_specs=[vmem] * 5,
-        out_shape=[f32(per_home, both_rows, LANES)] + packs,
-        scratch_shapes=[sems],
-        compiler_params=params,
-        cost_estimate=cost,
-        name="gather_rings",
-    )(owner_of_tile, received)
-    settle_rows = jnp.broadcast_to(jnp.repeat(settle_speed, TZ)[:, None], (rows, LANES))
-    share_rows = jnp.broadcast_to(
-        jnp.stack([bin_share, jnp.zeros_like(bin_share)], axis=1).reshape(-1, 1), (rows, LANES)
-    )
-    seen, later, *borders = pl.pallas_call(
-        functools.partial(advance_rings_kernel, **sizes),
-        in_specs=[smem] + [vmem] * 8,
-        out_specs=[vmem] * 6,
-        out_shape=[f32(per_home, rows, LANES)] * 2 + packs,
-        scratch_shapes=[ext],
-        compiler_params=params,
-        cost_estimate=cost,
-        name="advance_rings",
-    )(owner_of_tile, rings, *exchange_borders(borders), wind_ring, settle_rows, share_rows)
-    return pl.pallas_call(
-        functools.partial(send_seen_kernel, **sizes),
-        in_specs=[smem] + [vmem] * 6,
-        out_specs=hbm,
-        out_shape=f32(owners, both_rows, LANES),
-        scratch_shapes=[ext, pltpu.VMEM((per_home, both_rows, LANES), jnp.float32), sems],
-        compiler_params=params,
-        cost_estimate=cost,
-        name="send_seen",
-    )(owner_of_tile, later, *exchange_borders(borders), seen)
-
-
-def dust_kernel(
-    home_ref, settle_ref, share_ref, dust_ref, wind_hbm, seen_hbm, out_ref, wind, seen, wind_sems, seen_sems,
-    *, block, bins
-):
+    settle_rows = jnp.broadcast_to(settle_speed[:, None], settle_speed.shape + (LANES,))
+    share_rows = jnp.broadcast_to(bin_share[:, None], bin_share.shape + (LANES,))
+    outs = [f32(per_home, rows, LANES)] * 2 + border_shapes(tiles_x, tiles_y, rows)
+    advance = ring_call(advance_rings_kernel, tiles_x, tiles_y, rows, outs, [ext], "advance_rings")
+    seen, later, *borders = advance(owner_of_tile, rings, *borders, wind_ring, settle_rows, share_rows)
+    outs = [f32(owners, both_rows, LANES)]
+    scratch = [ext, pltpu.VMEM((per_home, both_rows, LANES), jnp.float32), pltpu.SemaphoreType.DMA((per_home,))]
+    send = ring_call(send_seen_kernel, tiles_x, tiles_y, rows, outs, scratch, "send_seen", hbm_out=True)
+    return send(owner_of_tile, later, *exchange_borders(borders), seen)
+
+
+def dust_kernel(home_ref, share_ref, settle_ref, dust_ref, shift_ref, wind_ref, *refs, block, bins, outer):
+    if outer:
+        side_ref, seen_ref, out_ref, coef, sides, edges, *work = refs
+    else:
+        out_ref, coef, *work = refs
+    lanes = len(work) // 2
     step = pl.program_id(0)
-    slots = wind.shape[0]
-
-    def wind_copy(s):
-        return pltpu.make_async_copy(wind_hbm.at[home_ref[s]], wind.at[s], wind_sems.at[s])
-
-    def seen_copy(s):
-        return pltpu.make_async_copy(seen_hbm.at[home_ref[s]], seen.at[s], seen_sems.at[s])
-
-    @pl.when(step == 0)
-    def _():
-        def start(s, carry):
-            wind_copy(s).start()
-            seen_copy(s).start()
-            return carry
-
-        lax.fori_loop(0, slots, start, 0)
-
-    row, lane = iotas()
+    each = TZ * bins
+    if outer:
+        for j in range(block):
+            edges[j] = seen_ref[home_ref[step * block + j]]
+        spread = jnp.dot(
+            jnp.concatenate(halves_of(edges[...].reshape(block * 2 * each, LANES)), axis=1),
+            side_ref[...],
+            preferred_element_type=jnp.float32,
+        )
+        for r in range(ROWS):
+            sides[r] = spread[:, r * LANES : (r + 1) * LANES]
+
+    _, lane = iotas()
     within = lane % TILE
     first_y, last_y = within == 0, within == TILE - 1
-    first_x = (row == 0) & (lane < TILE)
-    last_x = (row == ROWS - 1) & (lane >= LANES - TILE)
     low_lanes, high_lanes = lane < TILE, lane >= LANES - TILE
-    along = 4 * row + lane // TILE
-    from_sides = jnp.where(first_y, SOUTH * TILE, NORTH * TILE) + along
     mix = dust_step * diffusion
-    rows = bins * TZ
-
-    def one(j, carry):
-        s = step * block + j
-        wind_copy(s).wait()
-        seen_copy(s).wait()
-        plane = [wind[s, p * ROWS : (p + 1) * ROWS, :] * dust_step for p in range(PLANES)]
-        west_by, east_by, south_by, north_by, keep = [], [], [], [], []
+    chunks = bins // ROWS
+    settle = [dust_step * settle_ref[h * ROWS : (h + 1) * ROWS, :] for h in range(chunks)]
+    share = [share_ref[h * ROWS : (h + 1) * ROWS, :] for h in range(chunks)]
+
+    def prepare(k, j):
+        held = work[2 * k]
+        home = home_ref[step * block + j]
+        plane = [wind_ref[home, p * ROWS : (p + 1) * ROWS, :] * dust_step for p in range(PLANES)]
         for level in range(TZ):
             u, v = plane[level], plane[TZ + level]
-            west_by.append(mix + jnp.maximum(u, 0.0))
-            east_by.append(mix + jnp.maximum(-u, 0.0))
-            south_by.append(mix + jnp.maximum(v, 0.0))
-            north_by.append(mix + jnp.maximum(-v, 0.0))
-            keep.append(1.0 - 6.0 * mix - jnp.abs(u) - jnp.abs(v))
-        for b in range(bins):
-            q = [dust_ref[j, b, pl.ds(level, ROWS, stride=TZ), :] for level in range(TZ)]
-            settle = settle_ref[b] * dust_step
-            stay, mixed = [], []
+            south_by = mix + jnp.maximum(v, 0.0)
+            north_by = mix + jnp.maximum(-v, 0.0)
+            coef[k, 0, level] = mix + jnp.maximum(u, 0.0)
+            coef[k, 1, level] = mix + jnp.maximum(-u, 0.0)
+            coef[k, 4, level] = 1.0 - 6.0 * mix - jnp.abs(u) - jnp.abs(v)
+            coef[k, 5, level] = plane[2 * TZ + level]
+            if outer:
+                coef[k, 2, level] = south_by
+                coef[k, 3, level] = north_by
+                coef[k, 7, level] = jnp.where(first_y, south_by, jnp.where(last_y, north_by, 0.0))
+            else:
+                coef[k, 2, level] = jnp.where(first_y, 0.0, south_by)
+                coef[k, 3, level] = jnp.where(last_y, 0.0, north_by)
+        coef[k, 6, 0] = plane[PLANES - 1]
+        for r in range(ROWS):
             for level in range(TZ):
-                rise = plane[2 * TZ + level] - settle
-                up = jnp.maximum(rise, 0.0)
-                down = up - rise
-                stay.append(keep[level] - up - down)
-                mixed.append(mix + (down if level == 0 else up))
-            source = plane[PLANES - 1] * share_ref[b]
-            for substep in range(2):
-                new = []
+                at = (r * TZ + level) * bins
+                cells = dust_ref[j, pl.ds(r * TZ + level, bins, stride=ROWS * TZ), :]
+                if not outer:
+                    held[at : at + bins, :] = cells
+                    continue
+                for h in range(chunks):
+                    edge_at = level * bins + h * ROWS
+                    q = cells[h * ROWS : (h + 1) * ROWS]
+                    q = q + spread_rows(coef[k, 7, level, r : r + 1, :]) * sides[r, pl.ds(j * 2 * each + edge_at, ROWS), :]
+                    if r == 0 or r == ROWS - 1:
+                        edge = edges[j, edge_at : edge_at + ROWS, :]
+                        here = low_lanes if r == 0 else high_lanes
+                        by = spread_rows(coef[k, 0 if r == 0 else 1, level, r : r + 1, :])
+                        q = q + jnp.where(here, by * edge, 0.0)
+                    held[at + h * ROWS : at + (h + 1) * ROWS, :] = q
+
+    def shift(k):
+        held, shifts = work[2 * k], work[2 * k + 1]
+        shifts[...] = jnp.dot(
+            jnp.concatenate(halves_of(held[...]), axis=1), shift_ref[...], preferred_element_type=jnp.float32
+        )
+
+    def update(k, j):
+        held, shifts = work[2 * k], work[2 * k + 1]
+        nothing = jnp.zeros((ROWS, LANES), jnp.float32)
+        for r in range(ROWS):
+            for h in range(chunks):
+                cells = [held[(r * TZ + level) * bins + h * ROWS :][:ROWS] for level in range(TZ)]
                 for level in range(TZ):
-                    c = q[level]
-                    at = substep * rows + b * TZ + level
-                    edge = spread_rows(seen[s, at : at + 1, :])
-                    side = lane_gather(edge, from_sides)
-                    right = pltpu.roll(c, TILE, 1)
-                    left = pltpu.roll(c, LANES - TILE, 1)
-                    west = jnp.where(low_lanes, pltpu.roll(right, 1, 0), right)
-                    west = jnp.where(first_x, edge, west)
-                    east = jnp.where(high_lanes, pltpu.roll(left, ROWS - 1, 0), left)
-                    east = jnp.where(last_x, edge, east)
-                    south = jnp.where(first_y, side, pltpu.roll(c, 1, 1))
-                    north = jnp.where(last_y, side, pltpu.roll(c, LANES - 1, 1))
+                    at = (r * TZ + level) * bins + h * ROWS
+                    edge_at = each + level * bins + h * ROWS
+
+                    def moved(which, rows_up=0):
+                        first = at + rows_up * TZ * bins
+                        return shifts[first : first + ROWS, which * LANES : (which + 1) * LANES]
+
+                    def by(which):
+                        return spread_rows(coef[k, which, level, r : r + 1, :])
+
+                    edge = edges[j, edge_at : edge_at + ROWS, :] if outer else nothing
+                    before = edge if r == 0 else moved(2, -1)
+                    after = edge if r == ROWS - 1 else moved(3, 1)
+                    south, north = moved(0), moved(1)
+                    if outer:
+                        side = sides[r, pl.ds(j * 2 * each + edge_at, ROWS), :]
+                        south = jnp.where(first_y, side, south)
+                        north = jnp.where(last_y, side, north)
+                    west = jnp.where(low_lanes, before, moved(2))
+                    east = jnp.where(high_lanes, after, moved(3))
+                    rise = by(5) - settle[h]
+                    up = jnp.maximum(rise, 0.0)
+                    mixed = mix + (up - rise if level == 0 else up)
                     value = (
-                        stay[level] * c
-                        + west_by[level] * west
-                        + east_by[level] * east
-                        + south_by[level] * south
-                        + north_by[level] * north
-                        + mixed[level] * q[1 - level]
+                        (by(4) - jnp.abs(rise)) * cells[level]
+                        + by(0) * west
+                        + by(1) * east
+                        + by(2) * south
+                        + by(3) * north
+                        + mixed * cells[1 - level]
                     )
                     if level == 0:
-                        value = value + source
-                    new.append(value)
-                q = new
-            for level in range(TZ):
-                out_ref[j, b, pl.ds(level, ROWS, stride=TZ), :] = q[level]
-        return carry
-
-    lax.fori_loop(0, block, one, 0)
-
-
-def dust_steps(home_of_slot, dust, wind_recv, seen_recv, settle_speed, bin_share):
-    slots, bins = dust.shape[:2]
+                        value = value + spread_rows(coef[k, 6, 0, r : r + 1, :]) * share[h]
+                    first = h * ROWS * ROWS * TZ + r * TZ + level
+                    out_ref[j, pl.ds(first, ROWS, stride=ROWS * TZ), :] = value
+
+    def some(i, carry):
+        for k in range(lanes):
+            prepare(k, i * lanes + k)
+        for k in range(lanes):
+            shift(k)
+        for k in range(lanes):
+            update(k, i * lanes + k)
+        return carry
+
+    lax.fori_loop(0, block // lanes, some, 0)
+
+
+def dust_substep(home_of_slot, dust, wind_recv, settle_speed, bin_share, seen_recv=None):
+    slots, cells = dust.shape[:2]
+    bins = settle_speed.shape[0]
     block = 8 if slots % 8 == 0 else 4
+    lanes = 2
+    outer = seen_recv is not None
     smem = pl.BlockSpec(memory_space=pltpu.SMEM)
-    hbm = pl.BlockSpec(memory_space=pl.ANY)
-    tile = pl.BlockSpec((block,) + dust.shape[1:], lambda i: (i, 0, 0, 0))
+    vmem = pl.BlockSpec(memory_space=pltpu.VMEM)
+    tile = pl.BlockSpec((block, cells, LANES), lambda i: (i, 0, 0))
+    settle = jnp.broadcast_to(settle_speed[:, None], (bins, LANES))
+    share = jnp.broadcast_to(bin_share[:, None], (bins, LANES))
+    inputs = [home_of_slot, share, settle, dust, jnp.asarray(shift_matrix()), wind_recv]
+    scratch = [pltpu.VMEM((lanes, PLANES + 1, TZ, ROWS, LANES), jnp.float32)]
+    if outer:
+        inputs += [jnp.asarray(side_matrix()), seen_recv]
+        scratch += [
+            pltpu.VMEM((ROWS, block * seen_recv.shape[1], LANES), jnp.float32),
+            pltpu.VMEM((block,) + seen_recv.shape[1:], jnp.float32),
+        ]
+    scratch += [pltpu.VMEM((cells, LANES), jnp.float32), pltpu.VMEM((cells, 4 * LANES), jnp.float32)] * lanes
     return pl.pallas_call(
-        functools.partial(dust_kernel, block=block, bins=bins),
+        functools.partial(dust_kernel, block=block, bins=bins, outer=outer),
         grid=(slots // block,),
-        in_specs=[smem, smem, smem, tile, hbm, hbm],
+        in_specs=[smem, vmem, vmem, tile] + [vmem] * (len(inputs) - 4),
         out_specs=tile,
         out_shape=jax.ShapeDtypeStruct(dust.shape, jnp.float32),
-        scratch_shapes=[
-            pltpu.VMEM((slots,) + wind_recv.shape[1:], jnp.float32),
-            pltpu.VMEM((slots,) + seen_recv.shape[1:], jnp.float32),
-            pltpu.SemaphoreType.DMA((slots,)),
-            pltpu.SemaphoreType.DMA((slots,)),
-        ],
+        scratch_shapes=scratch,
         compiler_params=pltpu.CompilerParams(vmem_limit_bytes=32 << 20),
         cost_estimate=pl.CostEstimate(flops=60 * dust.size, bytes_accessed=dust.size * 12, transcendentals=0),
-        name="dust_steps",
-    )(home_of_slot, settle_speed, bin_share, dust, wind_recv, seen_recv)
+        name="dust_outer" if outer else "dust_inner",
+    )(*inputs)
 
 
 def relay_rows(rows):
@@ -635,21 +724,29 @@
     )
 
     dust = dust_mass.reshape(slots, bins, TZ, ROWS, LANES).transpose(0, 1, 3, 2, 4)
-    dust = dust.reshape(slots, bins, ROWS * TZ, LANES)
+    dust = dust.reshape(slots, bins * ROWS * TZ, LANES)
 
     xlo = shifted(velocity[:, :, -1, :], "gx", 1)
     xhi = shifted(velocity[:, :, 0, :], "gx", -1)
     ylo = shifted(velocity[:, :, :, -1], "gy", 1)
     yhi = shifted(velocity[:, :, :, 0], "gy", -1)
 
-    strips = relay_rows(dust_strips(home_of_slot, dust, owners))
+    strips_send = dust_strips(home_of_slot, dust, bins, owners)
+    strips_send, xlo, xhi, ylo, yhi = lax.optimization_barrier((strips_send, xlo, xhi, ylo, yhi))
+    strips = relay_rows(strips_send)
     new_velocity, wind_send, wind_ring = wind_step(
         owner_of_tile, velocity, xlo, xhi, ylo, yhi, threshold, owners
     )
+    rings, *borders = gather_rings(owner_of_tile, strips, tiles_x, tiles_y)
+    borders = exchange_borders(borders)
+    wind_send, *borders = lax.optimization_barrier((wind_send, *borders))
     wind_recv = relay_rows(wind_send)
-    seen_send = relay_strips(owner_of_tile, strips, wind_ring, settle_speed, bin_share, tiles_x, tiles_y)
+    seen_send = relay_rings(
+        owner_of_tile, rings, borders, wind_ring, settle_speed, bin_share, tiles_x, tiles_y, owners
+    )
     seen_recv = relay_rows(seen_send)
-    out = dust_steps(home_of_slot, dust, wind_recv, seen_recv, settle_speed, bin_share)
+    inner = dust_substep(home_of_slot, dust, wind_recv, settle_speed, bin_share)
+    out = dust_substep(home_of_slot, inner, wind_recv, settle_speed, bin_share, seen_recv)
     out = out.reshape(slots, bins, ROWS, TZ, LANES).transpose(0, 1, 3, 2, 4).reshape(dust_mass.shape)
     return new_velocity, out
 

time: 345 us -> 298 us (0.86)
  blocking collectives: 62.4 us -> 0 us
  waiting for transfers between devices: 68.7 us -> 111 us
  Pallas kernels: 138 us -> 101 us
  local copies, waits for them, and re-layouts: 31.5 us -> 41.4 us
    all_to_all x2 -> x3, waiting for transfers between devices: 0.01 us -> 84.9 us  [relay_rows(): return lax.all_to_all(rows, AXES, split_axis=0, concat_axis=0, tiled=True)]
    all_to_all x1 -> x0, blocking collectives: 62.4 us -> none  [relay_rows(): return lax.all_to_all(rows, AXES, split_axis=0, concat_axis=0, tiled=True)]
    ppermute x12, waiting for transfers between devices: 68.7 us -> 26.2 us  [shifted(): lax.ppermute(value, axis, [(source, (source + steps) % count) for source...]
    pallas_call x4 -> x5, Pallas kernels: 89.3 us -> 56.6 us  [the longest x2 32.2 us: dust_substep(): pl.pallas_call(functools.partial(dust_kernel, block=block, bins=bins, out...]
    unnamed x25 -> x42, local copies, waits for them, and re-layouts: 19.6 us -> 28.3 us
    pallas_call x1, Pallas kernels: 12.3 us -> 7.68 us  [dust_strips(): pl.pallas_call(functools.partial(strips_kernel, block=block, bins=bins),...]
    all_to_all x2 -> x3, starting transfers between devices: 20.8 us -> 21.6 us  [relay_rows(): return lax.all_to_all(rows, AXES, split_axis=0, concat_axis=0, tiled=True)]
  transfers between devices with their start and end apart: 14 -> 15, of which waited for: 7 -> 5; matrix products, arithmetic and copies ran while one was open for 5% -> 6% of each run, Pallas kernels for 18% -> 26%
where the time goes in v2:
time: 298 us
  waiting for transfers between devices  111 us (37%)
  Pallas kernels  101 us (34%)
  starting transfers between devices  42.8 us (14%)
  local copies, waits for them, and re-layouts  41.4 us (14%)
    all_to_all x3, waiting for transfers between devices, relay_rows(): return lax.all_to_all(rows, AXES, split_axis=0, concat_axis=0, tiled=True)  84.9 us
    pallas_call x1, Pallas kernels, wind_step(): pl.pallas_call(functools.partial(wind_kernel, levels=levels), in_specs=[s...  36.7 us
    pallas_call x2, Pallas kernels, dust_substep(): pl.pallas_call(functools.partial(dust_kernel, block=block, bins=bins, out...  32.2 us
    unnamed x42, local copies, waits for them, and re-layouts  28.3 us
    ppermute x12, waiting for transfers between devices, shifted(): lax.ppermute(value, axis, [(source, (source + steps) % count) for source...  26.2 us
    pallas_call x3, Pallas kernels, call(): pl.pallas_call(functools.partial(kernel, tiles_x=tiles_x, tiles_y=tiles_y...  24.4 us
    all_to_all x3, starting transfers between devices, relay_rows(): return lax.all_to_all(rows, AXES, split_axis=0, concat_axis=0, tiled=True)  21.6 us
    ppermute x12, starting transfers between devices, shifted(): lax.ppermute(value, axis, [(source, (source + steps) % count) for source...  21.3 us
  transfers between devices with their start and end apart: 15, of which 5 were waited for; matrix products, arithmetic and copies ran while one was open for 6% of the time, Pallas kernels for 26%

profile of v2, /device:TPU:1, one launch (start us, length us, event | category | flops | bytes accessed | tf_op | source)
XLA Modules:
  0.0 297.8 jit_solution(858859683886404763)
XLA Ops:
  5.6 4.5 %fusion.13 = (f32[3,6,256,1]{3,2,1,0:T(8,128)S(1)}, f32[3,6,256,1]{3,2,1,0:T(8,128)}) fusion(f32[3,6,256,256]{3,2,1,0:T(8,128)} %param.11), kind=kLoop, calls=%fused_computation.40 | loop fusion | bytes 73728 | tf_op jit(solution)/shard_map/slice | solution.py:732
  15.3 4.4 %collective-permute-start.3 = (f32[3,6,256]{2,1,0:T(8,128)S(1)}, f32[3,6,256]{2,1,0:T(8,128)S(1)}, u32[]{:S(2)}, u32[]{:S(2)}) collective-permute-start(f32[3,6,256]{2,1,0:T(8,128)S(1)} %bitcast.25), channel_id=1, source_target_pairs={{0,15},{1,0},{2,1},{3,2},{4,3},{5,4},{6,5},{7,6},{8,7},{9,8},{10,9... | collective-permute-start | bytes 55304 | tf_op jit(solution)/shard_map/ppermute | solution.py:481
  20.1 3.1 %copy-done = f32[56,16,2,1024]{3,2,1,0:T(2,128)S(1)} copy-done((f32[56,16,2,1024]{3,2,1,0:T(2,128)S(1)}, f32[56,16,2,1024]{3,2,1,0:T(2,128)}, u32[]{:S(2)}) %copy-start) | copy-done | bytes 7340056
  23.2 7.7 %dust_strips.1 = f32[128,64,128]{2,1,0:T(8,128)S(1)} custom-call(s32[56]{0:T(128)S(1)} %select_reduce_fusion.1.home_ref, f32[56,256,128]{2,1,0:T(8,128)S(1)} %bitcast.20, bf16[2048,256]{1,0:T(8,128)(2,1)S(1)} %copy-done.12), custom_call_target="tpu_custom_call" | custom-call | flops 36700160 | bytes 9175040 | tf_op jit(solution)/shard_map/dust_strips/pallas_call | solution.py:145
  32.9 7.1 %all-to-all-start = ((f32[128,64,128]{2,1,0:T(8,128)}), f32[128,64,128]{2,1,0:T(8,128)}, u32[]{:S(2)}, u32[]{:S(2)}) async-start(f32[128,64,128]{2,1,0:T(8,128)} %copy-done.5), calls=%async_computation | async-start | bytes 8388608 | tf_op jit(solution)/shard_map/all_to_all | solution.py:700
  40.3 51.8 %all-to-all-done.recv_ref = f32[128,64,128]{2,1,0:T(8,128)} async-done(((f32[128,64,128]{2,1,0:T(8,128)}), f32[128,64,128]{2,1,0:T(8,128)}, u32[]{:S(2)}, u32[]{:S(2)}) %all-to-all-start) | async-done | bytes 4194336 | tf_op jit(solution)/shard_map/all_to_all | solution.py:700
  92.1 3.0 %gather_rings.1 = (f32[64,64,128]{2,1,0:T(8,128)S(1)}, f32[2,32,128]{2,1,0:T(8,128)S(1)}, f32[2,32,128]{2,1,0:T(8,128)S(1)}, f32[2,32,128]{2,1,0:T(8,128)S(1)}, f32[2,32,128]{2,1,0:T(8,128)S(1)}) custom-call(s32[64]{0:T(128)S(1)} %select_reduce_fusion.owner_ref, f32[128,64,128]{2,1,0:T(8,128)} %all-to-all-done.recv_ref), custom_call_target="tpu_custom_call" | custom-call | flops 4194304 | bytes 4194304 | tf_op jit(solution)/shard_map/gather_rings/pallas_call | solution.py:499
  98.0 3.9 %collective-permute-start.7 = (f32[2,32,128]{2,1,0:T(8,128)S(1)}, f32[2,32,128]{2,1,0:T(8,128)S(1)}, u32[]{:S(2)}, u32[]{:S(2)}) collective-permute-start(f32[2,32,128]{2,1,0:T(8,128)S(1)} %get-tuple-element.36), channel_id=1, source_target_pairs={{0,15},{1,0},{2,1},{3,2},{4,3},{5,4},{6,5},{7,6},{8,7},{9,8},{10,9... | collective-permute-start | bytes 98312 | tf_op jit(solution)/shard_map/ppermute | solution.py:481
  105.7 3.6 %reshape.51.yhi_ref = f32[18,256,1]{2,1,0:T(8,128)} reshape(f32[3,6,256]{2,1,0:T(8,128)S(1)} %collective-permute-done.3) | data formatting | bytes 36864 | tf_op jit(solution)/shard_map/reshape | solution.py:291
  113.3 36.7 %wind_step.1 = (f32[18,256,256]{2,1,0:T(8,128)}, f32[128,56,128]{2,1,0:T(8,128)S(1)}, f32[64,8,128]{2,1,0:T(8,128)S(1)}) custom-call(s32[64]{0:T(128)S(1)} %select_reduce_fusion.owner_ref, f32[18,256,256]{2,1,0:T(8,128)S(1)} %bitcast.22, f32[18,1,256]{2,1,0:T(1,128)S(1)} %reshape.43.xlo_ref, f32[18,1,256]{2,1,0:T(1,128)S(1)} %reshape.44.xhi_ref, ...), custom_call_target="tpu_custom_call" | custom-call | flops 47185920 | bytes 11796480 | tf_op jit(solution)/shard_map/wind_step/pallas_call | solution.py:264
  151.9 8.0 %all-to-all-start.1 = ((f32[128,56,128]{2,1,0:T(8,128)}), f32[128,56,128]{2,1,0:T(8,128)}, u32[]{:S(2)}, u32[]{:S(2)}) async-start(f32[128,56,128]{2,1,0:T(8,128)} %copy-done.8), calls=%async_computation.1 | async-start | bytes 7340032 | tf_op jit(solution)/shard_map/all_to_all | solution.py:700
  160.1 12.1 %advance_rings.1 = (f32[64,32,128]{2,1,0:T(8,128)S(1)}, f32[64,32,128]{2,1,0:T(8,128)S(1)}, f32[2,32,128]{2,1,0:T(8,128)S(1)}, f32[2,32,128]{2,1,0:T(8,128)S(1)}...) custom-call(s32[64]{0:T(128)S(1)} %select_reduce_fusion.owner_ref, f32[64,64,128]{2,1,0:T(8,128)S(1)} %copy-done.10, ...), custom_call_target="tpu_custom_call" | custom-call | flops 4194304 | bytes 4194304 | tf_op jit(solution)/shard_map/advance_rings/pallas_call | solution.py:499
  175.4 3.9 %collective-permute-start.11 = (f32[2,32,128]{2,1,0:T(8,128)S(1)}, f32[2,32,128]{2,1,0:T(8,128)S(1)}, u32[]{:S(2)}, u32[]{:S(2)}) collective-permute-start(f32[2,32,128]{2,1,0:T(8,128)S(1)} %get-tuple-element.48), channel_id=1, source_target_pairs={{0,15},{1,0},{2,1},{3,2},{4,3},{5,4},{6,5},{7,6},{8,7},{9,8},{10,9... | collective-permute-start | bytes 98312 | tf_op jit(solution)/shard_map/ppermute | solution.py:481
  179.3 9.0 %collective-permute-done.8.fw_ref = f32[2,32,128]{2,1,0:T(8,128)S(1)} collective-permute-done((f32[2,32,128]{2,1,0:T(8,128)S(1)}, f32[2,32,128]{2,1,0:T(8,128)S(1)}, u32[]{:S(2)}, u32[]{:S(2)}) %collective-permute-start.8) | collective-permute-done | bytes 32800 | tf_op jit(solution)/shard_map/ppermute | solution.py:481
  188.3 9.3 %collective-permute-done.9.fe_ref = f32[2,32,128]{2,1,0:T(8,128)S(1)} collective-permute-done((f32[2,32,128]{2,1,0:T(8,128)S(1)}, f32[2,32,128]{2,1,0:T(8,128)S(1)}, u32[]{:S(2)}, u32[]{:S(2)}) %collective-permute-start.9) | collective-permute-done | bytes 32800 | tf_op jit(solution)/shard_map/ppermute | solution.py:481
  197.6 7.8 %collective-permute-done.10.fs_ref = f32[2,32,128]{2,1,0:T(8,128)S(1)} collective-permute-done((f32[2,32,128]{2,1,0:T(8,128)S(1)}, f32[2,32,128]{2,1,0:T(8,128)S(1)}, u32[]{:S(2)}, u32[]{:S(2)}) %collective-permute-start.10) | collective-permute-done | bytes 32800 | tf_op jit(solution)/shard_map/ppermute | solution.py:481
  205.5 9.2 %send_seen.1 = f32[128,64,128]{2,1,0:T(8,128)S(1)} custom-call(s32[64]{0:T(128)S(1)} %select_reduce_fusion.owner_ref, f32[64,32,128]{2,1,0:T(8,128)S(1)} %get-tuple-element.44.later_ref, f32[2,32,128]{2,1,0:T(8,128)S(1)} %collective-permute-done.8.fw_ref, f32[2,32,128]{2,1,0:T(8,128)S(1)} %collective-permute-done.9.fe_ref, ...), custom_call_target="tpu_custom_call" | custom-call | flops 4194304 | bytes 4194304 | tf_op jit(solution)/shard_map/send_seen/pallas_call | solution.py:499
  216.7 6.5 %all-to-all-start.2 = ((f32[128,64,128]{2,1,0:T(8,128)}), f32[128,64,128]{2,1,0:T(8,128)}, u32[]{:S(2)}, u32[]{:S(2)}) async-start(f32[128,64,128]{2,1,0:T(8,128)} %copy-done.6), calls=%async_computation.2 | async-start | bytes 8388608 | tf_op jit(solution)/shard_map/all_to_all | solution.py:700
  223.3 3.1 %copy-done.1 = f32[56,16,2,1024]{3,2,1,0:T(2,128)S(1)} copy-done((f32[56,16,2,1024]{3,2,1,0:T(2,128)S(1)}, f32[56,16,2,1024]{3,2,1,0:T(2,128)}, u32[]{:S(2)}) %copy-start.1) | copy-done | bytes 7340056
  226.3 12.8 %dust_inner.1.dust_ref = f32[56,256,128]{2,1,0:T(8,128)S(1)} custom-call(s32[56]{0:T(128)S(1)} %select_reduce_fusion.1.home_ref, f32[16,128]{1,0:T(8,128)S(1)} %broadcast_in_dim.34.share_ref, f32[16,128]{1,0:T(8,128)S(1)} %broadcast_in_dim.35.settle_ref, f32[56,256,128]{2,1,0:T(8,128)S(1)} %bitcast.21, bf16[256,512]{1,0:T(8,128)(2,1)S(1)} %copy-done.11, ...), custom_call_target="tpu_custom_call" | custom-call | flops 110100480 | bytes 22020096 | tf_op jit(solution)/shard_map/dust_inner/pallas_call | solution.py:686
  239.2 3.0 %copy-done.2 = f32[56,256,128]{2,1,0:T(8,128)} copy-done((f32[56,256,128]{2,1,0:T(8,128)}, f32[56,256,128]{2,1,0:T(8,128)S(1)}, u32[]{:S(2)}) %copy-start.2) | copy-done | bytes 7340056
  242.2 33.1 %all-to-all-done.2.refs_1_ = f32[128,64,128]{2,1,0:T(8,128)} async-done(((f32[128,64,128]{2,1,0:T(8,128)}), f32[128,64,128]{2,1,0:T(8,128)}, u32[]{:S(2)}, u32[]{:S(2)}) %all-to-all-start.2) | async-done | bytes 4194336 | tf_op jit(solution)/shard_map/all_to_all | solution.py:700
  275.4 3.1 %copy-done.3 = f32[56,256,128]{2,1,0:T(8,128)S(1)} copy-done((f32[56,256,128]{2,1,0:T(8,128)S(1)}, f32[56,256,128]{2,1,0:T(8,128)}, u32[]{:S(2)}) %copy-start.3) | copy-done | bytes 7340056
  278.4 19.4 %dust_outer.1 = f32[56,256,128]{2,1,0:T(8,128)} custom-call(s32[56]{0:T(128)S(1)} %select_reduce_fusion.1.home_ref, f32[16,128]{1,0:T(8,128)S(1)} %broadcast_in_dim.34.share_ref, f32[16,128]{1,0:T(8,128)S(1)} %broadcast_in_dim.35.settle_ref, f32[56,256,128]{2,1,0:T(8,128)S(1)} %copy-done.3, bf16[256,512]{1,0:T(8,128)(2,1)S(1)} %copy-done.11, ...), custom_call_target="tpu_custom_call" | custom-call | flops 110100480 | bytes 22020096 | tf_op jit(solution)/shard_map/dust_outer/pallas_call | solution.py:686
  (66 shorter events, 30.7 us)
Async XLA Ops:
  2.3 30.6 %collective-permute-start = (f32[3,6,256]{2,1,0:T(8,128)}, f32[3,6,256]{2,1,0:T(8,128)}, u32[]{:S(2)}, u32[]{:S(2)}) collective-permute-start(f32[3,6,256]{2,1,0:T(8,128)} %bitcast.19), channel_id=1, source_target_pairs={{0,16},{16,32},{32,48},{48,64},{64,80},{80,96},{96,112},{112,0},{1... | collective-permute-start | bytes 55304 | tf_op jit(solution)/shard_map/ppermute | solution.py:481
  5.6 27.3 %collective-permute-start.1 = (f32[3,6,256]{2,1,0:T(8,128)}, f32[3,6,256]{2,1,0:T(8,128)}, u32[]{:S(2)}, u32[]{:S(2)}) collective-permute-start(f32[3,6,256]{2,1,0:T(8,128)} %bitcast.18), channel_id=1, source_target_pairs={{0,112},{16,0},{32,16},{48,32},{64,48},{80,64},{96,80},{112,96},{1... | collective-permute-start | bytes 55304 | tf_op jit(solution)/shard_map/ppermute | solution.py:481
  10.1 9.6 %copy-start.15 = (s32[7168]{0:T(1024)S(1)}, s32[7168]{0:T(1024)}, u32[]{:S(2)}) copy-start(s32[7168]{0:T(1024)} %param.16) | copy-start | bytes 86020
  10.1 9.6 %copy-start.16 = (s32[7168]{0:T(1024)S(1)}, s32[7168]{0:T(1024)}, u32[]{:S(2)}) copy-start(s32[7168]{0:T(1024)} %param.17) | copy-start | bytes 86020
  10.1 10.0 %copy-start.12 = (bf16[2048,256]{1,0:T(8,128)(2,1)S(1)}, bf16[2048,256]{1,0:T(8,128)(2,1)}, u32[]{:S(2)}) copy-start(bf16[2048,256]{1,0:T(8,128)(2,1)} %constant.88.clone.matrix_ref) | copy-start | bytes 3145732
  12.7 20.1 %collective-permute-start.2 = (f32[3,6,256]{2,1,0:T(8,128)S(1)}, f32[3,6,256]{2,1,0:T(8,128)S(1)}, u32[]{:S(2)}, u32[]{:S(2)}) collective-permute-start(f32[3,6,256]{2,1,0:T(8,128)S(1)} %bitcast.24), channel_id=1, source_target_pairs={{0,1},{1,2},{2,3},{3,4},{4,5},{5,6},{6,7},{7,8},{8,9},{9,10},{10,1... | collective-permute-start | bytes 55304 | tf_op jit(solution)/shard_map/ppermute | solution.py:481
  15.3 17.5 %collective-permute-start.3 = (f32[3,6,256]{2,1,0:T(8,128)S(1)}, f32[3,6,256]{2,1,0:T(8,128)S(1)}, u32[]{:S(2)}, u32[]{:S(2)}) collective-permute-start(f32[3,6,256]{2,1,0:T(8,128)S(1)} %bitcast.25), channel_id=1, source_target_pairs={{0,15},{1,0},{2,1},{3,2},{4,3},{5,4},{6,5},{7,6},{8,7},{9,8},{10,9... | collective-permute-start | bytes 55304 | tf_op jit(solution)/shard_map/ppermute | solution.py:481
  32.9 59.2 %all-to-all-start = ((f32[128,64,128]{2,1,0:T(8,128)}), f32[128,64,128]{2,1,0:T(8,128)}, u32[]{:S(2)}, u32[]{:S(2)}) async-start(f32[128,64,128]{2,1,0:T(8,128)} %copy-done.5), calls=%async_computation | async-start | bytes 8388608 | tf_op jit(solution)/shard_map/all_to_all | solution.py:700
  96.5 55.4 %collective-permute-start.4 = (f32[2,32,128]{2,1,0:T(8,128)S(1)}, f32[2,32,128]{2,1,0:T(8,128)S(1)}, u32[]{:S(2)}, u32[]{:S(2)}) collective-permute-start(f32[2,32,128]{2,1,0:T(8,128)S(1)} %get-tuple-element.33), channel_id=1, source_target_pairs={{0,16},{16,32},{32,48},{48,64},{64,80},{80,96},{96,112},{112,0},{1... | collective-permute-start | bytes 98312 | tf_op jit(solution)/shard_map/ppermute | solution.py:481
  97.1 54.7 %collective-permute-start.5 = (f32[2,32,128]{2,1,0:T(8,128)S(1)}, f32[2,32,128]{2,1,0:T(8,128)S(1)}, u32[]{:S(2)}, u32[]{:S(2)}) collective-permute-start(f32[2,32,128]{2,1,0:T(8,128)S(1)} %get-tuple-element.34), channel_id=1, source_target_pairs={{0,112},{16,0},{32,16},{48,32},{64,48},{80,64},{96,80},{112,96},{1... | collective-permute-start | bytes 98312 | tf_op jit(solution)/shard_map/ppermute | solution.py:481
  97.1 54.7 %collective-permute-start.6 = (f32[2,32,128]{2,1,0:T(8,128)S(1)}, f32[2,32,128]{2,1,0:T(8,128)S(1)}, u32[]{:S(2)}, u32[]{:S(2)}) collective-permute-start(f32[2,32,128]{2,1,0:T(8,128)S(1)} %get-tuple-element.35), channel_id=1, source_target_pairs={{0,1},{1,2},{2,3},{3,4},{4,5},{5,6},{6,7},{7,8},{8,9},{9,10},{10,1... | collective-permute-start | bytes 98312 | tf_op jit(solution)/shard_map/ppermute | solution.py:481
  98.0 53.8 %collective-permute-start.7 = (f32[2,32,128]{2,1,0:T(8,128)S(1)}, f32[2,32,128]{2,1,0:T(8,128)S(1)}, u32[]{:S(2)}, u32[]{:S(2)}) collective-permute-start(f32[2,32,128]{2,1,0:T(8,128)S(1)} %get-tuple-element.36), channel_id=1, source_target_pairs={{0,15},{1,0},{2,1},{3,2},{4,3},{5,4},{6,5},{7,6},{8,7},{9,8},{10,9... | collective-permute-start | bytes 98312 | tf_op jit(solution)/shard_map/ppermute | solution.py:481
  103.4 5.9 %copy-start.14 = (f32[256,256]{1,0:T(8,128)S(1)}, f32[256,256]{1,0:T(8,128)}, u32[]{:S(2)}) copy-start(f32[256,256]{1,0:T(8,128)} %thr_ref.1) | copy-start | bytes 786436
  151.8 8.1 %copy-start.17 = (f32[16]{0:T(128)S(1)}, f32[16]{0:T(128)}, u32[]{:S(2)}) copy-start(f32[16]{0:T(128)} %param.14) | copy-start | bytes 196
  151.9 8.1 %copy-start.18 = (f32[16]{0:T(128)S(1)}, f32[16]{0:T(128)}, u32[]{:S(2)}) copy-start(f32[16]{0:T(128)} %param.15) | copy-start | bytes 196
  151.9 8.2 %copy-start.10 = (f32[64,64,128]{2,1,0:T(8,128)S(1)}, f32[64,64,128]{2,1,0:T(8,128)}, u32[]{:S(2)}) copy-start(f32[64,64,128]{2,1,0:T(8,128)} %copy-done.9) | copy-start | bytes 6291460
  151.9 64.9 %all-to-all-start.1 = ((f32[128,56,128]{2,1,0:T(8,128)}), f32[128,56,128]{2,1,0:T(8,128)}, u32[]{:S(2)}, u32[]{:S(2)}) async-start(f32[128,56,128]{2,1,0:T(8,128)} %copy-done.8), calls=%async_computation.1 | async-start | bytes 7340032 | tf_op jit(solution)/shard_map/all_to_all | solution.py:700
  172.2 16.1 %collective-permute-start.8 = (f32[2,32,128]{2,1,0:T(8,128)S(1)}, f32[2,32,128]{2,1,0:T(8,128)S(1)}, u32[]{:S(2)}, u32[]{:S(2)}) collective-permute-start(f32[2,32,128]{2,1,0:T(8,128)S(1)} %get-tuple-element.45), channel_id=1, source_target_pairs={{0,16},{16,32},{32,48},{48,64},{64,80},{80,96},{96,112},{112,0},{1... | collective-permute-start | bytes 98312 | tf_op jit(solution)/shard_map/ppermute | solution.py:481
  173.9 23.7 %collective-permute-start.9 = (f32[2,32,128]{2,1,0:T(8,128)S(1)}, f32[2,32,128]{2,1,0:T(8,128)S(1)}, u32[]{:S(2)}, u32[]{:S(2)}) collective-permute-start(f32[2,32,128]{2,1,0:T(8,128)S(1)} %get-tuple-element.46), channel_id=1, source_target_pairs={{0,112},{16,0},{32,16},{48,32},{64,48},{80,64},{96,80},{112,96},{1... | collective-permute-start | bytes 98312 | tf_op jit(solution)/shard_map/ppermute | solution.py:481
  173.9 31.5 %collective-permute-start.10 = (f32[2,32,128]{2,1,0:T(8,128)S(1)}, f32[2,32,128]{2,1,0:T(8,128)S(1)}, u32[]{:S(2)}, u32[]{:S(2)}) collective-permute-start(f32[2,32,128]{2,1,0:T(8,128)S(1)} %get-tuple-element.47), channel_id=1, source_target_pairs={{0,1},{1,2},{2,3},{3,4},{4,5},{5,6},{6,7},{7,8},{8,9},{9,10},{10,1... | collective-permute-start | bytes 98312 | tf_op jit(solution)/shard_map/ppermute | solution.py:481
  175.4 30.1 %collective-permute-start.11 = (f32[2,32,128]{2,1,0:T(8,128)S(1)}, f32[2,32,128]{2,1,0:T(8,128)S(1)}, u32[]{:S(2)}, u32[]{:S(2)}) collective-permute-start(f32[2,32,128]{2,1,0:T(8,128)S(1)} %get-tuple-element.48), channel_id=1, source_target_pairs={{0,15},{1,0},{2,1},{3,2},{4,3},{5,4},{6,5},{7,6},{8,7},{9,8},{10,9... | collective-permute-start | bytes 98312 | tf_op jit(solution)/shard_map/ppermute | solution.py:481
  216.7 6.5 %copy-start.11 = (bf16[256,512]{1,0:T(8,128)(2,1)S(1)}, bf16[256,512]{1,0:T(8,128)(2,1)}, u32[]{:S(2)}) copy-start(bf16[256,512]{1,0:T(8,128)(2,1)} %constant.89.clone.shift_ref) | copy-start | bytes 786436
  216.7 58.6 %all-to-all-start.2 = ((f32[128,64,128]{2,1,0:T(8,128)}), f32[128,64,128]{2,1,0:T(8,128)}, u32[]{:S(2)}, u32[]{:S(2)}) async-start(f32[128,64,128]{2,1,0:T(8,128)} %copy-done.6), calls=%async_computation.2 | async-start | bytes 8388608 | tf_op jit(solution)/shard_map/all_to_all | solution.py:700
  226.3 49.0 %copy-start.13 = (bf16[256,1024]{1,0:T(8,128)(2,1)S(1)}, bf16[256,1024]{1,0:T(8,128)(2,1)}, u32[]{:S(2)}) copy-start(bf16[256,1024]{1,0:T(8,128)(2,1)} %constant.90.clone.refs_0_) | copy-start | bytes 1572868
  (10 other events, 23.5 us)

commit v3 on v2

--- a/solution.py
+++ b/solution.py
@@ -52,6 +52,14 @@
 
 def spread_rows(row):
     return jnp.broadcast_to(row, (ROWS, LANES))
+
+
+def f32(*shape):
+    return jax.ShapeDtypeStruct(shape, jnp.float32)
+
+
+def in_hbm(x):
+    return pltpu.with_memory_space_constraint(x, pltpu.HBM)
 
 
 def halves_of(x):
@@ -150,8 +158,8 @@
             pl.BlockSpec((block, cells, LANES), lambda i: (i, 0, 0)),
             pl.BlockSpec(matrix.shape, lambda i: (0, 0)),
         ],
-        out_specs=pl.BlockSpec(memory_space=pl.ANY),
-        out_shape=jax.ShapeDtypeStruct((owners, rows, LANES), jnp.float32),
+        out_specs=pl.BlockSpec(memory_space=pltpu.HBM),
+        out_shape=pltpu.HBM((owners, rows, LANES), jnp.float32),
         scratch_shapes=[
             pltpu.VMEM((slots, rows, LANES), jnp.float32),
             pltpu.SemaphoreType.DMA((slots,)),
@@ -161,7 +169,7 @@
             flops=20 * dust.size, bytes_accessed=dust.size * 4 + slots * rows * LANES * 4, transcendentals=0
         ),
         name="dust_strips",
-    )(home_of_slot, dust, matrix)
+    )(home_of_slot, in_hbm(dust), matrix)
 
 
 def wind_kernel(
@@ -259,16 +267,16 @@
     fields = comps * levels
     per_home = (nx // TILE) * (ny // TILE)
     smem = pl.BlockSpec(memory_space=pltpu.SMEM)
-    hbm = pl.BlockSpec(memory_space=pl.ANY)
+    hbm = pl.BlockSpec(memory_space=pltpu.HBM)
     vmem = pl.BlockSpec(memory_space=pltpu.VMEM)
     new, send, ring = pl.pallas_call(
         functools.partial(wind_kernel, levels=levels),
         in_specs=[smem, hbm, vmem, vmem, vmem, vmem, vmem],
         out_specs=[vmem, hbm, vmem],
         out_shape=[
-            jax.ShapeDtypeStruct((fields, nx, ny), jnp.float32),
-            jax.ShapeDtypeStruct((owners, PLANES * ROWS, LANES), jnp.float32),
-            jax.ShapeDtypeStruct((per_home, 8, LANES), jnp.float32),
+            f32(fields, nx, ny),
+            pltpu.HBM((owners, PLANES * ROWS, LANES), jnp.float32),
+            f32(per_home, 8, LANES),
         ],
         scratch_shapes=[
             pltpu.VMEM((fields, nx + 16, ny), jnp.float32),
@@ -284,7 +292,7 @@
         name="wind_step",
     )(
         owner_of_tile,
-        velocity.reshape(fields, nx, ny),
+        in_hbm(velocity.reshape(fields, nx, ny)),
         xlo.reshape(fields, 1, ny),
         xhi.reshape(fields, 1, ny),
         ylo.reshape(fields, nx, 1),
@@ -486,10 +494,6 @@
     return shifted(east, "gx", 1), shifted(west, "gx", -1), shifted(north, "gy", 1), shifted(south, "gy", -1)
 
 
-def f32(*shape):
-    return jax.ShapeDtypeStruct(shape, jnp.float32)
-
-
 def ring_call(kernel, tiles_x, tiles_y, rows, outs, scratch, name, hbm_out=False):
     smem = pl.BlockSpec(memory_space=pltpu.SMEM)
     vmem = pl.BlockSpec(memory_space=pltpu.VMEM)
@@ -499,7 +503,7 @@
         return pl.pallas_call(
             functools.partial(kernel, tiles_x=tiles_x, tiles_y=tiles_y),
             in_specs=[smem] + [vmem] * len(inputs),
-            out_specs=pl.BlockSpec(memory_space=pl.ANY) if hbm_out else [vmem] * len(outs),
+            out_specs=pl.BlockSpec(memory_space=pltpu.HBM) if hbm_out else [vmem] * len(outs),
             out_shape=outs[0] if hbm_out else outs,
             scratch_shapes=scratch,
             compiler_params=pltpu.CompilerParams(vmem_limit_bytes=32 << 20),
@@ -530,7 +534,7 @@
     outs = [f32(per_home, rows, LANES)] * 2 + border_shapes(tiles_x, tiles_y, rows)
     advance = ring_call(advance_rings_kernel, tiles_x, tiles_y, rows, outs, [ext], "advance_rings")
     seen, later, *borders = advance(owner_of_tile, rings, *borders, wind_ring, settle_rows, share_rows)
-    outs = [f32(owners, both_rows, LANES)]
+    outs = [pltpu.HBM((owners, both_rows, LANES), jnp.float32)]
     scratch = [ext, pltpu.VMEM((per_home, both_rows, LANES), jnp.float32), pltpu.SemaphoreType.DMA((per_home,))]
     send = ring_call(send_seen_kernel, tiles_x, tiles_y, rows, outs, scratch, "send_seen", hbm_out=True)
     return send(owner_of_tile, later, *exchange_borders(borders), seen)
@@ -540,7 +544,7 @@
     if outer:
         side_ref, seen_ref, out_ref, coef, sides, edges, *work = refs
     else:
-        out_ref, coef, *work = refs
+        out_ref, kept_ref, coef, *work = refs
     lanes = len(work) // 2
     step = pl.program_id(0)
     each = TZ * bins
@@ -567,7 +571,10 @@
     def prepare(k, j):
         held = work[2 * k]
         home = home_ref[step * block + j]
-        plane = [wind_ref[home, p * ROWS : (p + 1) * ROWS, :] * dust_step for p in range(PLANES)]
+        if not outer:
+            kept_ref[j] = wind_ref[home]
+        wind_at = j if outer else home
+        plane = [wind_ref[wind_at, p * ROWS : (p + 1) * ROWS, :] * dust_step for p in range(PLANES)]
         for level in range(TZ):
             u, v = plane[level], plane[TZ + level]
             south_by = mix + jnp.maximum(v, 0.0)
@@ -663,7 +670,7 @@
     lax.fori_loop(0, block // lanes, some, 0)
 
 
-def dust_substep(home_of_slot, dust, wind_recv, settle_speed, bin_share, seen_recv=None):
+def dust_substep(home_of_slot, dust, wind, settle_speed, bin_share, seen_recv=None):
     slots, cells = dust.shape[:2]
     bins = settle_speed.shape[0]
     block = 8 if slots % 8 == 0 else 4
@@ -674,7 +681,8 @@
     tile = pl.BlockSpec((block, cells, LANES), lambda i: (i, 0, 0))
     settle = jnp.broadcast_to(settle_speed[:, None], (bins, LANES))
     share = jnp.broadcast_to(bin_share[:, None], (bins, LANES))
-    inputs = [home_of_slot, share, settle, dust, jnp.asarray(shift_matrix()), wind_recv]
+    wind_rows = pl.BlockSpec((block,) + wind.shape[1:], lambda i: (i, 0, 0))
+    inputs = [home_of_slot, share, settle, in_hbm(dust), jnp.asarray(shift_matrix()), in_hbm(wind) if outer else wind]
     scratch = [pltpu.VMEM((lanes, PLANES + 1, TZ, ROWS, LANES), jnp.float32)]
     if outer:
         inputs += [jnp.asarray(side_matrix()), seen_recv]
@@ -682,13 +690,16 @@
             pltpu.VMEM((ROWS, block * seen_recv.shape[1], LANES), jnp.float32),
             pltpu.VMEM((block,) + seen_recv.shape[1:], jnp.float32),
         ]
+    out_shape = f32(*dust.shape)
+    if not outer:
+        out_shape = [pltpu.HBM(dust.shape, jnp.float32), pltpu.HBM((slots,) + wind.shape[1:], jnp.float32)]
     scratch += [pltpu.VMEM((cells, LANES), jnp.float32), pltpu.VMEM((cells, 4 * LANES), jnp.float32)] * lanes
     return pl.pallas_call(
         functools.partial(dust_kernel, block=block, bins=bins, outer=outer),
         grid=(slots // block,),
-        in_specs=[smem, vmem, vmem, tile] + [vmem] * (len(inputs) - 4),
-        out_specs=tile,
-        out_shape=jax.ShapeDtypeStruct(dust.shape, jnp.float32),
+        in_specs=[smem, vmem, vmem, tile, vmem, wind_rows if outer else vmem] + [vmem] * (len(inputs) - 6),
+        out_specs=tile if outer else [tile, wind_rows],
+        out_shape=out_shape,
         scratch_shapes=scratch,
         compiler_params=pltpu.CompilerParams(vmem_limit_bytes=32 << 20),
         cost_estimate=pl.CostEstimate(flops=60 * dust.size, bytes_accessed=dust.size * 12, transcendentals=0),
@@ -737,6 +748,7 @@
     new_velocity, wind_send, wind_ring = wind_step(
         owner_of_tile, velocity, xlo, xhi, ylo, yhi, threshold, owners
     )
+    strips, wind_send, wind_ring = lax.optimization_barrier((strips, wind_send, wind_ring))
     rings, *borders = gather_rings(owner_of_tile, strips, tiles_x, tiles_y)
     borders = exchange_borders(borders)
     wind_send, *borders = lax.optimization_barrier((wind_send, *borders))
@@ -745,8 +757,8 @@
         owner_of_tile, rings, borders, wind_ring, settle_speed, bin_share, tiles_x, tiles_y, owners
     )
     seen_recv = relay_rows(seen_send)
-    inner = dust_substep(home_of_slot, dust, wind_recv, settle_speed, bin_share)
-    out = dust_substep(home_of_slot, inner, wind_recv, settle_speed, bin_share, seen_recv)
+    inner, wind_held = dust_substep(home_of_slot, dust, wind_recv, settle_speed, bin_share)
+    out = dust_substep(home_of_slot, inner, wind_held, settle_speed, bin_share, seen_recv)
     out = out.reshape(slots, bins, ROWS, TZ, LANES).transpose(0, 1, 3, 2, 4).reshape(dust_mass.shape)
     return new_velocity, out
 

time: 298 us -> 241 us (0.81)
  waiting for transfers between devices: 111 us -> 71.7 us
  local copies, waits for them, and re-layouts: 41.4 us -> 19.5 us
    all_to_all x3, waiting for transfers between devices: 84.9 us -> 44.2 us  [relay_rows(): return lax.all_to_all(rows, AXES, split_axis=0, concat_axis=0, tiled=True)]
    unnamed x42 -> x22, local copies, waits for them, and re-layouts: 28.3 us -> 6.49 us
  transfers between devices with their start and end apart: 15 -> 15, of which waited for: 5 -> 6; matrix products, arithmetic and copies ran while one was open for 6% -> 7% of each run, Pallas kernels for 26% -> 33%
where the time goes in v3:
time: 241 us; the launch traced here: 240 us
  Pallas kernels  102 us (42%)
  waiting for transfers between devices  71.7 us (30%)
  starting transfers between devices  45.4 us (19%)
  local copies, waits for them, and re-layouts  19.5 us (8%)
    all_to_all x3, waiting for transfers between devices, relay_rows(): return lax.all_to_all(rows, AXES, split_axis=0, concat_axis=0, tiled=True)  44.2 us
    pallas_call x1, Pallas kernels, wind_step(): pl.pallas_call(functools.partial(wind_kernel, levels=levels), in_specs=[s...  36 us
    pallas_call x2, Pallas kernels, dust_substep(): pl.pallas_call(functools.partial(dust_kernel, block=block, bins=bins, out...  34.3 us
    ppermute x12, waiting for transfers between devices, shifted(): lax.ppermute(value, axis, [(source, (source + steps) % count) for source...  27.5 us
    all_to_all x3, starting transfers between devices, relay_rows(): return lax.all_to_all(rows, AXES, split_axis=0, concat_axis=0, tiled=True)  24.2 us
    pallas_call x3, Pallas kernels, call(): pl.pallas_call(functools.partial(kernel, tiles_x=tiles_x, tiles_y=tiles_y...  23.2 us
    ppermute x12, starting transfers between devices, shifted(): lax.ppermute(value, axis, [(source, (source + steps) % count) for source...  21.1 us
    pallas_call x1, Pallas kernels, dust_strips(): pl.pallas_call(functools.partial(strips_kernel, block=block, bins=bins),...  8.4 us
  transfers between devices with their start and end apart: 15, of which 6 were waited for; matrix products, arithmetic and copies ran while one was open for 7% of the time, Pallas kernels for 33%

profile of v3, /device:TPU:1, one launch (start us, length us, event | category | flops | bytes accessed | tf_op | source)
XLA Modules:
  0.0 240.0 jit_solution(2009534280915885546)
XLA Ops:
  2.3 2.7 %collective-permute-start = (f32[3,6,256]{2,1,0:T(8,128)}, f32[3,6,256]{2,1,0:T(8,128)}, u32[]{:S(2)}, u32[]{:S(2)}) collective-permute-start(f32[3,6,256]{2,1,0:T(8,128)} %bitcast.19), channel_id=1, source_target_pairs={{0,16},{16,32},{32,48},{48,64},{64,80},{80,96},{96,112},{112,0},{1... | collective-permute-start | bytes 55304 | tf_op jit(solution)/shard_map/ppermute | solution.py:489
  5.6 4.5 %fusion.13 = (f32[3,6,256,1]{3,2,1,0:T(8,128)S(1)}, f32[3,6,256,1]{3,2,1,0:T(8,128)}) fusion(f32[3,6,256,256]{3,2,1,0:T(8,128)} %param.11), kind=kLoop, calls=%fused_computation.40 | loop fusion | bytes 73728 | tf_op jit(solution)/shard_map/slice | solution.py:743
  10.1 2.7 %copy.33 = f32[3,6,256,1]{2,1,0,3:T(8,128)S(1)} copy(f32[3,6,256,1]{3,2,1,0:T(8,128)} %get-tuple-element.63) | data formatting | bytes 36864
  12.8 1.7 collective-permute-start.2
  15.3 4.4 %collective-permute-start.3 = (f32[3,6,256]{2,1,0:T(8,128)S(1)}, f32[3,6,256]{2,1,0:T(8,128)S(1)}, u32[]{:S(2)}, u32[]{:S(2)}) collective-permute-start(f32[3,6,256]{2,1,0:T(8,128)S(1)} %bitcast.25), channel_id=1, source_target_pairs={{0,15},{1,0},{2,1},{3,2},{4,3},{5,4},{6,5},{7,6},{8,7},{9,8},{10,9... | collective-permute-start | bytes 55304 | tf_op jit(solution)/shard_map/ppermute | solution.py:489
  20.1 8.4 %dust_strips.1 = f32[128,64,128]{2,1,0:T(8,128)} custom-call(s32[56]{0:T(128)S(1)} %select_reduce_fusion.1.home_ref, f32[56,256,128]{2,1,0:T(8,128)} %bitcast.20, bf16[2048,256]{1,0:T(8,128)(2,1)S(1)} %copy-done.2), custom_call_target="tpu_custom_call" | custom-call | flops 36700160 | bytes 9175040 | tf_op jit(solution)/shard_map/dust_strips/pallas_call | solution.py:153
  28.5 7.1 %all-to-all-start = ((f32[128,64,128]{2,1,0:T(8,128)}), f32[128,64,128]{2,1,0:T(8,128)}, u32[]{:S(2)}, u32[]{:S(2)}) async-start(f32[128,64,128]{2,1,0:T(8,128)} %dust_strips.1), calls=%async_computation | async-start | bytes 8388608 | tf_op jit(solution)/shard_map/all_to_all | solution.py:711
  37.5 2.2 reshape.50.ylo_ref
  39.7 3.6 %reshape.51.yhi_ref = f32[18,256,1]{2,1,0:T(8,128)} reshape(f32[3,6,256]{2,1,0:T(8,128)S(1)} %collective-permute-done.3) | data formatting | bytes 36864 | tf_op jit(solution)/shard_map/reshape | solution.py:299
  45.0 36.0 %wind_step.1 = (f32[18,256,256]{2,1,0:T(8,128)}, f32[128,56,128]{2,1,0:T(8,128)}, f32[64,8,128]{2,1,0:T(8,128)S(1)}) custom-call(s32[64]{0:T(128)S(1)} %select_reduce_fusion.owner_ref, f32[18,256,256]{2,1,0:T(8,128)} %bitcast.22, f32[18,1,256]{2,1,0:T(1,128)S(1)} %reshape.43.xlo_ref, f32[18,1,256]{2,1,0:T(1,128)S(1)} %reshape.44.xhi_ref, ...), custom_call_target="tpu_custom_call" | custom-call | flops 47185920 | bytes 11796480 | tf_op jit(solution)/shard_map/wind_step/pallas_call | solution.py:272
  81.0 6.7 %all-to-all-done.recv_ref = f32[128,64,128]{2,1,0:T(8,128)} async-done(((f32[128,64,128]{2,1,0:T(8,128)}), f32[128,64,128]{2,1,0:T(8,128)}, u32[]{:S(2)}, u32[]{:S(2)}) %all-to-all-start) | async-done | bytes 4194336 | tf_op jit(solution)/shard_map/all_to_all | solution.py:711
  87.7 3.0 %gather_rings.1 = (f32[64,64,128]{2,1,0:T(8,128)S(1)}, f32[2,32,128]{2,1,0:T(8,128)S(1)}, f32[2,32,128]{2,1,0:T(8,128)S(1)}, f32[2,32,128]{2,1,0:T(8,128)S(1)}, f32[2,32,128]{2,1,0:T(8,128)S(1)}) custom-call(s32[64]{0:T(128)S(1)} %select_reduce_fusion.owner_ref, f32[128,64,128]{2,1,0:T(8,128)} %all-to-all-done.recv_ref), custom_call_target="tpu_custom_call" | custom-call | flops 4194304 | bytes 4194304 | tf_op jit(solution)/shard_map/gather_rings/pallas_call | solution.py:503
  92.3 3.9 %collective-permute-start.7 = (f32[2,32,128]{2,1,0:T(8,128)S(1)}, f32[2,32,128]{2,1,0:T(8,128)S(1)}, u32[]{:S(2)}, u32[]{:S(2)}) collective-permute-start(f32[2,32,128]{2,1,0:T(8,128)S(1)} %get-tuple-element.44), channel_id=1, source_target_pairs={{0,15},{1,0},{2,1},{3,2},{4,3},{5,4},{6,5},{7,6},{8,7},{9,8},{10,9... | collective-permute-start | bytes 98312 | tf_op jit(solution)/shard_map/ppermute | solution.py:489
  97.5 10.6 %all-to-all-start.1 = ((f32[128,56,128]{2,1,0:T(8,128)}), f32[128,56,128]{2,1,0:T(8,128)}, u32[]{:S(2)}, u32[]{:S(2)}) async-start(f32[128,56,128]{2,1,0:T(8,128)} %get-tuple-element.45), calls=%async_computation.1 | async-start | bytes 7340032 | tf_op jit(solution)/shard_map/all_to_all | solution.py:711
  108.3 12.1 %advance_rings.1 = (f32[64,32,128]{2,1,0:T(8,128)S(1)}, f32[64,32,128]{2,1,0:T(8,128)S(1)}, f32[2,32,128]{2,1,0:T(8,128)S(1)}, f32[2,32,128]{2,1,0:T(8,128)S(1)}...) custom-call(s32[64]{0:T(128)S(1)} %select_reduce_fusion.owner_ref, ...), custom_call_target="tpu_custom_call" | custom-call | flops 4194304 | bytes 4194304 | tf_op jit(solution)/shard_map/advance_rings/pallas_call | solution.py:503
  123.5 3.9 %collective-permute-start.11 = (f32[2,32,128]{2,1,0:T(8,128)S(1)}, f32[2,32,128]{2,1,0:T(8,128)S(1)}, u32[]{:S(2)}, u32[]{:S(2)}) collective-permute-start(f32[2,32,128]{2,1,0:T(8,128)S(1)} %get-tuple-element.58), channel_id=1, source_target_pairs={{0,15},{1,0},{2,1},{3,2},{4,3},{5,4},{6,5},{7,6},{8,7},{9,8},{10,9... | collective-permute-start | bytes 98312 | tf_op jit(solution)/shard_map/ppermute | solution.py:489
  127.4 10.6 %collective-permute-done.8.fw_ref = f32[2,32,128]{2,1,0:T(8,128)S(1)} collective-permute-done((f32[2,32,128]{2,1,0:T(8,128)S(1)}, f32[2,32,128]{2,1,0:T(8,128)S(1)}, u32[]{:S(2)}, u32[]{:S(2)}) %collective-permute-start.8) | collective-permute-done | bytes 32800 | tf_op jit(solution)/shard_map/ppermute | solution.py:489
  137.9 7.9 %collective-permute-done.9.fe_ref = f32[2,32,128]{2,1,0:T(8,128)S(1)} collective-permute-done((f32[2,32,128]{2,1,0:T(8,128)S(1)}, f32[2,32,128]{2,1,0:T(8,128)S(1)}, u32[]{:S(2)}, u32[]{:S(2)}) %collective-permute-start.9) | collective-permute-done | bytes 32800 | tf_op jit(solution)/shard_map/ppermute | solution.py:489
  145.8 7.8 %collective-permute-done.10.fs_ref = f32[2,32,128]{2,1,0:T(8,128)S(1)} collective-permute-done((f32[2,32,128]{2,1,0:T(8,128)S(1)}, f32[2,32,128]{2,1,0:T(8,128)S(1)}, u32[]{:S(2)}, u32[]{:S(2)}) %collective-permute-start.10) | collective-permute-done | bytes 32800 | tf_op jit(solution)/shard_map/ppermute | solution.py:489
  153.5 8.0 %send_seen.1 = f32[128,64,128]{2,1,0:T(8,128)} custom-call(s32[64]{0:T(128)S(1)} %select_reduce_fusion.owner_ref, f32[64,32,128]{2,1,0:T(8,128)S(1)} %get-tuple-element.54.later_ref, f32[2,32,128]{2,1,0:T(8,128)S(1)} %collective-permute-done.8.fw_ref, f32[2,32,128]{2,1,0:T(8,128)S(1)} %collective-permute-done.9.fe_ref, ...), custom_call_target="tpu_custom_call" | custom-call | flops 4194304 | bytes 4194304 | tf_op jit(solution)/shard_map/send_seen/pallas_call | solution.py:503
  161.6 6.6 %all-to-all-start.2 = ((f32[128,64,128]{2,1,0:T(8,128)}), f32[128,64,128]{2,1,0:T(8,128)}, u32[]{:S(2)}, u32[]{:S(2)}) async-start(f32[128,64,128]{2,1,0:T(8,128)} %send_seen.1), calls=%async_computation.2 | async-start | bytes 8388608 | tf_op jit(solution)/shard_map/all_to_all | solution.py:711
  168.2 14.6 %dust_inner.1 = (f32[56,256,128]{2,1,0:T(8,128)}, f32[56,56,128]{2,1,0:T(8,128)}) custom-call(s32[56]{0:T(128)S(1)} %select_reduce_fusion.1.home_ref, f32[16,128]{1,0:T(8,128)S(1)} %broadcast_in_dim.34.share_ref, f32[16,128]{1,0:T(8,128)S(1)} %broadcast_in_dim.35.settle_ref, f32[56,256,128]{2,1,0:T(8,128)} %bitcast.21, bf16[256,512]{1,0:T(8,128)(2,1)S(1)} %copy-done.1, ...), custom_call_target="tpu_custom_call" | custom-call | flops 110100480 | bytes 22020096 | tf_op jit(solution)/shard_map/dust_inner/pallas_call | solution.py:697
  182.8 37.4 %all-to-all-done.2.refs_1_ = f32[128,64,128]{2,1,0:T(8,128)} async-done(((f32[128,64,128]{2,1,0:T(8,128)}), f32[128,64,128]{2,1,0:T(8,128)}, u32[]{:S(2)}, u32[]{:S(2)}) %all-to-all-start.2) | async-done | bytes 4194336 | tf_op jit(solution)/shard_map/all_to_all | solution.py:711
  220.3 19.7 %dust_outer.1 = f32[56,256,128]{2,1,0:T(8,128)} custom-call(s32[56]{0:T(128)S(1)} %select_reduce_fusion.1.home_ref, f32[16,128]{1,0:T(8,128)S(1)} %broadcast_in_dim.34.share_ref, f32[16,128]{1,0:T(8,128)S(1)} %broadcast_in_dim.35.settle_ref, f32[56,256,128]{2,1,0:T(8,128)} %get-tuple-element.46.dust_ref, bf16[256,512]{1,0:T(8,128)(2,1)S(1)} %copy-done.1, ...), custom_call_target="tpu_custom_call" | custom-call | flops 110100480 | bytes 22020096 | tf_op jit(solution)/shard_map/dust_outer/pallas_call | solution.py:697
  (46 shorter events, 13.1 us)
Async XLA Ops:
  2.3 26.2 %collective-permute-start = (f32[3,6,256]{2,1,0:T(8,128)}, f32[3,6,256]{2,1,0:T(8,128)}, u32[]{:S(2)}, u32[]{:S(2)}) collective-permute-start(f32[3,6,256]{2,1,0:T(8,128)} %bitcast.19), channel_id=1, source_target_pairs={{0,16},{16,32},{32,48},{48,64},{64,80},{80,96},{96,112},{112,0},{1... | collective-permute-start | bytes 55304 | tf_op jit(solution)/shard_map/ppermute | solution.py:489
  5.5 23.0 %collective-permute-start.1 = (f32[3,6,256]{2,1,0:T(8,128)}, f32[3,6,256]{2,1,0:T(8,128)}, u32[]{:S(2)}, u32[]{:S(2)}) collective-permute-start(f32[3,6,256]{2,1,0:T(8,128)} %bitcast.18), channel_id=1, source_target_pairs={{0,112},{16,0},{32,16},{48,32},{64,48},{80,64},{96,80},{112,96},{1... | collective-permute-start | bytes 55304 | tf_op jit(solution)/shard_map/ppermute | solution.py:489
  10.1 9.6 %copy-start.5 = (s32[7168]{0:T(1024)S(1)}, s32[7168]{0:T(1024)}, u32[]{:S(2)}) copy-start(s32[7168]{0:T(1024)} %param.16) | copy-start | bytes 86020
  10.1 9.6 %copy-start.6 = (s32[7168]{0:T(1024)S(1)}, s32[7168]{0:T(1024)}, u32[]{:S(2)}) copy-start(s32[7168]{0:T(1024)} %param.17) | copy-start | bytes 86020
  10.1 10.0 %copy-start.2 = (bf16[2048,256]{1,0:T(8,128)(2,1)S(1)}, bf16[2048,256]{1,0:T(8,128)(2,1)}, u32[]{:S(2)}) copy-start(bf16[2048,256]{1,0:T(8,128)(2,1)} %constant.88.clone.matrix_ref) | copy-start | bytes 3145732
  12.8 15.8 %collective-permute-start.2 = (f32[3,6,256]{2,1,0:T(8,128)S(1)}, f32[3,6,256]{2,1,0:T(8,128)S(1)}, u32[]{:S(2)}, u32[]{:S(2)}) collective-permute-start(f32[3,6,256]{2,1,0:T(8,128)S(1)} %bitcast.24), channel_id=1, source_target_pairs={{0,1},{1,2},{2,3},{3,4},{4,5},{5,6},{6,7},{7,8},{8,9},{9,10},{10,1... | collective-permute-start | bytes 55304 | tf_op jit(solution)/shard_map/ppermute | solution.py:489
  15.3 13.2 %collective-permute-start.3 = (f32[3,6,256]{2,1,0:T(8,128)S(1)}, f32[3,6,256]{2,1,0:T(8,128)S(1)}, u32[]{:S(2)}, u32[]{:S(2)}) collective-permute-start(f32[3,6,256]{2,1,0:T(8,128)S(1)} %bitcast.25), channel_id=1, source_target_pairs={{0,15},{1,0},{2,1},{3,2},{4,3},{5,4},{6,5},{7,6},{8,7},{9,8},{10,9... | collective-permute-start | bytes 55304 | tf_op jit(solution)/shard_map/ppermute | solution.py:489
  28.5 59.2 %all-to-all-start = ((f32[128,64,128]{2,1,0:T(8,128)}), f32[128,64,128]{2,1,0:T(8,128)}, u32[]{:S(2)}, u32[]{:S(2)}) async-start(f32[128,64,128]{2,1,0:T(8,128)} %dust_strips.1), calls=%async_computation | async-start | bytes 8388608 | tf_op jit(solution)/shard_map/all_to_all | solution.py:711
  37.5 5.9 %copy-start.4 = (f32[256,256]{1,0:T(8,128)S(1)}, f32[256,256]{1,0:T(8,128)}, u32[]{:S(2)}) copy-start(f32[256,256]{1,0:T(8,128)} %thr_ref.1) | copy-start | bytes 786436
  43.4 1.7 copy-start
  90.8 5.5 %collective-permute-start.4 = (f32[2,32,128]{2,1,0:T(8,128)S(1)}, f32[2,32,128]{2,1,0:T(8,128)S(1)}, u32[]{:S(2)}, u32[]{:S(2)}) collective-permute-start(f32[2,32,128]{2,1,0:T(8,128)S(1)} %get-tuple-element.41), channel_id=1, source_target_pairs={{0,16},{16,32},{32,48},{48,64},{64,80},{80,96},{96,112},{112,0},{1... | collective-permute-start | bytes 98312 | tf_op jit(solution)/shard_map/ppermute | solution.py:489
  91.4 4.8 %collective-permute-start.5 = (f32[2,32,128]{2,1,0:T(8,128)S(1)}, f32[2,32,128]{2,1,0:T(8,128)S(1)}, u32[]{:S(2)}, u32[]{:S(2)}) collective-permute-start(f32[2,32,128]{2,1,0:T(8,128)S(1)} %get-tuple-element.42), channel_id=1, source_target_pairs={{0,112},{16,0},{32,16},{48,32},{64,48},{80,64},{96,80},{112,96},{1... | collective-permute-start | bytes 98312 | tf_op jit(solution)/shard_map/ppermute | solution.py:489
  91.4 6.1 %collective-permute-start.6 = (f32[2,32,128]{2,1,0:T(8,128)S(1)}, f32[2,32,128]{2,1,0:T(8,128)S(1)}, u32[]{:S(2)}, u32[]{:S(2)}) collective-permute-start(f32[2,32,128]{2,1,0:T(8,128)S(1)} %get-tuple-element.43), channel_id=1, source_target_pairs={{0,1},{1,2},{2,3},{3,4},{4,5},{5,6},{6,7},{7,8},{8,9},{9,10},{10,1... | collective-permute-start | bytes 98312 | tf_op jit(solution)/shard_map/ppermute | solution.py:489
  92.3 15.8 %copy-start.7 = (f32[16]{0:T(128)S(1)}, f32[16]{0:T(128)}, u32[]{:S(2)}) copy-start(f32[16]{0:T(128)} %param.14) | copy-start | bytes 196
  92.3 15.9 %copy-start.8 = (f32[16]{0:T(128)S(1)}, f32[16]{0:T(128)}, u32[]{:S(2)}) copy-start(f32[16]{0:T(128)} %param.15) | copy-start | bytes 196
  92.3 5.2 %collective-permute-start.7 = (f32[2,32,128]{2,1,0:T(8,128)S(1)}, f32[2,32,128]{2,1,0:T(8,128)S(1)}, u32[]{:S(2)}, u32[]{:S(2)}) collective-permute-start(f32[2,32,128]{2,1,0:T(8,128)S(1)} %get-tuple-element.44), channel_id=1, source_target_pairs={{0,15},{1,0},{2,1},{3,2},{4,3},{5,4},{6,5},{7,6},{8,7},{9,8},{10,9... | collective-permute-start | bytes 98312 | tf_op jit(solution)/shard_map/ppermute | solution.py:489
  97.5 64.0 %all-to-all-start.1 = ((f32[128,56,128]{2,1,0:T(8,128)}), f32[128,56,128]{2,1,0:T(8,128)}, u32[]{:S(2)}, u32[]{:S(2)}) async-start(f32[128,56,128]{2,1,0:T(8,128)} %get-tuple-element.45), calls=%async_computation.1 | async-start | bytes 7340032 | tf_op jit(solution)/shard_map/all_to_all | solution.py:711
  120.4 17.5 %collective-permute-start.8 = (f32[2,32,128]{2,1,0:T(8,128)S(1)}, f32[2,32,128]{2,1,0:T(8,128)S(1)}, u32[]{:S(2)}, u32[]{:S(2)}) collective-permute-start(f32[2,32,128]{2,1,0:T(8,128)S(1)} %get-tuple-element.55), channel_id=1, source_target_pairs={{0,16},{16,32},{32,48},{48,64},{64,80},{80,96},{96,112},{112,0},{1... | collective-permute-start | bytes 98312 | tf_op jit(solution)/shard_map/ppermute | solution.py:489
  122.1 23.7 %collective-permute-start.9 = (f32[2,32,128]{2,1,0:T(8,128)S(1)}, f32[2,32,128]{2,1,0:T(8,128)S(1)}, u32[]{:S(2)}, u32[]{:S(2)}) collective-permute-start(f32[2,32,128]{2,1,0:T(8,128)S(1)} %get-tuple-element.56), channel_id=1, source_target_pairs={{0,112},{16,0},{32,16},{48,32},{64,48},{80,64},{96,80},{112,96},{1... | collective-permute-start | bytes 98312 | tf_op jit(solution)/shard_map/ppermute | solution.py:489
  122.1 31.5 %collective-permute-start.10 = (f32[2,32,128]{2,1,0:T(8,128)S(1)}, f32[2,32,128]{2,1,0:T(8,128)S(1)}, u32[]{:S(2)}, u32[]{:S(2)}) collective-permute-start(f32[2,32,128]{2,1,0:T(8,128)S(1)} %get-tuple-element.57), channel_id=1, source_target_pairs={{0,1},{1,2},{2,3},{3,4},{4,5},{5,6},{6,7},{7,8},{8,9},{9,10},{10,1... | collective-permute-start | bytes 98312 | tf_op jit(solution)/shard_map/ppermute | solution.py:489
  123.5 30.1 %collective-permute-start.11 = (f32[2,32,128]{2,1,0:T(8,128)S(1)}, f32[2,32,128]{2,1,0:T(8,128)S(1)}, u32[]{:S(2)}, u32[]{:S(2)}) collective-permute-start(f32[2,32,128]{2,1,0:T(8,128)S(1)} %get-tuple-element.58), channel_id=1, source_target_pairs={{0,15},{1,0},{2,1},{3,2},{4,3},{5,4},{6,5},{7,6},{8,7},{9,8},{10,9... | collective-permute-start | bytes 98312 | tf_op jit(solution)/shard_map/ppermute | solution.py:489
  161.6 6.6 %copy-start.1 = (bf16[256,512]{1,0:T(8,128)(2,1)S(1)}, bf16[256,512]{1,0:T(8,128)(2,1)}, u32[]{:S(2)}) copy-start(bf16[256,512]{1,0:T(8,128)(2,1)} %constant.89.clone.shift_ref) | copy-start | bytes 786436
  161.6 58.7 %all-to-all-start.2 = ((f32[128,64,128]{2,1,0:T(8,128)}), f32[128,64,128]{2,1,0:T(8,128)}, u32[]{:S(2)}, u32[]{:S(2)}) async-start(f32[128,64,128]{2,1,0:T(8,128)} %send_seen.1), calls=%async_computation.2 | async-start | bytes 8388608 | tf_op jit(solution)/shard_map/all_to_all | solution.py:711
  168.2 52.1 %copy-start.3 = (bf16[256,1024]{1,0:T(8,128)(2,1)S(1)}, bf16[256,1024]{1,0:T(8,128)(2,1)}, u32[]{:S(2)}) copy-start(bf16[256,1024]{1,0:T(8,128)(2,1)} %constant.90.clone.refs_0_) | copy-start | bytes 1572868

commit v4 on v3

--- a/solution.py
+++ b/solution.py
@@ -104,45 +104,51 @@
     return moves(np.concatenate(columns))
 
 
-def strips_kernel(home_ref, dust_ref, matrix_ref, send_ref, rings, sems, *, block, bins):
-    step = pl.program_id(0)
+def strips_kernel(home_ref, dust_hbm, matrix_ref, send_ref, dust, rings, load_sems, sems, *, block, bins):
     slots = rings.shape[0]
     each = TZ * bins
 
-    parts = []
-    for r in range(ROWS):
-        x = jnp.concatenate(
-            [
-                dust_ref[j, pl.ds(r * TZ + level, bins, stride=ROWS * TZ), :]
-                for j in range(block)
-                for level in range(TZ)
-            ],
-            axis=0,
+    def load(i):
+        some = pl.ds(i * block, block)
+        return pltpu.make_async_copy(dust_hbm.at[some], dust.at[some], load_sems.at[i])
+
+    def send(s):
+        return pltpu.make_async_copy(rings.at[s], send_ref.at[home_ref[s]], sems.at[s])
+
+    for i in range(slots // block):
+        load(i).start()
+
+    def one(i, carry):
+        load(i).wait()
+        parts = []
+        for r in range(ROWS):
+            x = jnp.concatenate(
+                [
+                    dust[i * block + j, pl.ds(r * TZ + level, bins, stride=ROWS * TZ), :]
+                    for j in range(block)
+                    for level in range(TZ)
+                ],
+                axis=0,
+            )
+            parts += halves_of(x)
+        found = jnp.dot(
+            jnp.concatenate(parts, axis=1), matrix_ref[...], preferred_element_type=jnp.float32
         )
-        parts += halves_of(x)
-    found = jnp.dot(
-        jnp.concatenate(parts, axis=1), matrix_ref[...], preferred_element_type=jnp.float32
-    )
-    for j in range(block):
-        for depth in range(2):
-            rings[step * block + j, depth * each : (depth + 1) * each, :] = found[
-                j * each : (j + 1) * each, depth * LANES : (depth + 1) * LANES
-            ]
-
-    def send(j, carry):
-        s = step * block + j
-        pltpu.make_async_copy(rings.at[s], send_ref.at[home_ref[s]], sems.at[s]).start()
-        return carry
-
-    lax.fori_loop(0, block, send, 0)
-
-    @pl.when(step == pl.num_programs(0) - 1)
-    def _():
-        def wait(s, carry):
-            pltpu.make_async_copy(rings.at[s], send_ref.at[home_ref[s]], sems.at[s]).wait()
-            return carry
-
-        lax.fori_loop(0, slots, wait, 0)
+        for j in range(block):
+            for depth in range(2):
+                rings[i * block + j, depth * each : (depth + 1) * each, :] = found[
+                    j * each : (j + 1) * each, depth * LANES : (depth + 1) * LANES
+                ]
+            send(i * block + j).start()
+        return carry
+
+    lax.fori_loop(0, slots // block, one, 0)
+
+    def wait(s, carry):
+        send(s).wait()
+        return carry
+
+    lax.fori_loop(0, slots, wait, 0)
 
 
 def dust_strips(home_of_slot, dust, bins, owners):
@@ -150,18 +156,16 @@
     block = 8 if slots % 8 == 0 else 4
     rows = 2 * bins * TZ
     matrix = jnp.asarray(ring_matrix())
+    hbm = pl.BlockSpec(memory_space=pltpu.HBM)
     return pl.pallas_call(
         functools.partial(strips_kernel, block=block, bins=bins),
-        grid=(slots // block,),
-        in_specs=[
-            pl.BlockSpec(memory_space=pltpu.SMEM),
-            pl.BlockSpec((block, cells, LANES), lambda i: (i, 0, 0)),
-            pl.BlockSpec(matrix.shape, lambda i: (0, 0)),
-        ],
-        out_specs=pl.BlockSpec(memory_space=pltpu.HBM),
+        in_specs=[pl.BlockSpec(memory_space=pltpu.SMEM), hbm, pl.BlockSpec(memory_space=pltpu.VMEM)],
+        out_specs=hbm,
         out_shape=pltpu.HBM((owners, rows, LANES), jnp.float32),
         scratch_shapes=[
+            pltpu.VMEM(dust.shape, jnp.float32),
             pltpu.VMEM((slots, rows, LANES), jnp.float32),
+            pltpu.SemaphoreType.DMA((slots // block,)),
             pltpu.SemaphoreType.DMA((slots,)),
         ],
         compiler_params=pltpu.CompilerParams(vmem_limit_bytes=32 << 20),
@@ -172,6 +176,65 @@
     )(home_of_slot, in_hbm(dust), matrix)
 
 
+def faces_kernel(vel_ref, x_last_ref, x_first_ref, y_last_ref, y_first_ref, first, last, low, high, x_sems, y_sems):
+    fields, nx, ny = vel_ref.shape
+    x_copies = [
+        pltpu.make_async_copy(vel_ref.at[:, pl.ds(0, ROWS), :], first, x_sems.at[0]),
+        pltpu.make_async_copy(vel_ref.at[:, pl.ds(nx - ROWS, ROWS), :], last, x_sems.at[1]),
+    ]
+    y_copies = [
+        (
+            pltpu.make_async_copy(vel_ref.at[f, :, pl.ds(0, LANES)], low.at[f], y_sems.at[0, f]),
+            pltpu.make_async_copy(vel_ref.at[f, :, pl.ds(ny - LANES, LANES)], high.at[f], y_sems.at[1, f]),
+        )
+        for f in range(fields)
+    ]
+    for pair in y_copies:
+        for copy in pair:
+            copy.start()
+    for copy in x_copies:
+        copy.start()
+    lane = lax.broadcasted_iota(jnp.int32, (nx, LANES), 1)
+    for f, (low_copy, high_copy) in enumerate(y_copies):
+        low_copy.wait()
+        high_copy.wait()
+        from_low = pltpu.roll(low[f], f, 1) if f else low[f]
+        from_high = pltpu.roll(high[f], f + 1, 1)
+        if f == 0:
+            y_first_ref[...], y_last_ref[...] = from_low, from_high
+        else:
+            y_first_ref[...] = jnp.where(lane == f, from_low, y_first_ref[...])
+            y_last_ref[...] = jnp.where(lane == f, from_high, y_last_ref[...])
+    for copy in x_copies:
+        copy.wait()
+    for f in range(fields):
+        x_first_ref[f : f + 1, :] = first[f, 0:1, :]
+        x_last_ref[f : f + 1, :] = last[f, ROWS - 1 : ROWS, :]
+
+
+def wind_faces(velocity):
+    comps, levels, nx, ny = velocity.shape
+    fields = comps * levels
+    vmem = pl.BlockSpec(memory_space=pltpu.VMEM)
+    return pl.pallas_call(
+        faces_kernel,
+        in_specs=[pl.BlockSpec(memory_space=pltpu.HBM)],
+        out_specs=[vmem] * 4,
+        out_shape=[f32(fields, ny)] * 2 + [f32(nx, LANES)] * 2,
+        scratch_shapes=[
+            pltpu.VMEM((fields, ROWS, ny), jnp.float32),
+            pltpu.VMEM((fields, ROWS, ny), jnp.float32),
+            pltpu.VMEM((fields, nx, LANES), jnp.float32),
+            pltpu.VMEM((fields, nx, LANES), jnp.float32),
+            pltpu.SemaphoreType.DMA((2,)),
+            pltpu.SemaphoreType.DMA((2, fields)),
+        ],
+        compiler_params=pltpu.CompilerParams(vmem_limit_bytes=32 << 20),
+        cost_estimate=pl.CostEstimate(flops=velocity.size, bytes_accessed=velocity.size * 4, transcendentals=0),
+        name="wind_faces",
+    )(in_hbm(velocity.reshape(fields, nx, ny)))
+
+
 def wind_kernel(
     owner_ref, vel_ref, xlo_ref, xhi_ref, ylo_ref, yhi_ref, thr_ref,
     new_ref, send_ref, ring_ref, padded, strip, tiles, load_sem, sems, *, levels
@@ -180,8 +243,9 @@
     load = pltpu.make_async_copy(vel_ref, padded.at[:, pl.ds(8, nx), :], load_sem)
     load.start()
     load.wait()
-    padded[:, 7:8, :] = xlo_ref[...]
-    padded[:, 8 + nx : 9 + nx, :] = xhi_ref[...]
+    for f in range(fields):
+        padded[f, 7:8, :] = xlo_ref[f : f + 1, :]
+        padded[f, 8 + nx : 9 + nx, :] = xhi_ref[f : f + 1, :]
     half = 16
     halves = ny // LANES
     tiles_y = ny // TILE
@@ -194,6 +258,12 @@
             base = pl.multiple_of(ix * TILE + sub * half, 8)
             lane = lax.broadcasted_iota(jnp.int32, (half, ny), 1)
             low = {}
+            faces = [ref[pl.ds(base, half), :] for ref in (ylo_ref, yhi_ref)]
+
+            def face(which, f, to):
+                moved = pltpu.roll(faces[which], (to - f) % LANES, 1) if f != to else faces[which]
+                return jnp.concatenate([moved] * halves, axis=1)
+
             for z in range(levels):
                 u, v, w = (padded[c * levels + z, pl.ds(base + 8, half), :] for c in range(3))
                 for c in range(3):
@@ -202,10 +272,8 @@
                     centre = (u, v, w)[c]
                     west = pltpu.roll(block, 1, 0)[8 : 8 + half]
                     east = pltpu.roll(block, half + 15, 0)[8 : 8 + half]
-                    south = jnp.where(lane == 0, ylo_ref[f, pl.ds(base, half), :], pltpu.roll(centre, 1, 1))
-                    north = jnp.where(
-                        lane == ny - 1, yhi_ref[f, pl.ds(base, half), :], pltpu.roll(centre, ny - 1, 1)
-                    )
+                    south = jnp.where(lane == 0, face(0, f, 0), pltpu.roll(centre, 1, 1))
+                    north = jnp.where(lane == ny - 1, face(1, f, LANES - 1), pltpu.roll(centre, ny - 1, 1))
                     lower = -centre if z == 0 else padded[f - 1, pl.ds(base + 8, half), :]
                     upper = centre if z == levels - 1 else padded[f + 1, pl.ds(base + 8, half), :]
                     carried = 0.5 * (u * (east - west) + v * (north - south) + w * (upper - lower))
@@ -293,10 +361,10 @@
     )(
         owner_of_tile,
         in_hbm(velocity.reshape(fields, nx, ny)),
-        xlo.reshape(fields, 1, ny),
-        xhi.reshape(fields, 1, ny),
-        ylo.reshape(fields, nx, 1),
-        yhi.reshape(fields, nx, 1),
+        xlo,
+        xhi,
+        ylo,
+        yhi,
         threshold,
     )
     return new.reshape(velocity.shape), send, ring
@@ -347,9 +415,42 @@
     return jnp.where((lane // TILE) % 2 == 0, up, down)
 
 
-def gather_rings_kernel(owner_ref, recv_ref, rings_ref, e_ref, w_ref, n_ref, s_ref, *, tiles_x, tiles_y):
+def border_tiles(tiles_x, tiles_y):
+    return (
+        [(tiles_x - 1) * tiles_y + n for n in range(tiles_y)],
+        [n for n in range(tiles_y)],
+        [n * tiles_y + tiles_y - 1 for n in range(tiles_x)],
+        [n * tiles_y for n in range(tiles_x)],
+    )
+
+
+def pack_borders_kernel(owner_ref, recv_ref, e_ref, w_ref, n_ref, s_ref, strips, sems, *, tiles_x, tiles_y):
     rows = e_ref.shape[1]
-
+    used = sorted(set(sum(border_tiles(tiles_x, tiles_y), [])))
+
+    def copy(t):
+        return pltpu.make_async_copy(recv_ref.at[owner_ref[t], pl.ds(0, rows), :], strips.at[t], sems.at[t])
+
+    for t in used:
+
+        @pl.when(owner_ref[t] >= 0)
+        def _():
+            copy(t).start()
+
+        @pl.when(owner_ref[t] < 0)
+        def _():
+            strips[t] = jnp.zeros(strips.shape[1:], jnp.float32)
+
+    for t in used:
+
+        @pl.when(owner_ref[t] >= 0)
+        def _():
+            copy(t).wait()
+
+    pack_borders((e_ref, w_ref, n_ref, s_ref), lambda t: strips[t], tiles_x, tiles_y)
+
+
+def gather_rings_kernel(owner_ref, recv_ref, rings_ref, *, tiles_x, tiles_y):
     def one(t, carry):
         owner = owner_ref[t]
         rings = recv_ref[jnp.maximum(owner, 0)]
@@ -357,27 +458,21 @@
         return carry
 
     lax.fori_loop(0, tiles_x * tiles_y, one, 0)
-    pack_borders((e_ref, w_ref, n_ref, s_ref), lambda t: rings_ref[t, :rows, :], tiles_x, tiles_y)
-
-
-def advance_rings_kernel(
-    owner_ref, rings_ref, fw_ref, fe_ref, fs_ref, fn_ref, wind_ref, settle_ref, share_ref,
-    seen_ref, later_ref, e_ref, w_ref, n_ref, s_ref, ext, *, tiles_x, tiles_y
-):
-    per_home = tiles_x * tiles_y
-    rows = e_ref.shape[1]
-    wide = tiles_y + 2
-    fill_halo(ext, (fw_ref, fe_ref, fs_ref, fn_ref), tiles_x, tiles_y)
-
-    def place_of(t):
-        return (t // tiles_y + 1) * wide + t % tiles_y + 1
-
+
+
+def fill_tiles(ext, tile, tiles_x, tiles_y):
     def inner(t, carry):
-        ext[place_of(t)] = rings_ref[t, :rows, :]
-        return carry
-
-    lax.fori_loop(0, per_home, inner, 0)
-
+        ext[place_of(t, tiles_y)] = tile(t)
+        return carry
+
+    lax.fori_loop(0, tiles_x * tiles_y, inner, 0)
+
+
+def place_of(t, tiles_y):
+    return (t // tiles_y + 1) * (tiles_y + 2) + t % tiles_y + 1
+
+
+def advance_ring(t, owner_ref, rings_ref, wind_ref, settle_ref, share_ref, seen):
     _, lane = iotas()
     group, within = lane // TILE, lane % TILE
     on_x = (group == WEST) | (group == EAST)
@@ -388,100 +483,148 @@
         jnp.where(first, SOUTH, NORTH) * TILE + high,
         jnp.where(first, WEST, EAST) * TILE + high,
     )
-
-    def one(t, carry):
-        place = place_of(t)
-        seen = seen_by(ext, place, wide)
-        seen_ref[t] = seen
-
-        uplift = dust_step * spread_rows(wind_ref[t, PLANES - 1 : PLANES, :])
-        mix = dust_step * diffusion
-        active = owner_ref[t] >= 0
-        bins = rows // TZ
-        for chunk in range(rows // ROWS):
-            at = chunk * ROWS
-            level, bin_at = at // bins, at % bins
-            if bin_at == 0:
-                u, v, w = (
-                    dust_step * spread_rows(wind_ref[t, c * TZ + level : c * TZ + level + 1, :]) for c in range(3)
-                )
-                from_west = mix + jnp.maximum(u, 0.0)
-                from_east = mix + jnp.maximum(-u, 0.0)
-                from_south = mix + jnp.maximum(v, 0.0)
-                from_north = mix + jnp.maximum(-v, 0.0)
-                keep = 1.0 - 6.0 * mix - jnp.abs(u) - jnp.abs(v)
-            q = rings_ref[t, at : at + ROWS, :]
-            deep = rings_ref[t, rows + at : rows + at + ROWS, :]
-            out = seen[at : at + ROWS, :]
-            beyond = lane_gather(out, corner)
-            before = jnp.where(first, beyond, pltpu.roll(q, 1, 1))
-            after = jnp.where(last, beyond, pltpu.roll(q, LANES - 1, 1))
-            west = jnp.where(group == WEST, out, jnp.where(group == EAST, deep, before))
-            east = jnp.where(group == WEST, deep, jnp.where(group == EAST, out, after))
-            south = jnp.where(on_x, before, jnp.where(group == SOUTH, out, deep))
-            north = jnp.where(on_x, after, jnp.where(group == SOUTH, deep, out))
-            other_at = (1 - level) * bins + bin_at
-            other = rings_ref[t, other_at : other_at + ROWS, :]
-            rise = w - dust_step * settle_ref[bin_at : bin_at + ROWS, :]
-            up = jnp.maximum(rise, 0.0)
-            down = up - rise
-            new = (
-                (keep - up - down) * q
-                + from_west * west
-                + from_east * east
-                + from_south * south
-                + from_north * north
-                + (mix + (down if level == 0 else up)) * other
+    rows = rings_ref.shape[1] // 2
+    bins = rows // TZ
+    uplift = dust_step * spread_rows(wind_ref[t, PLANES - 1 : PLANES, :])
+    mix = dust_step * diffusion
+    active = owner_ref[t] >= 0
+    chunks = []
+    for at in range(0, rows, ROWS):
+        level, bin_at = at // bins, at % bins
+        if bin_at == 0:
+            u, v, w = (
+                dust_step * spread_rows(wind_ref[t, c * TZ + level : c * TZ + level + 1, :]) for c in range(3)
             )
-            if level == 0:
-                new = new + uplift * share_ref[bin_at : bin_at + ROWS, :]
-            later_ref[t, at : at + ROWS, :] = jnp.where(active, new, 0.0)
-        return carry
-
-    lax.fori_loop(0, per_home, one, 0)
+            from_west = mix + jnp.maximum(u, 0.0)
+            from_east = mix + jnp.maximum(-u, 0.0)
+            from_south = mix + jnp.maximum(v, 0.0)
+            from_north = mix + jnp.maximum(-v, 0.0)
+            keep = 1.0 - 6.0 * mix - jnp.abs(u) - jnp.abs(v)
+        q = rings_ref[t, at : at + ROWS, :]
+        deep = rings_ref[t, rows + at : rows + at + ROWS, :]
+        out = seen[at : at + ROWS, :]
+        beyond = lane_gather(out, corner)
+        before = jnp.where(first, beyond, pltpu.roll(q, 1, 1))
+        after = jnp.where(last, beyond, pltpu.roll(q, LANES - 1, 1))
+        west = jnp.where(group == WEST, out, jnp.where(group == EAST, deep, before))
+        east = jnp.where(group == WEST, deep, jnp.where(group == EAST, out, after))
+        south = jnp.where(on_x, before, jnp.where(group == SOUTH, out, deep))
+        north = jnp.where(on_x, after, jnp.where(group == SOUTH, deep, out))
+        other_at = (1 - level) * bins + bin_at
+        other = rings_ref[t, other_at : other_at + ROWS, :]
+        rise = w - dust_step * settle_ref[bin_at : bin_at + ROWS, :]
+        up = jnp.maximum(rise, 0.0)
+        down = up - rise
+        new = (
+            (keep - up - down) * q
+            + from_west * west
+            + from_east * east
+            + from_south * south
+            + from_north * north
+            + (mix + (down if level == 0 else up)) * other
+        )
+        if level == 0:
+            new = new + uplift * share_ref[bin_at : bin_at + ROWS, :]
+        chunks.append(jnp.where(active, new, 0.0))
+    return chunks
+
+
+def advance_borders_kernel(
+    owner_ref, rings_ref, fw_ref, fe_ref, fs_ref, fn_ref, wind_ref, settle_ref, share_ref,
+    seen_ref, later_ref, e_ref, w_ref, n_ref, s_ref, ext, *, tiles_x, tiles_y
+):
+    rows = e_ref.shape[1]
+    fill_halo(ext, (fw_ref, fe_ref, fs_ref, fn_ref), tiles_x, tiles_y)
+    fill_tiles(ext, lambda t: rings_ref[t, :rows, :], tiles_x, tiles_y)
+
+    def pair(tiles):
+        for t in tiles:
+            seen = seen_by(ext, place_of(t, tiles_y), tiles_y + 2)
+            seen_ref[t] = seen
+            chunks = advance_ring(t, owner_ref, rings_ref, wind_ref, settle_ref, share_ref, seen)
+            for n, chunk in enumerate(chunks):
+                later_ref[t, n * ROWS : (n + 1) * ROWS, :] = chunk
+
+    def along_y(n, carry):
+        pair((n, (tiles_x - 1) * tiles_y + n))
+        return carry
+
+    def along_x(n, carry):
+        pair((n * tiles_y, n * tiles_y + tiles_y - 1))
+        return carry
+
+    lax.fori_loop(0, tiles_y, along_y, 0)
+    lax.fori_loop(1, tiles_x - 1, along_x, 0)
     pack_borders((e_ref, w_ref, n_ref, s_ref), lambda t: later_ref[t], tiles_x, tiles_y)
 
 
 def send_seen_kernel(
-    owner_ref, later_ref, fw_ref, fe_ref, fs_ref, fn_ref, seen_ref, send_ref, ext, both, sems, *, tiles_x, tiles_y
+    owner_ref, rings_ref, wind_ref, settle_ref, share_ref, seen_ref, later_ref,
+    fw_ref, fe_ref, fs_ref, fn_ref, send_ref, ext, both, sems, *, tiles_x, tiles_y
 ):
-    per_home = tiles_x * tiles_y
     rows = later_ref.shape[1]
     wide = tiles_y + 2
+    fill_tiles(ext, lambda t: rings_ref[t, :rows, :], tiles_x, tiles_y)
+
+    def place(t):
+        return place_of(t, tiles_y)
+
+    def border(t):
+        x, y = t // tiles_y, t % tiles_y
+        return (x == 0) | (x == tiles_x - 1) | (y == 0) | (y == tiles_y - 1)
+
+    def before(t, carry):
+        @pl.when(border(t))
+        def _():
+            both[t, :rows, :] = seen_ref[t]
+
+        @pl.when(jnp.logical_not(border(t)))
+        def _():
+            both[t, :rows, :] = seen_by(ext, place(t), wide)
+
+        return carry
+
+    lax.fori_loop(0, tiles_x * tiles_y, before, 0)
     fill_halo(ext, (fw_ref, fe_ref, fs_ref, fn_ref), tiles_x, tiles_y)
 
-    def place_of(t):
-        return (t // tiles_y + 1) * wide + t % tiles_y + 1
-
-    def inner(t, carry):
-        ext[place_of(t)] = later_ref[t]
-        return carry
-
-    lax.fori_loop(0, per_home, inner, 0)
-
-    def one(t, carry):
-        both[t, :rows, :] = seen_ref[t]
-        both[t, rows:, :] = seen_by(ext, place_of(t), wide)
-        owner = owner_ref[t]
-
-        @pl.when(owner >= 0)
+    def advance(t, carry):
+        @pl.when(border(t))
         def _():
-            pltpu.make_async_copy(both.at[t], send_ref.at[owner], sems.at[t]).start()
-
-        return carry
-
-    lax.fori_loop(0, per_home, one, 0)
+            ext[place(t)] = later_ref[t]
+
+        @pl.when(jnp.logical_not(border(t)))
+        def _():
+            seen = both[t, :rows, :]
+            chunks = advance_ring(t, owner_ref, rings_ref, wind_ref, settle_ref, share_ref, seen)
+            for n, chunk in enumerate(chunks):
+                ext[place(t), n * ROWS : (n + 1) * ROWS, :] = chunk
+
+        return carry
+
+    lax.fori_loop(0, tiles_x * tiles_y, advance, 0)
+
+    def copy(t):
+        return pltpu.make_async_copy(both.at[t], send_ref.at[owner_ref[t]], sems.at[t])
+
+    def after(t, carry):
+        both[t, rows:, :] = seen_by(ext, place(t), wide)
+
+        @pl.when(owner_ref[t] >= 0)
+        def _():
+            copy(t).start()
+
+        return carry
+
+    lax.fori_loop(0, tiles_x * tiles_y, after, 0)
 
     def wait(t, carry):
-        owner = owner_ref[t]
-
-        @pl.when(owner >= 0)
+        @pl.when(owner_ref[t] >= 0)
         def _():
-            pltpu.make_async_copy(both.at[t], send_ref.at[owner], sems.at[t]).wait()
-
-        return carry
-
-    lax.fori_loop(0, per_home, wait, 0)
+            copy(t).wait()
+
+        return carry
+
+    lax.fori_loop(0, tiles_x * tiles_y, wait, 0)
 
 
 def shifted(value, axis, steps):
@@ -489,21 +632,26 @@
     return lax.ppermute(value, axis, [(source, (source + steps) % count) for source in range(count)])
 
 
+def relay_rows(rows):
+    return lax.all_to_all(rows, AXES, split_axis=0, concat_axis=0, tiled=True)
+
+
 def exchange_borders(borders):
     east, west, north, south = borders
     return shifted(east, "gx", 1), shifted(west, "gx", -1), shifted(north, "gy", 1), shifted(south, "gy", -1)
 
 
-def ring_call(kernel, tiles_x, tiles_y, rows, outs, scratch, name, hbm_out=False):
+def ring_call(kernel, tiles_x, tiles_y, rows, outs, scratch, name, hbm_in=False, hbm_out=False):
     smem = pl.BlockSpec(memory_space=pltpu.SMEM)
     vmem = pl.BlockSpec(memory_space=pltpu.VMEM)
+    hbm = pl.BlockSpec(memory_space=pltpu.HBM)
     size = tiles_x * tiles_y * rows * LANES
 
     def call(owner_of_tile, *inputs):
         return pl.pallas_call(
             functools.partial(kernel, tiles_x=tiles_x, tiles_y=tiles_y),
-            in_specs=[smem] + [vmem] * len(inputs),
-            out_specs=pl.BlockSpec(memory_space=pltpu.HBM) if hbm_out else [vmem] * len(outs),
+            in_specs=[smem] + [hbm if hbm_in else vmem] * len(inputs),
+            out_specs=hbm if hbm_out else [vmem] * len(outs),
             out_shape=outs[0] if hbm_out else outs,
             scratch_shapes=scratch,
             compiler_params=pltpu.CompilerParams(vmem_limit_bytes=32 << 20),
@@ -518,26 +666,41 @@
     return [f32(tiles_y // 4, rows, LANES)] * 2 + [f32(tiles_x // 4, rows, LANES)] * 2
 
 
-def gather_rings(owner_of_tile, received, tiles_x, tiles_y):
-    both_rows = received.shape[1]
+def relay_strips(owner_of_tile, received, wind_send, wind_ring, settle_speed, bin_share, tiles_x, tiles_y):
+    owners, both_rows, _ = received.shape
     rows = both_rows // 2
-    outs = [f32(tiles_x * tiles_y, both_rows, LANES)] + border_shapes(tiles_x, tiles_y, rows)
-    return ring_call(gather_rings_kernel, tiles_x, tiles_y, rows, outs, [], "gather_rings")(owner_of_tile, received)
-
-
-def relay_rings(owner_of_tile, rings, borders, wind_ring, settle_speed, bin_share, tiles_x, tiles_y, owners):
-    per_home, both_rows, _ = rings.shape
-    rows = both_rows // 2
+    per_home = tiles_x * tiles_y
+    packs = border_shapes(tiles_x, tiles_y, rows)
     ext = pltpu.VMEM(((tiles_x + 2) * (tiles_y + 2), rows, LANES), jnp.float32)
+    each_sem = pltpu.SemaphoreType.DMA((per_home,))
     settle_rows = jnp.broadcast_to(settle_speed[:, None], settle_speed.shape + (LANES,))
     share_rows = jnp.broadcast_to(bin_share[:, None], bin_share.shape + (LANES,))
-    outs = [f32(per_home, rows, LANES)] * 2 + border_shapes(tiles_x, tiles_y, rows)
-    advance = ring_call(advance_rings_kernel, tiles_x, tiles_y, rows, outs, [ext], "advance_rings")
-    seen, later, *borders = advance(owner_of_tile, rings, *borders, wind_ring, settle_rows, share_rows)
-    outs = [pltpu.HBM((owners, both_rows, LANES), jnp.float32)]
-    scratch = [ext, pltpu.VMEM((per_home, both_rows, LANES), jnp.float32), pltpu.SemaphoreType.DMA((per_home,))]
-    send = ring_call(send_seen_kernel, tiles_x, tiles_y, rows, outs, scratch, "send_seen", hbm_out=True)
-    return send(owner_of_tile, later, *exchange_borders(borders), seen)
+
+    def call(kernel, outs, scratch, name, *inputs, **places):
+        return ring_call(kernel, tiles_x, tiles_y, rows, outs, scratch, name, **places)(owner_of_tile, *inputs)
+
+    strips = pltpu.VMEM((per_home, rows, LANES), jnp.float32)
+    borders = call(
+        pack_borders_kernel, packs, [strips, each_sem], "pack_borders", in_hbm(received), hbm_in=True
+    )
+    borders = exchange_borders(borders)
+    (rings,) = call(gather_rings_kernel, [f32(per_home, both_rows, LANES)], [], "gather_rings", received)
+    seen, later, *borders = call(
+        advance_borders_kernel, [f32(per_home, rows, LANES)] * 2 + packs, [ext], "advance_borders",
+        rings, *borders, wind_ring, settle_rows, share_rows,
+    )
+    borders = exchange_borders(borders)
+    wind_send, *borders = lax.optimization_barrier((wind_send, *borders))
+    wind_recv = relay_rows(wind_send)
+    seen_send = call(
+        send_seen_kernel,
+        [pltpu.HBM((owners, both_rows, LANES), jnp.float32)],
+        [ext, pltpu.VMEM((per_home, both_rows, LANES), jnp.float32), each_sem],
+        "send_seen",
+        rings, wind_ring, settle_rows, share_rows, seen, later, *borders,
+        hbm_out=True,
+    )
+    return wind_recv, relay_rows(seen_send)
 
 
 def dust_kernel(home_ref, share_ref, settle_ref, dust_ref, shift_ref, wind_ref, *refs, block, bins, outer):
@@ -707,10 +870,6 @@
     )(*inputs)
 
 
-def relay_rows(rows):
-    return lax.all_to_all(rows, AXES, split_axis=0, concat_axis=0, tiled=True)
-
-
 def per_device(velocity, threshold, dust_mass, settle_speed, bin_share, active_tiles, tile_owner):
     owners = lax.axis_size(AXES)
     grid_cols = lax.axis_size("gy")
@@ -737,10 +896,7 @@
     dust = dust_mass.reshape(slots, bins, TZ, ROWS, LANES).transpose(0, 1, 3, 2, 4)
     dust = dust.reshape(slots, bins * ROWS * TZ, LANES)
 
-    xlo = shifted(velocity[:, :, -1, :], "gx", 1)
-    xhi = shifted(velocity[:, :, 0, :], "gx", -1)
-    ylo = shifted(velocity[:, :, :, -1], "gy", 1)
-    yhi = shifted(velocity[:, :, :, 0], "gy", -1)
+    xlo, xhi, ylo, yhi = exchange_borders(wind_faces(velocity))
 
     strips_send = dust_strips(home_of_slot, dust, bins, owners)
     strips_send, xlo, xhi, ylo, yhi = lax.optimization_barrier((strips_send, xlo, xhi, ylo, yhi))
@@ -749,14 +905,9 @@
         owner_of_tile, velocity, xlo, xhi, ylo, yhi, threshold, owners
     )
     strips, wind_send, wind_ring = lax.optimization_barrier((strips, wind_send, wind_ring))
-    rings, *borders = gather_rings(owner_of_tile, strips, tiles_x, tiles_y)
-    borders = exchange_borders(borders)
-    wind_send, *borders = lax.optimization_barrier((wind_send, *borders))
-    wind_recv = relay_rows(wind_send)
-    seen_send = relay_rings(
-        owner_of_tile, rings, borders, wind_ring, settle_speed, bin_share, tiles_x, tiles_y, owners
-    )
-    seen_recv = relay_rows(seen_send)
+    wind_recv, seen_recv = relay_strips(
+        owner_of_tile, strips, wind_send, wind_ring, settle_speed, bin_share, tiles_x, tiles_y
+    )
     inner, wind_held = dust_substep(home_of_slot, dust, wind_recv, settle_speed, bin_share)
     out = dust_substep(home_of_slot, inner, wind_held, settle_speed, bin_share, seen_recv)
     out = out.reshape(slots, bins, ROWS, TZ, LANES).transpose(0, 1, 3, 2, 4).reshape(dust_mass.shape)

time: 241 us -> 239 us (level)
  local copies, waits for them, and re-layouts: 19.5 us -> 2.99 us
  waiting for transfers between devices: 71.7 us -> 83.2 us
  Pallas kernels: 102 us -> 105 us
    all_to_all x3, waiting for transfers between devices: 44.2 us -> 81.8 us  [relay_rows(): return lax.all_to_all(rows, AXES, split_axis=0, concat_axis=0, tiled=True)]
    ppermute x12, waiting for transfers between devices: 27.5 us -> 1.32 us  [shifted(): lax.ppermute(value, axis, [(source, (source + steps) % count) for source...]
    reshape x4 -> x0, local copies, waits for them, and re-layouts: 7.36 us -> none  [the longest x1 3.63 us: wind_step(): yhi.reshape(fields, nx, 1)]
    slice x2 -> x0, local copies, waits for them, and re-layouts: 5.55 us -> none  [the longest x1 4.54 us: per_device(): yhi = shifted(velocity[:, :, :, 0], 'gy', -1)]
    pallas_call x0 -> x1, Pallas kernels: none -> 3.87 us  [wind_faces(): pl.pallas_call(faces_kernel, in_specs=[pl.BlockSpec(memory_space=pltpu.HB...]
    unnamed x22 -> x28, local copies, waits for them, and re-layouts: 6.49 us -> 2.85 us
    pallas_call x3 -> x4, Pallas kernels: 23.2 us -> 25.2 us  [call(): pl.pallas_call(functools.partial(kernel, tiles_x=tiles_x, tiles_y=tiles_y...]
  transfers between devices with their start and end apart: 15 -> 15, of which waited for: 6 -> 4; matrix products, arithmetic and copies ran while one was open for 7% -> 0% of each run, Pallas kernels for 33% -> 32%
where the time goes in v4:
time: 239 us; the launch traced here: 238 us
  Pallas kernels  105 us (44%)
  waiting for transfers between devices  83.2 us (35%)
  starting transfers between devices  45.2 us (19%)
  local copies, waits for them, and re-layouts  2.99 us (1%)
    all_to_all x3, waiting for transfers between devices, relay_rows(): return lax.all_to_all(rows, AXES, split_axis=0, concat_axis=0, tiled=True)  81.8 us
    pallas_call x1, Pallas kernels, wind_step(): pl.pallas_call(functools.partial(wind_kernel, levels=levels), in_specs=[s...  36.1 us
    pallas_call x2, Pallas kernels, dust_substep(): pl.pallas_call(functools.partial(dust_kernel, block=block, bins=bins, out...  33.9 us
    pallas_call x4, Pallas kernels, call(): pl.pallas_call(functools.partial(kernel, tiles_x=tiles_x, tiles_y=tiles_y...  25.2 us
    all_to_all x3, starting transfers between devices, relay_rows(): return lax.all_to_all(rows, AXES, split_axis=0, concat_axis=0, tiled=True)  23 us
    ppermute x12, starting transfers between devices, shifted(): lax.ppermute(value, axis, [(source, (source + steps) % count) for source...  22.3 us
    pallas_call x1, Pallas kernels, dust_strips(): pl.pallas_call(functools.partial(strips_kernel, block=block, bins=bins),...  6.29 us
  transfers between devices with their start and end apart: 15, of which 4 were waited for; matrix products, arithmetic and copies ran while one was open for 0% of the time, Pallas kernels for 32%

profile of v4, /device:TPU:1, one launch (start us, length us, event | category | flops | bytes accessed | tf_op | source)
XLA Modules:
  0.0 238.3 jit_solution(11607229680095929700)
XLA Ops:
  0.7 3.9 %wind_faces.1 = (f32[18,256]{1,0:T(8,128)S(1)}, f32[18,256]{1,0:T(8,128)S(1)}, f32[256,128]{1,0:T(8,128)S(1)}, f32[256,128]{1,0:T(8,128)S(1)}) custom-call(f32[18,256,256]{2,1,0:T(8,128)} %bitcast.14), custom_call_target="tpu_custom_call" | custom-call | flops 1179648 | bytes 4718592 | tf_op jit(solution)/shard_map/wind_faces/pallas_call | solution.py:219
  4.5 2.7 %collective-permute-start = (f32[18,256]{1,0:T(8,128)S(1)}, f32[18,256]{1,0:T(8,128)S(1)}, u32[]{:S(2)}, u32[]{:S(2)}) collective-permute-start(f32[18,256]{1,0:T(8,128)S(1)} %get-tuple-element.34), channel_id=1, source_target_pairs={{0,16},{16,32},{32,48},{48,64},{64,80},{80,96},{96,112},{112,0},{1... | collective-permute-start | bytes 55304 | tf_op jit(solution)/shard_map/ppermute | solution.py:632
  7.2 1.6 collective-permute-start.2
  8.9 4.3 %collective-permute-start.3 = (f32[256,128]{1,0:T(8,128)S(1)}, f32[256,128]{1,0:T(8,128)S(1)}, u32[]{:S(2)}, u32[]{:S(2)}) collective-permute-start(f32[256,128]{1,0:T(8,128)S(1)} %get-tuple-element.37), channel_id=1, source_target_pairs={{0,15},{1,0},{2,1},{3,2},{4,3},{5,4},{6,5},{7,6},{8,7},{9,8},{10,9... | collective-permute-start | bytes 393224 | tf_op jit(solution)/shard_map/ppermute | solution.py:632
  13.6 6.3 %dust_strips.1 = f32[128,64,128]{2,1,0:T(8,128)} custom-call(s32[56]{0:T(128)S(1)} %select_reduce_fusion.1.home_ref, f32[56,256,128]{2,1,0:T(8,128)} %bitcast.12, bf16[2048,256]{1,0:T(8,128)(2,1)S(1)} %copy-done.1), custom_call_target="tpu_custom_call" | custom-call | flops 36700160 | bytes 9175040 | tf_op jit(solution)/shard_map/dust_strips/pallas_call | solution.py:160
  19.9 7.1 %all-to-all-start = ((f32[128,64,128]{2,1,0:T(8,128)}), f32[128,64,128]{2,1,0:T(8,128)}, u32[]{:S(2)}, u32[]{:S(2)}) async-start(f32[128,64,128]{2,1,0:T(8,128)} %dust_strips.1), calls=%async_computation | async-start | bytes 8388608 | tf_op jit(solution)/shard_map/all_to_all | solution.py:636
  27.4 36.1 %wind_step.1 = (f32[18,256,256]{2,1,0:T(8,128)}, f32[128,56,128]{2,1,0:T(8,128)}, f32[64,8,128]{2,1,0:T(8,128)S(1)}) custom-call(s32[64]{0:T(128)S(1)} %select_reduce_fusion.owner_ref, f32[18,256,256]{2,1,0:T(8,128)} %bitcast.15, f32[18,256]{1,0:T(8,128)S(1)} %collective-permute-done.xlo_ref, f32[18,256]{1,0:T(8,128)S(1)} %collective-permute-done.1.xhi_ref, ...), custom_call_target="tpu_custom_call" | custom-call | flops 47185920 | bytes 11796480 | tf_op jit(solution)/shard_map/wind_step/pallas_call | solution.py:340
  63.5 15.6 %all-to-all-done.recv_ref = f32[128,64,128]{2,1,0:T(8,128)} async-done(((f32[128,64,128]{2,1,0:T(8,128)}), f32[128,64,128]{2,1,0:T(8,128)}, u32[]{:S(2)}, u32[]{:S(2)}) %all-to-all-start) | async-done | bytes 4194336 | tf_op jit(solution)/shard_map/all_to_all | solution.py:636
  79.1 2.3 pack_borders.1
  83.0 3.9 %collective-permute-start.7 = (f32[2,32,128]{2,1,0:T(8,128)S(1)}, f32[2,32,128]{2,1,0:T(8,128)S(1)}, u32[]{:S(2)}, u32[]{:S(2)}) collective-permute-start(f32[2,32,128]{2,1,0:T(8,128)S(1)} %get-tuple-element.51), channel_id=1, source_target_pairs={{0,15},{1,0},{2,1},{3,2},{4,3},{5,4},{6,5},{7,6},{8,7},{9,8},{10,9... | collective-permute-start | bytes 98312 | tf_op jit(solution)/shard_map/ppermute | solution.py:632
  87.0 2.9 %gather_rings.1.rings_ref = f32[64,64,128]{2,1,0:T(8,128)S(1)} custom-call(s32[64]{0:T(128)S(1)} %select_reduce_fusion.owner_ref, f32[128,64,128]{2,1,0:T(8,128)} %all-to-all-done.recv_ref), custom_call_target="tpu_custom_call" | custom-call | flops 4194304 | bytes 4194304 | tf_op jit(solution)/shard_map/gather_rings/pallas_call | solution.py:651
  90.0 4.0 %advance_borders.1 = (f32[64,32,128]{2,1,0:T(8,128)S(1)}, f32[64,32,128]{2,1,0:T(8,128)S(1)}, f32[2,32,128]{2,1,0:T(8,128)S(1)}, f32[2,32,128]{2,1,0:T(8,128)S(1...) custom-call(s32[64]{0:T(128)S(1)} %select_reduce_fusion.owner_ref, f32[64,64,128]{2,1,0:T(8,128)S(1)} %gather_rings.1.rings_ref, ...), custom_call_target="tpu_custom_call" | custom-call | flops 4194304 | bytes 4194304 | tf_op jit(solution)/shard_map/advance_borders/pallas_call | solution.py:651
  95.0 2.3 collective-permute-start.8
  97.3 1.1 collective-permute-start.9
  98.4 4.8 %collective-permute-start.11 = (f32[2,32,128]{2,1,0:T(8,128)S(1)}, f32[2,32,128]{2,1,0:T(8,128)S(1)}, u32[]{:S(2)}, u32[]{:S(2)}) collective-permute-start(f32[2,32,128]{2,1,0:T(8,128)S(1)} %get-tuple-element.56), channel_id=1, source_target_pairs={{0,15},{1,0},{2,1},{3,2},{4,3},{5,4},{6,5},{7,6},{8,7},{9,8},{10,9... | collective-permute-start | bytes 98312 | tf_op jit(solution)/shard_map/ppermute | solution.py:632
  103.2 1.3 collective-permute-done.10.fs_ref
  104.5 10.7 %all-to-all-start.1 = ((f32[128,56,128]{2,1,0:T(8,128)}), f32[128,56,128]{2,1,0:T(8,128)}, u32[]{:S(2)}, u32[]{:S(2)}) async-start(f32[128,56,128]{2,1,0:T(8,128)} %get-tuple-element.57), calls=%async_computation.1 | async-start | bytes 7340032 | tf_op jit(solution)/shard_map/all_to_all | solution.py:636
  115.2 1.2 copy-done.3
  117.0 16.0 %send_seen.1 = f32[128,64,128]{2,1,0:T(8,128)} custom-call(s32[64]{0:T(128)S(1)} %copy-done.7, f32[64,64,128]{2,1,0:T(8,128)S(1)} %gather_rings.1.rings_ref, f32[64,8,128]{2,1,0:T(8,128)S(1)} %get-tuple-element.52.wind_ref, f32[16,128]{1,0:T(8,128)S(1)} %broadcast_in_dim.35.settle_ref, f32[16,128]{1,0:T(8,128)S(1)} %broadcast_in_dim.34.share_ref, ...), custom_call_target="tpu_custom_call" | custom-call | flops 4194304 | bytes 4194304 | tf_op jit(solution)/shard_map/send_seen/pallas_call | solution.py:651
  133.1 28.6 %all-to-all-done.1.wind_ref = f32[128,56,128]{2,1,0:T(8,128)} async-done(((f32[128,56,128]{2,1,0:T(8,128)}), f32[128,56,128]{2,1,0:T(8,128)}, u32[]{:S(2)}, u32[]{:S(2)}) %all-to-all-start.1) | async-done | bytes 3670048 | tf_op jit(solution)/shard_map/all_to_all | solution.py:636
  161.7 5.2 %all-to-all-start.2 = ((f32[128,64,128]{2,1,0:T(8,128)}), f32[128,64,128]{2,1,0:T(8,128)}, u32[]{:S(2)}, u32[]{:S(2)}) async-start(f32[128,64,128]{2,1,0:T(8,128)} %send_seen.1), calls=%async_computation.2 | async-start | bytes 8388608 | tf_op jit(solution)/shard_map/all_to_all | solution.py:636
  166.9 14.6 %dust_inner.1 = (f32[56,256,128]{2,1,0:T(8,128)}, f32[56,56,128]{2,1,0:T(8,128)}) custom-call(s32[56]{0:T(128)S(1)} %copy-done.9, f32[16,128]{1,0:T(8,128)S(1)} %broadcast_in_dim.34.share_ref, f32[16,128]{1,0:T(8,128)S(1)} %broadcast_in_dim.35.settle_ref, f32[56,256,128]{2,1,0:T(8,128)} %bitcast.13, bf16[256,512]{1,0:T(8,128)(2,1)S(1)} %copy-done, ...), custom_call_target="tpu_custom_call" | custom-call | flops 110100480 | bytes 22020096 | tf_op jit(solution)/shard_map/dust_inner/pallas_call | solution.py:860
  181.5 37.6 %all-to-all-done.2.refs_1_ = f32[128,64,128]{2,1,0:T(8,128)} async-done(((f32[128,64,128]{2,1,0:T(8,128)}), f32[128,64,128]{2,1,0:T(8,128)}, u32[]{:S(2)}, u32[]{:S(2)}) %all-to-all-start.2) | async-done | bytes 4194336 | tf_op jit(solution)/shard_map/all_to_all | solution.py:636
  219.1 19.2 %dust_outer.1 = f32[56,256,128]{2,1,0:T(8,128)} custom-call(s32[56]{0:T(128)S(1)} %copy-done.9, f32[16,128]{1,0:T(8,128)S(1)} %broadcast_in_dim.34.share_ref, f32[16,128]{1,0:T(8,128)S(1)} %broadcast_in_dim.35.settle_ref, f32[56,256,128]{2,1,0:T(8,128)} %get-tuple-element.58.dust_ref, bf16[256,512]{1,0:T(8,128)(2,1)S(1)} %copy-done, ...), custom_call_target="tpu_custom_call" | custom-call | flops 110100480 | bytes 22020096 | tf_op jit(solution)/shard_map/dust_outer/pallas_call | solution.py:860
  (48 shorter events, 4.1 us)
Async XLA Ops:
  0.6 12.6 %copy-start.10 = (s32[7168]{0:T(1024)S(1)}, s32[7168]{0:T(1024)}, u32[]{:S(2)}) copy-start(s32[7168]{0:T(1024)} %param.16) | copy-start | bytes 86020
  0.6 12.6 %copy-start.11 = (s32[7168]{0:T(1024)S(1)}, s32[7168]{0:T(1024)}, u32[]{:S(2)}) copy-start(s32[7168]{0:T(1024)} %param.17) | copy-start | bytes 86020
  0.6 12.9 %copy-start.1 = (bf16[2048,256]{1,0:T(8,128)(2,1)S(1)}, bf16[2048,256]{1,0:T(8,128)(2,1)}, u32[]{:S(2)}) copy-start(bf16[2048,256]{1,0:T(8,128)(2,1)} %constant.88.clone.matrix_ref) | copy-start | bytes 3145732
  4.5 15.4 %collective-permute-start = (f32[18,256]{1,0:T(8,128)S(1)}, f32[18,256]{1,0:T(8,128)S(1)}, u32[]{:S(2)}, u32[]{:S(2)}) collective-permute-start(f32[18,256]{1,0:T(8,128)S(1)} %get-tuple-element.34), channel_id=1, source_target_pairs={{0,16},{16,32},{32,48},{48,64},{64,80},{80,96},{96,112},{112,0},{1... | collective-permute-start | bytes 55304 | tf_op jit(solution)/shard_map/ppermute | solution.py:632
  7.2 12.7 %collective-permute-start.1 = (f32[18,256]{1,0:T(8,128)S(1)}, f32[18,256]{1,0:T(8,128)S(1)}, u32[]{:S(2)}, u32[]{:S(2)}) collective-permute-start(f32[18,256]{1,0:T(8,128)S(1)} %get-tuple-element.35), channel_id=1, source_target_pairs={{0,112},{16,0},{32,16},{48,32},{64,48},{80,64},{96,80},{112,96},{1... | collective-permute-start | bytes 55304 | tf_op jit(solution)/shard_map/ppermute | solution.py:632
  7.2 12.7 %collective-permute-start.2 = (f32[256,128]{1,0:T(8,128)S(1)}, f32[256,128]{1,0:T(8,128)S(1)}, u32[]{:S(2)}, u32[]{:S(2)}) collective-permute-start(f32[256,128]{1,0:T(8,128)S(1)} %get-tuple-element.36), channel_id=1, source_target_pairs={{0,1},{1,2},{2,3},{3,4},{4,5},{5,6},{6,7},{7,8},{8,9},{9,10},{10,1... | collective-permute-start | bytes 393224 | tf_op jit(solution)/shard_map/ppermute | solution.py:632
  8.9 11.1 %collective-permute-start.3 = (f32[256,128]{1,0:T(8,128)S(1)}, f32[256,128]{1,0:T(8,128)S(1)}, u32[]{:S(2)}, u32[]{:S(2)}) collective-permute-start(f32[256,128]{1,0:T(8,128)S(1)} %get-tuple-element.37), channel_id=1, source_target_pairs={{0,15},{1,0},{2,1},{3,2},{4,3},{5,4},{6,5},{7,6},{8,7},{9,8},{10,9... | collective-permute-start | bytes 393224 | tf_op jit(solution)/shard_map/ppermute | solution.py:632
  19.9 7.5 %copy-start.5 = (f32[256,256]{1,0:T(8,128)S(1)}, f32[256,256]{1,0:T(8,128)}, u32[]{:S(2)}) copy-start(f32[256,256]{1,0:T(8,128)} %thr_ref.1) | copy-start | bytes 786436
  19.9 59.2 %all-to-all-start = ((f32[128,64,128]{2,1,0:T(8,128)}), f32[128,64,128]{2,1,0:T(8,128)}, u32[]{:S(2)}, u32[]{:S(2)}) async-start(f32[128,64,128]{2,1,0:T(8,128)} %dust_strips.1), calls=%async_computation | async-start | bytes 8388608 | tf_op jit(solution)/shard_map/all_to_all | solution.py:636
  27.4 62.6 %copy-start.6 = (s32[64]{0:T(128)}, s32[64]{0:T(128)S(1)}, u32[]{:S(2)}) copy-start(s32[64]{0:T(128)S(1)} %select_reduce_fusion.owner_ref) | copy-start | bytes 772
  81.5 8.3 %collective-permute-start.4 = (f32[2,32,128]{2,1,0:T(8,128)S(1)}, f32[2,32,128]{2,1,0:T(8,128)S(1)}, u32[]{:S(2)}, u32[]{:S(2)}) collective-permute-start(f32[2,32,128]{2,1,0:T(8,128)S(1)} %get-tuple-element.48), channel_id=1, source_target_pairs={{0,16},{16,32},{32,48},{48,64},{64,80},{80,96},{96,112},{112,0},{1... | collective-permute-start | bytes 98312 | tf_op jit(solution)/shard_map/ppermute | solution.py:632
  82.2 7.7 %collective-permute-start.5 = (f32[2,32,128]{2,1,0:T(8,128)S(1)}, f32[2,32,128]{2,1,0:T(8,128)S(1)}, u32[]{:S(2)}, u32[]{:S(2)}) collective-permute-start(f32[2,32,128]{2,1,0:T(8,128)S(1)} %get-tuple-element.49), channel_id=1, source_target_pairs={{0,112},{16,0},{32,16},{48,32},{64,48},{80,64},{96,80},{112,96},{1... | collective-permute-start | bytes 98312 | tf_op jit(solution)/shard_map/ppermute | solution.py:632
  82.2 7.7 %collective-permute-start.6 = (f32[2,32,128]{2,1,0:T(8,128)S(1)}, f32[2,32,128]{2,1,0:T(8,128)S(1)}, u32[]{:S(2)}, u32[]{:S(2)}) collective-permute-start(f32[2,32,128]{2,1,0:T(8,128)S(1)} %get-tuple-element.50), channel_id=1, source_target_pairs={{0,1},{1,2},{2,3},{3,4},{4,5},{5,6},{6,7},{7,8},{8,9},{9,10},{10,1... | collective-permute-start | bytes 98312 | tf_op jit(solution)/shard_map/ppermute | solution.py:632
  83.0 6.9 %copy-start.13 = (f32[16]{0:T(128)S(1)}, f32[16]{0:T(128)}, u32[]{:S(2)}) copy-start(f32[16]{0:T(128)} %param.15) | copy-start | bytes 196
  83.0 6.8 %collective-permute-start.7 = (f32[2,32,128]{2,1,0:T(8,128)S(1)}, f32[2,32,128]{2,1,0:T(8,128)S(1)}, u32[]{:S(2)}, u32[]{:S(2)}) collective-permute-start(f32[2,32,128]{2,1,0:T(8,128)S(1)} %get-tuple-element.51), channel_id=1, source_target_pairs={{0,15},{1,0},{2,1},{3,2},{4,3},{5,4},{6,5},{7,6},{8,7},{9,8},{10,9... | collective-permute-start | bytes 98312 | tf_op jit(solution)/shard_map/ppermute | solution.py:632
  95.0 8.2 %collective-permute-start.8 = (f32[2,32,128]{2,1,0:T(8,128)S(1)}, f32[2,32,128]{2,1,0:T(8,128)S(1)}, u32[]{:S(2)}, u32[]{:S(2)}) collective-permute-start(f32[2,32,128]{2,1,0:T(8,128)S(1)} %get-tuple-element.53), channel_id=1, source_target_pairs={{0,16},{16,32},{32,48},{48,64},{64,80},{80,96},{96,112},{112,0},{1... | collective-permute-start | bytes 98312 | tf_op jit(solution)/shard_map/ppermute | solution.py:632
  97.3 5.9 %collective-permute-start.9 = (f32[2,32,128]{2,1,0:T(8,128)S(1)}, f32[2,32,128]{2,1,0:T(8,128)S(1)}, u32[]{:S(2)}, u32[]{:S(2)}) collective-permute-start(f32[2,32,128]{2,1,0:T(8,128)S(1)} %get-tuple-element.54), channel_id=1, source_target_pairs={{0,112},{16,0},{32,16},{48,32},{64,48},{80,64},{96,80},{112,96},{1... | collective-permute-start | bytes 98312 | tf_op jit(solution)/shard_map/ppermute | solution.py:632
  98.4 6.1 %collective-permute-start.10 = (f32[2,32,128]{2,1,0:T(8,128)S(1)}, f32[2,32,128]{2,1,0:T(8,128)S(1)}, u32[]{:S(2)}, u32[]{:S(2)}) collective-permute-start(f32[2,32,128]{2,1,0:T(8,128)S(1)} %get-tuple-element.55), channel_id=1, source_target_pairs={{0,1},{1,2},{2,3},{3,4},{4,5},{5,6},{6,7},{7,8},{8,9},{9,10},{10,1... | collective-permute-start | bytes 98312 | tf_op jit(solution)/shard_map/ppermute | solution.py:632
  98.4 6.1 %collective-permute-start.11 = (f32[2,32,128]{2,1,0:T(8,128)S(1)}, f32[2,32,128]{2,1,0:T(8,128)S(1)}, u32[]{:S(2)}, u32[]{:S(2)}) collective-permute-start(f32[2,32,128]{2,1,0:T(8,128)S(1)} %get-tuple-element.56), channel_id=1, source_target_pairs={{0,15},{1,0},{2,1},{3,2},{4,3},{5,4},{6,5},{7,6},{8,7},{9,8},{10,9... | collective-permute-start | bytes 98312 | tf_op jit(solution)/shard_map/ppermute | solution.py:632
  104.5 57.2 %all-to-all-start.1 = ((f32[128,56,128]{2,1,0:T(8,128)}), f32[128,56,128]{2,1,0:T(8,128)}, u32[]{:S(2)}, u32[]{:S(2)}) async-start(f32[128,56,128]{2,1,0:T(8,128)} %get-tuple-element.57), calls=%async_computation.1 | async-start | bytes 7340032 | tf_op jit(solution)/shard_map/all_to_all | solution.py:636
  133.0 33.8 %copy-start = (bf16[256,512]{1,0:T(8,128)(2,1)S(1)}, bf16[256,512]{1,0:T(8,128)(2,1)}, u32[]{:S(2)}) copy-start(bf16[256,512]{1,0:T(8,128)(2,1)} %constant.89.clone.shift_ref) | copy-start | bytes 786436
  133.1 33.8 %copy-start.9 = (s32[56]{0:T(128)S(1)}, s32[56]{0:T(128)}, u32[]{:S(2)}) copy-start(s32[56]{0:T(128)} %copy-done.8) | copy-start | bytes 676
  161.7 57.4 %all-to-all-start.2 = ((f32[128,64,128]{2,1,0:T(8,128)}), f32[128,64,128]{2,1,0:T(8,128)}, u32[]{:S(2)}, u32[]{:S(2)}) async-start(f32[128,64,128]{2,1,0:T(8,128)} %send_seen.1), calls=%async_computation.2 | async-start | bytes 8388608 | tf_op jit(solution)/shard_map/all_to_all | solution.py:636
  166.9 52.2 %copy-start.4 = (bf16[256,1024]{1,0:T(8,128)(2,1)S(1)}, bf16[256,1024]{1,0:T(8,128)(2,1)}, u32[]{:S(2)}) copy-start(bf16[256,1024]{1,0:T(8,128)(2,1)} %constant.90.clone.refs_0_) | copy-start | bytes 1572868
  (5 other events, 16.0 us)

commit v5 on v4

--- a/solution.py
+++ b/solution.py
@@ -370,37 +370,25 @@
     return new.reshape(velocity.shape), send, ring
 
 
-def pack_borders(outs, ring_at, tiles_x, tiles_y):
-    rows = outs[0].shape[1]
-    lane = lax.broadcasted_iota(jnp.int32, (rows, LANES), 1)
-    borders = (
-        (EAST, [((tiles_x - 1) * tiles_y + n) for n in range(tiles_y)]),
+def border_tiles(tiles_x, tiles_y):
+    return (
+        (EAST, [(tiles_x - 1) * tiles_y + n for n in range(tiles_y)]),
         (WEST, [n for n in range(tiles_y)]),
         (NORTH, [n * tiles_y + tiles_y - 1 for n in range(tiles_x)]),
         (SOUTH, [n * tiles_y for n in range(tiles_x)]),
     )
-    for out, (side, tiles) in zip(outs, borders):
-        for g in range(len(tiles) // 4):
-            packed = None
-            for q in range(4):
-                strip = ring_at(tiles[4 * g + q])
-                if q != side:
-                    strip = pltpu.roll(strip, ((q - side) * TILE) % LANES, 1)
-                packed = strip if packed is None else jnp.where(lane // TILE == q, strip, packed)
-            out[g] = packed
-
-
-def fill_halo(ext, borders, tiles_x, tiles_y):
-    from_west, from_east, from_south, from_north = borders
+
+
+def fill_halo(ext, strips, tiles_x, tiles_y):
     wide = tiles_y + 2
-    for ref, side, places in (
-        (from_west, EAST, [n + 1 for n in range(tiles_y)]),
-        (from_east, WEST, [(tiles_x + 1) * wide + n + 1 for n in range(tiles_y)]),
-        (from_south, NORTH, [(n + 1) * wide for n in range(tiles_x)]),
-        (from_north, SOUTH, [(n + 1) * wide + tiles_y + 1 for n in range(tiles_x)]),
+    for strip_of, side, places in (
+        (strips[0], EAST, [n + 1 for n in range(tiles_y)]),
+        (strips[1], WEST, [(tiles_x + 1) * wide + n + 1 for n in range(tiles_y)]),
+        (strips[2], NORTH, [(n + 1) * wide for n in range(tiles_x)]),
+        (strips[3], SOUTH, [(n + 1) * wide + tiles_y + 1 for n in range(tiles_x)]),
     ):
         for n, place in enumerate(places):
-            strip = ref[n // 4]
+            strip = strip_of(n // 4)
             if n % 4 != side:
                 strip = pltpu.roll(strip, ((side - n % 4) * TILE) % LANES, 1)
             ext[place] = strip
@@ -415,21 +403,17 @@
     return jnp.where((lane // TILE) % 2 == 0, up, down)
 
 
-def border_tiles(tiles_x, tiles_y):
-    return (
-        [(tiles_x - 1) * tiles_y + n for n in range(tiles_y)],
-        [n for n in range(tiles_y)],
-        [n * tiles_y + tiles_y - 1 for n in range(tiles_x)],
-        [n * tiles_y for n in range(tiles_x)],
-    )
-
-
-def pack_borders_kernel(owner_ref, recv_ref, e_ref, w_ref, n_ref, s_ref, strips, sems, *, tiles_x, tiles_y):
-    rows = e_ref.shape[1]
-    used = sorted(set(sum(border_tiles(tiles_x, tiles_y), [])))
+FLAG = 7
+
+
+def pack_borders_kernel(owner_ref, recv_ref, wind_ref, *refs, tiles_x, tiles_y):
+    *outs, rings, sems = refs
+    both_rows = rings.shape[1]
+    borders = border_tiles(tiles_x, tiles_y)
+    used = sorted({t for _, tiles in borders for t in tiles})
 
     def copy(t):
-        return pltpu.make_async_copy(recv_ref.at[owner_ref[t], pl.ds(0, rows), :], strips.at[t], sems.at[t])
+        return pltpu.make_async_copy(recv_ref.at[owner_ref[t]], rings.at[t], sems.at[t])
 
     for t in used:
 
@@ -439,7 +423,7 @@
 
         @pl.when(owner_ref[t] < 0)
         def _():
-            strips[t] = jnp.zeros(strips.shape[1:], jnp.float32)
+            rings[t] = jnp.zeros(rings.shape[1:], jnp.float32)
 
     for t in used:
 
@@ -447,7 +431,37 @@
         def _():
             copy(t).wait()
 
-    pack_borders((e_ref, w_ref, n_ref, s_ref), lambda t: strips[t], tiles_x, tiles_y)
+    lane = lax.broadcasted_iota(jnp.int32, (both_rows, LANES), 1) // TILE
+    row8, lane8 = iotas()
+    group8 = lane8 // TILE
+    for out, (side, tiles) in zip(outs, borders):
+        for g in range(len(tiles) // 4):
+            strips = winds = None
+            for q in range(4):
+                t = tiles[4 * g + q]
+                strip, wind = rings[t], wind_ref[t]
+                if q != side:
+                    strip = pltpu.roll(strip, ((q - side) * TILE) % LANES, 1)
+                    wind = pltpu.roll(wind, ((q - side) * TILE) % LANES, 1)
+                wind = jnp.where(row8 == FLAG, jnp.where(owner_ref[t] >= 0, 1.0, 0.0), wind)
+                strips = strip if strips is None else jnp.where(lane == q, strip, strips)
+                winds = wind if winds is None else jnp.where(group8 == q, wind, winds)
+            at = g * (both_rows + ROWS)
+            out[at : at + both_rows, :] = strips
+            out[at + both_rows : at + both_rows + ROWS, :] = winds
+
+
+def add_corners_kernel(owner_ref, e_ref, w_ref, fs_ref, fn_ref, e_out, w_out, *, tiles_x, tiles_y):
+    size = e_ref.shape[0]
+    rows = e_out.shape[0] - size
+    last = fs_ref.shape[0] - (2 * rows + ROWS)
+    lane = lax.broadcasted_iota(jnp.int32, (rows, LANES), 1)
+    e_out[:size, :] = e_ref[...]
+    w_out[:size, :] = w_ref[...]
+    e_out[size:, :] = jnp.where(
+        lane == 0, pltpu.roll(fs_ref[last : last + rows, :], 1, 1), fn_ref[last : last + rows, :]
+    )
+    w_out[size:, :] = jnp.where(lane == 0, fs_ref[:rows, :], pltpu.roll(fn_ref[:rows, :], LANES - 1, 1))
 
 
 def gather_rings_kernel(owner_ref, recv_ref, rings_ref, *, tiles_x, tiles_y):
@@ -529,79 +543,106 @@
     return chunks
 
 
-def advance_borders_kernel(
-    owner_ref, rings_ref, fw_ref, fe_ref, fs_ref, fn_ref, wind_ref, settle_ref, share_ref,
-    seen_ref, later_ref, e_ref, w_ref, n_ref, s_ref, ext, *, tiles_x, tiles_y
+def advance_strip(side, message, ours, low_end, high_end, settle_ref, share_ref, out, rows):
+    _, lane = iotas()
+    bins = rows // TZ
+    each = 2 * rows + ROWS
+    groups = out.shape[0]
+    mix = dust_step * diffusion
+    for g in range(groups):
+        wind_at = g * each + 2 * rows
+
+        def wind_row(p):
+            return spread_rows(message[wind_at + p : wind_at + p + 1, :])
+
+        for at in range(0, rows, ROWS):
+            level, bin_at = at // bins, at % bins
+            u, v, w = (dust_step * wind_row(c * TZ + level) for c in range(3))
+
+            def cells(group, first):
+                return message[group * each + first : group * each + first + ROWS, :]
+
+            q = cells(g, at)
+            deep = cells(g, rows + at)
+            near = ours[g * each + at : g * each + at + ROWS, :]
+            low = low_end(at) if g == 0 else pltpu.roll(cells(g - 1, at), 1, 1)
+            high = high_end(at) if g == groups - 1 else pltpu.roll(cells(g + 1, at), LANES - 1, 1)
+            before = jnp.where(lane == 0, low, pltpu.roll(q, 1, 1))
+            after = jnp.where(lane == LANES - 1, high, pltpu.roll(q, LANES - 1, 1))
+            across = (deep, near) if side in (WEST, SOUTH) else (near, deep)
+            (west, east), (south, north) = (
+                (across, (before, after)) if side in (WEST, EAST) else ((before, after), across)
+            )
+            other = cells(g, (1 - level) * bins + bin_at)
+            rise = w - dust_step * settle_ref[bin_at : bin_at + ROWS, :]
+            up = jnp.maximum(rise, 0.0)
+            down = up - rise
+            new = (
+                (1.0 - 6.0 * mix - jnp.abs(u) - jnp.abs(v) - up - down) * q
+                + (mix + jnp.maximum(u, 0.0)) * west
+                + (mix + jnp.maximum(-u, 0.0)) * east
+                + (mix + jnp.maximum(v, 0.0)) * south
+                + (mix + jnp.maximum(-v, 0.0)) * north
+                + (mix + (down if level == 0 else up)) * other
+            )
+            if level == 0:
+                new = new + dust_step * wind_row(PLANES - 1) * share_ref[bin_at : bin_at + ROWS, :]
+            out[g, at : at + ROWS, :] = jnp.where(wind_row(FLAG) > 0.0, new, 0.0)
+
+
+def send_seen_kernel(
+    owner_ref, rings_ref, wind_ref, settle_ref, share_ref, e_ref, w_ref, n_ref, s_ref, fw_ref, fe_ref, fs_ref, fn_ref,
+    send_ref, ext, both, lw_ref, le_ref, ls_ref, ln_ref, sems, *, tiles_x, tiles_y
 ):
-    rows = e_ref.shape[1]
-    fill_halo(ext, (fw_ref, fe_ref, fs_ref, fn_ref), tiles_x, tiles_y)
-    fill_tiles(ext, lambda t: rings_ref[t, :rows, :], tiles_x, tiles_y)
-
-    def pair(tiles):
-        for t in tiles:
-            seen = seen_by(ext, place_of(t, tiles_y), tiles_y + 2)
-            seen_ref[t] = seen
-            chunks = advance_ring(t, owner_ref, rings_ref, wind_ref, settle_ref, share_ref, seen)
-            for n, chunk in enumerate(chunks):
-                later_ref[t, n * ROWS : (n + 1) * ROWS, :] = chunk
-
-    def along_y(n, carry):
-        pair((n, (tiles_x - 1) * tiles_y + n))
-        return carry
-
-    def along_x(n, carry):
-        pair((n * tiles_y, n * tiles_y + tiles_y - 1))
-        return carry
-
-    lax.fori_loop(0, tiles_y, along_y, 0)
-    lax.fori_loop(1, tiles_x - 1, along_x, 0)
-    pack_borders((e_ref, w_ref, n_ref, s_ref), lambda t: later_ref[t], tiles_x, tiles_y)
-
-
-def send_seen_kernel(
-    owner_ref, rings_ref, wind_ref, settle_ref, share_ref, seen_ref, later_ref,
-    fw_ref, fe_ref, fs_ref, fn_ref, send_ref, ext, both, sems, *, tiles_x, tiles_y
-):
-    rows = later_ref.shape[1]
+    rows = rings_ref.shape[1] // 2
     wide = tiles_y + 2
-    fill_tiles(ext, lambda t: rings_ref[t, :rows, :], tiles_x, tiles_y)
+    each = 2 * rows + ROWS
+    messages = (fw_ref, fe_ref, fs_ref, fn_ref)
+    later = (lw_ref, le_ref, ls_ref, ln_ref)
 
     def place(t):
         return place_of(t, tiles_y)
 
-    def border(t):
-        x, y = t // tiles_y, t % tiles_y
-        return (x == 0) | (x == tiles_x - 1) | (y == 0) | (y == tiles_y - 1)
+    fill_halo(
+        ext, [lambda g, m=m: m[g * each : g * each + rows, :] for m in messages], tiles_x, tiles_y
+    )
+    fill_tiles(ext, lambda t: rings_ref[t, :rows, :], tiles_x, tiles_y)
 
     def before(t, carry):
-        @pl.when(border(t))
-        def _():
-            both[t, :rows, :] = seen_ref[t]
-
-        @pl.when(jnp.logical_not(border(t)))
-        def _():
-            both[t, :rows, :] = seen_by(ext, place(t), wide)
-
+        both[t, :rows, :] = seen_by(ext, place(t), wide)
         return carry
 
     lax.fori_loop(0, tiles_x * tiles_y, before, 0)
-    fill_halo(ext, (fw_ref, fe_ref, fs_ref, fn_ref), tiles_x, tiles_y)
-
-    def advance(t, carry):
-        @pl.when(border(t))
-        def _():
-            ext[place(t)] = later_ref[t]
-
-        @pl.when(jnp.logical_not(border(t)))
-        def _():
-            seen = both[t, :rows, :]
-            chunks = advance_ring(t, owner_ref, rings_ref, wind_ref, settle_ref, share_ref, seen)
+
+    def advance(i, carry):
+        for t in (2 * i, 2 * i + 1):
+            chunks = advance_ring(t, owner_ref, rings_ref, wind_ref, settle_ref, share_ref, both[t, :rows, :])
             for n, chunk in enumerate(chunks):
                 ext[place(t), n * ROWS : (n + 1) * ROWS, :] = chunk
-
-        return carry
-
-    lax.fori_loop(0, tiles_x * tiles_y, advance, 0)
+        return carry
+
+    lax.fori_loop(0, tiles_x * tiles_y // 2, advance, 0)
+
+    def corner(ref, shift):
+        first = ref.shape[0] - rows
+
+        def of(at):
+            cells = ref[first + at : first + at + ROWS, :]
+            return pltpu.roll(cells, shift, 1) if shift else cells
+
+        return of
+
+    ends = (
+        (corner(fw_ref, 0), corner(fw_ref, 0)),
+        (corner(fe_ref, 0), corner(fe_ref, 0)),
+        (corner(fw_ref, 0), corner(fe_ref, LANES - 1)),
+        (corner(fw_ref, 1), corner(fe_ref, 0)),
+    )
+    for side, message, ours, (low, high), out in zip(
+        (WEST, EAST, SOUTH, NORTH), messages, (w_ref, e_ref, s_ref, n_ref), ends, later
+    ):
+        advance_strip(side, message, ours, low, high, settle_ref, share_ref, out, rows)
+    fill_halo(ext, [lambda g, m=m: m[g] for m in later], tiles_x, tiles_y)
 
     def copy(t):
         return pltpu.make_async_copy(both.at[t], send_ref.at[owner_ref[t]], sems.at[t])
@@ -641,7 +682,7 @@
     return shifted(east, "gx", 1), shifted(west, "gx", -1), shifted(north, "gy", 1), shifted(south, "gy", -1)
 
 
-def ring_call(kernel, tiles_x, tiles_y, rows, outs, scratch, name, hbm_in=False, hbm_out=False):
+def ring_call(kernel, tiles_x, tiles_y, rows, outs, scratch, name, hbm_in=0, hbm_out=False):
     smem = pl.BlockSpec(memory_space=pltpu.SMEM)
     vmem = pl.BlockSpec(memory_space=pltpu.VMEM)
     hbm = pl.BlockSpec(memory_space=pltpu.HBM)
@@ -650,7 +691,7 @@
     def call(owner_of_tile, *inputs):
         return pl.pallas_call(
             functools.partial(kernel, tiles_x=tiles_x, tiles_y=tiles_y),
-            in_specs=[smem] + [hbm if hbm_in else vmem] * len(inputs),
+            in_specs=[smem] + [hbm] * hbm_in + [vmem] * (len(inputs) - hbm_in),
             out_specs=hbm if hbm_out else [vmem] * len(outs),
             out_shape=outs[0] if hbm_out else outs,
             scratch_shapes=scratch,
@@ -662,16 +703,13 @@
     return call
 
 
-def border_shapes(tiles_x, tiles_y, rows):
-    return [f32(tiles_y // 4, rows, LANES)] * 2 + [f32(tiles_x // 4, rows, LANES)] * 2
-
-
 def relay_strips(owner_of_tile, received, wind_send, wind_ring, settle_speed, bin_share, tiles_x, tiles_y):
     owners, both_rows, _ = received.shape
     rows = both_rows // 2
     per_home = tiles_x * tiles_y
-    packs = border_shapes(tiles_x, tiles_y, rows)
+    each = both_rows + ROWS
     ext = pltpu.VMEM(((tiles_x + 2) * (tiles_y + 2), rows, LANES), jnp.float32)
+    all_rings = pltpu.VMEM((per_home, both_rows, LANES), jnp.float32)
     each_sem = pltpu.SemaphoreType.DMA((per_home,))
     settle_rows = jnp.broadcast_to(settle_speed[:, None], settle_speed.shape + (LANES,))
     share_rows = jnp.broadcast_to(bin_share[:, None], bin_share.shape + (LANES,))
@@ -679,25 +717,38 @@
     def call(kernel, outs, scratch, name, *inputs, **places):
         return ring_call(kernel, tiles_x, tiles_y, rows, outs, scratch, name, **places)(owner_of_tile, *inputs)
 
-    strips = pltpu.VMEM((per_home, rows, LANES), jnp.float32)
-    borders = call(
-        pack_borders_kernel, packs, [strips, each_sem], "pack_borders", in_hbm(received), hbm_in=True
-    )
-    borders = exchange_borders(borders)
+    along_x, along_y = tiles_y // 4, tiles_x // 4
+    east, west, north, south = call(
+        pack_borders_kernel,
+        [f32(along_x * each, LANES)] * 2 + [f32(along_y * each, LANES)] * 2,
+        [all_rings, each_sem],
+        "pack_borders",
+        in_hbm(received),
+        wind_ring,
+        hbm_in=1,
+    )
+    from_south, from_north = shifted(north, "gy", 1), shifted(south, "gy", -1)
     (rings,) = call(gather_rings_kernel, [f32(per_home, both_rows, LANES)], [], "gather_rings", received)
-    seen, later, *borders = call(
-        advance_borders_kernel, [f32(per_home, rows, LANES)] * 2 + packs, [ext], "advance_borders",
-        rings, *borders, wind_ring, settle_rows, share_rows,
-    )
-    borders = exchange_borders(borders)
-    wind_send, *borders = lax.optimization_barrier((wind_send, *borders))
+    east_full, west_full = call(
+        add_corners_kernel,
+        [f32(along_x * each + rows, LANES)] * 2,
+        [],
+        "add_corners",
+        east, west, from_south, from_north,
+    )
+    from_west, from_east = shifted(east_full, "gx", 1), shifted(west_full, "gx", -1)
+    wind_send, from_west, from_east = lax.optimization_barrier((wind_send, from_west, from_east))
     wind_recv = relay_rows(wind_send)
     seen_send = call(
         send_seen_kernel,
         [pltpu.HBM((owners, both_rows, LANES), jnp.float32)],
-        [ext, pltpu.VMEM((per_home, both_rows, LANES), jnp.float32), each_sem],
+        [ext, all_rings]
+        + [pltpu.VMEM((along_x, rows, LANES), jnp.float32)] * 2
+        + [pltpu.VMEM((along_y, rows, LANES), jnp.float32)] * 2
+        + [each_sem],
         "send_seen",
-        rings, wind_ring, settle_rows, share_rows, seen, later, *borders,
+        rings, wind_ring, settle_rows, share_rows, east, west, north, south,
+        from_west, from_east, from_south, from_north,
         hbm_out=True,
     )
     return wind_recv, relay_rows(seen_send)

time: 239 us -> 229 us (0.958)
  starting transfers between devices: 45.2 us -> 37.2 us
  local copies, waits for them, and re-layouts: 2.99 us -> 0.19 us
  waiting for transfers between devices: 83.2 us -> 85.7 us
    ppermute x12 -> x8, starting transfers between devices: 22.3 us -> 15.3 us  [shifted(): lax.ppermute(value, axis, [(source, (source + steps) % count) for source...]
    ppermute x12 -> x8, waiting for transfers between devices: 1.32 us -> 6 us  [shifted(): lax.ppermute(value, axis, [(source, (source + steps) % count) for source...]
    unnamed x28 -> x16, local copies, waits for them, and re-layouts: 2.85 us -> 0.05 us
  transfers between devices with their start and end apart: 15 -> 11, of which waited for: 4 -> 6; matrix products, arithmetic and copies ran while one was open for 0% -> 0% of each run, Pallas kernels for 32% -> 34%
where the time goes in v5:
time: 229 us; the launch traced here: 228 us
  Pallas kernels  104 us (45%)
  waiting for transfers between devices  85.7 us (37%)
  starting transfers between devices  37.2 us (16%)
    all_to_all x3, waiting for transfers between devices, relay_rows(): return lax.all_to_all(rows, AXES, split_axis=0, concat_axis=0, tiled=True)  79.7 us
    pallas_call x1, Pallas kernels, wind_step(): pl.pallas_call(functools.partial(wind_kernel, levels=levels), in_specs=[s...  36.2 us
    pallas_call x2, Pallas kernels, dust_substep(): pl.pallas_call(functools.partial(dust_kernel, block=block, bins=bins, out...  34.3 us
    pallas_call x4, Pallas kernels, call(): pl.pallas_call(functools.partial(kernel, tiles_x=tiles_x, tiles_y=tiles_y...  22.9 us
    all_to_all x3, starting transfers between devices, relay_rows(): return lax.all_to_all(rows, AXES, split_axis=0, concat_axis=0, tiled=True)  21.8 us
    ppermute x8, starting transfers between devices, shifted(): lax.ppermute(value, axis, [(source, (source + steps) % count) for source...  15.3 us
    pallas_call x1, Pallas kernels, dust_strips(): pl.pallas_call(functools.partial(strips_kernel, block=block, bins=bins),...  6.28 us
    ppermute x8, waiting for transfers between devices, shifted(): lax.ppermute(value, axis, [(source, (source + steps) % count) for source...  6 us
  transfers between devices with their start and end apart: 11, of which 6 were waited for; matrix products, arithmetic and copies ran while one was open for 0% of the time, Pallas kernels for 34%

profile of v5, /device:TPU:1, one launch (start us, length us, event | category | flops | bytes accessed | tf_op | source)
XLA Modules:
  0.0 228.1 jit_solution(17411598467734048804)
XLA Ops:
  0.7 3.9 %wind_faces.1 = (f32[18,256]{1,0:T(8,128)S(1)}, f32[18,256]{1,0:T(8,128)S(1)}, f32[256,128]{1,0:T(8,128)S(1)}, f32[256,128]{1,0:T(8,128)S(1)}) custom-call(f32[18,256,256]{2,1,0:T(8,128)} %bitcast.14), custom_call_target="tpu_custom_call" | custom-call | flops 1179648 | bytes 4718592 | tf_op jit(solution)/shard_map/wind_faces/pallas_call | solution.py:219
  4.5 2.7 %collective-permute-start = (f32[18,256]{1,0:T(8,128)S(1)}, f32[18,256]{1,0:T(8,128)S(1)}, u32[]{:S(2)}, u32[]{:S(2)}) collective-permute-start(f32[18,256]{1,0:T(8,128)S(1)} %get-tuple-element.28), channel_id=1, source_target_pairs={{0,16},{16,32},{32,48},{48,64},{64,80},{80,96},{96,112},{112,0},{1... | collective-permute-start | bytes 55304 | tf_op jit(solution)/shard_map/ppermute | solution.py:673
  7.2 1.6 collective-permute-start.2
  8.9 4.3 %collective-permute-start.3 = (f32[256,128]{1,0:T(8,128)S(1)}, f32[256,128]{1,0:T(8,128)S(1)}, u32[]{:S(2)}, u32[]{:S(2)}) collective-permute-start(f32[256,128]{1,0:T(8,128)S(1)} %get-tuple-element.31), channel_id=1, source_target_pairs={{0,15},{1,0},{2,1},{3,2},{4,3},{5,4},{6,5},{7,6},{8,7},{9,8},{10,9... | collective-permute-start | bytes 393224 | tf_op jit(solution)/shard_map/ppermute | solution.py:673
  13.6 6.3 %dust_strips.1 = f32[128,64,128]{2,1,0:T(8,128)} custom-call(s32[56]{0:T(128)S(1)} %select_reduce_fusion.1.home_ref, f32[56,256,128]{2,1,0:T(8,128)} %bitcast.12, bf16[2048,256]{1,0:T(8,128)(2,1)S(1)} %copy-done.1), custom_call_target="tpu_custom_call" | custom-call | flops 36700160 | bytes 9175040 | tf_op jit(solution)/shard_map/dust_strips/pallas_call | solution.py:160
  19.9 7.1 %all-to-all-start = ((f32[128,64,128]{2,1,0:T(8,128)}), f32[128,64,128]{2,1,0:T(8,128)}, u32[]{:S(2)}, u32[]{:S(2)}) async-start(f32[128,64,128]{2,1,0:T(8,128)} %dust_strips.1), calls=%async_computation | async-start | bytes 8388608 | tf_op jit(solution)/shard_map/all_to_all | solution.py:677
  27.0 0.3 select_reduce_fusion.owner_ref
  27.4 36.2 %wind_step.1 = (f32[18,256,256]{2,1,0:T(8,128)}, f32[128,56,128]{2,1,0:T(8,128)}, f32[64,8,128]{2,1,0:T(8,128)S(1)}) custom-call(s32[64]{0:T(128)S(1)} %select_reduce_fusion.owner_ref, f32[18,256,256]{2,1,0:T(8,128)} %bitcast.15, f32[18,256]{1,0:T(8,128)S(1)} %collective-permute-done.xlo_ref, f32[18,256]{1,0:T(8,128)S(1)} %collective-permute-done.1.xhi_ref, ...), custom_call_target="tpu_custom_call" | custom-call | flops 47185920 | bytes 11796480 | tf_op jit(solution)/shard_map/wind_step/pallas_call | solution.py:340
  63.6 15.6 %all-to-all-done.recv_ref = f32[128,64,128]{2,1,0:T(8,128)} async-done(((f32[128,64,128]{2,1,0:T(8,128)}), f32[128,64,128]{2,1,0:T(8,128)}, u32[]{:S(2)}, u32[]{:S(2)}) %all-to-all-start) | async-done | bytes 4194336 | tf_op jit(solution)/shard_map/all_to_all | solution.py:677
  79.1 2.6 %pack_borders.1 = (f32[144,128]{1,0:T(8,128)S(1)}, f32[144,128]{1,0:T(8,128)S(1)}, f32[144,128]{1,0:T(8,128)S(1)}, f32[144,128]{1,0:T(8,128)S(1)}) custom-call(s32[64]{0:T(128)S(1)} %select_reduce_fusion.owner_ref, f32[128,64,128]{2,1,0:T(8,128)} %all-to-all-done.recv_ref, f32[64,8,128]{2,1,0:T(8,128)S(1)} %get-tuple-element.42.wind_ref), custom_call_target="tpu_custom_call" | custom-call | flops 4194304 | bytes 4194304 | tf_op jit(solution)/shard_map/pack_borders/pallas_call | solution.py:692
  82.0 4.5 %collective-permute-start.5 = (f32[144,128]{1,0:T(8,128)S(1)}, f32[144,128]{1,0:T(8,128)S(1)}, u32[]{:S(2)}, u32[]{:S(2)}) collective-permute-start(f32[144,128]{1,0:T(8,128)S(1)} %get-tuple-element.46.s_ref), channel_id=1, source_target_pairs={{0,15},{1,0},{2,1},{3,2},{4,3},{5,4},{6,5},{7,6},{8,7},{9,8},{10,9... | collective-permute-start | bytes 221192 | tf_op jit(solution)/shard_map/ppermute | solution.py:673
  86.5 1.7 collective-permute-done.4.fs_ref
  88.3 0.6 add_corners.1
  88.9 1.8 collective-permute-start.6
  90.7 1.6 collective-permute-done.6.fw_ref
  92.3 2.7 %collective-permute-done.7.fe_ref = f32[176,128]{1,0:T(8,128)S(1)} collective-permute-done((f32[176,128]{1,0:T(8,128)S(1)}, f32[176,128]{1,0:T(8,128)S(1)}, u32[]{:S(2)}, u32[]{:S(2)}) %collective-permute-start.7) | collective-permute-done | bytes 90144 | tf_op jit(solution)/shard_map/ppermute | solution.py:673
  95.0 9.6 %all-to-all-start.1 = ((f32[128,56,128]{2,1,0:T(8,128)}), f32[128,56,128]{2,1,0:T(8,128)}, u32[]{:S(2)}, u32[]{:S(2)}) async-start(f32[128,56,128]{2,1,0:T(8,128)} %get-tuple-element.49), calls=%async_computation.1 | async-start | bytes 7340032 | tf_op jit(solution)/shard_map/all_to_all | solution.py:677
  104.6 2.9 %gather_rings.1.rings_ref = f32[64,64,128]{2,1,0:T(8,128)S(1)} custom-call(s32[64]{0:T(128)S(1)} %select_reduce_fusion.owner_ref, f32[128,64,128]{2,1,0:T(8,128)} %all-to-all-done.recv_ref), custom_call_target="tpu_custom_call" | custom-call | flops 4194304 | bytes 4194304 | tf_op jit(solution)/shard_map/gather_rings/pallas_call | solution.py:692
  107.6 16.8 %send_seen.1 = f32[128,64,128]{2,1,0:T(8,128)} custom-call(s32[64]{0:T(128)S(1)} %select_reduce_fusion.owner_ref, f32[64,64,128]{2,1,0:T(8,128)S(1)} %gather_rings.1.rings_ref, f32[64,8,128]{2,1,0:T(8,128)S(1)} %get-tuple-element.42.wind_ref, f32[16,128]{1,0:T(8,128)S(1)} %broadcast_in_dim.35.settle_ref, f32[16,128]{1,0:T(8,128)S(1)} %broadcast_in_dim.34.share_ref, ...), custom_call_target="tpu_custom_call" | custom-call | flops 4194304 | bytes 4194304 | tf_op jit(solution)/shard_map/send_seen/pallas_call | solution.py:692
  124.5 26.6 %all-to-all-done.1.wind_ref = f32[128,56,128]{2,1,0:T(8,128)} async-done(((f32[128,56,128]{2,1,0:T(8,128)}), f32[128,56,128]{2,1,0:T(8,128)}, u32[]{:S(2)}, u32[]{:S(2)}) %all-to-all-start.1) | async-done | bytes 3670048 | tf_op jit(solution)/shard_map/all_to_all | solution.py:677
  151.1 5.2 %all-to-all-start.2 = ((f32[128,64,128]{2,1,0:T(8,128)}), f32[128,64,128]{2,1,0:T(8,128)}, u32[]{:S(2)}, u32[]{:S(2)}) async-start(f32[128,64,128]{2,1,0:T(8,128)} %send_seen.1), calls=%async_computation.2 | async-start | bytes 8388608 | tf_op jit(solution)/shard_map/all_to_all | solution.py:677
  156.2 14.7 %dust_inner.1 = (f32[56,256,128]{2,1,0:T(8,128)}, f32[56,56,128]{2,1,0:T(8,128)}) custom-call(s32[56]{0:T(128)S(1)} %select_reduce_fusion.1.home_ref, f32[16,128]{1,0:T(8,128)S(1)} %broadcast_in_dim.34.share_ref, f32[16,128]{1,0:T(8,128)S(1)} %broadcast_in_dim.35.settle_ref, f32[56,256,128]{2,1,0:T(8,128)} %bitcast.13, bf16[256,512]{1,0:T(8,128)(2,1)S(1)} %copy-done, ...), custom_call_target="tpu_custom_call" | custom-call | flops 110100480 | bytes 22020096 | tf_op jit(solution)/shard_map/dust_inner/pallas_call | solution.py:911
  170.9 37.6 %all-to-all-done.2.refs_1_ = f32[128,64,128]{2,1,0:T(8,128)} async-done(((f32[128,64,128]{2,1,0:T(8,128)}), f32[128,64,128]{2,1,0:T(8,128)}, u32[]{:S(2)}, u32[]{:S(2)}) %all-to-all-start.2) | async-done | bytes 4194336 | tf_op jit(solution)/shard_map/all_to_all | solution.py:677
  208.5 19.7 %dust_outer.1 = f32[56,256,128]{2,1,0:T(8,128)} custom-call(s32[56]{0:T(128)S(1)} %select_reduce_fusion.1.home_ref, f32[16,128]{1,0:T(8,128)S(1)} %broadcast_in_dim.34.share_ref, f32[16,128]{1,0:T(8,128)S(1)} %broadcast_in_dim.35.settle_ref, f32[56,256,128]{2,1,0:T(8,128)} %get-tuple-element.50.dust_ref, bf16[256,512]{1,0:T(8,128)(2,1)S(1)} %copy-done, ...), custom_call_target="tpu_custom_call" | custom-call | flops 110100480 | bytes 22020096 | tf_op jit(solution)/shard_map/dust_outer/pallas_call | solution.py:911
  (28 shorter events, 0.9 us)
Async XLA Ops:
  0.6 12.6 %copy-start.4 = (s32[7168]{0:T(1024)S(1)}, s32[7168]{0:T(1024)}, u32[]{:S(2)}) copy-start(s32[7168]{0:T(1024)} %param.16) | copy-start | bytes 86020
  0.6 12.6 %copy-start.5 = (s32[7168]{0:T(1024)S(1)}, s32[7168]{0:T(1024)}, u32[]{:S(2)}) copy-start(s32[7168]{0:T(1024)} %param.17) | copy-start | bytes 86020
  0.6 12.9 %copy-start.1 = (bf16[2048,256]{1,0:T(8,128)(2,1)S(1)}, bf16[2048,256]{1,0:T(8,128)(2,1)}, u32[]{:S(2)}) copy-start(bf16[2048,256]{1,0:T(8,128)(2,1)} %constant.88.clone.matrix_ref) | copy-start | bytes 3145732
  4.5 15.3 %collective-permute-start = (f32[18,256]{1,0:T(8,128)S(1)}, f32[18,256]{1,0:T(8,128)S(1)}, u32[]{:S(2)}, u32[]{:S(2)}) collective-permute-start(f32[18,256]{1,0:T(8,128)S(1)} %get-tuple-element.28), channel_id=1, source_target_pairs={{0,16},{16,32},{32,48},{48,64},{64,80},{80,96},{96,112},{112,0},{1... | collective-permute-start | bytes 55304 | tf_op jit(solution)/shard_map/ppermute | solution.py:673
  7.2 12.7 %collective-permute-start.1 = (f32[18,256]{1,0:T(8,128)S(1)}, f32[18,256]{1,0:T(8,128)S(1)}, u32[]{:S(2)}, u32[]{:S(2)}) collective-permute-start(f32[18,256]{1,0:T(8,128)S(1)} %get-tuple-element.29), channel_id=1, source_target_pairs={{0,112},{16,0},{32,16},{48,32},{64,48},{80,64},{96,80},{112,96},{1... | collective-permute-start | bytes 55304 | tf_op jit(solution)/shard_map/ppermute | solution.py:673
  7.2 12.7 %collective-permute-start.2 = (f32[256,128]{1,0:T(8,128)S(1)}, f32[256,128]{1,0:T(8,128)S(1)}, u32[]{:S(2)}, u32[]{:S(2)}) collective-permute-start(f32[256,128]{1,0:T(8,128)S(1)} %get-tuple-element.30), channel_id=1, source_target_pairs={{0,1},{1,2},{2,3},{3,4},{4,5},{5,6},{6,7},{7,8},{8,9},{9,10},{10,1... | collective-permute-start | bytes 393224 | tf_op jit(solution)/shard_map/ppermute | solution.py:673
  8.9 11.0 %collective-permute-start.3 = (f32[256,128]{1,0:T(8,128)S(1)}, f32[256,128]{1,0:T(8,128)S(1)}, u32[]{:S(2)}, u32[]{:S(2)}) collective-permute-start(f32[256,128]{1,0:T(8,128)S(1)} %get-tuple-element.31), channel_id=1, source_target_pairs={{0,15},{1,0},{2,1},{3,2},{4,3},{5,4},{6,5},{7,6},{8,7},{9,8},{10,9... | collective-permute-start | bytes 393224 | tf_op jit(solution)/shard_map/ppermute | solution.py:673
  19.9 7.5 %copy-start.3 = (f32[256,256]{1,0:T(8,128)S(1)}, f32[256,256]{1,0:T(8,128)}, u32[]{:S(2)}) copy-start(f32[256,256]{1,0:T(8,128)} %thr_ref.1) | copy-start | bytes 786436
  19.9 59.2 %all-to-all-start = ((f32[128,64,128]{2,1,0:T(8,128)}), f32[128,64,128]{2,1,0:T(8,128)}, u32[]{:S(2)}, u32[]{:S(2)}) async-start(f32[128,64,128]{2,1,0:T(8,128)} %dust_strips.1), calls=%async_computation | async-start | bytes 8388608 | tf_op jit(solution)/shard_map/all_to_all | solution.py:677
  81.7 6.6 %collective-permute-start.4 = (f32[144,128]{1,0:T(8,128)S(1)}, f32[144,128]{1,0:T(8,128)S(1)}, u32[]{:S(2)}, u32[]{:S(2)}) collective-permute-start(f32[144,128]{1,0:T(8,128)S(1)} %get-tuple-element.45.n_ref), channel_id=1, source_target_pairs={{0,1},{1,2},{2,3},{3,4},{4,5},{5,6},{6,7},{7,8},{8,9},{9,10},{10,1... | collective-permute-start | bytes 221192 | tf_op jit(solution)/shard_map/ppermute | solution.py:673
  82.0 6.3 %collective-permute-start.5 = (f32[144,128]{1,0:T(8,128)S(1)}, f32[144,128]{1,0:T(8,128)S(1)}, u32[]{:S(2)}, u32[]{:S(2)}) collective-permute-start(f32[144,128]{1,0:T(8,128)S(1)} %get-tuple-element.46.s_ref), channel_id=1, source_target_pairs={{0,15},{1,0},{2,1},{3,2},{4,3},{5,4},{6,5},{7,6},{8,7},{9,8},{10,9... | collective-permute-start | bytes 221192 | tf_op jit(solution)/shard_map/ppermute | solution.py:673
  88.9 3.4 %collective-permute-start.6 = (f32[176,128]{1,0:T(8,128)S(1)}, f32[176,128]{1,0:T(8,128)S(1)}, u32[]{:S(2)}, u32[]{:S(2)}) collective-permute-start(f32[176,128]{1,0:T(8,128)S(1)} %get-tuple-element.47), channel_id=1, source_target_pairs={{0,16},{16,32},{32,48},{48,64},{64,80},{80,96},{96,112},{112,0},{1... | collective-permute-start | bytes 270344 | tf_op jit(solution)/shard_map/ppermute | solution.py:673
  90.7 4.2 %collective-permute-start.7 = (f32[176,128]{1,0:T(8,128)S(1)}, f32[176,128]{1,0:T(8,128)S(1)}, u32[]{:S(2)}, u32[]{:S(2)}) collective-permute-start(f32[176,128]{1,0:T(8,128)S(1)} %get-tuple-element.48), channel_id=1, source_target_pairs={{0,112},{16,0},{32,16},{48,32},{64,48},{80,64},{96,80},{112,96},{1... | collective-permute-start | bytes 270344 | tf_op jit(solution)/shard_map/ppermute | solution.py:673
  95.0 56.1 %all-to-all-start.1 = ((f32[128,56,128]{2,1,0:T(8,128)}), f32[128,56,128]{2,1,0:T(8,128)}, u32[]{:S(2)}, u32[]{:S(2)}) async-start(f32[128,56,128]{2,1,0:T(8,128)} %get-tuple-element.49), calls=%async_computation.1 | async-start | bytes 7340032 | tf_op jit(solution)/shard_map/all_to_all | solution.py:677
  104.6 2.9 %copy-start.6 = (f32[16]{0:T(128)S(1)}, f32[16]{0:T(128)}, u32[]{:S(2)}) copy-start(f32[16]{0:T(128)} %param.14) | copy-start | bytes 196
  104.6 3.0 %copy-start.7 = (f32[16]{0:T(128)S(1)}, f32[16]{0:T(128)}, u32[]{:S(2)}) copy-start(f32[16]{0:T(128)} %param.15) | copy-start | bytes 196
  124.5 31.8 %copy-start = (bf16[256,512]{1,0:T(8,128)(2,1)S(1)}, bf16[256,512]{1,0:T(8,128)(2,1)}, u32[]{:S(2)}) copy-start(bf16[256,512]{1,0:T(8,128)(2,1)} %constant.89.clone.shift_ref) | copy-start | bytes 786436
  151.1 57.4 %all-to-all-start.2 = ((f32[128,64,128]{2,1,0:T(8,128)}), f32[128,64,128]{2,1,0:T(8,128)}, u32[]{:S(2)}, u32[]{:S(2)}) async-start(f32[128,64,128]{2,1,0:T(8,128)} %send_seen.1), calls=%async_computation.2 | async-start | bytes 8388608 | tf_op jit(solution)/shard_map/all_to_all | solution.py:677
  156.2 52.2 %copy-start.2 = (bf16[256,1024]{1,0:T(8,128)(2,1)S(1)}, bf16[256,1024]{1,0:T(8,128)(2,1)}, u32[]{:S(2)}) copy-start(bf16[256,1024]{1,0:T(8,128)(2,1)} %constant.90.clone.refs_0_) | copy-start | bytes 1572868

commit v6 on v5

--- a/solution.py
+++ b/solution.py
@@ -67,8 +67,8 @@
     return high, (x - high.astype(jnp.float32)).astype(jnp.bfloat16)
 
 
-def moves(sources):
-    lanes = np.arange(LANES)[:, None]
+def moves(sources, width=LANES):
+    lanes = np.arange(width)[:, None]
     once = (lanes == np.asarray(sources)[None, :]).astype(ml_dtypes.bfloat16)
     return np.concatenate([once, once], axis=0)
 
@@ -94,14 +94,16 @@
     return moves(np.concatenate([(lane + d) % LANES for d in (-1, 1, -TILE, TILE)]))
 
 
-def side_matrix():
-    lane = np.arange(LANES)
-    columns = []
-    for r in range(ROWS):
-        along = 4 * r + lane // TILE
-        source = np.where(lane % TILE == 0, SOUTH * TILE + along, -1)
-        columns.append(np.where(lane % TILE == TILE - 1, NORTH * TILE + along, source))
-    return moves(np.concatenate(columns))
+def spread_matrix():
+    i, j = np.divmod(np.arange(TILE * TILE), TILE)
+    source = np.full(TILE * TILE, -1)
+    for depth in (1, 0):
+        at = depth * LANES
+        source = np.where(j == depth, at + SOUTH * TILE + i, source)
+        source = np.where(j == TILE - 1 - depth, at + NORTH * TILE + i, source)
+        source = np.where(i == depth, at + WEST * TILE + j, source)
+        source = np.where(i == TILE - 1 - depth, at + EAST * TILE + j, source)
+    return moves(source, 2 * LANES)
 
 
 def strips_kernel(home_ref, dust_hbm, matrix_ref, send_ref, dust, rings, load_sems, sems, *, block, bins):
@@ -249,7 +251,7 @@
     half = 16
     halves = ny // LANES
     tiles_y = ny // TILE
-    pattern = ring_pattern(0)
+    patterns = [ring_pattern(0), ring_pattern(1)]
     _, lane8 = iotas()
     group = lane8 // TILE
 
@@ -301,7 +303,8 @@
                         moved = pltpu.roll(parts[k], ((k - t) * TILE) % LANES, 1) if k != t else parts[k]
                         cells = jnp.where(group == k, moved, cells)
                     tiles[tile, p * ROWS : (p + 1) * ROWS, :] = cells
-                    ring_ref[tile, p : p + 1, :] = ring_of(cells, pattern)
+                    for depth in range(2):
+                        ring_ref[tile, depth * 8 + p : depth * 8 + p + 1, :] = ring_of(cells, patterns[depth])
 
         def send(t, inner):
             tile = ix * tiles_y + t
@@ -344,7 +347,7 @@
         out_shape=[
             f32(fields, nx, ny),
             pltpu.HBM((owners, PLANES * ROWS, LANES), jnp.float32),
-            f32(per_home, 8, LANES),
+            f32(per_home, 16, LANES),
         ],
         scratch_shapes=[
             pltpu.VMEM((fields, nx + 16, ny), jnp.float32),
@@ -439,7 +442,7 @@
             strips = winds = None
             for q in range(4):
                 t = tiles[4 * g + q]
-                strip, wind = rings[t], wind_ref[t]
+                strip, wind = rings[t], wind_ref[t, :ROWS, :]
                 if q != side:
                     strip = pltpu.roll(strip, ((q - side) * TILE) % LANES, 1)
                     wind = pltpu.roll(wind, ((q - side) * TILE) % LANES, 1)
@@ -486,17 +489,81 @@
     return (t // tiles_y + 1) * (tiles_y + 2) + t % tiles_y + 1
 
 
+def corner_index(inset):
+    _, lane = iotas()
+    group, within = lane // TILE, lane % TILE
+    on_x = (group == WEST) | (group == EAST)
+    low = within < TILE // 2
+    along = jnp.where((group == EAST) | (group == NORTH), TILE - 1 - inset, inset)
+    return jnp.where(on_x, jnp.where(low, SOUTH, NORTH), jnp.where(low, WEST, EAST)) * TILE + along
+
+
+def ring_effect(t, wind_ref, settle_ref, seen, seen_later):
+    row, lane = iotas()
+    group, within = lane // TILE, lane % TILE
+    on_x = (group == WEST) | (group == EAST)
+    low_side = (group == WEST) | (group == SOUTH)
+    first, last = within == 0, within == TILE - 1
+    second, last_but_one = within == 1, within == TILE - 2
+    corner, inner = corner_index(0), corner_index(1)
+    rows = seen.shape[0]
+    bins = rows // TZ
+    mix = dust_step * diffusion
+
+    def wind(depth, p):
+        return dust_step * spread_rows(wind_ref[t, depth * 8 + p : depth * 8 + p + 1, :])
+
+    inflow, later_in = [], []
+    coefs = []
+    for level in range(TZ):
+        u, v, w = (wind(0, c * TZ + level) for c in range(3))
+        across, along = jnp.where(on_x, u, v), jnp.where(on_x, v, u)
+        outward = jnp.where(low_side, across, -across)
+        from_out = mix + jnp.maximum(outward, 0.0)
+        from_in = jnp.where(first | last, mix + jnp.maximum(-outward, 0.0), 0.0)
+        from_before, from_after = mix + jnp.maximum(along, 0.0), mix + jnp.maximum(-along, 0.0)
+        from_corner = jnp.where(first, from_before, jnp.where(last, from_after, 0.0))
+        from_before = jnp.where(first, 0.0, from_before)
+        from_after = jnp.where(last, 0.0, from_after)
+        keep = 1.0 - 6.0 * mix - jnp.abs(u) - jnp.abs(v)
+        u2, v2 = (wind(1, c * TZ + level) for c in range(2))
+        across2, along2 = jnp.where(on_x, u2, v2), jnp.where(on_x, v2, u2)
+        deep_out = mix + jnp.maximum(jnp.where(low_side, across2, -across2), 0.0)
+        deep_corner = jnp.where(
+            second, mix + jnp.maximum(along2, 0.0), jnp.where(last_but_one, mix + jnp.maximum(-along2, 0.0), 0.0)
+        )
+        coefs.append((w, keep, from_in, from_before, from_after, deep_out, deep_corner))
+        for at in range(level * bins, (level + 1) * bins, ROWS):
+            for view, taken in ((seen, inflow), (seen_later, later_in)):
+                g = view[at : at + ROWS, :]
+                taken.append(from_out * g + from_corner * lane_gather(g, corner))
+    outer, deep = [], []
+    for n, e in enumerate(inflow):
+        level, bin_at = n * ROWS // bins, n * ROWS % bins
+        w, keep, from_in, from_before, from_after, deep_out, deep_corner = coefs[level]
+        other = inflow[n + len(inflow) // 2 if level == 0 else n - len(inflow) // 2]
+        rise = w - dust_step * settle_ref[bin_at : bin_at + ROWS, :]
+        up = jnp.maximum(rise, 0.0)
+        down = up - rise
+        turned = lane_gather(e, inner)
+        outer.append(
+            (keep - up - down) * e
+            + from_before * pltpu.roll(e, 1, 1)
+            + from_after * pltpu.roll(e, LANES - 1, 1)
+            + from_in * turned
+            + (mix + (down if level == 0 else up)) * other
+            + later_in[n]
+        )
+        deep.append(deep_out * e + deep_corner * turned)
+    return outer, deep
+
+
 def advance_ring(t, owner_ref, rings_ref, wind_ref, settle_ref, share_ref, seen):
     _, lane = iotas()
     group, within = lane // TILE, lane % TILE
     on_x = (group == WEST) | (group == EAST)
     first, last = within == 0, within == TILE - 1
-    high = jnp.where((group == EAST) | (group == NORTH), TILE - 1, 0)
-    corner = jnp.where(
-        on_x,
-        jnp.where(first, SOUTH, NORTH) * TILE + high,
-        jnp.where(first, WEST, EAST) * TILE + high,
-    )
+    corner = corner_index(0)
     rows = rings_ref.shape[1] // 2
     bins = rows // TZ
     uplift = dust_step * spread_rows(wind_ref[t, PLANES - 1 : PLANES, :])
@@ -648,7 +715,10 @@
         return pltpu.make_async_copy(both.at[t], send_ref.at[owner_ref[t]], sems.at[t])
 
     def after(t, carry):
-        both[t, rows:, :] = seen_by(ext, place(t), wide)
+        effect = ring_effect(t, wind_ref, settle_ref, both[t, :rows, :], seen_by(ext, place(t), wide))
+        for depth, chunks in enumerate(effect):
+            for n, chunk in enumerate(chunks):
+                both[t, depth * rows + n * ROWS : depth * rows + (n + 1) * ROWS, :] = chunk
 
         @pl.when(owner_ref[t] >= 0)
         def _():
@@ -754,74 +824,35 @@
     return wind_recv, relay_rows(seen_send)
 
 
-def dust_kernel(home_ref, share_ref, settle_ref, dust_ref, shift_ref, wind_ref, *refs, block, bins, outer):
-    if outer:
-        side_ref, seen_ref, out_ref, coef, sides, edges, *work = refs
-    else:
-        out_ref, kept_ref, coef, *work = refs
+def dust_kernel(home_ref, share_ref, settle_ref, dust_ref, shift_ref, wind_ref, out_ref, coef, *work, block, bins):
     lanes = len(work) // 2
     step = pl.program_id(0)
-    each = TZ * bins
-    if outer:
-        for j in range(block):
-            edges[j] = seen_ref[home_ref[step * block + j]]
-        spread = jnp.dot(
-            jnp.concatenate(halves_of(edges[...].reshape(block * 2 * each, LANES)), axis=1),
-            side_ref[...],
-            preferred_element_type=jnp.float32,
-        )
-        for r in range(ROWS):
-            sides[r] = spread[:, r * LANES : (r + 1) * LANES]
-
     _, lane = iotas()
     within = lane % TILE
-    first_y, last_y = within == 0, within == TILE - 1
     low_lanes, high_lanes = lane < TILE, lane >= LANES - TILE
     mix = dust_step * diffusion
     chunks = bins // ROWS
     settle = [dust_step * settle_ref[h * ROWS : (h + 1) * ROWS, :] for h in range(chunks)]
     share = [share_ref[h * ROWS : (h + 1) * ROWS, :] for h in range(chunks)]
+    nothing = jnp.zeros((ROWS, LANES), jnp.float32)
 
     def prepare(k, j):
         held = work[2 * k]
         home = home_ref[step * block + j]
-        if not outer:
-            kept_ref[j] = wind_ref[home]
-        wind_at = j if outer else home
-        plane = [wind_ref[wind_at, p * ROWS : (p + 1) * ROWS, :] * dust_step for p in range(PLANES)]
+        plane = [wind_ref[home, p * ROWS : (p + 1) * ROWS, :] * dust_step for p in range(PLANES)]
         for level in range(TZ):
             u, v = plane[level], plane[TZ + level]
-            south_by = mix + jnp.maximum(v, 0.0)
-            north_by = mix + jnp.maximum(-v, 0.0)
             coef[k, 0, level] = mix + jnp.maximum(u, 0.0)
             coef[k, 1, level] = mix + jnp.maximum(-u, 0.0)
+            coef[k, 2, level] = jnp.where(within == 0, 0.0, mix + jnp.maximum(v, 0.0))
+            coef[k, 3, level] = jnp.where(within == TILE - 1, 0.0, mix + jnp.maximum(-v, 0.0))
             coef[k, 4, level] = 1.0 - 6.0 * mix - jnp.abs(u) - jnp.abs(v)
             coef[k, 5, level] = plane[2 * TZ + level]
-            if outer:
-                coef[k, 2, level] = south_by
-                coef[k, 3, level] = north_by
-                coef[k, 7, level] = jnp.where(first_y, south_by, jnp.where(last_y, north_by, 0.0))
-            else:
-                coef[k, 2, level] = jnp.where(first_y, 0.0, south_by)
-                coef[k, 3, level] = jnp.where(last_y, 0.0, north_by)
         coef[k, 6, 0] = plane[PLANES - 1]
         for r in range(ROWS):
             for level in range(TZ):
                 at = (r * TZ + level) * bins
-                cells = dust_ref[j, pl.ds(r * TZ + level, bins, stride=ROWS * TZ), :]
-                if not outer:
-                    held[at : at + bins, :] = cells
-                    continue
-                for h in range(chunks):
-                    edge_at = level * bins + h * ROWS
-                    q = cells[h * ROWS : (h + 1) * ROWS]
-                    q = q + spread_rows(coef[k, 7, level, r : r + 1, :]) * sides[r, pl.ds(j * 2 * each + edge_at, ROWS), :]
-                    if r == 0 or r == ROWS - 1:
-                        edge = edges[j, edge_at : edge_at + ROWS, :]
-                        here = low_lanes if r == 0 else high_lanes
-                        by = spread_rows(coef[k, 0 if r == 0 else 1, level, r : r + 1, :])
-                        q = q + jnp.where(here, by * edge, 0.0)
-                    held[at + h * ROWS : at + (h + 1) * ROWS, :] = q
+                held[at : at + bins, :] = dust_ref[j, pl.ds(r * TZ + level, bins, stride=ROWS * TZ), :]
 
     def shift(k):
         held, shifts = work[2 * k], work[2 * k + 1]
@@ -829,15 +860,13 @@
             jnp.concatenate(halves_of(held[...]), axis=1), shift_ref[...], preferred_element_type=jnp.float32
         )
 
-    def update(k, j):
+    def update(k, j, substep):
         held, shifts = work[2 * k], work[2 * k + 1]
-        nothing = jnp.zeros((ROWS, LANES), jnp.float32)
         for r in range(ROWS):
             for h in range(chunks):
                 cells = [held[(r * TZ + level) * bins + h * ROWS :][:ROWS] for level in range(TZ)]
                 for level in range(TZ):
                     at = (r * TZ + level) * bins + h * ROWS
-                    edge_at = each + level * bins + h * ROWS
 
                     def moved(which, rows_up=0):
                         first = at + rows_up * TZ * bins
@@ -846,14 +875,8 @@
                     def by(which):
                         return spread_rows(coef[k, which, level, r : r + 1, :])
 
-                    edge = edges[j, edge_at : edge_at + ROWS, :] if outer else nothing
-                    before = edge if r == 0 else moved(2, -1)
-                    after = edge if r == ROWS - 1 else moved(3, 1)
-                    south, north = moved(0), moved(1)
-                    if outer:
-                        side = sides[r, pl.ds(j * 2 * each + edge_at, ROWS), :]
-                        south = jnp.where(first_y, side, south)
-                        north = jnp.where(last_y, side, north)
+                    before = nothing if r == 0 else moved(2, -1)
+                    after = nothing if r == ROWS - 1 else moved(3, 1)
                     west = jnp.where(low_lanes, before, moved(2))
                     east = jnp.where(high_lanes, after, moved(3))
                     rise = by(5) - settle[h]
@@ -863,62 +886,129 @@
                         (by(4) - jnp.abs(rise)) * cells[level]
                         + by(0) * west
                         + by(1) * east
-                        + by(2) * south
-                        + by(3) * north
+                        + by(2) * moved(0)
+                        + by(3) * moved(1)
                         + mixed * cells[1 - level]
                     )
                     if level == 0:
                         value = value + spread_rows(coef[k, 6, 0, r : r + 1, :]) * share[h]
-                    first = h * ROWS * ROWS * TZ + r * TZ + level
-                    out_ref[j, pl.ds(first, ROWS, stride=ROWS * TZ), :] = value
+                    if substep == 0:
+                        held[at : at + ROWS, :] = value
+                    else:
+                        first = h * ROWS * ROWS * TZ + r * TZ + level
+                        out_ref[j, pl.ds(first, ROWS, stride=ROWS * TZ), :] = value
 
     def some(i, carry):
         for k in range(lanes):
             prepare(k, i * lanes + k)
-        for k in range(lanes):
-            shift(k)
-        for k in range(lanes):
-            update(k, i * lanes + k)
+        for substep in range(2):
+            for k in range(lanes):
+                shift(k)
+            for k in range(lanes):
+                update(k, i * lanes + k, substep)
         return carry
 
     lax.fori_loop(0, block // lanes, some, 0)
 
 
-def dust_substep(home_of_slot, dust, wind, settle_speed, bin_share, seen_recv=None):
+def dust_inner(home_of_slot, dust, wind_recv, settle_speed, bin_share):
     slots, cells = dust.shape[:2]
     bins = settle_speed.shape[0]
     block = 8 if slots % 8 == 0 else 4
     lanes = 2
-    outer = seen_recv is not None
     smem = pl.BlockSpec(memory_space=pltpu.SMEM)
     vmem = pl.BlockSpec(memory_space=pltpu.VMEM)
     tile = pl.BlockSpec((block, cells, LANES), lambda i: (i, 0, 0))
     settle = jnp.broadcast_to(settle_speed[:, None], (bins, LANES))
     share = jnp.broadcast_to(bin_share[:, None], (bins, LANES))
-    wind_rows = pl.BlockSpec((block,) + wind.shape[1:], lambda i: (i, 0, 0))
-    inputs = [home_of_slot, share, settle, in_hbm(dust), jnp.asarray(shift_matrix()), in_hbm(wind) if outer else wind]
-    scratch = [pltpu.VMEM((lanes, PLANES + 1, TZ, ROWS, LANES), jnp.float32)]
-    if outer:
-        inputs += [jnp.asarray(side_matrix()), seen_recv]
-        scratch += [
-            pltpu.VMEM((ROWS, block * seen_recv.shape[1], LANES), jnp.float32),
-            pltpu.VMEM((block,) + seen_recv.shape[1:], jnp.float32),
-        ]
-    out_shape = f32(*dust.shape)
-    if not outer:
-        out_shape = [pltpu.HBM(dust.shape, jnp.float32), pltpu.HBM((slots,) + wind.shape[1:], jnp.float32)]
-    scratch += [pltpu.VMEM((cells, LANES), jnp.float32), pltpu.VMEM((cells, 4 * LANES), jnp.float32)] * lanes
     return pl.pallas_call(
-        functools.partial(dust_kernel, block=block, bins=bins, outer=outer),
+        functools.partial(dust_kernel, block=block, bins=bins),
         grid=(slots // block,),
-        in_specs=[smem, vmem, vmem, tile, vmem, wind_rows if outer else vmem] + [vmem] * (len(inputs) - 6),
-        out_specs=tile if outer else [tile, wind_rows],
-        out_shape=out_shape,
-        scratch_shapes=scratch,
-        compiler_params=pltpu.CompilerParams(vmem_limit_bytes=32 << 20),
-        cost_estimate=pl.CostEstimate(flops=60 * dust.size, bytes_accessed=dust.size * 12, transcendentals=0),
-        name="dust_outer" if outer else "dust_inner",
-    )(*inputs)
+        in_specs=[smem, vmem, vmem, tile, vmem, vmem],
+        out_specs=tile,
+        out_shape=pltpu.HBM(dust.shape, jnp.float32),
+        scratch_shapes=[pltpu.VMEM((lanes, PLANES, TZ, ROWS, LANES), jnp.float32)]
+        + [pltpu.VMEM((cells, LANES), jnp.float32), pltpu.VMEM((cells, 4 * LANES), jnp.float32)] * lanes,
+        compiler_params=pltpu.CompilerParams(vmem_limit_bytes=24 << 20),
+        cost_estimate=pl.CostEstimate(flops=120 * dust.size, bytes_accessed=dust.size * 12, transcendentals=0),
+        name="dust_inner",
+    )(home_of_slot, share, settle, in_hbm(dust), jnp.asarray(shift_matrix()), wind_recv)
+
+
+def dust_outer_kernel(
+    home_ref, inner_hbm, matrix_ref, effect_hbm, out_hbm, effect, dust, effect_sems, load_sems, sems, *, block, bins
+):
+    slots = dust.shape[0]
+    rows = TZ * bins
+
+    def arrive(s):
+        return pltpu.make_async_copy(effect_hbm.at[home_ref[s]], effect.at[s], effect_sems.at[s])
+
+    def load(i):
+        some = pl.ds(i * block, block)
+        return pltpu.make_async_copy(inner_hbm.at[some], dust.at[some], load_sems.at[i])
+
+    def store(i):
+        some = pl.ds(i * block, block)
+        return pltpu.make_async_copy(dust.at[some], out_hbm.at[some], sems.at[i])
+
+    def start(i, carry):
+        for j in range(block):
+            arrive(i * block + j).start()
+        load(i).start()
+        return carry
+
+    lax.fori_loop(0, slots // block, start, 0)
+
+    def one(i, carry):
+        for j in range(block):
+            arrive(i * block + j).wait()
+        rings = jnp.concatenate(
+            [
+                jnp.concatenate([effect[i * block + j, depth * rows : (depth + 1) * rows, :] for depth in range(2)], axis=1)
+                for j in range(block)
+            ],
+            axis=0,
+        )
+        added = jnp.dot(
+            jnp.concatenate(halves_of(rings), axis=1), matrix_ref[...], preferred_element_type=jnp.float32
+        )
+        load(i).wait()
+        for j in range(block):
+            for r in range(ROWS):
+                for level in range(TZ):
+                    at = pl.ds(r * TZ + level, bins, stride=ROWS * TZ)
+                    first = j * rows + level * bins
+                    dust[i * block + j, at, :] += added[first : first + bins, r * LANES : (r + 1) * LANES]
+        store(i).start()
+        return carry
+
+    lax.fori_loop(0, slots // block, one, 0)
+    for i in range(slots // block):
+        store(i).wait()
+
+
+def dust_outer(home_of_slot, inner, effect, bins):
+    slots = inner.shape[0]
+    block = 8 if slots % 8 == 0 else 4
+    hbm = pl.BlockSpec(memory_space=pltpu.HBM)
+    vmem = pl.BlockSpec(memory_space=pltpu.VMEM)
+    return pl.pallas_call(
+        functools.partial(dust_outer_kernel, block=block, bins=bins),
+        in_specs=[pl.BlockSpec(memory_space=pltpu.SMEM), hbm, vmem, hbm],
+        out_specs=hbm,
+        out_shape=pltpu.HBM(inner.shape, jnp.float32),
+        scratch_shapes=[
+            pltpu.VMEM((slots,) + effect.shape[1:], jnp.float32),
+            pltpu.VMEM(inner.shape, jnp.float32),
+            pltpu.SemaphoreType.DMA((slots,)),
+            pltpu.SemaphoreType.DMA((slots // block,)),
+            pltpu.SemaphoreType.DMA((slots // block,)),
+        ],
+        compiler_params=pltpu.CompilerParams(vmem_limit_bytes=24 << 20),
+        cost_estimate=pl.CostEstimate(flops=2 * inner.size, bytes_accessed=inner.size * 8, transcendentals=0),
+        name="dust_outer",
+    )(home_of_slot, in_hbm(inner), jnp.asarray(spread_matrix()), in_hbm(effect))
 
 
 def per_device(velocity, threshold, dust_mass, settle_speed, bin_share, active_tiles, tile_owner):
@@ -956,11 +1046,11 @@
         owner_of_tile, velocity, xlo, xhi, ylo, yhi, threshold, owners
     )
     strips, wind_send, wind_ring = lax.optimization_barrier((strips, wind_send, wind_ring))
-    wind_recv, seen_recv = relay_strips(
+    wind_recv, effect = relay_strips(
         owner_of_tile, strips, wind_send, wind_ring, settle_speed, bin_share, tiles_x, tiles_y
     )
-    inner, wind_held = dust_substep(home_of_slot, dust, wind_recv, settle_speed, bin_share)
-    out = dust_substep(home_of_slot, inner, wind_held, settle_speed, bin_share, seen_recv)
+    inner = dust_inner(home_of_slot, dust, wind_recv, settle_speed, bin_share)
+    out = dust_outer(home_of_slot, inner, effect, bins)
     out = out.reshape(slots, bins, ROWS, TZ, LANES).transpose(0, 1, 3, 2, 4).reshape(dust_mass.shape)
     return new_velocity, out
 

time: 229 us -> 220 us (0.961)
  waiting for transfers between devices: 85.7 us -> 68.8 us
  Pallas kernels: 104 us -> 111 us
    all_to_all x3, waiting for transfers between devices: 79.7 us -> 62.8 us  [relay_rows(): return lax.all_to_all(rows, AXES, split_axis=0, concat_axis=0, tiled=True)]
    pallas_call x4, Pallas kernels: 22.9 us -> 28.6 us  [call(): pl.pallas_call(functools.partial(kernel, tiles_x=tiles_x, tiles_y=tiles_y...]
    pallas_call x1, Pallas kernels: 36.2 us -> 40 us  [wind_step(): pl.pallas_call(functools.partial(wind_kernel, levels=levels), in_specs=[s...]
  transfers between devices with their start and end apart: 11 -> 11, of which waited for: 6 -> 6; matrix products, arithmetic and copies ran while one was open for 0% -> 0% of each run, Pallas kernels for 34% -> 43%
where the time goes in v6:
time: 220 us; the launch traced here: 219 us
  Pallas kernels  111 us (50%)
  waiting for transfers between devices  68.8 us (31%)
  starting transfers between devices  37.4 us (17%)
    all_to_all x3, waiting for transfers between devices, relay_rows(): return lax.all_to_all(rows, AXES, split_axis=0, concat_axis=0, tiled=True)  62.8 us
    pallas_call x1, Pallas kernels, wind_step(): pl.pallas_call(functools.partial(wind_kernel, levels=levels), in_specs=[s...  40 us
    pallas_call x4, Pallas kernels, call(): pl.pallas_call(functools.partial(kernel, tiles_x=tiles_x, tiles_y=tiles_y...  28.6 us
    all_to_all x3, starting transfers between devices, relay_rows(): return lax.all_to_all(rows, AXES, split_axis=0, concat_axis=0, tiled=True)  22.2 us
    pallas_call x1, Pallas kernels, dust_inner(): pl.pallas_call(functools.partial(dust_kernel, block=block, bins=bins), gr...  21.9 us
    ppermute x8, starting transfers between devices, shifted(): lax.ppermute(value, axis, [(source, (source + steps) % count) for source...  15.2 us
    pallas_call x1, Pallas kernels, dust_outer(): pl.pallas_call(functools.partial(dust_outer_kernel, block=block, bins=bin...  10.3 us
    pallas_call x1, Pallas kernels, dust_strips(): pl.pallas_call(functools.partial(strips_kernel, block=block, bins=bins),...  6.29 us
  transfers between devices with their start and end apart: 11, of which 6 were waited for; matrix products, arithmetic and copies ran while one was open for 0% of the time, Pallas kernels for 43%

profile of v6, /device:TPU:1, one launch (start us, length us, event | category | flops | bytes accessed | tf_op | source)
XLA Modules:
  0.0 219.0 jit_solution(14061263808250028140)
XLA Ops:
  0.7 3.9 %wind_faces.1 = (f32[18,256]{1,0:T(8,128)S(1)}, f32[18,256]{1,0:T(8,128)S(1)}, f32[256,128]{1,0:T(8,128)S(1)}, f32[256,128]{1,0:T(8,128)S(1)}) custom-call(f32[18,256,256]{2,1,0:T(8,128)} %bitcast.14), custom_call_target="tpu_custom_call" | custom-call | flops 1179648 | bytes 4718592 | tf_op jit(solution)/shard_map/wind_faces/pallas_call | solution.py:221
  4.5 2.7 %collective-permute-start = (f32[18,256]{1,0:T(8,128)S(1)}, f32[18,256]{1,0:T(8,128)S(1)}, u32[]{:S(2)}, u32[]{:S(2)}) collective-permute-start(f32[18,256]{1,0:T(8,128)S(1)} %get-tuple-element.26), channel_id=1, source_target_pairs={{0,16},{16,32},{32,48},{48,64},{64,80},{80,96},{96,112},{112,0},{1... | collective-permute-start | bytes 55304 | tf_op jit(solution)/shard_map/ppermute | solution.py:743
  7.2 1.6 collective-permute-start.2
  8.9 4.3 %collective-permute-start.3 = (f32[256,128]{1,0:T(8,128)S(1)}, f32[256,128]{1,0:T(8,128)S(1)}, u32[]{:S(2)}, u32[]{:S(2)}) collective-permute-start(f32[256,128]{1,0:T(8,128)S(1)} %get-tuple-element.29), channel_id=1, source_target_pairs={{0,15},{1,0},{2,1},{3,2},{4,3},{5,4},{6,5},{7,6},{8,7},{9,8},{10,9... | collective-permute-start | bytes 393224 | tf_op jit(solution)/shard_map/ppermute | solution.py:743
  13.6 6.3 %dust_strips.1 = f32[128,64,128]{2,1,0:T(8,128)} custom-call(s32[56]{0:T(128)S(1)} %select_reduce_fusion.1.home_ref, f32[56,256,128]{2,1,0:T(8,128)} %bitcast.12, bf16[2048,256]{1,0:T(8,128)(2,1)S(1)} %copy-done.1), custom_call_target="tpu_custom_call" | custom-call | flops 36700160 | bytes 9175040 | tf_op jit(solution)/shard_map/dust_strips/pallas_call | solution.py:162
  19.9 7.1 %all-to-all-start = ((f32[128,64,128]{2,1,0:T(8,128)}), f32[128,64,128]{2,1,0:T(8,128)}, u32[]{:S(2)}, u32[]{:S(2)}) async-start(f32[128,64,128]{2,1,0:T(8,128)} %dust_strips.1), calls=%async_computation | async-start | bytes 8388608 | tf_op jit(solution)/shard_map/all_to_all | solution.py:747
  27.0 0.3 select_reduce_fusion.owner_ref
  27.4 40.0 %wind_step.1 = (f32[18,256,256]{2,1,0:T(8,128)}, f32[128,56,128]{2,1,0:T(8,128)}, f32[64,16,128]{2,1,0:T(8,128)S(1)}) custom-call(s32[64]{0:T(128)S(1)} %select_reduce_fusion.owner_ref, f32[18,256,256]{2,1,0:T(8,128)} %bitcast.15, f32[18,256]{1,0:T(8,128)S(1)} %collective-permute-done.xlo_ref, f32[18,256]{1,0:T(8,128)S(1)} %collective-permute-done.1.xhi_ref, ...), custom_call_target="tpu_custom_call" | custom-call | flops 47185920 | bytes 11796480 | tf_op jit(solution)/shard_map/wind_step/pallas_call | solution.py:343
  67.4 11.7 %all-to-all-done.recv_ref = f32[128,64,128]{2,1,0:T(8,128)} async-done(((f32[128,64,128]{2,1,0:T(8,128)}), f32[128,64,128]{2,1,0:T(8,128)}, u32[]{:S(2)}, u32[]{:S(2)}) %all-to-all-start) | async-done | bytes 4194336 | tf_op jit(solution)/shard_map/all_to_all | solution.py:747
  79.1 2.6 %pack_borders.1 = (f32[144,128]{1,0:T(8,128)S(1)}, f32[144,128]{1,0:T(8,128)S(1)}, f32[144,128]{1,0:T(8,128)S(1)}, f32[144,128]{1,0:T(8,128)S(1)}) custom-call(s32[64]{0:T(128)S(1)} %select_reduce_fusion.owner_ref, f32[128,64,128]{2,1,0:T(8,128)} %all-to-all-done.recv_ref, f32[64,16,128]{2,1,0:T(8,128)S(1)} %get-tuple-element.40.wind_ref), custom_call_target="tpu_custom_call" | custom-call | flops 4194304 | bytes 4194304 | tf_op jit(solution)/shard_map/pack_borders/pallas_call | solution.py:762
  82.0 4.6 %collective-permute-start.5 = (f32[144,128]{1,0:T(8,128)S(1)}, f32[144,128]{1,0:T(8,128)S(1)}, u32[]{:S(2)}, u32[]{:S(2)}) collective-permute-start(f32[144,128]{1,0:T(8,128)S(1)} %get-tuple-element.44.s_ref), channel_id=1, source_target_pairs={{0,15},{1,0},{2,1},{3,2},{4,3},{5,4},{6,5},{7,6},{8,7},{9,8},{10,9... | collective-permute-start | bytes 221192 | tf_op jit(solution)/shard_map/ppermute | solution.py:743
  86.6 1.7 collective-permute-done.4.fs_ref
  88.3 0.6 add_corners.1
  88.9 1.6 collective-permute-start.6
  90.6 1.5 collective-permute-done.6.fw_ref
  92.1 2.7 %collective-permute-done.7.fe_ref = f32[176,128]{1,0:T(8,128)S(1)} collective-permute-done((f32[176,128]{1,0:T(8,128)S(1)}, f32[176,128]{1,0:T(8,128)S(1)}, u32[]{:S(2)}, u32[]{:S(2)}) %collective-permute-start.7) | collective-permute-done | bytes 90144 | tf_op jit(solution)/shard_map/ppermute | solution.py:743
  94.8 10.0 %all-to-all-start.1 = ((f32[128,56,128]{2,1,0:T(8,128)}), f32[128,56,128]{2,1,0:T(8,128)}, u32[]{:S(2)}, u32[]{:S(2)}) async-start(f32[128,56,128]{2,1,0:T(8,128)} %get-tuple-element.47), calls=%async_computation.1 | async-start | bytes 7340032 | tf_op jit(solution)/shard_map/all_to_all | solution.py:747
  104.8 2.9 %gather_rings.1.rings_ref = f32[64,64,128]{2,1,0:T(8,128)S(1)} custom-call(s32[64]{0:T(128)S(1)} %select_reduce_fusion.owner_ref, f32[128,64,128]{2,1,0:T(8,128)} %all-to-all-done.recv_ref), custom_call_target="tpu_custom_call" | custom-call | flops 4194304 | bytes 4194304 | tf_op jit(solution)/shard_map/gather_rings/pallas_call | solution.py:762
  107.8 22.6 %send_seen.1 = f32[128,64,128]{2,1,0:T(8,128)} custom-call(s32[64]{0:T(128)S(1)} %select_reduce_fusion.owner_ref, f32[64,64,128]{2,1,0:T(8,128)S(1)} %gather_rings.1.rings_ref, f32[64,16,128]{2,1,0:T(8,128)S(1)} %get-tuple-element.40.wind_ref, f32[16,128]{1,0:T(8,128)S(1)} %broadcast_in_dim.35.settle_ref, f32[16,128]{1,0:T(8,128)S(1)} %broadcast_in_dim.34.share_ref, ...), custom_call_target="tpu_custom_call" | custom-call | flops 4194304 | bytes 4194304 | tf_op jit(solution)/shard_map/send_seen/pallas_call | solution.py:762
  130.4 20.8 %all-to-all-done.1.wind_ref = f32[128,56,128]{2,1,0:T(8,128)} async-done(((f32[128,56,128]{2,1,0:T(8,128)}), f32[128,56,128]{2,1,0:T(8,128)}, u32[]{:S(2)}, u32[]{:S(2)}) %all-to-all-start.1) | async-done | bytes 3670048 | tf_op jit(solution)/shard_map/all_to_all | solution.py:747
  151.3 5.1 %all-to-all-start.2 = ((f32[128,64,128]{2,1,0:T(8,128)}), f32[128,64,128]{2,1,0:T(8,128)}, u32[]{:S(2)}, u32[]{:S(2)}) async-start(f32[128,64,128]{2,1,0:T(8,128)} %send_seen.1), calls=%async_computation.2 | async-start | bytes 8388608 | tf_op jit(solution)/shard_map/all_to_all | solution.py:747
  156.4 21.9 %dust_inner.1.inner_hbm = f32[56,256,128]{2,1,0:T(8,128)} custom-call(s32[56]{0:T(128)S(1)} %select_reduce_fusion.1.home_ref, f32[16,128]{1,0:T(8,128)S(1)} %broadcast_in_dim.34.share_ref, f32[16,128]{1,0:T(8,128)S(1)} %broadcast_in_dim.35.settle_ref, f32[56,256,128]{2,1,0:T(8,128)} %bitcast.13, bf16[256,512]{1,0:T(8,128)(2,1)S(1)} %copy-done.2, ...), custom_call_target="tpu_custom_call" | custom-call | flops 220200960 | bytes 22020096 | tf_op jit(solution)/shard_map/dust_inner/pallas_call | solution.py:924
  178.3 30.3 %all-to-all-done.2.effect_hbm = f32[128,64,128]{2,1,0:T(8,128)} async-done(((f32[128,64,128]{2,1,0:T(8,128)}), f32[128,64,128]{2,1,0:T(8,128)}, u32[]{:S(2)}, u32[]{:S(2)}) %all-to-all-start.2) | async-done | bytes 4194336 | tf_op jit(solution)/shard_map/all_to_all | solution.py:747
  208.7 10.3 %dust_outer.1 = f32[56,256,128]{2,1,0:T(8,128)} custom-call(s32[56]{0:T(128)S(1)} %select_reduce_fusion.1.home_ref, f32[56,256,128]{2,1,0:T(8,128)} %dust_inner.1.inner_hbm, bf16[512,1024]{1,0:T(8,128)(2,1)S(1)} %copy-done, f32[128,64,128]{2,1,0:T(8,128)} %all-to-all-done.2.effect_hbm), custom_call_target="tpu_custom_call" | custom-call | flops 3670016 | bytes 14680064 | tf_op jit(solution)/shard_map/dust_outer/pallas_call | solution.py:996
  (28 shorter events, 0.9 us)
Async XLA Ops:
  0.6 12.9 %copy-start.1 = (bf16[2048,256]{1,0:T(8,128)(2,1)S(1)}, bf16[2048,256]{1,0:T(8,128)(2,1)}, u32[]{:S(2)}) copy-start(bf16[2048,256]{1,0:T(8,128)(2,1)} %constant.88.clone.matrix_ref) | copy-start | bytes 3145732
  0.6 12.6 %copy-start.5 = (s32[7168]{0:T(1024)S(1)}, s32[7168]{0:T(1024)}, u32[]{:S(2)}) copy-start(s32[7168]{0:T(1024)} %param.16) | copy-start | bytes 86020
  0.7 12.5 %copy-start.4 = (s32[7168]{0:T(1024)S(1)}, s32[7168]{0:T(1024)}, u32[]{:S(2)}) copy-start(s32[7168]{0:T(1024)} %param.15) | copy-start | bytes 86020
  4.5 15.3 %collective-permute-start = (f32[18,256]{1,0:T(8,128)S(1)}, f32[18,256]{1,0:T(8,128)S(1)}, u32[]{:S(2)}, u32[]{:S(2)}) collective-permute-start(f32[18,256]{1,0:T(8,128)S(1)} %get-tuple-element.26), channel_id=1, source_target_pairs={{0,16},{16,32},{32,48},{48,64},{64,80},{80,96},{96,112},{112,0},{1... | collective-permute-start | bytes 55304 | tf_op jit(solution)/shard_map/ppermute | solution.py:743
  7.2 12.7 %collective-permute-start.1 = (f32[18,256]{1,0:T(8,128)S(1)}, f32[18,256]{1,0:T(8,128)S(1)}, u32[]{:S(2)}, u32[]{:S(2)}) collective-permute-start(f32[18,256]{1,0:T(8,128)S(1)} %get-tuple-element.27), channel_id=1, source_target_pairs={{0,112},{16,0},{32,16},{48,32},{64,48},{80,64},{96,80},{112,96},{1... | collective-permute-start | bytes 55304 | tf_op jit(solution)/shard_map/ppermute | solution.py:743
  7.2 12.7 %collective-permute-start.2 = (f32[256,128]{1,0:T(8,128)S(1)}, f32[256,128]{1,0:T(8,128)S(1)}, u32[]{:S(2)}, u32[]{:S(2)}) collective-permute-start(f32[256,128]{1,0:T(8,128)S(1)} %get-tuple-element.28), channel_id=1, source_target_pairs={{0,1},{1,2},{2,3},{3,4},{4,5},{5,6},{6,7},{7,8},{8,9},{9,10},{10,1... | collective-permute-start | bytes 393224 | tf_op jit(solution)/shard_map/ppermute | solution.py:743
  8.9 11.0 %collective-permute-start.3 = (f32[256,128]{1,0:T(8,128)S(1)}, f32[256,128]{1,0:T(8,128)S(1)}, u32[]{:S(2)}, u32[]{:S(2)}) collective-permute-start(f32[256,128]{1,0:T(8,128)S(1)} %get-tuple-element.29), channel_id=1, source_target_pairs={{0,15},{1,0},{2,1},{3,2},{4,3},{5,4},{6,5},{7,6},{8,7},{9,8},{10,9... | collective-permute-start | bytes 393224 | tf_op jit(solution)/shard_map/ppermute | solution.py:743
  19.9 7.5 %copy-start.3 = (f32[256,256]{1,0:T(8,128)S(1)}, f32[256,256]{1,0:T(8,128)}, u32[]{:S(2)}) copy-start(f32[256,256]{1,0:T(8,128)} %thr_ref.1) | copy-start | bytes 786436
  19.9 59.2 %all-to-all-start = ((f32[128,64,128]{2,1,0:T(8,128)}), f32[128,64,128]{2,1,0:T(8,128)}, u32[]{:S(2)}, u32[]{:S(2)}) async-start(f32[128,64,128]{2,1,0:T(8,128)} %dust_strips.1), calls=%async_computation | async-start | bytes 8388608 | tf_op jit(solution)/shard_map/all_to_all | solution.py:747
  81.7 6.6 %collective-permute-start.4 = (f32[144,128]{1,0:T(8,128)S(1)}, f32[144,128]{1,0:T(8,128)S(1)}, u32[]{:S(2)}, u32[]{:S(2)}) collective-permute-start(f32[144,128]{1,0:T(8,128)S(1)} %get-tuple-element.43.n_ref), channel_id=1, source_target_pairs={{0,1},{1,2},{2,3},{3,4},{4,5},{5,6},{6,7},{7,8},{8,9},{9,10},{10,1... | collective-permute-start | bytes 221192 | tf_op jit(solution)/shard_map/ppermute | solution.py:743
  82.0 6.3 %collective-permute-start.5 = (f32[144,128]{1,0:T(8,128)S(1)}, f32[144,128]{1,0:T(8,128)S(1)}, u32[]{:S(2)}, u32[]{:S(2)}) collective-permute-start(f32[144,128]{1,0:T(8,128)S(1)} %get-tuple-element.44.s_ref), channel_id=1, source_target_pairs={{0,15},{1,0},{2,1},{3,2},{4,3},{5,4},{6,5},{7,6},{8,7},{9,8},{10,9... | collective-permute-start | bytes 221192 | tf_op jit(solution)/shard_map/ppermute | solution.py:743
  88.9 3.2 %collective-permute-start.6 = (f32[176,128]{1,0:T(8,128)S(1)}, f32[176,128]{1,0:T(8,128)S(1)}, u32[]{:S(2)}, u32[]{:S(2)}) collective-permute-start(f32[176,128]{1,0:T(8,128)S(1)} %get-tuple-element.45), channel_id=1, source_target_pairs={{0,16},{16,32},{32,48},{48,64},{64,80},{80,96},{96,112},{112,0},{1... | collective-permute-start | bytes 270344 | tf_op jit(solution)/shard_map/ppermute | solution.py:743
  90.5 4.2 %collective-permute-start.7 = (f32[176,128]{1,0:T(8,128)S(1)}, f32[176,128]{1,0:T(8,128)S(1)}, u32[]{:S(2)}, u32[]{:S(2)}) collective-permute-start(f32[176,128]{1,0:T(8,128)S(1)} %get-tuple-element.46), channel_id=1, source_target_pairs={{0,112},{16,0},{32,16},{48,32},{64,48},{80,64},{96,80},{112,96},{1... | collective-permute-start | bytes 270344 | tf_op jit(solution)/shard_map/ppermute | solution.py:743
  94.8 56.5 %all-to-all-start.1 = ((f32[128,56,128]{2,1,0:T(8,128)}), f32[128,56,128]{2,1,0:T(8,128)}, u32[]{:S(2)}, u32[]{:S(2)}) async-start(f32[128,56,128]{2,1,0:T(8,128)} %get-tuple-element.47), calls=%async_computation.1 | async-start | bytes 7340032 | tf_op jit(solution)/shard_map/all_to_all | solution.py:747
  104.8 2.9 %copy-start.6 = (f32[16]{0:T(128)S(1)}, f32[16]{0:T(128)}, u32[]{:S(2)}) copy-start(f32[16]{0:T(128)} %param.13) | copy-start | bytes 196
  104.8 3.0 %copy-start.7 = (f32[16]{0:T(128)S(1)}, f32[16]{0:T(128)}, u32[]{:S(2)}) copy-start(f32[16]{0:T(128)} %param.14) | copy-start | bytes 196
  130.4 26.0 %copy-start.2 = (bf16[256,512]{1,0:T(8,128)(2,1)S(1)}, bf16[256,512]{1,0:T(8,128)(2,1)}, u32[]{:S(2)}) copy-start(bf16[256,512]{1,0:T(8,128)(2,1)} %constant.89.clone.shift_ref) | copy-start | bytes 786436
  151.3 57.4 %all-to-all-start.2 = ((f32[128,64,128]{2,1,0:T(8,128)}), f32[128,64,128]{2,1,0:T(8,128)}, u32[]{:S(2)}, u32[]{:S(2)}) async-start(f32[128,64,128]{2,1,0:T(8,128)} %send_seen.1), calls=%async_computation.2 | async-start | bytes 8388608 | tf_op jit(solution)/shard_map/all_to_all | solution.py:747
  156.4 52.2 %copy-start = (bf16[512,1024]{1,0:T(8,128)(2,1)S(1)}, bf16[512,1024]{1,0:T(8,128)(2,1)}, u32[]{:S(2)}) copy-start(bf16[512,1024]{1,0:T(8,128)(2,1)} %constant.90.clone.matrix_ref) | copy-start | bytes 3145732

commit v7 on v6

--- a/solution.py
+++ b/solution.py
@@ -154,8 +154,8 @@
 
 
 def dust_strips(home_of_slot, dust, bins, owners):
-    slots, cells = dust.shape[:2]
-    block = 8 if slots % 8 == 0 else 4
+    slots = dust.shape[0]
+    block = 14 if slots % 14 == 0 else 4
     rows = 2 * bins * TZ
     matrix = jnp.asarray(ring_matrix())
     hbm = pl.BlockSpec(memory_space=pltpu.HBM)
@@ -452,19 +452,6 @@
             at = g * (both_rows + ROWS)
             out[at : at + both_rows, :] = strips
             out[at + both_rows : at + both_rows + ROWS, :] = winds
-
-
-def add_corners_kernel(owner_ref, e_ref, w_ref, fs_ref, fn_ref, e_out, w_out, *, tiles_x, tiles_y):
-    size = e_ref.shape[0]
-    rows = e_out.shape[0] - size
-    last = fs_ref.shape[0] - (2 * rows + ROWS)
-    lane = lax.broadcasted_iota(jnp.int32, (rows, LANES), 1)
-    e_out[:size, :] = e_ref[...]
-    w_out[:size, :] = w_ref[...]
-    e_out[size:, :] = jnp.where(
-        lane == 0, pltpu.roll(fs_ref[last : last + rows, :], 1, 1), fn_ref[last : last + rows, :]
-    )
-    w_out[size:, :] = jnp.where(lane == 0, fs_ref[:rows, :], pltpu.roll(fn_ref[:rows, :], LANES - 1, 1))
 
 
 def gather_rings_kernel(owner_ref, recv_ref, rings_ref, *, tiles_x, tiles_y):
@@ -610,7 +597,7 @@
     return chunks
 
 
-def advance_strip(side, message, ours, low_end, high_end, settle_ref, share_ref, out, rows):
+def advance_strip(side, message, ours, settle_ref, share_ref, out, rows):
     _, lane = iotas()
     bins = rows // TZ
     each = 2 * rows + ROWS
@@ -632,8 +619,8 @@
             q = cells(g, at)
             deep = cells(g, rows + at)
             near = ours[g * each + at : g * each + at + ROWS, :]
-            low = low_end(at) if g == 0 else pltpu.roll(cells(g - 1, at), 1, 1)
-            high = high_end(at) if g == groups - 1 else pltpu.roll(cells(g + 1, at), LANES - 1, 1)
+            low = 0.0 if g == 0 else pltpu.roll(cells(g - 1, at), 1, 1)
+            high = 0.0 if g == groups - 1 else pltpu.roll(cells(g + 1, at), LANES - 1, 1)
             before = jnp.where(lane == 0, low, pltpu.roll(q, 1, 1))
             after = jnp.where(lane == LANES - 1, high, pltpu.roll(q, LANES - 1, 1))
             across = (deep, near) if side in (WEST, SOUTH) else (near, deep)
@@ -659,7 +646,7 @@
 
 def send_seen_kernel(
     owner_ref, rings_ref, wind_ref, settle_ref, share_ref, e_ref, w_ref, n_ref, s_ref, fw_ref, fe_ref, fs_ref, fn_ref,
-    send_ref, ext, both, lw_ref, le_ref, ls_ref, ln_ref, sems, *, tiles_x, tiles_y
+    send_ref, corner_ref, ext, both, lw_ref, le_ref, ls_ref, ln_ref, sems, *, tiles_x, tiles_y
 ):
     rows = rings_ref.shape[1] // 2
     wide = tiles_y + 2
@@ -690,29 +677,19 @@
 
     lax.fori_loop(0, tiles_x * tiles_y // 2, advance, 0)
 
-    def corner(ref, shift):
-        first = ref.shape[0] - rows
-
-        def of(at):
-            cells = ref[first + at : first + at + ROWS, :]
-            return pltpu.roll(cells, shift, 1) if shift else cells
-
-        return of
-
-    ends = (
-        (corner(fw_ref, 0), corner(fw_ref, 0)),
-        (corner(fe_ref, 0), corner(fe_ref, 0)),
-        (corner(fw_ref, 0), corner(fe_ref, LANES - 1)),
-        (corner(fw_ref, 1), corner(fe_ref, 0)),
-    )
-    for side, message, ours, (low, high), out in zip(
-        (WEST, EAST, SOUTH, NORTH), messages, (w_ref, e_ref, s_ref, n_ref), ends, later
+    for side, message, ours, out in zip(
+        (WEST, EAST, SOUTH, NORTH), messages, (w_ref, e_ref, s_ref, n_ref), later
     ):
-        advance_strip(side, message, ours, low, high, settle_ref, share_ref, out, rows)
+        advance_strip(side, message, ours, settle_ref, share_ref, out, rows)
     fill_halo(ext, [lambda g, m=m: m[g] for m in later], tiles_x, tiles_y)
 
     def copy(t):
         return pltpu.make_async_copy(both.at[t], send_ref.at[owner_ref[t]], sems.at[t])
+
+    def sent_now(t):
+        x, y = t // tiles_y, t % tiles_y
+        at_corner = ((x == 0) | (x == tiles_x - 1)) & ((y == 0) | (y == tiles_y - 1))
+        return (owner_ref[t] >= 0) & jnp.logical_not(at_corner)
 
     def after(t, carry):
         effect = ring_effect(t, wind_ref, settle_ref, both[t, :rows, :], seen_by(ext, place(t), wide))
@@ -720,22 +697,103 @@
             for n, chunk in enumerate(chunks):
                 both[t, depth * rows + n * ROWS : depth * rows + (n + 1) * ROWS, :] = chunk
 
+        @pl.when(sent_now(t))
+        def _():
+            copy(t).start()
+
+        return carry
+
+    lax.fori_loop(0, tiles_x * tiles_y, after, 0)
+    for n, (_, _, t) in enumerate(corner_tiles(tiles_x, tiles_y)):
+        corner_ref[n] = both[t]
+
+    def wait(t, carry):
+        @pl.when(sent_now(t))
+        def _():
+            copy(t).wait()
+
+        return carry
+
+    lax.fori_loop(0, tiles_x * tiles_y, wait, 0)
+
+
+def corner_tiles(tiles_x, tiles_y):
+    return [
+        (side_x, side_y, x * tiles_y + y)
+        for side_x, x in ((WEST, 0), (EAST, tiles_x - 1))
+        for side_y, y in ((SOUTH, 0), (NORTH, tiles_y - 1))
+    ]
+
+
+def send_corners_kernel(
+    owner_ref, _, effect_ref, wind_ref, fw_ref, fe_ref, fs_ref, fn_ref, cw_ref, ce_ref, send_ref, sums, sems,
+    *, tiles_x, tiles_y
+):
+    rows = cw_ref.shape[0] // 2
+    each = 2 * rows + ROWS
+    bins = rows // TZ
+    mix = dust_step * diffusion
+    _, lane = iotas()
+    group, within = lane // TILE, lane % TILE
+    on_x = (group == WEST) | (group == EAST)
+    low_side = (group == WEST) | (group == SOUTH)
+    first, last = within == 0, within == TILE - 1
+    corner = corner_index(0)
+    tiles = corner_tiles(tiles_x, tiles_y)
+
+    def copy(n, t):
+        return pltpu.make_async_copy(sums.at[n], send_ref.at[owner_ref[t]], sems.at[n])
+
+    for n, (side_x, side_y, t) in enumerate(tiles):
+        strip_x = fw_ref if side_x == WEST else fe_ref
+        strip_y = fs_ref if side_y == SOUTH else fn_ref
+        cells_ref, cell_lane = (cw_ref, LANES - 1) if side_x == WEST else (ce_ref, 0)
+        cells_at = 0 if side_y == SOUTH else rows
+        low_x, low_y = side_x == WEST, side_y == SOUTH
+        end_x = 0 if low_y else strip_x.shape[0] - each
+        end_y = 0 if low_x else strip_y.shape[0] - each
+        to_x = side_x * TILE + (0 if low_y else TILE - 1)
+        to_y = side_y * TILE + (0 if low_x else TILE - 1)
+
+        def from_end(strip, at, c, level, low):
+            def row(p):
+                value = strip[at + 2 * rows + p : at + 2 * rows + p + 1, :]
+                return lane_gather(spread_rows(value), jnp.full((ROWS, LANES), 0 if low else LANES - 1, jnp.int32))
+
+            along = dust_step * row(c * TZ + level)
+            return jnp.where(row(FLAG) > 0.0, mix + jnp.maximum(along if low else -along, 0.0), 0.0)
+
+        for at in range(0, rows, ROWS):
+            level = at // bins
+            if at % bins == 0:
+                u, v = (
+                    dust_step * spread_rows(wind_ref[t, c * TZ + level : c * TZ + level + 1, :]) for c in range(2)
+                )
+                across, along = jnp.where(on_x, u, v), jnp.where(on_x, v, u)
+                from_out = mix + jnp.maximum(jnp.where(low_side, across, -across), 0.0)
+                from_corner = jnp.where(
+                    first, mix + jnp.maximum(along, 0.0), jnp.where(last, mix + jnp.maximum(-along, 0.0), 0.0)
+                )
+                by_x = from_end(strip_x, end_x, 1, level, low_y)
+                by_y = from_end(strip_y, end_y, 0, level, low_x)
+            cells = lane_gather(
+                cells_ref[cells_at + at : cells_at + at + ROWS, :], jnp.full((ROWS, LANES), cell_lane, jnp.int32)
+            )
+            more = jnp.where(lane == to_x, by_x * cells, jnp.where(lane == to_y, by_y * cells, 0.0))
+            sums[n, at : at + ROWS, :] = (
+                effect_ref[n, at : at + ROWS, :] + from_out * more + from_corner * lane_gather(more, corner)
+            )
+        sums[n, rows:, :] = effect_ref[n, rows:, :]
+
         @pl.when(owner_ref[t] >= 0)
         def _():
-            copy(t).start()
-
-        return carry
-
-    lax.fori_loop(0, tiles_x * tiles_y, after, 0)
-
-    def wait(t, carry):
+            copy(n, t).start()
+
+    for n, (_, _, t) in enumerate(tiles):
+
         @pl.when(owner_ref[t] >= 0)
         def _():
-            copy(t).wait()
-
-        return carry
-
-    lax.fori_loop(0, tiles_x * tiles_y, wait, 0)
+            copy(n, t).wait()
 
 
 def shifted(value, axis, steps):
@@ -752,7 +810,7 @@
     return shifted(east, "gx", 1), shifted(west, "gx", -1), shifted(north, "gy", 1), shifted(south, "gy", -1)
 
 
-def ring_call(kernel, tiles_x, tiles_y, rows, outs, scratch, name, hbm_in=0, hbm_out=False):
+def ring_call(kernel, tiles_x, tiles_y, rows, outs, scratch, name, hbm_in=0, hbm_out=0, aliases={}):
     smem = pl.BlockSpec(memory_space=pltpu.SMEM)
     vmem = pl.BlockSpec(memory_space=pltpu.VMEM)
     hbm = pl.BlockSpec(memory_space=pltpu.HBM)
@@ -762,9 +820,10 @@
         return pl.pallas_call(
             functools.partial(kernel, tiles_x=tiles_x, tiles_y=tiles_y),
             in_specs=[smem] + [hbm] * hbm_in + [vmem] * (len(inputs) - hbm_in),
-            out_specs=hbm if hbm_out else [vmem] * len(outs),
-            out_shape=outs[0] if hbm_out else outs,
+            out_specs=[hbm] * hbm_out + [vmem] * (len(outs) - hbm_out),
+            out_shape=outs,
             scratch_shapes=scratch,
+            input_output_aliases=aliases,
             compiler_params=pltpu.CompilerParams(vmem_limit_bytes=32 << 20),
             cost_estimate=pl.CostEstimate(flops=16 * size, bytes_accessed=16 * size, transcendentals=0),
             name=name,
@@ -797,29 +856,38 @@
         wind_ring,
         hbm_in=1,
     )
-    from_south, from_north = shifted(north, "gy", 1), shifted(south, "gy", -1)
+    from_west, from_east, from_south, from_north = exchange_borders((east, west, north, south))
+    wind_send, from_west, from_east, from_south, from_north = lax.optimization_barrier(
+        (wind_send, from_west, from_east, from_south, from_north)
+    )
+    wind_recv = relay_rows(wind_send)
+    top = (along_y - 1) * each
+    across_low = jnp.concatenate([from_south[:rows], from_north[:rows]])
+    across_high = jnp.concatenate([from_south[top : top + rows], from_north[top : top + rows]])
+    corner_west, corner_east = shifted(across_high, "gx", 1), shifted(across_low, "gx", -1)
     (rings,) = call(gather_rings_kernel, [f32(per_home, both_rows, LANES)], [], "gather_rings", received)
-    east_full, west_full = call(
-        add_corners_kernel,
-        [f32(along_x * each + rows, LANES)] * 2,
-        [],
-        "add_corners",
-        east, west, from_south, from_north,
-    )
-    from_west, from_east = shifted(east_full, "gx", 1), shifted(west_full, "gx", -1)
-    wind_send, from_west, from_east = lax.optimization_barrier((wind_send, from_west, from_east))
-    wind_recv = relay_rows(wind_send)
-    seen_send = call(
+    send_buffer = pltpu.HBM((owners, both_rows, LANES), jnp.float32)
+    messages = (from_west, from_east, from_south, from_north)
+    seen_send, corners = call(
         send_seen_kernel,
-        [pltpu.HBM((owners, both_rows, LANES), jnp.float32)],
+        [send_buffer, f32(4, both_rows, LANES)],
         [ext, all_rings]
         + [pltpu.VMEM((along_x, rows, LANES), jnp.float32)] * 2
         + [pltpu.VMEM((along_y, rows, LANES), jnp.float32)] * 2
         + [each_sem],
         "send_seen",
-        rings, wind_ring, settle_rows, share_rows, east, west, north, south,
-        from_west, from_east, from_south, from_north,
-        hbm_out=True,
+        rings, wind_ring, settle_rows, share_rows, east, west, north, south, *messages,
+        hbm_out=1,
+    )
+    (seen_send,) = call(
+        send_corners_kernel,
+        [send_buffer],
+        [pltpu.VMEM((4, both_rows, LANES), jnp.float32), pltpu.SemaphoreType.DMA((4,))],
+        "send_corners",
+        seen_send, corners, wind_ring, *messages, corner_west, corner_east,
+        hbm_in=1,
+        hbm_out=1,
+        aliases={1: 0},
     )
     return wind_recv, relay_rows(seen_send)
 

time: 220 us -> 214 us (0.973)
  waiting for transfers between devices: 68.8 us -> 61.1 us
    all_to_all x3, waiting for transfers between devices: 62.8 us -> 49.3 us  [relay_rows(): return lax.all_to_all(rows, AXES, split_axis=0, concat_axis=0, tiled=True)]
    ppermute x8 -> x10, waiting for transfers between devices: 5.93 us -> 11.8 us  [shifted(): lax.ppermute(value, axis, [(source, (source + steps) % count) for source...]
    ppermute x8 -> x10, starting transfers between devices: 15.2 us -> 15.8 us  [shifted(): lax.ppermute(value, axis, [(source, (source + steps) % count) for source...]
  transfers between devices with their start and end apart: 11 -> 13, of which waited for: 6 -> 6; matrix products, arithmetic and copies ran while one was open for 0% -> 0% of each run, Pallas kernels for 43% -> 45%
where the time goes in v7:
time: 214 us; the launch traced here: 213 us
  Pallas kernels  112 us (52%)
  waiting for transfers between devices  61.1 us (29%)
  starting transfers between devices  38.7 us (18%)
    all_to_all x3, waiting for transfers between devices, relay_rows(): return lax.all_to_all(rows, AXES, split_axis=0, concat_axis=0, tiled=True)  49.3 us
    pallas_call x1, Pallas kernels, wind_step(): pl.pallas_call(functools.partial(wind_kernel, levels=levels), in_specs=[s...  40 us
    pallas_call x4, Pallas kernels, call(): pl.pallas_call(functools.partial(kernel, tiles_x=tiles_x, tiles_y=tiles_y...  29.7 us
    all_to_all x3, starting transfers between devices, relay_rows(): return lax.all_to_all(rows, AXES, split_axis=0, concat_axis=0, tiled=True)  23 us
    pallas_call x1, Pallas kernels, dust_inner(): pl.pallas_call(functools.partial(dust_kernel, block=block, bins=bins), gr...  21.9 us
    ppermute x10, starting transfers between devices, shifted(): lax.ppermute(value, axis, [(source, (source + steps) % count) for source...  15.8 us
    ppermute x10, waiting for transfers between devices, shifted(): lax.ppermute(value, axis, [(source, (source + steps) % count) for source...  11.8 us
    pallas_call x1, Pallas kernels, dust_outer(): pl.pallas_call(functools.partial(dust_outer_kernel, block=block, bins=bin...  10.3 us
  transfers between devices with their start and end apart: 13, of which 6 were waited for; matrix products, arithmetic and copies ran while one was open for 0% of the time, Pallas kernels for 45%

profile of v7, /device:TPU:1, one launch (start us, length us, event | category | flops | bytes accessed | tf_op | source)
XLA Modules:
  0.0 213.4 jit_solution(10196766155435326236)
XLA Ops:
  0.7 3.9 %wind_faces.1 = (f32[18,256]{1,0:T(8,128)S(1)}, f32[18,256]{1,0:T(8,128)S(1)}, f32[256,128]{1,0:T(8,128)S(1)}, f32[256,128]{1,0:T(8,128)S(1)}) custom-call(f32[18,256,256]{2,1,0:T(8,128)} %bitcast.14), custom_call_target="tpu_custom_call" | custom-call | flops 1179648 | bytes 4718592 | tf_op jit(solution)/shard_map/wind_faces/pallas_call | solution.py:221
  4.5 2.7 %collective-permute-start = (f32[18,256]{1,0:T(8,128)S(1)}, f32[18,256]{1,0:T(8,128)S(1)}, u32[]{:S(2)}, u32[]{:S(2)}) collective-permute-start(f32[18,256]{1,0:T(8,128)S(1)} %get-tuple-element.28), channel_id=1, source_target_pairs={{0,16},{16,32},{32,48},{48,64},{64,80},{80,96},{96,112},{112,0},{1... | collective-permute-start | bytes 55304 | tf_op jit(solution)/shard_map/ppermute | solution.py:801
  7.2 1.6 collective-permute-start.2
  8.9 4.3 %collective-permute-start.3 = (f32[256,128]{1,0:T(8,128)S(1)}, f32[256,128]{1,0:T(8,128)S(1)}, u32[]{:S(2)}, u32[]{:S(2)}) collective-permute-start(f32[256,128]{1,0:T(8,128)S(1)} %get-tuple-element.31), channel_id=1, source_target_pairs={{0,15},{1,0},{2,1},{3,2},{4,3},{5,4},{6,5},{7,6},{8,7},{9,8},{10,9... | collective-permute-start | bytes 393224 | tf_op jit(solution)/shard_map/ppermute | solution.py:801
  13.6 6.0 %dust_strips.1 = f32[128,64,128]{2,1,0:T(8,128)} custom-call(s32[56]{0:T(128)S(1)} %select_reduce_fusion.1.home_ref, f32[56,256,128]{2,1,0:T(8,128)} %bitcast.12, bf16[2048,256]{1,0:T(8,128)(2,1)S(1)} %copy-done.1), custom_call_target="tpu_custom_call" | custom-call | flops 36700160 | bytes 9175040 | tf_op jit(solution)/shard_map/dust_strips/pallas_call | solution.py:162
  19.6 7.1 %all-to-all-start = ((f32[128,64,128]{2,1,0:T(8,128)}), f32[128,64,128]{2,1,0:T(8,128)}, u32[]{:S(2)}, u32[]{:S(2)}) async-start(f32[128,64,128]{2,1,0:T(8,128)} %dust_strips.1), calls=%async_computation | async-start | bytes 8388608 | tf_op jit(solution)/shard_map/all_to_all | solution.py:805
  27.1 40.0 %wind_step.1 = (f32[18,256,256]{2,1,0:T(8,128)}, f32[128,56,128]{2,1,0:T(8,128)}, f32[64,16,128]{2,1,0:T(8,128)S(1)}) custom-call(s32[64]{0:T(128)S(1)} %select_reduce_fusion.owner_ref, f32[18,256,256]{2,1,0:T(8,128)} %bitcast.15, f32[18,256]{1,0:T(8,128)S(1)} %collective-permute-done.xlo_ref, f32[18,256]{1,0:T(8,128)S(1)} %collective-permute-done.1.xhi_ref, ...), custom_call_target="tpu_custom_call" | custom-call | flops 47185920 | bytes 11796480 | tf_op jit(solution)/shard_map/wind_step/pallas_call | solution.py:343
  67.1 11.7 %all-to-all-done.recv_ref = f32[128,64,128]{2,1,0:T(8,128)} async-done(((f32[128,64,128]{2,1,0:T(8,128)}), f32[128,64,128]{2,1,0:T(8,128)}, u32[]{:S(2)}, u32[]{:S(2)}) %all-to-all-start) | async-done | bytes 4194336 | tf_op jit(solution)/shard_map/all_to_all | solution.py:805
  78.8 2.6 %pack_borders.1 = (f32[144,128]{1,0:T(8,128)S(1)}, f32[144,128]{1,0:T(8,128)S(1)}, f32[144,128]{1,0:T(8,128)S(1)}, f32[144,128]{1,0:T(8,128)S(1)}) custom-call(s32[64]{0:T(128)S(1)} %select_reduce_fusion.owner_ref, f32[128,64,128]{2,1,0:T(8,128)} %all-to-all-done.recv_ref, f32[64,16,128]{2,1,0:T(8,128)S(1)} %get-tuple-element.42.wind_ref), custom_call_target="tpu_custom_call" | custom-call | flops 4194304 | bytes 4194304 | tf_op jit(solution)/shard_map/pack_borders/pallas_call | solution.py:820
  82.1 0.9 collective-permute-start.6
  82.9 3.9 %collective-permute-start.7 = (f32[144,128]{1,0:T(8,128)S(1)}, f32[144,128]{1,0:T(8,128)S(1)}, u32[]{:S(2)}, u32[]{:S(2)}) collective-permute-start(f32[144,128]{1,0:T(8,128)S(1)} %get-tuple-element.46.s_ref), channel_id=1, source_target_pairs={{0,15},{1,0},{2,1},{3,2},{4,3},{5,4},{6,5},{7,6},{8,7},{9,8},{10,9... | collective-permute-start | bytes 221192 | tf_op jit(solution)/shard_map/ppermute | solution.py:801
  86.9 1.7 collective-permute-done.6.fs_ref
  88.6 10.6 %all-to-all-start.1 = ((f32[128,56,128]{2,1,0:T(8,128)}), f32[128,56,128]{2,1,0:T(8,128)}, u32[]{:S(2)}, u32[]{:S(2)}) async-start(f32[128,56,128]{2,1,0:T(8,128)} %get-tuple-element.47), calls=%async_computation.1 | async-start | bytes 7340032 | tf_op jit(solution)/shard_map/all_to_all | solution.py:805
  99.3 1.6 collective-permute-start.8
  100.9 2.9 %gather_rings.1.rings_ref = f32[64,64,128]{2,1,0:T(8,128)S(1)} custom-call(s32[64]{0:T(128)S(1)} %select_reduce_fusion.owner_ref, f32[128,64,128]{2,1,0:T(8,128)} %all-to-all-done.recv_ref), custom_call_target="tpu_custom_call" | custom-call | flops 4194304 | bytes 4194304 | tf_op jit(solution)/shard_map/gather_rings/pallas_call | solution.py:820
  103.9 22.9 %send_seen.1 = (f32[128,64,128]{2,1,0:T(8,128)}, f32[4,64,128]{2,1,0:T(8,128)S(1)}) custom-call(s32[64]{0:T(128)S(1)} %select_reduce_fusion.owner_ref, f32[64,64,128]{2,1,0:T(8,128)S(1)} %gather_rings.1.rings_ref, f32[64,16,128]{2,1,0:T(8,128)S(1)} %get-tuple-element.42.wind_ref, f32[16,128]{1,0:T(8,128)S(1)} %broadcast_in_dim.35.settle_ref, ...), custom_call_target="tpu_custom_call" | custom-call | flops 4194304 | bytes 4194304 | tf_op jit(solution)/shard_map/send_seen/pallas_call | solution.py:820
  126.8 2.2 %collective-permute-done.8.cw_ref = f32[64,128]{1,0:T(8,128)S(1)} collective-permute-done((f32[64,128]{1,0:T(8,128)S(1)}, f32[64,128]{1,0:T(8,128)S(1)}, u32[]{:S(2)}, u32[]{:S(2)}) %collective-permute-start.8) | collective-permute-done | bytes 32800 | tf_op jit(solution)/shard_map/ppermute | solution.py:801
  129.0 7.9 %collective-permute-done.9.ce_ref = f32[64,128]{1,0:T(8,128)S(1)} collective-permute-done((f32[64,128]{1,0:T(8,128)S(1)}, f32[64,128]{1,0:T(8,128)S(1)}, u32[]{:S(2)}, u32[]{:S(2)}) %collective-permute-start.9) | collective-permute-done | bytes 32800 | tf_op jit(solution)/shard_map/ppermute | solution.py:801
  136.9 1.4 send_corners.1
  138.3 7.4 %all-to-all-done.1.wind_ref = f32[128,56,128]{2,1,0:T(8,128)} async-done(((f32[128,56,128]{2,1,0:T(8,128)}), f32[128,56,128]{2,1,0:T(8,128)}, u32[]{:S(2)}, u32[]{:S(2)}) %all-to-all-start.1) | async-done | bytes 3670048 | tf_op jit(solution)/shard_map/all_to_all | solution.py:805
  145.7 5.3 %all-to-all-start.2 = ((f32[128,64,128]{2,1,0:T(8,128)}), f32[128,64,128]{2,1,0:T(8,128)}, u32[]{:S(2)}, u32[]{:S(2)}) async-start(f32[128,64,128]{2,1,0:T(8,128)} %send_corners.1), calls=%async_computation.2 | async-start | bytes 8388608 | tf_op jit(solution)/shard_map/all_to_all | solution.py:805
  151.0 21.9 %dust_inner.1.inner_hbm = f32[56,256,128]{2,1,0:T(8,128)} custom-call(s32[56]{0:T(128)S(1)} %select_reduce_fusion.1.home_ref, f32[16,128]{1,0:T(8,128)S(1)} %broadcast_in_dim.34.share_ref, f32[16,128]{1,0:T(8,128)S(1)} %broadcast_in_dim.35.settle_ref, f32[56,256,128]{2,1,0:T(8,128)} %bitcast.13, bf16[256,512]{1,0:T(8,128)(2,1)S(1)} %copy-done.2, ...), custom_call_target="tpu_custom_call" | custom-call | flops 220200960 | bytes 22020096 | tf_op jit(solution)/shard_map/dust_inner/pallas_call | solution.py:992
  172.9 30.2 %all-to-all-done.2.effect_hbm = f32[128,64,128]{2,1,0:T(8,128)} async-done(((f32[128,64,128]{2,1,0:T(8,128)}), f32[128,64,128]{2,1,0:T(8,128)}, u32[]{:S(2)}, u32[]{:S(2)}) %all-to-all-start.2) | async-done | bytes 4194336 | tf_op jit(solution)/shard_map/all_to_all | solution.py:805
  203.1 10.3 %dust_outer.1 = f32[56,256,128]{2,1,0:T(8,128)} custom-call(s32[56]{0:T(128)S(1)} %select_reduce_fusion.1.home_ref, f32[56,256,128]{2,1,0:T(8,128)} %dust_inner.1.inner_hbm, bf16[512,1024]{1,0:T(8,128)(2,1)S(1)} %copy-done, f32[128,64,128]{2,1,0:T(8,128)} %all-to-all-done.2.effect_hbm), custom_call_target="tpu_custom_call" | custom-call | flops 3670016 | bytes 14680064 | tf_op jit(solution)/shard_map/dust_outer/pallas_call | solution.py:1064
  (36 shorter events, 1.6 us)
Async XLA Ops:
  0.6 12.9 %copy-start.1 = (bf16[2048,256]{1,0:T(8,128)(2,1)S(1)}, bf16[2048,256]{1,0:T(8,128)(2,1)}, u32[]{:S(2)}) copy-start(bf16[2048,256]{1,0:T(8,128)(2,1)} %constant.88.clone.matrix_ref) | copy-start | bytes 3145732
  0.6 12.6 %copy-start.5 = (s32[7168]{0:T(1024)S(1)}, s32[7168]{0:T(1024)}, u32[]{:S(2)}) copy-start(s32[7168]{0:T(1024)} %param.16) | copy-start | bytes 86020
  0.7 12.5 %copy-start.4 = (s32[7168]{0:T(1024)S(1)}, s32[7168]{0:T(1024)}, u32[]{:S(2)}) copy-start(s32[7168]{0:T(1024)} %param.15) | copy-start | bytes 86020
  4.5 15.0 %collective-permute-start = (f32[18,256]{1,0:T(8,128)S(1)}, f32[18,256]{1,0:T(8,128)S(1)}, u32[]{:S(2)}, u32[]{:S(2)}) collective-permute-start(f32[18,256]{1,0:T(8,128)S(1)} %get-tuple-element.28), channel_id=1, source_target_pairs={{0,16},{16,32},{32,48},{48,64},{64,80},{80,96},{96,112},{112,0},{1... | collective-permute-start | bytes 55304 | tf_op jit(solution)/shard_map/ppermute | solution.py:801
  7.2 12.3 %collective-permute-start.1 = (f32[18,256]{1,0:T(8,128)S(1)}, f32[18,256]{1,0:T(8,128)S(1)}, u32[]{:S(2)}, u32[]{:S(2)}) collective-permute-start(f32[18,256]{1,0:T(8,128)S(1)} %get-tuple-element.29), channel_id=1, source_target_pairs={{0,112},{16,0},{32,16},{48,32},{64,48},{80,64},{96,80},{112,96},{1... | collective-permute-start | bytes 55304 | tf_op jit(solution)/shard_map/ppermute | solution.py:801
  7.2 12.4 %collective-permute-start.2 = (f32[256,128]{1,0:T(8,128)S(1)}, f32[256,128]{1,0:T(8,128)S(1)}, u32[]{:S(2)}, u32[]{:S(2)}) collective-permute-start(f32[256,128]{1,0:T(8,128)S(1)} %get-tuple-element.30), channel_id=1, source_target_pairs={{0,1},{1,2},{2,3},{3,4},{4,5},{5,6},{6,7},{7,8},{8,9},{9,10},{10,1... | collective-permute-start | bytes 393224 | tf_op jit(solution)/shard_map/ppermute | solution.py:801
  8.9 10.7 %collective-permute-start.3 = (f32[256,128]{1,0:T(8,128)S(1)}, f32[256,128]{1,0:T(8,128)S(1)}, u32[]{:S(2)}, u32[]{:S(2)}) collective-permute-start(f32[256,128]{1,0:T(8,128)S(1)} %get-tuple-element.31), channel_id=1, source_target_pairs={{0,15},{1,0},{2,1},{3,2},{4,3},{5,4},{6,5},{7,6},{8,7},{9,8},{10,9... | collective-permute-start | bytes 393224 | tf_op jit(solution)/shard_map/ppermute | solution.py:801
  19.6 7.5 %copy-start.3 = (f32[256,256]{1,0:T(8,128)S(1)}, f32[256,256]{1,0:T(8,128)}, u32[]{:S(2)}) copy-start(f32[256,256]{1,0:T(8,128)} %thr_ref.1) | copy-start | bytes 786436
  19.6 59.2 %all-to-all-start = ((f32[128,64,128]{2,1,0:T(8,128)}), f32[128,64,128]{2,1,0:T(8,128)}, u32[]{:S(2)}, u32[]{:S(2)}) async-start(f32[128,64,128]{2,1,0:T(8,128)} %dust_strips.1), calls=%async_computation | async-start | bytes 8388608 | tf_op jit(solution)/shard_map/all_to_all | solution.py:805
  81.4 5.5 %collective-permute-start.4 = (f32[144,128]{1,0:T(8,128)S(1)}, f32[144,128]{1,0:T(8,128)S(1)}, u32[]{:S(2)}, u32[]{:S(2)}) collective-permute-start(f32[144,128]{1,0:T(8,128)S(1)} %get-tuple-element.43.e_ref), channel_id=1, source_target_pairs={{0,16},{16,32},{32,48},{48,64},{64,80},{80,96},{96,112},{112,0},{1... | collective-permute-start | bytes 221192 | tf_op jit(solution)/shard_map/ppermute | solution.py:801
  82.1 4.8 %collective-permute-start.5 = (f32[144,128]{1,0:T(8,128)S(1)}, f32[144,128]{1,0:T(8,128)S(1)}, u32[]{:S(2)}, u32[]{:S(2)}) collective-permute-start(f32[144,128]{1,0:T(8,128)S(1)} %get-tuple-element.44.w_ref), channel_id=1, source_target_pairs={{0,112},{16,0},{32,16},{48,32},{64,48},{80,64},{96,80},{112,96},{1... | collective-permute-start | bytes 221192 | tf_op jit(solution)/shard_map/ppermute | solution.py:801
  82.1 6.5 %collective-permute-start.6 = (f32[144,128]{1,0:T(8,128)S(1)}, f32[144,128]{1,0:T(8,128)S(1)}, u32[]{:S(2)}, u32[]{:S(2)}) collective-permute-start(f32[144,128]{1,0:T(8,128)S(1)} %get-tuple-element.45.n_ref), channel_id=1, source_target_pairs={{0,1},{1,2},{2,3},{3,4},{4,5},{5,6},{6,7},{7,8},{8,9},{9,10},{10,1... | collective-permute-start | bytes 221192 | tf_op jit(solution)/shard_map/ppermute | solution.py:801
  82.9 5.7 %collective-permute-start.7 = (f32[144,128]{1,0:T(8,128)S(1)}, f32[144,128]{1,0:T(8,128)S(1)}, u32[]{:S(2)}, u32[]{:S(2)}) collective-permute-start(f32[144,128]{1,0:T(8,128)S(1)} %get-tuple-element.46.s_ref), channel_id=1, source_target_pairs={{0,15},{1,0},{2,1},{3,2},{4,3},{5,4},{6,5},{7,6},{8,7},{9,8},{10,9... | collective-permute-start | bytes 221192 | tf_op jit(solution)/shard_map/ppermute | solution.py:801
  88.6 57.1 %all-to-all-start.1 = ((f32[128,56,128]{2,1,0:T(8,128)}), f32[128,56,128]{2,1,0:T(8,128)}, u32[]{:S(2)}, u32[]{:S(2)}) async-start(f32[128,56,128]{2,1,0:T(8,128)} %get-tuple-element.47), calls=%async_computation.1 | async-start | bytes 7340032 | tf_op jit(solution)/shard_map/all_to_all | solution.py:805
  99.2 4.6 %copy-start.6 = (f32[16]{0:T(128)S(1)}, f32[16]{0:T(128)}, u32[]{:S(2)}) copy-start(f32[16]{0:T(128)} %param.13) | copy-start | bytes 196
  99.2 4.7 %copy-start.7 = (f32[16]{0:T(128)S(1)}, f32[16]{0:T(128)}, u32[]{:S(2)}) copy-start(f32[16]{0:T(128)} %param.14) | copy-start | bytes 196
  99.3 29.7 %collective-permute-start.8 = (f32[64,128]{1,0:T(8,128)S(1)}, f32[64,128]{1,0:T(8,128)S(1)}, u32[]{:S(2)}, u32[]{:S(2)}) collective-permute-start(f32[64,128]{1,0:T(8,128)S(1)} %pad_maximum_fusion), channel_id=1, source_target_pairs={{0,16},{16,32},{32,48},{48,64},{64,80},{80,96},{96,112},{112,0},{1... | collective-permute-start | bytes 98312 | tf_op jit(solution)/shard_map/ppermute | solution.py:801
  100.9 36.0 %collective-permute-start.9 = (f32[64,128]{1,0:T(8,128)S(1)}, f32[64,128]{1,0:T(8,128)S(1)}, u32[]{:S(2)}, u32[]{:S(2)}) collective-permute-start(f32[64,128]{1,0:T(8,128)S(1)} %pad_maximum_fusion.1), channel_id=1, source_target_pairs={{0,112},{16,0},{32,16},{48,32},{64,48},{80,64},{96,80},{112,96},{1... | collective-permute-start | bytes 98312 | tf_op jit(solution)/shard_map/ppermute | solution.py:801
  138.3 12.7 %copy-start.2 = (bf16[256,512]{1,0:T(8,128)(2,1)S(1)}, bf16[256,512]{1,0:T(8,128)(2,1)}, u32[]{:S(2)}) copy-start(bf16[256,512]{1,0:T(8,128)(2,1)} %constant.89.clone.shift_ref) | copy-start | bytes 786436
  145.7 57.4 %all-to-all-start.2 = ((f32[128,64,128]{2,1,0:T(8,128)}), f32[128,64,128]{2,1,0:T(8,128)}, u32[]{:S(2)}, u32[]{:S(2)}) async-start(f32[128,64,128]{2,1,0:T(8,128)} %send_corners.1), calls=%async_computation.2 | async-start | bytes 8388608 | tf_op jit(solution)/shard_map/all_to_all | solution.py:805
  151.0 52.1 %copy-start = (bf16[512,1024]{1,0:T(8,128)(2,1)S(1)}, bf16[512,1024]{1,0:T(8,128)(2,1)}, u32[]{:S(2)}) copy-start(bf16[512,1024]{1,0:T(8,128)(2,1)} %constant.90.clone.matrix_ref) | copy-start | bytes 3145732

commit v8 on v7

--- a/solution.py
+++ b/solution.py
@@ -178,40 +178,22 @@
     )(home_of_slot, in_hbm(dust), matrix)
 
 
-def faces_kernel(vel_ref, x_last_ref, x_first_ref, y_last_ref, y_first_ref, first, last, low, high, x_sems, y_sems):
+def faces_kernel(vel_ref, x_last_ref, x_first_ref, y_last_ref, y_first_ref, wind, sems):
     fields, nx, ny = vel_ref.shape
-    x_copies = [
-        pltpu.make_async_copy(vel_ref.at[:, pl.ds(0, ROWS), :], first, x_sems.at[0]),
-        pltpu.make_async_copy(vel_ref.at[:, pl.ds(nx - ROWS, ROWS), :], last, x_sems.at[1]),
-    ]
-    y_copies = [
-        (
-            pltpu.make_async_copy(vel_ref.at[f, :, pl.ds(0, LANES)], low.at[f], y_sems.at[0, f]),
-            pltpu.make_async_copy(vel_ref.at[f, :, pl.ds(ny - LANES, LANES)], high.at[f], y_sems.at[1, f]),
-        )
-        for f in range(fields)
-    ]
-    for pair in y_copies:
-        for copy in pair:
-            copy.start()
-    for copy in x_copies:
+    copies = [pltpu.make_async_copy(vel_ref.at[f], wind.at[f], sems.at[f]) for f in range(fields)]
+    for copy in copies:
         copy.start()
     lane = lax.broadcasted_iota(jnp.int32, (nx, LANES), 1)
-    for f, (low_copy, high_copy) in enumerate(y_copies):
-        low_copy.wait()
-        high_copy.wait()
-        from_low = pltpu.roll(low[f], f, 1) if f else low[f]
-        from_high = pltpu.roll(high[f], f + 1, 1)
+    for f, copy in enumerate(copies):
+        copy.wait()
+        x_first_ref[f : f + 1, :] = wind[f, 0:1, :]
+        x_last_ref[f : f + 1, :] = wind[f, nx - 1 : nx, :]
+        both = pltpu.roll(jnp.where(lane < LANES // 2, wind[f, :, :LANES], wind[f, :, ny - LANES :]), f + 1, 1)
         if f == 0:
-            y_first_ref[...], y_last_ref[...] = from_low, from_high
+            y_first_ref[...], y_last_ref[...] = both, both
         else:
-            y_first_ref[...] = jnp.where(lane == f, from_low, y_first_ref[...])
-            y_last_ref[...] = jnp.where(lane == f, from_high, y_last_ref[...])
-    for copy in x_copies:
-        copy.wait()
-    for f in range(fields):
-        x_first_ref[f : f + 1, :] = first[f, 0:1, :]
-        x_last_ref[f : f + 1, :] = last[f, ROWS - 1 : ROWS, :]
+            y_first_ref[...] = jnp.where(lane == f + 1, both, y_first_ref[...])
+            y_last_ref[...] = jnp.where(lane == f, both, y_last_ref[...])
 
 
 def wind_faces(velocity):
@@ -223,14 +205,7 @@
         in_specs=[pl.BlockSpec(memory_space=pltpu.HBM)],
         out_specs=[vmem] * 4,
         out_shape=[f32(fields, ny)] * 2 + [f32(nx, LANES)] * 2,
-        scratch_shapes=[
-            pltpu.VMEM((fields, ROWS, ny), jnp.float32),
-            pltpu.VMEM((fields, ROWS, ny), jnp.float32),
-            pltpu.VMEM((fields, nx, LANES), jnp.float32),
-            pltpu.VMEM((fields, nx, LANES), jnp.float32),
-            pltpu.SemaphoreType.DMA((2,)),
-            pltpu.SemaphoreType.DMA((2, fields)),
-        ],
+        scratch_shapes=[pltpu.VMEM((fields, nx, ny), jnp.float32), pltpu.SemaphoreType.DMA((fields,))],
         compiler_params=pltpu.CompilerParams(vmem_limit_bytes=32 << 20),
         cost_estimate=pl.CostEstimate(flops=velocity.size, bytes_accessed=velocity.size * 4, transcendentals=0),
         name="wind_faces",
@@ -263,7 +238,7 @@
             faces = [ref[pl.ds(base, half), :] for ref in (ylo_ref, yhi_ref)]
 
             def face(which, f, to):
-                moved = pltpu.roll(faces[which], (to - f) % LANES, 1) if f != to else faces[which]
+                moved = pltpu.roll(faces[which], (to - f - which) % LANES, 1) if f + which != to else faces[which]
                 return jnp.concatenate([moved] * halves, axis=1)
 
             for z in range(levels):
@@ -413,26 +388,15 @@
     *outs, rings, sems = refs
     both_rows = rings.shape[1]
     borders = border_tiles(tiles_x, tiles_y)
-    used = sorted({t for _, tiles in borders for t in tiles})
+    used = list(dict.fromkeys(t for _, tiles in borders for t in tiles))
 
     def copy(t):
-        return pltpu.make_async_copy(recv_ref.at[owner_ref[t]], rings.at[t], sems.at[t])
+        return pltpu.make_async_copy(recv_ref.at[jnp.maximum(owner_ref[t], 0)], rings.at[t], sems.at[t])
 
     for t in used:
-
-        @pl.when(owner_ref[t] >= 0)
-        def _():
-            copy(t).start()
-
-        @pl.when(owner_ref[t] < 0)
-        def _():
-            rings[t] = jnp.zeros(rings.shape[1:], jnp.float32)
-
+        copy(t).start()
     for t in used:
-
-        @pl.when(owner_ref[t] >= 0)
-        def _():
-            copy(t).wait()
+        copy(t).wait()
 
     lane = lax.broadcasted_iota(jnp.int32, (both_rows, LANES), 1) // TILE
     row8, lane8 = iotas()
@@ -442,11 +406,12 @@
             strips = winds = None
             for q in range(4):
                 t = tiles[4 * g + q]
-                strip, wind = rings[t], wind_ref[t, :ROWS, :]
+                active = owner_ref[t] >= 0
+                strip, wind = jnp.where(active, rings[t], 0.0), wind_ref[t, :ROWS, :]
                 if q != side:
                     strip = pltpu.roll(strip, ((q - side) * TILE) % LANES, 1)
                     wind = pltpu.roll(wind, ((q - side) * TILE) % LANES, 1)
-                wind = jnp.where(row8 == FLAG, jnp.where(owner_ref[t] >= 0, 1.0, 0.0), wind)
+                wind = jnp.where(row8 == FLAG, jnp.where(active, 1.0, 0.0), wind)
                 strips = strip if strips is None else jnp.where(lane == q, strip, strips)
                 winds = wind if winds is None else jnp.where(group8 == q, wind, winds)
             at = g * (both_rows + ROWS)
@@ -1004,7 +969,7 @@
 
 
 def dust_outer_kernel(
-    home_ref, inner_hbm, matrix_ref, effect_hbm, out_hbm, effect, dust, effect_sems, load_sems, sems, *, block, bins
+    home_ref, inner_hbm, matrix_ref, effect_hbm, out_hbm, effect, dust, added, effect_sems, load_sems, sems, *, block, bins
 ):
     slots = dust.shape[0]
     rows = TZ * bins
@@ -1026,11 +991,14 @@
         load(i).start()
         return carry
 
-    lax.fori_loop(0, slots // block, start, 0)
-
-    def one(i, carry):
+    count = slots // block
+    lax.fori_loop(0, count, start, 0)
+
+    def wait_for(i):
         for j in range(block):
             arrive(i * block + j).wait()
+
+    def expand(i):
         rings = jnp.concatenate(
             [
                 jnp.concatenate([effect[i * block + j, depth * rows : (depth + 1) * rows, :] for depth in range(2)], axis=1)
@@ -1038,21 +1006,34 @@
             ],
             axis=0,
         )
-        added = jnp.dot(
+        return jnp.dot(
             jnp.concatenate(halves_of(rings), axis=1), matrix_ref[...], preferred_element_type=jnp.float32
         )
+
+    wait_for(0)
+    added[0] = expand(0)
+
+    def one(i, carry):
+        later = jnp.minimum(i + 1, count - 1)
+
+        @pl.when(i + 1 < count)
+        def _():
+            wait_for(later)
+
         load(i).wait()
+        now = lax.rem(i, 2)
+        added[1 - now] = expand(later)
         for j in range(block):
             for r in range(ROWS):
                 for level in range(TZ):
                     at = pl.ds(r * TZ + level, bins, stride=ROWS * TZ)
                     first = j * rows + level * bins
-                    dust[i * block + j, at, :] += added[first : first + bins, r * LANES : (r + 1) * LANES]
+                    dust[i * block + j, at, :] += added[now, first : first + bins, r * LANES : (r + 1) * LANES]
         store(i).start()
         return carry
 
-    lax.fori_loop(0, slots // block, one, 0)
-    for i in range(slots // block):
+    lax.fori_loop(0, count, one, 0)
+    for i in range(count):
         store(i).wait()
 
 
@@ -1069,6 +1050,7 @@
         scratch_shapes=[
             pltpu.VMEM((slots,) + effect.shape[1:], jnp.float32),
             pltpu.VMEM(inner.shape, jnp.float32),
+            pltpu.VMEM((2, block * bins * TZ, TILE * TILE), jnp.float32),
             pltpu.SemaphoreType.DMA((slots,)),
             pltpu.SemaphoreType.DMA((slots // block,)),
             pltpu.SemaphoreType.DMA((slots // block,)),

time: 214 us -> 213 us (level)
  no operation moved by 1% of the time
where the time goes in v8:
time: 213 us; the launch traced here: 212 us
  Pallas kernels  110 us (52%)
  waiting for transfers between devices  61.1 us (29%)
  starting transfers between devices  38.8 us (18%)
    all_to_all x3, waiting for transfers between devices, relay_rows(): return lax.all_to_all(rows, AXES, split_axis=0, concat_axis=0, tiled=True)  49.4 us
    pallas_call x1, Pallas kernels, wind_step(): pl.pallas_call(functools.partial(wind_kernel, levels=levels), in_specs=[s...  40 us
    pallas_call x4, Pallas kernels, call(): pl.pallas_call(functools.partial(kernel, tiles_x=tiles_x, tiles_y=tiles_y...  29.7 us
    all_to_all x3, starting transfers between devices, relay_rows(): return lax.all_to_all(rows, AXES, split_axis=0, concat_axis=0, tiled=True)  23.1 us
    pallas_call x1, Pallas kernels, dust_inner(): pl.pallas_call(functools.partial(dust_kernel, block=block, bins=bins), gr...  21.8 us
    ppermute x10, starting transfers between devices, shifted(): lax.ppermute(value, axis, [(source, (source + steps) % count) for source...  15.8 us
    ppermute x10, waiting for transfers between devices, shifted(): lax.ppermute(value, axis, [(source, (source + steps) % count) for source...  11.8 us
    pallas_call x1, Pallas kernels, dust_outer(): pl.pallas_call(functools.partial(dust_outer_kernel, block=block, bins=bin...  9.69 us
  transfers between devices with their start and end apart: 13, of which 6 were waited for; matrix products, arithmetic and copies ran while one was open for 0% of the time, Pallas kernels for 45%

profile of v8, /device:TPU:1, one launch (start us, length us, event | category | flops | bytes accessed | tf_op | source)
XLA Modules:
  0.0 212.0 jit_solution(9339966714380202750)
XLA Ops:
  0.7 3.1 %wind_faces.1 = (f32[18,256]{1,0:T(8,128)S(1)}, f32[18,256]{1,0:T(8,128)S(1)}, f32[256,128]{1,0:T(8,128)S(1)}, f32[256,128]{1,0:T(8,128)S(1)}) custom-call(f32[18,256,256]{2,1,0:T(8,128)} %bitcast.14), custom_call_target="tpu_custom_call" | custom-call | flops 1179648 | bytes 4718592 | tf_op jit(solution)/shard_map/wind_faces/pallas_call | solution.py:203
  3.7 2.7 %collective-permute-start = (f32[18,256]{1,0:T(8,128)S(1)}, f32[18,256]{1,0:T(8,128)S(1)}, u32[]{:S(2)}, u32[]{:S(2)}) collective-permute-start(f32[18,256]{1,0:T(8,128)S(1)} %get-tuple-element.28), channel_id=1, source_target_pairs={{0,16},{16,32},{32,48},{48,64},{64,80},{80,96},{96,112},{112,0},{1... | collective-permute-start | bytes 55304 | tf_op jit(solution)/shard_map/ppermute | solution.py:766
  6.4 1.6 collective-permute-start.2
  8.1 4.3 %collective-permute-start.3 = (f32[256,128]{1,0:T(8,128)S(1)}, f32[256,128]{1,0:T(8,128)S(1)}, u32[]{:S(2)}, u32[]{:S(2)}) collective-permute-start(f32[256,128]{1,0:T(8,128)S(1)} %get-tuple-element.31), channel_id=1, source_target_pairs={{0,15},{1,0},{2,1},{3,2},{4,3},{5,4},{6,5},{7,6},{8,7},{9,8},{10,9... | collective-permute-start | bytes 393224 | tf_op jit(solution)/shard_map/ppermute | solution.py:766
  12.8 6.0 %dust_strips.1 = f32[128,64,128]{2,1,0:T(8,128)} custom-call(s32[56]{0:T(128)S(1)} %select_reduce_fusion.1.home_ref, f32[56,256,128]{2,1,0:T(8,128)} %bitcast.12, bf16[2048,256]{1,0:T(8,128)(2,1)S(1)} %copy-done.1), custom_call_target="tpu_custom_call" | custom-call | flops 36700160 | bytes 9175040 | tf_op jit(solution)/shard_map/dust_strips/pallas_call | solution.py:162
  18.8 7.1 %all-to-all-start = ((f32[128,64,128]{2,1,0:T(8,128)}), f32[128,64,128]{2,1,0:T(8,128)}, u32[]{:S(2)}, u32[]{:S(2)}) async-start(f32[128,64,128]{2,1,0:T(8,128)} %dust_strips.1), calls=%async_computation | async-start | bytes 8388608 | tf_op jit(solution)/shard_map/all_to_all | solution.py:770
  26.3 40.0 %wind_step.1 = (f32[18,256,256]{2,1,0:T(8,128)}, f32[128,56,128]{2,1,0:T(8,128)}, f32[64,16,128]{2,1,0:T(8,128)S(1)}) custom-call(s32[64]{0:T(128)S(1)} %select_reduce_fusion.owner_ref, f32[18,256,256]{2,1,0:T(8,128)} %bitcast.15, f32[18,256]{1,0:T(8,128)S(1)} %collective-permute-done.xlo_ref, f32[18,256]{1,0:T(8,128)S(1)} %collective-permute-done.1.xhi_ref, ...), custom_call_target="tpu_custom_call" | custom-call | flops 47185920 | bytes 11796480 | tf_op jit(solution)/shard_map/wind_step/pallas_call | solution.py:318
  66.3 11.7 %all-to-all-done.recv_ref = f32[128,64,128]{2,1,0:T(8,128)} async-done(((f32[128,64,128]{2,1,0:T(8,128)}), f32[128,64,128]{2,1,0:T(8,128)}, u32[]{:S(2)}, u32[]{:S(2)}) %all-to-all-start) | async-done | bytes 4194336 | tf_op jit(solution)/shard_map/all_to_all | solution.py:770
  78.0 2.5 %pack_borders.1 = (f32[144,128]{1,0:T(8,128)S(1)}, f32[144,128]{1,0:T(8,128)S(1)}, f32[144,128]{1,0:T(8,128)S(1)}, f32[144,128]{1,0:T(8,128)S(1)}) custom-call(s32[64]{0:T(128)S(1)} %select_reduce_fusion.owner_ref, f32[128,64,128]{2,1,0:T(8,128)} %all-to-all-done.recv_ref, f32[64,16,128]{2,1,0:T(8,128)S(1)} %get-tuple-element.42.wind_ref), custom_call_target="tpu_custom_call" | custom-call | flops 4194304 | bytes 4194304 | tf_op jit(solution)/shard_map/pack_borders/pallas_call | solution.py:785
  81.2 0.9 collective-permute-start.6
  82.1 3.9 %collective-permute-start.7 = (f32[144,128]{1,0:T(8,128)S(1)}, f32[144,128]{1,0:T(8,128)S(1)}, u32[]{:S(2)}, u32[]{:S(2)}) collective-permute-start(f32[144,128]{1,0:T(8,128)S(1)} %get-tuple-element.46.s_ref), channel_id=1, source_target_pairs={{0,15},{1,0},{2,1},{3,2},{4,3},{5,4},{6,5},{7,6},{8,7},{9,8},{10,9... | collective-permute-start | bytes 221192 | tf_op jit(solution)/shard_map/ppermute | solution.py:766
  86.0 1.7 collective-permute-done.6.fs_ref
  87.8 10.6 %all-to-all-start.1 = ((f32[128,56,128]{2,1,0:T(8,128)}), f32[128,56,128]{2,1,0:T(8,128)}, u32[]{:S(2)}, u32[]{:S(2)}) async-start(f32[128,56,128]{2,1,0:T(8,128)} %get-tuple-element.47), calls=%async_computation.1 | async-start | bytes 7340032 | tf_op jit(solution)/shard_map/all_to_all | solution.py:770
  98.4 1.6 collective-permute-start.8
  100.1 2.9 %gather_rings.1.rings_ref = f32[64,64,128]{2,1,0:T(8,128)S(1)} custom-call(s32[64]{0:T(128)S(1)} %select_reduce_fusion.owner_ref, f32[128,64,128]{2,1,0:T(8,128)} %all-to-all-done.recv_ref), custom_call_target="tpu_custom_call" | custom-call | flops 4194304 | bytes 4194304 | tf_op jit(solution)/shard_map/gather_rings/pallas_call | solution.py:785
  103.1 22.9 %send_seen.1 = (f32[128,64,128]{2,1,0:T(8,128)}, f32[4,64,128]{2,1,0:T(8,128)S(1)}) custom-call(s32[64]{0:T(128)S(1)} %select_reduce_fusion.owner_ref, f32[64,64,128]{2,1,0:T(8,128)S(1)} %gather_rings.1.rings_ref, f32[64,16,128]{2,1,0:T(8,128)S(1)} %get-tuple-element.42.wind_ref, f32[16,128]{1,0:T(8,128)S(1)} %broadcast_in_dim.35.settle_ref, ...), custom_call_target="tpu_custom_call" | custom-call | flops 4194304 | bytes 4194304 | tf_op jit(solution)/shard_map/send_seen/pallas_call | solution.py:785
  126.0 2.2 %collective-permute-done.8.cw_ref = f32[64,128]{1,0:T(8,128)S(1)} collective-permute-done((f32[64,128]{1,0:T(8,128)S(1)}, f32[64,128]{1,0:T(8,128)S(1)}, u32[]{:S(2)}, u32[]{:S(2)}) %collective-permute-start.8) | collective-permute-done | bytes 32800 | tf_op jit(solution)/shard_map/ppermute | solution.py:766
  128.1 7.9 %collective-permute-done.9.ce_ref = f32[64,128]{1,0:T(8,128)S(1)} collective-permute-done((f32[64,128]{1,0:T(8,128)S(1)}, f32[64,128]{1,0:T(8,128)S(1)}, u32[]{:S(2)}, u32[]{:S(2)}) %collective-permute-start.9) | collective-permute-done | bytes 32800 | tf_op jit(solution)/shard_map/ppermute | solution.py:766
  136.0 1.4 send_corners.1
  137.4 7.4 %all-to-all-done.1.wind_ref = f32[128,56,128]{2,1,0:T(8,128)} async-done(((f32[128,56,128]{2,1,0:T(8,128)}), f32[128,56,128]{2,1,0:T(8,128)}, u32[]{:S(2)}, u32[]{:S(2)}) %all-to-all-start.1) | async-done | bytes 3670048 | tf_op jit(solution)/shard_map/all_to_all | solution.py:770
  144.8 5.4 %all-to-all-start.2 = ((f32[128,64,128]{2,1,0:T(8,128)}), f32[128,64,128]{2,1,0:T(8,128)}, u32[]{:S(2)}, u32[]{:S(2)}) async-start(f32[128,64,128]{2,1,0:T(8,128)} %send_corners.1), calls=%async_computation.2 | async-start | bytes 8388608 | tf_op jit(solution)/shard_map/all_to_all | solution.py:770
  150.3 21.8 %dust_inner.1.inner_hbm = f32[56,256,128]{2,1,0:T(8,128)} custom-call(s32[56]{0:T(128)S(1)} %select_reduce_fusion.1.home_ref, f32[16,128]{1,0:T(8,128)S(1)} %broadcast_in_dim.34.share_ref, f32[16,128]{1,0:T(8,128)S(1)} %broadcast_in_dim.35.settle_ref, f32[56,256,128]{2,1,0:T(8,128)} %bitcast.13, bf16[256,512]{1,0:T(8,128)(2,1)S(1)} %copy-done.2, ...), custom_call_target="tpu_custom_call" | custom-call | flops 220200960 | bytes 22020096 | tf_op jit(solution)/shard_map/dust_inner/pallas_call | solution.py:957
  172.1 30.3 %all-to-all-done.2.effect_hbm = f32[128,64,128]{2,1,0:T(8,128)} async-done(((f32[128,64,128]{2,1,0:T(8,128)}), f32[128,64,128]{2,1,0:T(8,128)}, u32[]{:S(2)}, u32[]{:S(2)}) %all-to-all-start.2) | async-done | bytes 4194336 | tf_op jit(solution)/shard_map/all_to_all | solution.py:770
  202.4 9.7 %dust_outer.1 = f32[56,256,128]{2,1,0:T(8,128)} custom-call(s32[56]{0:T(128)S(1)} %select_reduce_fusion.1.home_ref, f32[56,256,128]{2,1,0:T(8,128)} %dust_inner.1.inner_hbm, bf16[512,1024]{1,0:T(8,128)(2,1)S(1)} %copy-done, f32[128,64,128]{2,1,0:T(8,128)} %all-to-all-done.2.effect_hbm), custom_call_target="tpu_custom_call" | custom-call | flops 3670016 | bytes 14680064 | tf_op jit(solution)/shard_map/dust_outer/pallas_call | solution.py:1045
  (36 shorter events, 1.6 us)
Async XLA Ops:
  0.6 12.1 %copy-start.1 = (bf16[2048,256]{1,0:T(8,128)(2,1)S(1)}, bf16[2048,256]{1,0:T(8,128)(2,1)}, u32[]{:S(2)}) copy-start(bf16[2048,256]{1,0:T(8,128)(2,1)} %constant.88.clone.matrix_ref) | copy-start | bytes 3145732
  0.6 11.8 %copy-start.5 = (s32[7168]{0:T(1024)S(1)}, s32[7168]{0:T(1024)}, u32[]{:S(2)}) copy-start(s32[7168]{0:T(1024)} %param.16) | copy-start | bytes 86020
  0.7 11.7 %copy-start.4 = (s32[7168]{0:T(1024)S(1)}, s32[7168]{0:T(1024)}, u32[]{:S(2)}) copy-start(s32[7168]{0:T(1024)} %param.15) | copy-start | bytes 86020
  3.7 15.0 %collective-permute-start = (f32[18,256]{1,0:T(8,128)S(1)}, f32[18,256]{1,0:T(8,128)S(1)}, u32[]{:S(2)}, u32[]{:S(2)}) collective-permute-start(f32[18,256]{1,0:T(8,128)S(1)} %get-tuple-element.28), channel_id=1, source_target_pairs={{0,16},{16,32},{32,48},{48,64},{64,80},{80,96},{96,112},{112,0},{1... | collective-permute-start | bytes 55304 | tf_op jit(solution)/shard_map/ppermute | solution.py:766
  6.4 12.4 %collective-permute-start.1 = (f32[18,256]{1,0:T(8,128)S(1)}, f32[18,256]{1,0:T(8,128)S(1)}, u32[]{:S(2)}, u32[]{:S(2)}) collective-permute-start(f32[18,256]{1,0:T(8,128)S(1)} %get-tuple-element.29), channel_id=1, source_target_pairs={{0,112},{16,0},{32,16},{48,32},{64,48},{80,64},{96,80},{112,96},{1... | collective-permute-start | bytes 55304 | tf_op jit(solution)/shard_map/ppermute | solution.py:766
  6.4 12.4 %collective-permute-start.2 = (f32[256,128]{1,0:T(8,128)S(1)}, f32[256,128]{1,0:T(8,128)S(1)}, u32[]{:S(2)}, u32[]{:S(2)}) collective-permute-start(f32[256,128]{1,0:T(8,128)S(1)} %get-tuple-element.30), channel_id=1, source_target_pairs={{0,1},{1,2},{2,3},{3,4},{4,5},{5,6},{6,7},{7,8},{8,9},{9,10},{10,1... | collective-permute-start | bytes 393224 | tf_op jit(solution)/shard_map/ppermute | solution.py:766
  8.1 10.7 %collective-permute-start.3 = (f32[256,128]{1,0:T(8,128)S(1)}, f32[256,128]{1,0:T(8,128)S(1)}, u32[]{:S(2)}, u32[]{:S(2)}) collective-permute-start(f32[256,128]{1,0:T(8,128)S(1)} %get-tuple-element.31), channel_id=1, source_target_pairs={{0,15},{1,0},{2,1},{3,2},{4,3},{5,4},{6,5},{7,6},{8,7},{9,8},{10,9... | collective-permute-start | bytes 393224 | tf_op jit(solution)/shard_map/ppermute | solution.py:766
  18.8 7.5 %copy-start.3 = (f32[256,256]{1,0:T(8,128)S(1)}, f32[256,256]{1,0:T(8,128)}, u32[]{:S(2)}) copy-start(f32[256,256]{1,0:T(8,128)} %thr_ref.1) | copy-start | bytes 786436
  18.8 59.2 %all-to-all-start = ((f32[128,64,128]{2,1,0:T(8,128)}), f32[128,64,128]{2,1,0:T(8,128)}, u32[]{:S(2)}, u32[]{:S(2)}) async-start(f32[128,64,128]{2,1,0:T(8,128)} %dust_strips.1), calls=%async_computation | async-start | bytes 8388608 | tf_op jit(solution)/shard_map/all_to_all | solution.py:770
  80.6 5.5 %collective-permute-start.4 = (f32[144,128]{1,0:T(8,128)S(1)}, f32[144,128]{1,0:T(8,128)S(1)}, u32[]{:S(2)}, u32[]{:S(2)}) collective-permute-start(f32[144,128]{1,0:T(8,128)S(1)} %get-tuple-element.43.e_ref), channel_id=1, source_target_pairs={{0,16},{16,32},{32,48},{48,64},{64,80},{80,96},{96,112},{112,0},{1... | collective-permute-start | bytes 221192 | tf_op jit(solution)/shard_map/ppermute | solution.py:766
  81.2 4.8 %collective-permute-start.5 = (f32[144,128]{1,0:T(8,128)S(1)}, f32[144,128]{1,0:T(8,128)S(1)}, u32[]{:S(2)}, u32[]{:S(2)}) collective-permute-start(f32[144,128]{1,0:T(8,128)S(1)} %get-tuple-element.44.w_ref), channel_id=1, source_target_pairs={{0,112},{16,0},{32,16},{48,32},{64,48},{80,64},{96,80},{112,96},{1... | collective-permute-start | bytes 221192 | tf_op jit(solution)/shard_map/ppermute | solution.py:766
  81.2 6.5 %collective-permute-start.6 = (f32[144,128]{1,0:T(8,128)S(1)}, f32[144,128]{1,0:T(8,128)S(1)}, u32[]{:S(2)}, u32[]{:S(2)}) collective-permute-start(f32[144,128]{1,0:T(8,128)S(1)} %get-tuple-element.45.n_ref), channel_id=1, source_target_pairs={{0,1},{1,2},{2,3},{3,4},{4,5},{5,6},{6,7},{7,8},{8,9},{9,10},{10,1... | collective-permute-start | bytes 221192 | tf_op jit(solution)/shard_map/ppermute | solution.py:766
  82.1 5.7 %collective-permute-start.7 = (f32[144,128]{1,0:T(8,128)S(1)}, f32[144,128]{1,0:T(8,128)S(1)}, u32[]{:S(2)}, u32[]{:S(2)}) collective-permute-start(f32[144,128]{1,0:T(8,128)S(1)} %get-tuple-element.46.s_ref), channel_id=1, source_target_pairs={{0,15},{1,0},{2,1},{3,2},{4,3},{5,4},{6,5},{7,6},{8,7},{9,8},{10,9... | collective-permute-start | bytes 221192 | tf_op jit(solution)/shard_map/ppermute | solution.py:766
  87.8 57.1 %all-to-all-start.1 = ((f32[128,56,128]{2,1,0:T(8,128)}), f32[128,56,128]{2,1,0:T(8,128)}, u32[]{:S(2)}, u32[]{:S(2)}) async-start(f32[128,56,128]{2,1,0:T(8,128)} %get-tuple-element.47), calls=%async_computation.1 | async-start | bytes 7340032 | tf_op jit(solution)/shard_map/all_to_all | solution.py:770
  98.4 4.6 %copy-start.6 = (f32[16]{0:T(128)S(1)}, f32[16]{0:T(128)}, u32[]{:S(2)}) copy-start(f32[16]{0:T(128)} %param.13) | copy-start | bytes 196
  98.4 4.7 %copy-start.7 = (f32[16]{0:T(128)S(1)}, f32[16]{0:T(128)}, u32[]{:S(2)}) copy-start(f32[16]{0:T(128)} %param.14) | copy-start | bytes 196
  98.4 29.7 %collective-permute-start.8 = (f32[64,128]{1,0:T(8,128)S(1)}, f32[64,128]{1,0:T(8,128)S(1)}, u32[]{:S(2)}, u32[]{:S(2)}) collective-permute-start(f32[64,128]{1,0:T(8,128)S(1)} %pad_maximum_fusion), channel_id=1, source_target_pairs={{0,16},{16,32},{32,48},{48,64},{64,80},{80,96},{96,112},{112,0},{1... | collective-permute-start | bytes 98312 | tf_op jit(solution)/shard_map/ppermute | solution.py:766
  100.1 36.0 %collective-permute-start.9 = (f32[64,128]{1,0:T(8,128)S(1)}, f32[64,128]{1,0:T(8,128)S(1)}, u32[]{:S(2)}, u32[]{:S(2)}) collective-permute-start(f32[64,128]{1,0:T(8,128)S(1)} %pad_maximum_fusion.1), channel_id=1, source_target_pairs={{0,112},{16,0},{32,16},{48,32},{64,48},{80,64},{96,80},{112,96},{1... | collective-permute-start | bytes 98312 | tf_op jit(solution)/shard_map/ppermute | solution.py:766
  137.4 12.8 %copy-start.2 = (bf16[256,512]{1,0:T(8,128)(2,1)S(1)}, bf16[256,512]{1,0:T(8,128)(2,1)}, u32[]{:S(2)}) copy-start(bf16[256,512]{1,0:T(8,128)(2,1)} %constant.89.clone.shift_ref) | copy-start | bytes 786436
  144.8 57.5 %all-to-all-start.2 = ((f32[128,64,128]{2,1,0:T(8,128)}), f32[128,64,128]{2,1,0:T(8,128)}, u32[]{:S(2)}, u32[]{:S(2)}) async-start(f32[128,64,128]{2,1,0:T(8,128)} %send_corners.1), calls=%async_computation.2 | async-start | bytes 8388608 | tf_op jit(solution)/shard_map/all_to_all | solution.py:770
  150.3 52.1 %copy-start = (bf16[512,1024]{1,0:T(8,128)(2,1)S(1)}, bf16[512,1024]{1,0:T(8,128)(2,1)}, u32[]{:S(2)}) copy-start(bf16[512,1024]{1,0:T(8,128)(2,1)} %constant.90.clone.matrix_ref) | copy-start | bytes 3145732

commit v9 on v8

--- a/solution.py
+++ b/solution.py
@@ -76,17 +76,31 @@
 def ring_matrix():
     lane = np.arange(LANES)
     group, within = lane // TILE, lane % TILE
+    on_y = (group == SOUTH) | (group == NORTH)
     blocks = []
-    for r in range(ROWS):
+    for p in range(ROWS // 2):
         columns = []
         for depth in range(2):
-            side = np.where(group == SOUTH, depth, TILE - 1 - depth)
-            source = np.where(within // 4 == r, (within % 4) * TILE + side, -1)
-            source = np.where(group == WEST, depth * TILE + within if r == 0 else -1, source)
-            source = np.where(group == EAST, (3 - depth) * TILE + within if r == ROWS - 1 else -1, source)
-            columns.append(source)
+            cell = (within % 4) * TILE + np.where(group == SOUTH, depth, TILE - 1 - depth)
+            source = np.where(within // 4 == p, cell, -1)
+            source = np.where(within // 4 == p + ROWS // 2, (cell + 4) % LANES, source)
+            columns.append(np.where(on_y, source, -1))
         blocks.append(moves(np.concatenate(columns)))
+    columns = [
+        np.where(group == WEST, depth * TILE + within, np.where(group == EAST, (3 - depth) * TILE + within, -1))
+        for depth in range(2)
+    ]
+    blocks.append(moves(np.concatenate(columns)))
     return np.concatenate(blocks, axis=0)
+
+
+def ring_parts(rows):
+    lane = lax.broadcasted_iota(jnp.int32, rows[0].shape, 1)
+    within = lane % TILE
+    kept = (within < 2) | (within >= TILE - 2)
+    half = len(rows) // 2
+    parts = [jnp.where(kept, rows[p], pltpu.roll(rows[p + half], 4, 1)) for p in range(half)]
+    return parts + [jnp.where(lane < LANES // 2, rows[0], rows[-1])]
 
 
 def shift_matrix():
@@ -122,9 +136,8 @@
 
     def one(i, carry):
         load(i).wait()
-        parts = []
-        for r in range(ROWS):
-            x = jnp.concatenate(
+        cells = [
+            jnp.concatenate(
                 [
                     dust[i * block + j, pl.ds(r * TZ + level, bins, stride=ROWS * TZ), :]
                     for j in range(block)
@@ -132,7 +145,9 @@
                 ],
                 axis=0,
             )
-            parts += halves_of(x)
+            for r in range(ROWS)
+        ]
+        parts = [half for x in ring_parts(cells) for half in halves_of(x)]
         found = jnp.dot(
             jnp.concatenate(parts, axis=1), matrix_ref[...], preferred_element_type=jnp.float32
         )

time: 213 us -> 213 us (level)
  no operation moved by 1% of the time
where the time goes in v9:
time: 213 us; the launch traced here: 212 us
  Pallas kernels  110 us (52%)
  waiting for transfers between devices  61.1 us (29%)
  starting transfers between devices  38.8 us (18%)
    all_to_all x3, waiting for transfers between devices, relay_rows(): return lax.all_to_all(rows, AXES, split_axis=0, concat_axis=0, tiled=True)  49.3 us
    pallas_call x1, Pallas kernels, wind_step(): pl.pallas_call(functools.partial(wind_kernel, levels=levels), in_specs=[s...  40 us
    pallas_call x4, Pallas kernels, call(): pl.pallas_call(functools.partial(kernel, tiles_x=tiles_x, tiles_y=tiles_y...  29.7 us
    all_to_all x3, starting transfers between devices, relay_rows(): return lax.all_to_all(rows, AXES, split_axis=0, concat_axis=0, tiled=True)  23.1 us
    pallas_call x1, Pallas kernels, dust_inner(): pl.pallas_call(functools.partial(dust_kernel, block=block, bins=bins), gr...  21.9 us
    ppermute x10, starting transfers between devices, shifted(): lax.ppermute(value, axis, [(source, (source + steps) % count) for source...  15.8 us
    ppermute x10, waiting for transfers between devices, shifted(): lax.ppermute(value, axis, [(source, (source + steps) % count) for source...  11.8 us
    pallas_call x1, Pallas kernels, dust_outer(): pl.pallas_call(functools.partial(dust_outer_kernel, block=block, bins=bin...  9.69 us
  transfers between devices with their start and end apart: 13, of which 6 were waited for; matrix products, arithmetic and copies ran while one was open for 0% of the time, Pallas kernels for 45%

profile of v9, /device:TPU:1, one launch (start us, length us, event | category | flops | bytes accessed | tf_op | source)
XLA Modules:
  0.0 212.1 jit_solution(5264436350919632811)
XLA Ops:
  0.7 3.0 %wind_faces.1 = (f32[18,256]{1,0:T(8,128)S(1)}, f32[18,256]{1,0:T(8,128)S(1)}, f32[256,128]{1,0:T(8,128)S(1)}, f32[256,128]{1,0:T(8,128)S(1)}) custom-call(f32[18,256,256]{2,1,0:T(8,128)} %bitcast.14), custom_call_target="tpu_custom_call" | custom-call | flops 1179648 | bytes 4718592 | tf_op jit(solution)/shard_map/wind_faces/pallas_call | solution.py:218
  3.7 2.7 %collective-permute-start = (f32[18,256]{1,0:T(8,128)S(1)}, f32[18,256]{1,0:T(8,128)S(1)}, u32[]{:S(2)}, u32[]{:S(2)}) collective-permute-start(f32[18,256]{1,0:T(8,128)S(1)} %get-tuple-element.28), channel_id=1, source_target_pairs={{0,16},{16,32},{32,48},{48,64},{64,80},{80,96},{96,112},{112,0},{1... | collective-permute-start | bytes 55304 | tf_op jit(solution)/shard_map/ppermute | solution.py:781
  6.4 1.6 collective-permute-start.2
  8.0 4.3 %collective-permute-start.3 = (f32[256,128]{1,0:T(8,128)S(1)}, f32[256,128]{1,0:T(8,128)S(1)}, u32[]{:S(2)}, u32[]{:S(2)}) collective-permute-start(f32[256,128]{1,0:T(8,128)S(1)} %get-tuple-element.31), channel_id=1, source_target_pairs={{0,15},{1,0},{2,1},{3,2},{4,3},{5,4},{6,5},{7,6},{8,7},{9,8},{10,9... | collective-permute-start | bytes 393224 | tf_op jit(solution)/shard_map/ppermute | solution.py:781
  12.7 6.1 %dust_strips.1 = f32[128,64,128]{2,1,0:T(8,128)} custom-call(s32[56]{0:T(128)S(1)} %select_reduce_fusion.1.home_ref, f32[56,256,128]{2,1,0:T(8,128)} %bitcast.12, bf16[1280,256]{1,0:T(8,128)(2,1)S(1)} %copy-done.1), custom_call_target="tpu_custom_call" | custom-call | flops 36700160 | bytes 9175040 | tf_op jit(solution)/shard_map/dust_strips/pallas_call | solution.py:177
  18.9 7.1 %all-to-all-start = ((f32[128,64,128]{2,1,0:T(8,128)}), f32[128,64,128]{2,1,0:T(8,128)}, u32[]{:S(2)}, u32[]{:S(2)}) async-start(f32[128,64,128]{2,1,0:T(8,128)} %dust_strips.1), calls=%async_computation | async-start | bytes 8388608 | tf_op jit(solution)/shard_map/all_to_all | solution.py:785
  26.4 40.0 %wind_step.1 = (f32[18,256,256]{2,1,0:T(8,128)}, f32[128,56,128]{2,1,0:T(8,128)}, f32[64,16,128]{2,1,0:T(8,128)S(1)}) custom-call(s32[64]{0:T(128)S(1)} %select_reduce_fusion.owner_ref, f32[18,256,256]{2,1,0:T(8,128)} %bitcast.15, f32[18,256]{1,0:T(8,128)S(1)} %collective-permute-done.xlo_ref, f32[18,256]{1,0:T(8,128)S(1)} %collective-permute-done.1.xhi_ref, ...), custom_call_target="tpu_custom_call" | custom-call | flops 47185920 | bytes 11796480 | tf_op jit(solution)/shard_map/wind_step/pallas_call | solution.py:333
  66.4 11.7 %all-to-all-done.recv_ref = f32[128,64,128]{2,1,0:T(8,128)} async-done(((f32[128,64,128]{2,1,0:T(8,128)}), f32[128,64,128]{2,1,0:T(8,128)}, u32[]{:S(2)}, u32[]{:S(2)}) %all-to-all-start) | async-done | bytes 4194336 | tf_op jit(solution)/shard_map/all_to_all | solution.py:785
  78.1 2.5 %pack_borders.1 = (f32[144,128]{1,0:T(8,128)S(1)}, f32[144,128]{1,0:T(8,128)S(1)}, f32[144,128]{1,0:T(8,128)S(1)}, f32[144,128]{1,0:T(8,128)S(1)}) custom-call(s32[64]{0:T(128)S(1)} %select_reduce_fusion.owner_ref, f32[128,64,128]{2,1,0:T(8,128)} %all-to-all-done.recv_ref, f32[64,16,128]{2,1,0:T(8,128)S(1)} %get-tuple-element.42.wind_ref), custom_call_target="tpu_custom_call" | custom-call | flops 4194304 | bytes 4194304 | tf_op jit(solution)/shard_map/pack_borders/pallas_call | solution.py:800
  81.3 0.9 collective-permute-start.6
  82.2 3.9 %collective-permute-start.7 = (f32[144,128]{1,0:T(8,128)S(1)}, f32[144,128]{1,0:T(8,128)S(1)}, u32[]{:S(2)}, u32[]{:S(2)}) collective-permute-start(f32[144,128]{1,0:T(8,128)S(1)} %get-tuple-element.46.s_ref), channel_id=1, source_target_pairs={{0,15},{1,0},{2,1},{3,2},{4,3},{5,4},{6,5},{7,6},{8,7},{9,8},{10,9... | collective-permute-start | bytes 221192 | tf_op jit(solution)/shard_map/ppermute | solution.py:781
  86.1 1.7 collective-permute-done.6.fs_ref
  87.9 10.6 %all-to-all-start.1 = ((f32[128,56,128]{2,1,0:T(8,128)}), f32[128,56,128]{2,1,0:T(8,128)}, u32[]{:S(2)}, u32[]{:S(2)}) async-start(f32[128,56,128]{2,1,0:T(8,128)} %get-tuple-element.47), calls=%async_computation.1 | async-start | bytes 7340032 | tf_op jit(solution)/shard_map/all_to_all | solution.py:785
  98.5 1.6 collective-permute-start.8
  100.2 2.9 %gather_rings.1.rings_ref = f32[64,64,128]{2,1,0:T(8,128)S(1)} custom-call(s32[64]{0:T(128)S(1)} %select_reduce_fusion.owner_ref, f32[128,64,128]{2,1,0:T(8,128)} %all-to-all-done.recv_ref), custom_call_target="tpu_custom_call" | custom-call | flops 4194304 | bytes 4194304 | tf_op jit(solution)/shard_map/gather_rings/pallas_call | solution.py:800
  103.2 22.9 %send_seen.1 = (f32[128,64,128]{2,1,0:T(8,128)}, f32[4,64,128]{2,1,0:T(8,128)S(1)}) custom-call(s32[64]{0:T(128)S(1)} %select_reduce_fusion.owner_ref, f32[64,64,128]{2,1,0:T(8,128)S(1)} %gather_rings.1.rings_ref, f32[64,16,128]{2,1,0:T(8,128)S(1)} %get-tuple-element.42.wind_ref, f32[16,128]{1,0:T(8,128)S(1)} %broadcast_in_dim.35.settle_ref, ...), custom_call_target="tpu_custom_call" | custom-call | flops 4194304 | bytes 4194304 | tf_op jit(solution)/shard_map/send_seen/pallas_call | solution.py:800
  126.1 2.2 %collective-permute-done.8.cw_ref = f32[64,128]{1,0:T(8,128)S(1)} collective-permute-done((f32[64,128]{1,0:T(8,128)S(1)}, f32[64,128]{1,0:T(8,128)S(1)}, u32[]{:S(2)}, u32[]{:S(2)}) %collective-permute-start.8) | collective-permute-done | bytes 32800 | tf_op jit(solution)/shard_map/ppermute | solution.py:781
  128.2 7.9 %collective-permute-done.9.ce_ref = f32[64,128]{1,0:T(8,128)S(1)} collective-permute-done((f32[64,128]{1,0:T(8,128)S(1)}, f32[64,128]{1,0:T(8,128)S(1)}, u32[]{:S(2)}, u32[]{:S(2)}) %collective-permute-start.9) | collective-permute-done | bytes 32800 | tf_op jit(solution)/shard_map/ppermute | solution.py:781
  136.1 1.4 send_corners.1
  137.5 7.4 %all-to-all-done.1.wind_ref = f32[128,56,128]{2,1,0:T(8,128)} async-done(((f32[128,56,128]{2,1,0:T(8,128)}), f32[128,56,128]{2,1,0:T(8,128)}, u32[]{:S(2)}, u32[]{:S(2)}) %all-to-all-start.1) | async-done | bytes 3670048 | tf_op jit(solution)/shard_map/all_to_all | solution.py:785
  144.9 5.4 %all-to-all-start.2 = ((f32[128,64,128]{2,1,0:T(8,128)}), f32[128,64,128]{2,1,0:T(8,128)}, u32[]{:S(2)}, u32[]{:S(2)}) async-start(f32[128,64,128]{2,1,0:T(8,128)} %send_corners.1), calls=%async_computation.2 | async-start | bytes 8388608 | tf_op jit(solution)/shard_map/all_to_all | solution.py:785
  150.4 21.9 %dust_inner.1.inner_hbm = f32[56,256,128]{2,1,0:T(8,128)} custom-call(s32[56]{0:T(128)S(1)} %select_reduce_fusion.1.home_ref, f32[16,128]{1,0:T(8,128)S(1)} %broadcast_in_dim.34.share_ref, f32[16,128]{1,0:T(8,128)S(1)} %broadcast_in_dim.35.settle_ref, f32[56,256,128]{2,1,0:T(8,128)} %bitcast.13, bf16[256,512]{1,0:T(8,128)(2,1)S(1)} %copy-done.2, ...), custom_call_target="tpu_custom_call" | custom-call | flops 220200960 | bytes 22020096 | tf_op jit(solution)/shard_map/dust_inner/pallas_call | solution.py:972
  172.2 30.2 %all-to-all-done.2.effect_hbm = f32[128,64,128]{2,1,0:T(8,128)} async-done(((f32[128,64,128]{2,1,0:T(8,128)}), f32[128,64,128]{2,1,0:T(8,128)}, u32[]{:S(2)}, u32[]{:S(2)}) %all-to-all-start.2) | async-done | bytes 4194336 | tf_op jit(solution)/shard_map/all_to_all | solution.py:785
  202.4 9.7 %dust_outer.1 = f32[56,256,128]{2,1,0:T(8,128)} custom-call(s32[56]{0:T(128)S(1)} %select_reduce_fusion.1.home_ref, f32[56,256,128]{2,1,0:T(8,128)} %dust_inner.1.inner_hbm, bf16[512,1024]{1,0:T(8,128)(2,1)S(1)} %copy-done, f32[128,64,128]{2,1,0:T(8,128)} %all-to-all-done.2.effect_hbm), custom_call_target="tpu_custom_call" | custom-call | flops 3670016 | bytes 14680064 | tf_op jit(solution)/shard_map/dust_outer/pallas_call | solution.py:1060
  (36 shorter events, 1.6 us)
Async XLA Ops:
  0.6 12.1 %copy-start.1 = (bf16[1280,256]{1,0:T(8,128)(2,1)S(1)}, bf16[1280,256]{1,0:T(8,128)(2,1)}, u32[]{:S(2)}) copy-start(bf16[1280,256]{1,0:T(8,128)(2,1)} %constant.88.clone.matrix_ref) | copy-start | bytes 1966084
  0.6 11.7 %copy-start.5 = (s32[7168]{0:T(1024)S(1)}, s32[7168]{0:T(1024)}, u32[]{:S(2)}) copy-start(s32[7168]{0:T(1024)} %param.16) | copy-start | bytes 86020
  0.7 11.7 %copy-start.4 = (s32[7168]{0:T(1024)S(1)}, s32[7168]{0:T(1024)}, u32[]{:S(2)}) copy-start(s32[7168]{0:T(1024)} %param.15) | copy-start | bytes 86020
  3.7 15.1 %collective-permute-start = (f32[18,256]{1,0:T(8,128)S(1)}, f32[18,256]{1,0:T(8,128)S(1)}, u32[]{:S(2)}, u32[]{:S(2)}) collective-permute-start(f32[18,256]{1,0:T(8,128)S(1)} %get-tuple-element.28), channel_id=1, source_target_pairs={{0,16},{16,32},{32,48},{48,64},{64,80},{80,96},{96,112},{112,0},{1... | collective-permute-start | bytes 55304 | tf_op jit(solution)/shard_map/ppermute | solution.py:781
  6.4 12.5 %collective-permute-start.1 = (f32[18,256]{1,0:T(8,128)S(1)}, f32[18,256]{1,0:T(8,128)S(1)}, u32[]{:S(2)}, u32[]{:S(2)}) collective-permute-start(f32[18,256]{1,0:T(8,128)S(1)} %get-tuple-element.29), channel_id=1, source_target_pairs={{0,112},{16,0},{32,16},{48,32},{64,48},{80,64},{96,80},{112,96},{1... | collective-permute-start | bytes 55304 | tf_op jit(solution)/shard_map/ppermute | solution.py:781
  6.4 12.5 %collective-permute-start.2 = (f32[256,128]{1,0:T(8,128)S(1)}, f32[256,128]{1,0:T(8,128)S(1)}, u32[]{:S(2)}, u32[]{:S(2)}) collective-permute-start(f32[256,128]{1,0:T(8,128)S(1)} %get-tuple-element.30), channel_id=1, source_target_pairs={{0,1},{1,2},{2,3},{3,4},{4,5},{5,6},{6,7},{7,8},{8,9},{9,10},{10,1... | collective-permute-start | bytes 393224 | tf_op jit(solution)/shard_map/ppermute | solution.py:781
  8.0 10.8 %collective-permute-start.3 = (f32[256,128]{1,0:T(8,128)S(1)}, f32[256,128]{1,0:T(8,128)S(1)}, u32[]{:S(2)}, u32[]{:S(2)}) collective-permute-start(f32[256,128]{1,0:T(8,128)S(1)} %get-tuple-element.31), channel_id=1, source_target_pairs={{0,15},{1,0},{2,1},{3,2},{4,3},{5,4},{6,5},{7,6},{8,7},{9,8},{10,9... | collective-permute-start | bytes 393224 | tf_op jit(solution)/shard_map/ppermute | solution.py:781
  18.8 7.5 %copy-start.3 = (f32[256,256]{1,0:T(8,128)S(1)}, f32[256,256]{1,0:T(8,128)}, u32[]{:S(2)}) copy-start(f32[256,256]{1,0:T(8,128)} %thr_ref.1) | copy-start | bytes 786436
  18.9 59.2 %all-to-all-start = ((f32[128,64,128]{2,1,0:T(8,128)}), f32[128,64,128]{2,1,0:T(8,128)}, u32[]{:S(2)}, u32[]{:S(2)}) async-start(f32[128,64,128]{2,1,0:T(8,128)} %dust_strips.1), calls=%async_computation | async-start | bytes 8388608 | tf_op jit(solution)/shard_map/all_to_all | solution.py:785
  80.6 5.5 %collective-permute-start.4 = (f32[144,128]{1,0:T(8,128)S(1)}, f32[144,128]{1,0:T(8,128)S(1)}, u32[]{:S(2)}, u32[]{:S(2)}) collective-permute-start(f32[144,128]{1,0:T(8,128)S(1)} %get-tuple-element.43.e_ref), channel_id=1, source_target_pairs={{0,16},{16,32},{32,48},{48,64},{64,80},{80,96},{96,112},{112,0},{1... | collective-permute-start | bytes 221192 | tf_op jit(solution)/shard_map/ppermute | solution.py:781
  81.3 4.8 %collective-permute-start.5 = (f32[144,128]{1,0:T(8,128)S(1)}, f32[144,128]{1,0:T(8,128)S(1)}, u32[]{:S(2)}, u32[]{:S(2)}) collective-permute-start(f32[144,128]{1,0:T(8,128)S(1)} %get-tuple-element.44.w_ref), channel_id=1, source_target_pairs={{0,112},{16,0},{32,16},{48,32},{64,48},{80,64},{96,80},{112,96},{1... | collective-permute-start | bytes 221192 | tf_op jit(solution)/shard_map/ppermute | solution.py:781
  81.3 6.5 %collective-permute-start.6 = (f32[144,128]{1,0:T(8,128)S(1)}, f32[144,128]{1,0:T(8,128)S(1)}, u32[]{:S(2)}, u32[]{:S(2)}) collective-permute-start(f32[144,128]{1,0:T(8,128)S(1)} %get-tuple-element.45.n_ref), channel_id=1, source_target_pairs={{0,1},{1,2},{2,3},{3,4},{4,5},{5,6},{6,7},{7,8},{8,9},{9,10},{10,1... | collective-permute-start | bytes 221192 | tf_op jit(solution)/shard_map/ppermute | solution.py:781
  82.2 5.7 %collective-permute-start.7 = (f32[144,128]{1,0:T(8,128)S(1)}, f32[144,128]{1,0:T(8,128)S(1)}, u32[]{:S(2)}, u32[]{:S(2)}) collective-permute-start(f32[144,128]{1,0:T(8,128)S(1)} %get-tuple-element.46.s_ref), channel_id=1, source_target_pairs={{0,15},{1,0},{2,1},{3,2},{4,3},{5,4},{6,5},{7,6},{8,7},{9,8},{10,9... | collective-permute-start | bytes 221192 | tf_op jit(solution)/shard_map/ppermute | solution.py:781
  87.9 57.1 %all-to-all-start.1 = ((f32[128,56,128]{2,1,0:T(8,128)}), f32[128,56,128]{2,1,0:T(8,128)}, u32[]{:S(2)}, u32[]{:S(2)}) async-start(f32[128,56,128]{2,1,0:T(8,128)} %get-tuple-element.47), calls=%async_computation.1 | async-start | bytes 7340032 | tf_op jit(solution)/shard_map/all_to_all | solution.py:785
  98.4 4.6 %copy-start.6 = (f32[16]{0:T(128)S(1)}, f32[16]{0:T(128)}, u32[]{:S(2)}) copy-start(f32[16]{0:T(128)} %param.13) | copy-start | bytes 196
  98.4 4.7 %copy-start.7 = (f32[16]{0:T(128)S(1)}, f32[16]{0:T(128)}, u32[]{:S(2)}) copy-start(f32[16]{0:T(128)} %param.14) | copy-start | bytes 196
  98.5 29.7 %collective-permute-start.8 = (f32[64,128]{1,0:T(8,128)S(1)}, f32[64,128]{1,0:T(8,128)S(1)}, u32[]{:S(2)}, u32[]{:S(2)}) collective-permute-start(f32[64,128]{1,0:T(8,128)S(1)} %pad_maximum_fusion), channel_id=1, source_target_pairs={{0,16},{16,32},{32,48},{48,64},{64,80},{80,96},{96,112},{112,0},{1... | collective-permute-start | bytes 98312 | tf_op jit(solution)/shard_map/ppermute | solution.py:781
  100.2 36.0 %collective-permute-start.9 = (f32[64,128]{1,0:T(8,128)S(1)}, f32[64,128]{1,0:T(8,128)S(1)}, u32[]{:S(2)}, u32[]{:S(2)}) collective-permute-start(f32[64,128]{1,0:T(8,128)S(1)} %pad_maximum_fusion.1), channel_id=1, source_target_pairs={{0,112},{16,0},{32,16},{48,32},{64,48},{80,64},{96,80},{112,96},{1... | collective-permute-start | bytes 98312 | tf_op jit(solution)/shard_map/ppermute | solution.py:781
  137.5 12.8 %copy-start.2 = (bf16[256,512]{1,0:T(8,128)(2,1)S(1)}, bf16[256,512]{1,0:T(8,128)(2,1)}, u32[]{:S(2)}) copy-start(bf16[256,512]{1,0:T(8,128)(2,1)} %constant.89.clone.shift_ref) | copy-start | bytes 786436
  144.9 57.5 %all-to-all-start.2 = ((f32[128,64,128]{2,1,0:T(8,128)}), f32[128,64,128]{2,1,0:T(8,128)}, u32[]{:S(2)}, u32[]{:S(2)}) async-start(f32[128,64,128]{2,1,0:T(8,128)} %send_corners.1), calls=%async_computation.2 | async-start | bytes 8388608 | tf_op jit(solution)/shard_map/all_to_all | solution.py:785
  150.3 52.1 %copy-start = (bf16[512,1024]{1,0:T(8,128)(2,1)S(1)}, bf16[512,1024]{1,0:T(8,128)(2,1)}, u32[]{:S(2)}) copy-start(bf16[512,1024]{1,0:T(8,128)(2,1)} %constant.90.clone.matrix_ref) | copy-start | bytes 3145732
